TPU v7x, 32 devices: a whole 2x2x4 slice. The times are simulated.
32 devices in a mesh: groups: 2 (over y), blk: 4 (over z), shard: 2 (over x), sub: 2 (over core).
Axes of the slice: x: 2, y: 2, z: 4, core: 2. Of those that a mesh axis runs over, the one named last changes fastest.
Arguments:
- embeddings: bfloat16 [4096, 1024], P(('groups', 'blk', 'shard', 'sub')), parts along dimension 0, may hold values from -100 to 100
- assignment: int32 [4096, 1], P(('groups', 'blk', 'shard', 'sub')), parts along dimension 0, may hold values from 0 to 15, as said below
Outputs:
- best_similarity: float32 [4096], P(('groups', 'blk', 'shard', 'sub')), parts along dimension 0
There are 2 independent parts, one for each index of `groups`. A program takes and returns all parts, laid end to end along the dimension named above; each array names one. Nothing has to cross between parts.
Inputs may be any that keep to these rules, and one draw needn't show every extreme that they name: `assignment`: among the 128 rows of one device at most 16 belong to one cluster; one cluster has exactly 16 rows on every device; every cluster has at least one row in the group.
All inputs are finite; a program needn't handle non-finite values.
Results may differ from a plain program's by a relative error of at most 0.0013.
Values may be sent and summed in bfloat16 or wider, within the bound.
No kernel may reach another device: no remote copies, remote signals or barrier semaphores. Data moves between devices by JAX's collectives and lax.ppermute only.
A program may use at most 64 MiB of HBM per device.

v0:
```python
import math

import jax
import jax.numpy as jnp
from jax import lax
from jax.sharding import PartitionSpec as P

CLUSTERS = 16
CAP = 16


def normalize(embeddings):
    values = embeddings.astype(jnp.float32)
    scaled = values * lax.rsqrt(jnp.mean(values * values, axis=1, keepdims=True) + 1e-06)
    return (scaled * (1.0 / math.sqrt(values.shape[1]))).astype(jnp.bfloat16)


def local(embeddings, assignment):
    unit_rows = normalize(embeddings)
    owners = lax.axis_size("blk")
    group_slots = CLUSTERS // owners * CAP
    slot_count = CLUSTERS * CAP
    cluster = assignment[:, 0]
    labels = jnp.arange(CLUSTERS, dtype=jnp.int32)
    member = (cluster[:, None] == labels[None, :]).astype(jnp.int32)
    earlier = jnp.cumsum(member, axis=0) - member
    within = jnp.sum(earlier * member, axis=1)
    target = cluster * CAP + within
    send_units = jnp.zeros((slot_count, unit_rows.shape[1]), jnp.bfloat16).at[target].set(unit_rows)
    send_valid = jnp.zeros((slot_count,), jnp.int32).at[target].set(1)
    got_units, got_valid = (
        lax.all_to_all(send_units, "blk", split_axis=0, concat_axis=0, tiled=True),
        lax.all_to_all(send_valid, "blk", split_axis=0, concat_axis=0, tiled=True),
    )
    cycle_index = lax.axis_index(("shard", "sub"))
    slot_pos = jnp.arange(slot_count, dtype=jnp.int32)
    slot_cluster = slot_pos % group_slots // CAP
    own_global = cycle_index * slot_count + slot_pos
    initial = jnp.full((slot_count,), -2.0, jnp.float32)
    other_units = lax.all_gather(got_units, ("shard", "sub"), axis=0, tiled=True)
    other_valid = lax.all_gather(got_valid, ("shard", "sub"), axis=0, tiled=True)
    global_pos = jnp.arange(other_units.shape[0], dtype=jnp.int32)
    other_cluster = global_pos % group_slots // CAP
    kept_pairs = (slot_cluster[:, None] == other_cluster[None, :]) & (other_valid[None, :] > 0)
    kept_pairs = kept_pairs & (own_global[:, None] != global_pos[None, :])
    masked = jnp.where(
        kept_pairs,
        lax.dot_general(
            got_units, other_units, (((1,), (1,)), ((), ())), preferred_element_type=jnp.float32
        ),
        -2.0,
    )
    best_slots = jnp.maximum(initial, jnp.max(masked, axis=1))
    returned_best = lax.all_to_all(best_slots, "blk", split_axis=0, concat_axis=0, tiled=True)
    return returned_best[target]


def solution(mesh):
    placed = (
        P(("groups", "blk", "shard", "sub"), None),
        P(("groups", "blk", "shard", "sub"), None),
    )
    return jax.shard_map(
        local,
        mesh=mesh,
        in_specs=placed,
        out_specs=P(("groups", "blk", "shard", "sub")),
        check_vma=False,
    )
```

profile of v0, /device:TPU:0, one launch (start us, length us, event | category | flops | bytes accessed | tf_op | source)
XLA Modules:
  0.0 77.8 jit_solution(8044981641400999283)
XLA Ops:
  6.5 0.0 all-gather.3.cloned.1.call-start
  6.5 1.1 %fusion.2 = f32[128]{0:T(128)S(1)} fusion(bf16[128,1024]{1,0:T(8,128)(2,1)} %param.2), kind=kLoop, calls=%fused_computation.9 | loop fusion | flops 393088 | bytes 262656 | tf_op jit(solution)/shard_map/reduce_sum | solution.py:14
  7.6 0.7 fusion.10
  8.4 0.2 reduce_window_sum.11
  8.6 0.8 %select_reduce_fusion = s32[128]{0:T(128)S(1)} fusion(s32[128,16]{1,0:T(8,128)S(1)} %reduce_window_sum.11, s32[128]{0:T(128)} %bitcast.21), kind=kLoop, calls=%fused_computation.16 | loop fusion | flops 10112 | bytes 9216 | tf_op jit(solution)/shard_map/reduce_sum | solution.py:27
  9.4 0.7 fusion.17
  10.1 1.8 %scatter_custom_fusion.1 = bf16[256,1024]{1,0:T(8,128)(2,1)S(1)} fusion(s32[128]{0:T(128)S(1)} %fusion.17, bf16[128,1024]{1,0:T(8,128)(2,1)} %param.2, f32[]{:T(128)} %constant.84.clone.1, f32[128]{0:T(128)S(1)} %add_rsqrt_fusion, bf16[]{:T(256)} %constant.80.clone.1), kind=kCustom, calls=%fused_computation.12 | custom fusion | flops 524288 | bytes 786950 | tf_op jit(solution)/shard_map/scatter | solution.py:29
  11.9 20.7 %all_to_all.33 = bf16[4,64,1024]{2,1,0:T(8,128)(2,1)} all-to-all(bf16[4,64,1024]{2,1,0:T(8,128)(2,1)S(1)} %bitcast.19), channel_id=1, replica_groups=mesh['groups'=2,'blk'=4,'shard'=2,'sub'=2] {'blk'}, dimensions={0} | all-to-all | bytes 1048576 | tf_op jit(solution)/shard_map/all_to_all | solution.py:32
  32.6 0.0 all-gather.3.cloned.1.call-update
  32.6 1.0 %scatter_custom_fusion = s32[256]{0:T(256)S(1)} fusion(s32[128]{0:T(128)S(1)} %fusion.17, s32[128]{0:T(128)S(1)} %broadcast.149, s32[]{:T(128)} %constant.70.clone.1), kind=kCustom, calls=%fused_computation.45 | custom fusion | bytes 1028 | tf_op jit(solution)/shard_map/scatter | solution.py:30
  33.6 0.7 all_to_all.22
  34.3 3.2 %all-to-all-start = ((s32[4,64,1]{1,2,0:T(1,128)}), s32[4,64,1]{1,2,0:T(1,128)S(1)}, u32[]{:S(2)}, u32[]{:S(2)}) async-start(s32[4,64,1]{1,2,0:T(1,128)} %bitcast.3), calls=%async_computation | async-start | bytes 4096 | tf_op jit(solution)/shard_map/all_to_all | solution.py:33
  37.5 5.5 %all-to-all-done = s32[4,64,1]{1,2,0:T(1,128)S(1)} async-done(((s32[4,64,1]{1,2,0:T(1,128)}), s32[4,64,1]{1,2,0:T(1,128)S(1)}, u32[]{:S(2)}, u32[]{:S(2)}) %all-to-all-start) | async-done | bytes 1056 | tf_op jit(solution)/shard_map/all_to_all | solution.py:33
  42.9 0.5 broadcast.169
  43.5 0.7 reduce.8
  44.1 0.1 reshape.105
  44.2 5.1 %all-gather = s32[4,1,256]{2,1,0:T(1,128)S(1)} all-gather(s32[1,1,256]{2,1,0:T(1,128)S(1)} %reshape.105), channel_id=1, replica_groups=mesh['groups'=2,'blk'=4,'shard'=2,'sub'=2] {'shard','sub'}, dimensions={0}, use_global_device_ids=true | all-gather | bytes 5120 | tf_op jit(solution)/shard_map/all_gather | solution.py:41
  49.3 5.2 %all-gather.3.cloned.1.call-done = bf16[1024,1024]{1,0:T(8,128)(2,1)} async-done(((bf16[256,1024]{1,0:T(8,128)(2,1)}), bf16[1024,1024]{1,0:T(8,128)(2,1)}) %all-gather.3.cloned.1.call-update) | async-done | bytes 2097168 | tf_op jit(solution)/shard_map/all_gather | solution.py:40
  54.5 2.7 %fusion = f32[256]{0:T(256)S(1)} fusion(bf16[256,1024]{1,0:T(8,128)(2,1)} %bitcast.18, bf16[1024,1024]{1,0:T(8,128)(2,1)} %all-gather.3.cloned.1.call-done, s32[256]{0:T(256)S(1)} %get-tuple-element.6, s32[1024]{0:T(1024)S(1)} %add_select_fusion, s32[256]{0:T(256)S(1)} %get-tuple-element.5, pred[1024]{0:T(1024)(128)(4,1)S(1)} %reshape.108), kind=kOutput, calls=%fused_computation.4 | convolution fusion | flops 538443520 | bytes 2629632 | tf_op jit(solution)/shard_map/dot_general | solution.py:48
  57.2 0.7 max_broadcast_in_dim.14
  57.9 4.6 %all-to-all-start.2 = ((f32[4,64,1]{1,2,0:T(1,128)}), f32[4,64,1]{1,2,0:T(1,128)S(1)}, u32[]{:S(2)}, u32[]{:S(2)}) async-start(f32[4,64,1]{1,2,0:T(1,128)} %bitcast.6), calls=%async_computation.2 | async-start | bytes 4096 | tf_op jit(solution)/shard_map/all_to_all | solution.py:54
  62.5 5.4 %all-to-all-done.2 = f32[4,64,1]{1,2,0:T(1,128)S(1)} async-done(((f32[4,64,1]{1,2,0:T(1,128)}), f32[4,64,1]{1,2,0:T(1,128)S(1)}, u32[]{:S(2)}, u32[]{:S(2)}) %all-to-all-start.2) | async-done | bytes 1056 | tf_op jit(solution)/shard_map/all_to_all | solution.py:54
  67.9 0.5 broadcast.170
  68.4 0.7 reduce.9
  69.1 0.1 all_to_all.29
  69.1 1.8 %gather_fusion = f32[128]{0:T(128)} fusion(f32[256]{0:T(256)S(1)} %all_to_all.29, s32[1024]{0:T(1024)S(1)} %pad_clamp_fusion), kind=kCustom, calls=%fused_computation | custom fusion | bytes 1536 | tf_op jit(solution)/shard_map/gather | solution.py:55
  (8 shorter events, 0.1 us)
Async XLA Ops:
  6.5 47.9 %all-gather.3.cloned.1.call-start = ((), (), s32[]{:S(2)}) async-start(), calls=%async_computation.3 | async-start | bytes 2621440 | tf_op jit(solution)/shard_map/all_gather | solution.py:40
  34.3 8.7 %all-to-all-start = ((s32[4,64,1]{1,2,0:T(1,128)}), s32[4,64,1]{1,2,0:T(1,128)S(1)}, u32[]{:S(2)}, u32[]{:S(2)}) async-start(s32[4,64,1]{1,2,0:T(1,128)} %bitcast.3), calls=%async_computation | async-start | bytes 4096 | tf_op jit(solution)/shard_map/all_to_all | solution.py:33
  57.9 10.0 %all-to-all-start.2 = ((f32[4,64,1]{1,2,0:T(1,128)}), f32[4,64,1]{1,2,0:T(1,128)S(1)}, u32[]{:S(2)}, u32[]{:S(2)}) async-start(f32[4,64,1]{1,2,0:T(1,128)} %bitcast.6), calls=%async_computation.2 | async-start | bytes 4096 | tf_op jit(solution)/shard_map/all_to_all | solution.py:54
Sparse Core Ops, SparseCore 0:
  32.7 21.7 all-gather.2
where the time goes:
time: 78.1 us; the launch traced here: 77.8 us
  blocking collectives  25.8 us (33%)
  waiting for transfers between devices  16 us (20%)
  between operations  13.5 us (17%)
  starting transfers between devices  7.78 us (10%)
  other arithmetic  6.68 us (9%)
  local copies, waits for them, and re-layouts  5.28 us (7%)
  matrix products  2.72 us (3%)
    all_to_all x1, blocking collectives, local(): lax.all_to_all(send_units, 'blk', split_axis=0, concat_axis=0, tiled=True)  20.7 us
    all_to_all x1, waiting for transfers between devices, local(): lax.all_to_all(send_valid, 'blk', split_axis=0, concat_axis=0, tiled=True)  5.48 us
    all_to_all x1, waiting for transfers between devices, local(): lax.all_to_all(best_slots, 'blk', split_axis=0, concat_axis=0, tiled=True)  5.38 us
    all_gather x1, waiting for transfers between devices, local(): lax.all_gather(got_units, ('shard', 'sub'), axis=0, tiled=True)  5.17 us
    all_gather x1, blocking collectives, local(): lax.all_gather(got_valid, ('shard', 'sub'), axis=0, tiled=True)  5.06 us
    all_to_all x1, starting transfers between devices, local(): lax.all_to_all(best_slots, 'blk', split_axis=0, concat_axis=0, tiled=True)  4.6 us
    all_to_all x1, starting transfers between devices, local(): lax.all_to_all(send_valid, 'blk', split_axis=0, concat_axis=0, tiled=True)  3.17 us
    dot_general x1, matrix products, local(): lax.dot_general(got_units, other_units, (((1,), (1,)), ((), ())), preferr...  2.72 us
  transfers between devices with their start and end apart: 3, of which 3 were waited for; matrix products, arithmetic and copies ran while one was open for 3% of the time, Pallas kernels for 0%

commit v1 on v0

v1 whole, which is shorter than its diff:
```python
import functools
import math

import jax
import jax.numpy as jnp
from jax import lax
from jax.experimental import pallas as pl
from jax.experimental.pallas import tpu as pltpu
from jax.sharding import PartitionSpec as P

CLUSTERS = 16
CAP = 16
SLOTS = CLUSTERS * CAP
LANES = 128
EMPTY = 4.0
NONE = -2.0

VMEM = pl.BlockSpec(memory_space=pltpu.VMEM)


def placement(cluster):
    rows = cluster.shape[1]
    label = lax.broadcasted_iota(jnp.int32, (CLUSTERS, rows), 0)
    member = (cluster == label).astype(jnp.float32)
    before = lax.broadcasted_iota(jnp.int32, (rows, rows), 0) < lax.broadcasted_iota(
        jnp.int32, (rows, rows), 1
    )
    earlier = jnp.dot(
        member.astype(jnp.bfloat16),
        before.astype(jnp.float32).astype(jnp.bfloat16),
        preferred_element_type=jnp.float32,
    )
    within = jnp.sum(earlier * member, axis=0, keepdims=True).astype(jnp.int32)
    target = cluster * CAP + within
    return lax.broadcasted_iota(jnp.int32, (SLOTS, rows), 0) == target


def pack_kernel(rows_ref, cluster_ref, out_ref):
    values = rows_ref[...].astype(jnp.float32)
    width = values.shape[1]
    scaled = values * lax.rsqrt(jnp.mean(values * values, axis=1, keepdims=True) + 1e-06)
    unit = (scaled * (1.0 / math.sqrt(width))).astype(jnp.bfloat16)
    placed = placement(cluster_ref[...]).astype(jnp.float32)
    slots = jnp.dot(placed.astype(jnp.bfloat16), unit, preferred_element_type=jnp.float32)
    used = jnp.sum(placed, axis=1, keepdims=True)
    first = lax.broadcasted_iota(jnp.int32, slots.shape, 1) == 0
    slots = jnp.where(first & (used < 0.5), EMPTY, slots)
    out_ref[...] = slots.astype(jnp.bfloat16)


def pack(embeddings, assignment):
    rows, width = embeddings.shape
    return pl.pallas_call(
        pack_kernel,
        out_shape=jax.ShapeDtypeStruct((SLOTS, width), jnp.bfloat16),
        in_specs=[VMEM] * 2,
        out_specs=VMEM,
        name="pack",
    )(embeddings, assignment.reshape(1, rows))


def best_kernel(count, slots_ref, others_ref, first_ref, out_ref, best_ref):
    step = pl.program_id(0)
    slots, others = slots_ref[...], others_ref[...]
    similar = lax.dot_general(
        others, slots, (((1,), (1,)), ((), ())), preferred_element_type=jnp.float32
    )
    used = others[:, :1].astype(jnp.float32) < 2.0
    row = lax.broadcasted_iota(jnp.int32, similar.shape, 0)
    column = lax.broadcasted_iota(jnp.int32, similar.shape, 1)
    kept = used & (row + step * slots.shape[0] != column + first_ref[0, 0])
    if count > CAP:
        kept = kept & (row % count // CAP == column % count // CAP)
    best = jnp.max(jnp.where(kept, similar, NONE), axis=0, keepdims=True)

    @pl.when(step == 0)
    def _():
        best_ref[...] = best

    @pl.when(step > 0)
    def _():
        best_ref[...] = jnp.maximum(best_ref[...], best)

    @pl.when(step == pl.num_programs(0) - 1)
    def _():
        for source in range(out_ref.shape[0]):
            piece = best_ref[:, source * count : (source + 1) * count]
            out_ref[source, :, :count] = jnp.broadcast_to(piece, (8, count))
            if count < LANES:
                out_ref[source, :, count:] = jnp.full((8, LANES - count), NONE)


def best_of(slots, others, first, owners):
    size, width = slots.shape
    count = size // owners
    return pl.pallas_call(
        functools.partial(best_kernel, count),
        grid=(others.shape[0] // size,),
        out_shape=jax.ShapeDtypeStruct((owners, 8, LANES), jnp.float32),
        in_specs=[
            pl.BlockSpec((size, width), lambda i: (0, 0)),
            pl.BlockSpec((size, width), lambda i: (i, 0)),
            pl.BlockSpec((1, 1), lambda i: (0, 0), memory_space=pltpu.SMEM),
        ],
        out_specs=pl.BlockSpec((owners, 8, LANES), lambda i: (0, 0, 0)),
        scratch_shapes=[pltpu.VMEM((1, size), jnp.float32)],
        name="best",
    )(slots, others, first)


def unpack_kernel(returned_ref, cluster_ref, out_ref):
    owners = returned_ref.shape[0]
    count = SLOTS // owners
    placed = placement(cluster_ref[...])
    returned = jnp.broadcast_to(returned_ref[:, :1, :], (owners, count, LANES)).reshape(SLOTS, LANES)
    slot = lax.broadcasted_iota(jnp.int32, (SLOTS, LANES), 0) % count
    lane = lax.broadcasted_iota(jnp.int32, (SLOTS, LANES), 1)
    by_slot = jnp.max(jnp.where(slot == lane, returned, NONE), axis=1, keepdims=True)
    out_ref[...] = jnp.max(jnp.where(placed, by_slot, NONE), axis=0, keepdims=True)


def unpack(returned, assignment):
    rows = assignment.shape[0]
    return pl.pallas_call(
        unpack_kernel,
        out_shape=jax.ShapeDtypeStruct((1, rows), jnp.float32),
        in_specs=[VMEM] * 2,
        out_specs=VMEM,
        name="unpack",
    )(returned, assignment.reshape(1, rows))


def local(route, gather, embeddings, assignment):
    send = pack(embeddings, assignment)
    got = lax.all_to_all(send, route, split_axis=0, concat_axis=0, tiled=True)
    owners = lax.axis_size(route)
    if gather:
        others = lax.all_gather(got, gather, axis=0, tiled=True)
        first = (lax.axis_index(gather) * SLOTS).astype(jnp.int32).reshape(1, 1)
    else:
        others, first = got, jnp.zeros((1, 1), jnp.int32)
    best = best_of(got, others, first, owners)
    returned = lax.all_to_all(best, route, split_axis=0, concat_axis=0, tiled=True)
    return unpack(returned, assignment).reshape(-1)


def solution(mesh):
    placed = (
        P(("groups", "blk", "shard", "sub"), None),
        P(("groups", "blk", "shard", "sub"), None),
    )
    axes = ("blk", "shard", "sub")
    split = 3 if CLUSTERS % math.prod(mesh.shape[a] for a in axes) == 0 else 1
    return jax.shard_map(
        functools.partial(local, axes[:split], axes[split:]),
        mesh=mesh,
        in_specs=placed,
        out_specs=P(("groups", "blk", "shard", "sub")),
        check_vma=False,
    )
```

time: 78.1 us -> 39.4 us (0.50)
  waiting for transfers between devices: 16 us -> 0 us
  between operations: 13.5 us -> 0.01 us
  starting transfers between devices: 7.78 us -> 0 us
  blocking collectives: 25.8 us -> 33 us
  other arithmetic: 6.68 us -> 0 us
  Pallas kernels: 0 us -> 5.96 us
  local copies, waits for them, and re-layouts: 5.28 us -> 0 us
  matrix products: 2.72 us -> 0 us
    all_to_all x1 -> x2, blocking collectives: 20.7 us -> 33 us  [the longest x1 21.9 us: local(): got = lax.all_to_all(send, route, split_axis=0, concat_axis=0, tiled=True)]
    all_to_all x2 -> x0, waiting for transfers between devices: 10.9 us -> none  [the longest x1 5.48 us: local(): lax.all_to_all(send_valid, 'blk', split_axis=0, concat_axis=0, tiled=True)]
    all_to_all x2 -> x0, starting transfers between devices: 7.77 us -> none  [the longest x1 4.6 us: local(): lax.all_to_all(best_slots, 'blk', split_axis=0, concat_axis=0, tiled=True)]
    pallas_call x0 -> x3, Pallas kernels: none -> 5.96 us  [the longest x1 2.26 us: best_of(): pl.pallas_call(functools.partial(best_kernel, count), grid=(others.shape[...]
    all_gather x1 -> x0, waiting for transfers between devices: 5.17 us -> none  [local(): lax.all_gather(got_units, ('shard', 'sub'), axis=0, tiled=True)]
    all_gather x1 -> x0, blocking collectives: 5.06 us -> none  [local(): lax.all_gather(got_valid, ('shard', 'sub'), axis=0, tiled=True)]
    dot_general x1 -> x0, matrix products: 2.72 us -> none  [local(): lax.dot_general(got_units, other_units, (((1,), (1,)), ((), ())), preferr...]
    reduce_sum x2 -> x0, other arithmetic: 1.91 us -> none  [the longest x1 1.08 us: normalize(): jnp.mean(values * values, axis=1, keepdims=True) + 1e-06]
  transfers between devices with their start and end apart: 3 -> 0, of which waited for: 3 -> 0; matrix products, arithmetic and copies ran while one was open for 3% -> 0% of each run, Pallas kernels for 0% -> 0%
where the time goes in v1:
time: 39.4 us; the launch traced here: 39 us
  blocking collectives  33 us (84%)
  Pallas kernels  5.96 us (15%)
    all_to_all x1, blocking collectives, local(): got = lax.all_to_all(send, route, split_axis=0, concat_axis=0, tiled=True)  21.9 us
    all_to_all x1, blocking collectives, local(): lax.all_to_all(best, route, split_axis=0, concat_axis=0, tiled=True)  11.1 us
    pallas_call x1, Pallas kernels, best_of(): pl.pallas_call(functools.partial(best_kernel, count), grid=(others.shape[...  2.26 us
    pallas_call x1, Pallas kernels, pack(): pl.pallas_call(pack_kernel, out_shape=jax.ShapeDtypeStruct((SLOTS, width)...  2.18 us
    pallas_call x1, Pallas kernels, unpack(): pl.pallas_call(unpack_kernel, out_shape=jax.ShapeDtypeStruct((1, rows), j...  1.52 us

profile of v1, /device:TPU:0, one launch (start us, length us, event | category | flops | bytes accessed | tf_op | source)
XLA Modules:
  0.0 39.0 jit_solution(18341050650873204419)
XLA Ops:
  0.0 2.2 %pack.1 = bf16[256,1024]{1,0:T(8,128)(2,1)} custom-call(bf16[128,1024]{1,0:T(8,128)(2,1)} %rows_ref.1, s32[1,128]{1,0:T(1,128)} %bitcast.7), custom_call_target="tpu_custom_call" | custom-call | tf_op jit(solution)/shard_map/pack/pallas_call | solution.py:53
  2.2 21.9 %all_to_all.16 = bf16[16,16,1024]{2,1,0:T(8,128)(2,1)} all-to-all(bf16[16,16,1024]{2,1,0:T(8,128)(2,1)} %bitcast.6), channel_id=1, replica_groups=mesh['groups'=2,'blk'=4,'shard'=2,'sub'=2] {'blk','shard','sub'}, dimensions={0} | all-to-all | bytes 1048576 | tf_op jit(solution)/shard_map/all_to_all | solution.py:135
  24.1 2.3 %best.1 = f32[16,8,128]{2,1,0:T(8,128)} custom-call(bf16[256,1024]{1,0:T(8,128)(2,1)} %bitcast.4, bf16[256,1024]{1,0:T(8,128)(2,1)} %bitcast.5, s32[1,1]{1,0:T(1,128)} %constant.0.clone.1.first_ref), custom_call_target="tpu_custom_call" | custom-call | tf_op jit(solution)/shard_map/best/pallas_call | solution.py:96
  26.4 11.1 %all_to_all.17.returned_ref = f32[16,8,128]{2,1,0:T(8,128)} all-to-all(f32[16,8,128]{2,1,0:T(8,128)} %best.1), channel_id=1, replica_groups=mesh['groups'=2,'blk'=4,'shard'=2,'sub'=2] {'blk','shard','sub'}, dimensions={0} | all-to-all | bytes 131072 | tf_op jit(solution)/shard_map/all_to_all | solution.py:143
  37.5 1.5 %unpack.1 = f32[1,128]{1,0:T(1,128)} custom-call(f32[16,8,128]{2,1,0:T(8,128)} %all_to_all.17.returned_ref, s32[1,128]{1,0:T(1,128)} %bitcast.8), custom_call_target="tpu_custom_call" | custom-call | tf_op jit(solution)/shard_map/unpack/pallas_call | solution.py:124

commit v2 on v1

v2 whole, which is shorter than its diff:
```python
import functools
import math

import jax
import jax.numpy as jnp
from jax import lax
from jax.experimental import pallas as pl
from jax.experimental.pallas import tpu as pltpu
from jax.sharding import PartitionSpec as P

CLUSTERS = 16
CAP = 16
SLOTS = CLUSTERS * CAP
LANES = 128
EMPTY = 4.0
NONE = -2.0
AXES = ("blk", "shard", "sub")

VMEM = pl.BlockSpec(memory_space=pltpu.VMEM)
SMEM = pl.BlockSpec(memory_space=pltpu.SMEM)


def placement(cluster, flip):
    rows = cluster.shape[1]
    label = lax.broadcasted_iota(jnp.int32, (CLUSTERS, rows), 0)
    member = (cluster == label).astype(jnp.float32)
    before = lax.broadcasted_iota(jnp.int32, (rows, rows), 0) < lax.broadcasted_iota(
        jnp.int32, (rows, rows), 1
    )
    earlier = jnp.dot(
        member.astype(jnp.bfloat16),
        before.astype(jnp.float32).astype(jnp.bfloat16),
        preferred_element_type=jnp.float32,
    )
    within = jnp.sum(earlier * member, axis=0, keepdims=True).astype(jnp.int32)
    target = (cluster ^ flip) * CAP + within
    return lax.broadcasted_iota(jnp.int32, (SLOTS, rows), 0) == target


def pack_kernel(flip_ref, rows_ref, cluster_ref, *out_refs):
    values = rows_ref[...].astype(jnp.float32)
    width = values.shape[1]
    scaled = values * lax.rsqrt(jnp.mean(values * values, axis=1, keepdims=True) + 1e-06)
    unit = (scaled * (1.0 / math.sqrt(width))).astype(jnp.bfloat16)
    placed = placement(cluster_ref[...], flip_ref[0, 0]).astype(jnp.float32)
    slots = jnp.dot(placed.astype(jnp.bfloat16), unit, preferred_element_type=jnp.float32)
    used = jnp.sum(placed, axis=1, keepdims=True)
    first = lax.broadcasted_iota(jnp.int32, slots.shape, 1) == 0
    slots = jnp.where(first & (used < 0.5), EMPTY, slots).astype(jnp.bfloat16)
    count = SLOTS // len(out_refs)
    for block, out_ref in enumerate(out_refs):
        out_ref[...] = slots[block * count : (block + 1) * count]


def pack(flip, embeddings, assignment, blocks):
    rows, width = embeddings.shape
    return pl.pallas_call(
        pack_kernel,
        out_shape=[jax.ShapeDtypeStruct((SLOTS // blocks, width), jnp.bfloat16)] * blocks,
        in_specs=[SMEM, VMEM, VMEM],
        out_specs=[VMEM] * blocks,
        name="pack",
    )(flip, embeddings, assignment.reshape(1, rows))


def best_kernel(*refs):
    half = len(refs) // 2
    slots = jnp.concatenate([ref[...] for ref in refs[:half]], axis=0)
    similar = lax.dot_general(
        slots, slots, (((1,), (1,)), ((), ())), preferred_element_type=jnp.float32
    )
    used = slots[:, :1].astype(jnp.float32) < 2.0
    row = lax.broadcasted_iota(jnp.int32, similar.shape, 0)
    column = lax.broadcasted_iota(jnp.int32, similar.shape, 1)
    best = jnp.max(jnp.where(used & (row != column), similar, NONE), axis=0, keepdims=True)
    for block, out_ref in enumerate(refs[half:]):
        piece = best[:, block * CAP : (block + 1) * CAP]
        out_ref[:, :CAP] = jnp.broadcast_to(piece, (8, CAP))
        out_ref[:, CAP:] = jnp.full((8, LANES - CAP), NONE)


def best_of(blocks):
    return pl.pallas_call(
        best_kernel,
        out_shape=[jax.ShapeDtypeStruct((8, LANES), jnp.float32)] * len(blocks),
        in_specs=[VMEM] * len(blocks),
        out_specs=[VMEM] * len(blocks),
        name="best",
    )(*blocks)


def shared_best_kernel(count, first_ref, slots_ref, others_ref, out_ref, best_ref):
    step = pl.program_id(0)
    slots, others = slots_ref[...], others_ref[...]
    similar = lax.dot_general(
        others, slots, (((1,), (1,)), ((), ())), preferred_element_type=jnp.float32
    )
    used = others[:, :1].astype(jnp.float32) < 2.0
    row = lax.broadcasted_iota(jnp.int32, similar.shape, 0)
    column = lax.broadcasted_iota(jnp.int32, similar.shape, 1)
    kept = used & (row + step * slots.shape[0] != column + first_ref[0, 0])
    kept = kept & (row % count // CAP == column % count // CAP)
    best = jnp.max(jnp.where(kept, similar, NONE), axis=0, keepdims=True)

    @pl.when(step == 0)
    def _():
        best_ref[...] = best

    @pl.when(step > 0)
    def _():
        best_ref[...] = jnp.maximum(best_ref[...], best)

    @pl.when(step == pl.num_programs(0) - 1)
    def _():
        for source in range(out_ref.shape[0]):
            piece = best_ref[:, source * count : (source + 1) * count]
            out_ref[source, :, :count] = jnp.broadcast_to(piece, (8, count))
            if count < LANES:
                out_ref[source, :, count:] = jnp.full((8, LANES - count), NONE)


def shared_best_of(slots, others, first, owners):
    size, width = slots.shape
    return pl.pallas_call(
        functools.partial(shared_best_kernel, size // owners),
        grid=(others.shape[0] // size,),
        out_shape=jax.ShapeDtypeStruct((owners, 8, LANES), jnp.float32),
        in_specs=[
            pl.BlockSpec((1, 1), lambda i: (0, 0), memory_space=pltpu.SMEM),
            pl.BlockSpec((size, width), lambda i: (0, 0)),
            pl.BlockSpec((size, width), lambda i: (i, 0)),
        ],
        out_specs=pl.BlockSpec((owners, 8, LANES), lambda i: (0, 0, 0)),
        scratch_shapes=[pltpu.VMEM((1, size), jnp.float32)],
        name="shared_best",
    )(first, slots, others)


def unpack_kernel(flip_ref, cluster_ref, *refs):
    returned_refs, out_ref = refs[:-1], refs[-1]
    count = SLOTS // len(returned_refs)
    placed = placement(cluster_ref[...], flip_ref[0, 0])
    returned = jnp.concatenate(
        [jnp.broadcast_to(ref[:1, :], (count, LANES)) for ref in returned_refs], axis=0
    )
    slot = lax.broadcasted_iota(jnp.int32, (SLOTS, LANES), 0) % count
    lane = lax.broadcasted_iota(jnp.int32, (SLOTS, LANES), 1)
    by_slot = jnp.max(jnp.where(slot == lane, returned, NONE), axis=1, keepdims=True)
    out_ref[...] = jnp.max(jnp.where(placed, by_slot, NONE), axis=0, keepdims=True)


def unpack(flip, returned, assignment):
    rows = assignment.shape[0]
    return pl.pallas_call(
        unpack_kernel,
        out_shape=jax.ShapeDtypeStruct((1, rows), jnp.float32),
        in_specs=[SMEM, VMEM] + [VMEM] * len(returned),
        out_specs=VMEM,
        name="unpack",
    )(flip, assignment.reshape(1, rows), *returned).reshape(-1)


def exchange(blocks):
    size = len(blocks)
    return [blocks[0]] + [
        lax.ppermute(blocks[r], AXES, [(i, i ^ r) for i in range(size)]) for r in range(1, size)
    ]


def one_owner(embeddings, assignment):
    flip = lax.axis_index(AXES).astype(jnp.int32).reshape(1, 1)
    sent = pack(flip, embeddings, assignment, CLUSTERS)
    best = best_of(exchange(sent))
    return unpack(flip, exchange(best), assignment)


def shared_owner(embeddings, assignment):
    route, gather = AXES[:1], AXES[1:]
    owners = lax.axis_size(route)
    flip = jnp.zeros((1, 1), jnp.int32)
    (sent,) = pack(flip, embeddings, assignment, 1)
    got = lax.all_to_all(sent, route, split_axis=0, concat_axis=0, tiled=True)
    others = lax.all_gather(got, gather, axis=0, tiled=True)
    first = (lax.axis_index(gather) * SLOTS).astype(jnp.int32).reshape(1, 1)
    best = shared_best_of(got, others, first, owners)
    returned = lax.all_to_all(best, route, split_axis=0, concat_axis=0, tiled=True)
    return unpack(flip, [returned[i] for i in range(owners)], assignment)


def solution(mesh):
    placed = (
        P(("groups", "blk", "shard", "sub"), None),
        P(("groups", "blk", "shard", "sub"), None),
    )
    one = math.prod(mesh.shape[axis] for axis in AXES) == CLUSTERS
    return jax.shard_map(
        one_owner if one else shared_owner,
        mesh=mesh,
        in_specs=placed,
        out_specs=P(("groups", "blk", "shard", "sub")),
        check_vma=False,
    )
```

time: 39.4 us -> 58.9 us (1.49)
  starting transfers between devices: 0 us -> 43 us
  blocking collectives: 33 us -> 0 us
  waiting for transfers between devices: 0 us -> 8.56 us
  local copies, waits for them, and re-layouts: 0 us -> 1.12 us
    ppermute x0 -> x30, starting transfers between devices: none -> 43 us  [exchange(): lax.ppermute(blocks[r], AXES, [(i, i ^ r) for i in range(size)])]
    all_to_all x2 -> x0, blocking collectives: 33 us -> none  [the longest x1 21.9 us: local(): got = lax.all_to_all(send, route, split_axis=0, concat_axis=0, tiled=True)]
    ppermute x0 -> x30, waiting for transfers between devices: none -> 8.56 us  [exchange(): lax.ppermute(blocks[r], AXES, [(i, i ^ r) for i in range(size)])]
    unnamed x0 -> x74, local copies, waits for them, and re-layouts: none -> 1.12 us
  transfers between devices with their start and end apart: 0 -> 30, of which waited for: 0 -> 5; matrix products, arithmetic and copies ran while one was open for 0% -> 0% of each run, Pallas kernels for 0% -> 0%
where the time goes in v2:
time: 58.9 us; the launch traced here: 58.6 us
  starting transfers between devices  43 us (73%)
  waiting for transfers between devices  8.56 us (15%)
  Pallas kernels  5.65 us (10%)
  local copies, waits for them, and re-layouts  1.12 us (2%)
    ppermute x30, starting transfers between devices, exchange(): lax.ppermute(blocks[r], AXES, [(i, i ^ r) for i in range(size)])  43 us
    ppermute x30, waiting for transfers between devices, exchange(): lax.ppermute(blocks[r], AXES, [(i, i ^ r) for i in range(size)])  8.56 us
    pallas_call x1, Pallas kernels, pack(): pl.pallas_call(pack_kernel, out_shape=[jax.ShapeDtypeStruct((SLOTS // blo...  2.12 us
    pallas_call x1, Pallas kernels, best_of(): pl.pallas_call(best_kernel, out_shape=[jax.ShapeDtypeStruct((8, LANES), j...  2.08 us
    pallas_call x1, Pallas kernels, unpack(): pl.pallas_call(unpack_kernel, out_shape=jax.ShapeDtypeStruct((1, rows), j...  1.44 us
  transfers between devices with their start and end apart: 30, of which 5 were waited for; matrix products, arithmetic and copies ran while one was open for 0% of the time, Pallas kernels for 0%

profile of v2, /device:TPU:0, one launch (start us, length us, event | category | flops | bytes accessed | tf_op | source)
XLA Modules:
  0.0 58.6 jit_solution(5197697170416633715)
XLA Ops:
  0.0 2.1 %pack.1 = (bf16[16,1024]{1,0:T(8,128)(2,1)}, bf16[16,1024]{1,0:T(8,128)(2,1)}, bf16[16,1024]{1,0:T(8,128)(2,1)}, bf16[16,1024]{1,0:T(8,128)(2,1)}, bf16[16,1024]...) custom-call(s32[1,1]{1,0:T(1,128)} %bitcast.flip_ref, ...), custom_call_target="tpu_custom_call" | custom-call | tf_op jit(solution)/shard_map/pack/pallas_call | solution.py:57
  2.1 0.5 collective-permute-start
  2.6 2.6 %collective-permute-start.1 = (bf16[16,1024]{1,0:T(8,128)(2,1)}, bf16[16,1024]{1,0:T(8,128)(2,1)S(1)}, u32[]{:S(2)}, u32[]{:S(2)}) collective-permute-start(bf16[16,1024]{1,0:T(8,128)(2,1)} %get-tuple-element.39), channel_id=1, source_target_pairs={{0,2},{1,3},{2,0},{3,1},{4,6},{5,7},{6,4},{7,5},{8,10},{9,11},{10,... | collective-permute-start | bytes 98312 | tf_op jit(solution)/shard_map/ppermute | solution.py:166
  5.2 0.1 collective-permute-start.2
  5.2 1.8 %collective-permute-start.3 = (bf16[16,1024]{1,0:T(8,128)(2,1)}, bf16[16,1024]{1,0:T(8,128)(2,1)S(1)}, u32[]{:S(2)}, u32[]{:S(2)}) collective-permute-start(bf16[16,1024]{1,0:T(8,128)(2,1)} %get-tuple-element.41), channel_id=1, source_target_pairs={{0,4},{1,5},{2,6},{3,7},{4,0},{5,1},{6,2},{7,3},{8,12},{9,13},{10,... | collective-permute-start | bytes 98312 | tf_op jit(solution)/shard_map/ppermute | solution.py:166
  7.1 0.0 collective-permute-start.4
  7.1 0.0 collective-permute-done.refs_1_
  7.1 2.6 %collective-permute-start.5 = (bf16[16,1024]{1,0:T(8,128)(2,1)}, bf16[16,1024]{1,0:T(8,128)(2,1)S(1)}, u32[]{:S(2)}, u32[]{:S(2)}) collective-permute-start(bf16[16,1024]{1,0:T(8,128)(2,1)} %get-tuple-element.43), channel_id=1, source_target_pairs={{0,6},{1,7},{2,4},{3,5},{4,2},{5,3},{6,0},{7,1},{8,14},{9,15},{10,... | collective-permute-start | bytes 98312 | tf_op jit(solution)/shard_map/ppermute | solution.py:166
  9.7 0.0 collective-permute-done.1.refs_2_
  9.7 0.1 collective-permute-start.6
  9.8 0.0 collective-permute-done.2.refs_3_
  9.8 2.6 %collective-permute-start.7 = (bf16[16,1024]{1,0:T(8,128)(2,1)}, bf16[16,1024]{1,0:T(8,128)(2,1)S(1)}, u32[]{:S(2)}, u32[]{:S(2)}) collective-permute-start(bf16[16,1024]{1,0:T(8,128)(2,1)} %get-tuple-element.45), channel_id=1, source_target_pairs={{0,8},{1,9},{2,10},{3,11},{4,12},{5,13},{6,14},{7,15},{8,0},{9,1},... | collective-permute-start | bytes 98312 | tf_op jit(solution)/shard_map/ppermute | solution.py:166
  12.5 0.0 collective-permute-done.3.refs_4_
  12.5 0.5 collective-permute-start.8
  13.0 0.0 collective-permute-done.4.refs_5_
  13.0 3.0 %collective-permute-start.9 = (bf16[16,1024]{1,0:T(8,128)(2,1)}, bf16[16,1024]{1,0:T(8,128)(2,1)S(1)}, u32[]{:S(2)}, u32[]{:S(2)}) collective-permute-start(bf16[16,1024]{1,0:T(8,128)(2,1)} %get-tuple-element.47), channel_id=1, source_target_pairs={{0,10},{1,11},{2,8},{3,9},{4,14},{5,15},{6,12},{7,13},{8,2},{9,3},... | collective-permute-start | bytes 98312 | tf_op jit(solution)/shard_map/ppermute | solution.py:166
  16.0 0.0 collective-permute-done.5.refs_6_
  16.0 0.3 collective-permute-start.10
  16.3 0.0 collective-permute-done.6.refs_7_
  16.3 3.4 %collective-permute-start.11 = (bf16[16,1024]{1,0:T(8,128)(2,1)}, bf16[16,1024]{1,0:T(8,128)(2,1)S(1)}, u32[]{:S(2)}, u32[]{:S(2)}) collective-permute-start(bf16[16,1024]{1,0:T(8,128)(2,1)} %get-tuple-element.49), channel_id=1, source_target_pairs={{0,12},{1,13},{2,14},{3,15},{4,8},{5,9},{6,10},{7,11},{8,4},{9,5},... | collective-permute-start | bytes 98312 | tf_op jit(solution)/shard_map/ppermute | solution.py:166
  19.7 0.0 collective-permute-done.7.refs_8_
  19.7 0.5 collective-permute-start.12
  20.2 0.0 collective-permute-done.8.refs_9_
  20.2 4.0 %collective-permute-start.13 = (bf16[16,1024]{1,0:T(8,128)(2,1)}, bf16[16,1024]{1,0:T(8,128)(2,1)S(1)}, u32[]{:S(2)}, u32[]{:S(2)}) collective-permute-start(bf16[16,1024]{1,0:T(8,128)(2,1)} %get-tuple-element.51), channel_id=1, source_target_pairs={{0,14},{1,15},{2,12},{3,13},{4,10},{5,11},{6,8},{7,9},{8,6},{9,7},... | collective-permute-start | bytes 98312 | tf_op jit(solution)/shard_map/ppermute | solution.py:166
  24.1 0.0 collective-permute-done.9.refs_10_
  24.1 0.2 collective-permute-start.14
  24.3 0.0 collective-permute-done.10.refs_11_
  24.3 0.0 collective-permute-done.11.refs_12_
  24.3 0.9 %collective-permute-done.12.refs_13_ = bf16[16,1024]{1,0:T(8,128)(2,1)S(1)} collective-permute-done((bf16[16,1024]{1,0:T(8,128)(2,1)}, bf16[16,1024]{1,0:T(8,128)(2,1)S(1)}, u32[]{:S(2)}, u32[]{:S(2)}) %collective-permute-start.12) | collective-permute-done | bytes 32800 | tf_op jit(solution)/shard_map/ppermute | solution.py:166
  25.2 1.9 %collective-permute-done.13.refs_14_ = bf16[16,1024]{1,0:T(8,128)(2,1)S(1)} collective-permute-done((bf16[16,1024]{1,0:T(8,128)(2,1)}, bf16[16,1024]{1,0:T(8,128)(2,1)S(1)}, u32[]{:S(2)}, u32[]{:S(2)}) %collective-permute-start.13) | collective-permute-done | bytes 32800 | tf_op jit(solution)/shard_map/ppermute | solution.py:166
  27.1 3.2 %collective-permute-done.14.refs_15_ = bf16[16,1024]{1,0:T(8,128)(2,1)S(1)} collective-permute-done((bf16[16,1024]{1,0:T(8,128)(2,1)}, bf16[16,1024]{1,0:T(8,128)(2,1)S(1)}, u32[]{:S(2)}, u32[]{:S(2)}) %collective-permute-start.14) | collective-permute-done | bytes 32800 | tf_op jit(solution)/shard_map/ppermute | solution.py:166
  30.5 0.5 copy-done.14
  31.0 2.1 %best.1 = (f32[8,128]{1,0:T(8,128)}, f32[8,128]{1,0:T(8,128)}, f32[8,128]{1,0:T(8,128)}, f32[8,128]{1,0:T(8,128)}, f32[8,128]{1,0:T(8,128)}, /*index=5*/f32[8,12...) custom-call(bf16[16,1024]{1,0:T(8,128)(2,1)} %get-tuple-element.37.r, ...), custom_call_target="tpu_custom_call" | custom-call | tf_op jit(solution)/shard_map/best/pallas_call | solution.py:83
  33.1 0.2 collective-permute-start.15
  33.3 0.5 collective-permute-start.16
  33.9 1.2 %collective-permute-start.17 = (f32[8,128]{1,0:T(8,128)}, f32[8,128]{1,0:T(8,128)S(1)}, u32[]{:S(2)}, u32[]{:S(2)}) collective-permute-start(f32[8,128]{1,0:T(8,128)} %get-tuple-element.56), channel_id=1, source_target_pairs={{0,3},{1,2},{2,1},{3,0},{4,7},{5,6},{6,5},{7,4},{8,11},{9,10},{10,... | collective-permute-start | bytes 12296 | tf_op jit(solution)/shard_map/ppermute | solution.py:166
  35.0 0.0 collective-permute-start.18
  35.0 1.8 %collective-permute-start.19 = (f32[8,128]{1,0:T(8,128)}, f32[8,128]{1,0:T(8,128)S(1)}, u32[]{:S(2)}, u32[]{:S(2)}) collective-permute-start(f32[8,128]{1,0:T(8,128)} %get-tuple-element.58), channel_id=1, source_target_pairs={{0,5},{1,4},{2,7},{3,6},{4,1},{5,0},{6,3},{7,2},{8,13},{9,12},{10,... | collective-permute-start | bytes 12296 | tf_op jit(solution)/shard_map/ppermute | solution.py:166
  36.8 0.0 collective-permute-done.15.refs_1_
  36.8 0.3 collective-permute-start.20
  37.1 0.0 collective-permute-done.16.refs_2_
  37.1 2.3 %collective-permute-start.21 = (f32[8,128]{1,0:T(8,128)}, f32[8,128]{1,0:T(8,128)S(1)}, u32[]{:S(2)}, u32[]{:S(2)}) collective-permute-start(f32[8,128]{1,0:T(8,128)} %get-tuple-element.60), channel_id=1, source_target_pairs={{0,7},{1,6},{2,5},{3,4},{4,3},{5,2},{6,1},{7,0},{8,15},{9,14},{10,... | collective-permute-start | bytes 12296 | tf_op jit(solution)/shard_map/ppermute | solution.py:166
  39.4 0.0 collective-permute-done.17.refs_3_
  39.4 0.0 collective-permute-start.22
  39.4 0.0 collective-permute-done.18.refs_4_
  39.5 2.7 %collective-permute-start.23 = (f32[8,128]{1,0:T(8,128)S(1)}, f32[8,128]{1,0:T(8,128)S(1)}, u32[]{:S(2)}, u32[]{:S(2)}) collective-permute-start(f32[8,128]{1,0:T(8,128)S(1)} %copy-done.36), channel_id=1, source_target_pairs={{0,9},{1,8},{2,11},{3,10},{4,13},{5,12},{6,15},{7,14},{8,1},{9,0},... | collective-permute-start | bytes 12296 | tf_op jit(solution)/shard_map/ppermute | solution.py:166
  42.2 0.0 collective-permute-done.19.refs_5_
  42.2 0.3 collective-permute-start.24
  42.6 0.0 collective-permute-done.20.refs_6_
  42.6 3.3 %collective-permute-start.25 = (f32[8,128]{1,0:T(8,128)S(1)}, f32[8,128]{1,0:T(8,128)S(1)}, u32[]{:S(2)}, u32[]{:S(2)}) collective-permute-start(f32[8,128]{1,0:T(8,128)S(1)} %copy-done.34), channel_id=1, source_target_pairs={{0,11},{1,10},{2,9},{3,8},{4,15},{5,14},{6,13},{7,12},{8,3},{9,2},... | collective-permute-start | bytes 12296 | tf_op jit(solution)/shard_map/ppermute | solution.py:166
  45.9 0.0 collective-permute-done.21.refs_7_
  45.9 0.7 %collective-permute-start.26 = (f32[8,128]{1,0:T(8,128)S(1)}, f32[8,128]{1,0:T(8,128)S(1)}, u32[]{:S(2)}, u32[]{:S(2)}) collective-permute-start(f32[8,128]{1,0:T(8,128)S(1)} %copy-done.33), channel_id=1, source_target_pairs={{0,12},{1,13},{2,14},{3,15},{4,8},{5,9},{6,10},{7,11},{8,4},{9,5},... | collective-permute-start | bytes 12296 | tf_op jit(solution)/shard_map/ppermute | solution.py:166
  46.6 0.0 collective-permute-done.22.refs_8_
  46.6 3.1 %collective-permute-start.27 = (f32[8,128]{1,0:T(8,128)S(1)}, f32[8,128]{1,0:T(8,128)S(1)}, u32[]{:S(2)}, u32[]{:S(2)}) collective-permute-start(f32[8,128]{1,0:T(8,128)S(1)} %copy-done.32), channel_id=1, source_target_pairs={{0,13},{1,12},{2,15},{3,14},{4,9},{5,8},{6,11},{7,10},{8,5},{9,4},... | collective-permute-start | bytes 12296 | tf_op jit(solution)/shard_map/ppermute | solution.py:166
  49.6 0.0 collective-permute-done.23.refs_9_
  49.6 1.2 %collective-permute-start.28 = (f32[8,128]{1,0:T(8,128)S(1)}, f32[8,128]{1,0:T(8,128)S(1)}, u32[]{:S(2)}, u32[]{:S(2)}) collective-permute-start(f32[8,128]{1,0:T(8,128)S(1)} %copy-done.31), channel_id=1, source_target_pairs={{0,14},{1,15},{2,12},{3,13},{4,10},{5,11},{6,8},{7,9},{8,6},{9,7},... | collective-permute-start | bytes 12296 | tf_op jit(solution)/shard_map/ppermute | solution.py:166
  50.8 0.0 collective-permute-done.24.refs_10_
  50.8 3.3 %collective-permute-start.29 = (f32[8,128]{1,0:T(8,128)S(1)}, f32[8,128]{1,0:T(8,128)S(1)}, u32[]{:S(2)}, u32[]{:S(2)}) collective-permute-start(f32[8,128]{1,0:T(8,128)S(1)} %copy-done.30), channel_id=1, source_target_pairs={{0,15},{1,14},{2,13},{3,12},{4,11},{5,10},{6,9},{7,8},{8,7},{9,6},... | collective-permute-start | bytes 12296 | tf_op jit(solution)/shard_map/ppermute | solution.py:166
  54.1 0.0 collective-permute-done.25.refs_11_
  54.2 0.0 collective-permute-done.26.refs_12_
  54.2 1.8 %collective-permute-done.28.refs_14_ = f32[8,128]{1,0:T(8,128)S(1)} collective-permute-done((f32[8,128]{1,0:T(8,128)S(1)}, f32[8,128]{1,0:T(8,128)S(1)}, u32[]{:S(2)}, u32[]{:S(2)}) %collective-permute-start.28) | collective-permute-done | bytes 4128 | tf_op jit(solution)/shard_map/ppermute | solution.py:166
  56.0 0.6 collective-permute-done.29.refs_15_
  56.7 0.5 copy-done.29
  57.2 1.4 %unpack.1 = f32[1,128]{1,0:T(1,128)} custom-call(s32[1,1]{1,0:T(1,128)} %bitcast.flip_ref, s32[1,128]{1,0:T(1,128)} %bitcast.4, f32[8,128]{1,0:T(8,128)} %get-tuple-element.53.refs_0_, f32[8,128]{1,0:T(8,128)} %copy-done.15, f32[8,128]{1,0:T(8,128)} %copy-done.16, f32[8,128]{1,0:T(8,128)} %copy-done.17, f32[8,128]{1,0:T(8,128)} %copy-done.18, ...), custom_call_target="tpu_custom_call" | custom-call | tf_op jit(solution)/shard_map/unpack/pallas_call | solution.py:154
  (73 shorter events, 0.1 us)
Async XLA Ops:
  2.1 4.9 %collective-permute-start = (bf16[16,1024]{1,0:T(8,128)(2,1)}, bf16[16,1024]{1,0:T(8,128)(2,1)S(1)}, u32[]{:S(2)}, u32[]{:S(2)}) collective-permute-start(bf16[16,1024]{1,0:T(8,128)(2,1)} %get-tuple-element.38), channel_id=1, source_target_pairs={{0,1},{1,0},{2,3},{3,2},{4,5},{5,4},{6,7},{7,6},{8,9},{9,8},{10,11... | collective-permute-start | bytes 98312 | tf_op jit(solution)/shard_map/ppermute | solution.py:166
  2.6 7.1 %collective-permute-start.1 = (bf16[16,1024]{1,0:T(8,128)(2,1)}, bf16[16,1024]{1,0:T(8,128)(2,1)S(1)}, u32[]{:S(2)}, u32[]{:S(2)}) collective-permute-start(bf16[16,1024]{1,0:T(8,128)(2,1)} %get-tuple-element.39), channel_id=1, source_target_pairs={{0,2},{1,3},{2,0},{3,1},{4,6},{5,7},{6,4},{7,5},{8,10},{9,11},{10,... | collective-permute-start | bytes 98312 | tf_op jit(solution)/shard_map/ppermute | solution.py:166
  5.2 4.7 %collective-permute-start.2 = (bf16[16,1024]{1,0:T(8,128)(2,1)}, bf16[16,1024]{1,0:T(8,128)(2,1)S(1)}, u32[]{:S(2)}, u32[]{:S(2)}) collective-permute-start(bf16[16,1024]{1,0:T(8,128)(2,1)} %get-tuple-element.40), channel_id=1, source_target_pairs={{0,3},{1,2},{2,1},{3,0},{4,7},{5,6},{6,5},{7,4},{8,11},{9,10},{10,... | collective-permute-start | bytes 98312 | tf_op jit(solution)/shard_map/ppermute | solution.py:166
  5.2 7.2 %collective-permute-start.3 = (bf16[16,1024]{1,0:T(8,128)(2,1)}, bf16[16,1024]{1,0:T(8,128)(2,1)S(1)}, u32[]{:S(2)}, u32[]{:S(2)}) collective-permute-start(bf16[16,1024]{1,0:T(8,128)(2,1)} %get-tuple-element.41), channel_id=1, source_target_pairs={{0,4},{1,5},{2,6},{3,7},{4,0},{5,1},{6,2},{7,3},{8,12},{9,13},{10,... | collective-permute-start | bytes 98312 | tf_op jit(solution)/shard_map/ppermute | solution.py:166
  7.1 6.0 %collective-permute-start.4 = (bf16[16,1024]{1,0:T(8,128)(2,1)}, bf16[16,1024]{1,0:T(8,128)(2,1)S(1)}, u32[]{:S(2)}, u32[]{:S(2)}) collective-permute-start(bf16[16,1024]{1,0:T(8,128)(2,1)} %get-tuple-element.42), channel_id=1, source_target_pairs={{0,5},{1,4},{2,7},{3,6},{4,1},{5,0},{6,3},{7,2},{8,13},{9,12},{10,... | collective-permute-start | bytes 98312 | tf_op jit(solution)/shard_map/ppermute | solution.py:166
  7.1 23.3 %copy-start = (bf16[16,1024]{1,0:T(8,128)(2,1)}, bf16[16,1024]{1,0:T(8,128)(2,1)S(1)}, u32[]{:S(2)}) copy-start(bf16[16,1024]{1,0:T(8,128)(2,1)S(1)} %collective-permute-done.refs_1_) | copy-start | bytes 98308
  7.1 8.9 %collective-permute-start.5 = (bf16[16,1024]{1,0:T(8,128)(2,1)}, bf16[16,1024]{1,0:T(8,128)(2,1)S(1)}, u32[]{:S(2)}, u32[]{:S(2)}) collective-permute-start(bf16[16,1024]{1,0:T(8,128)(2,1)} %get-tuple-element.43), channel_id=1, source_target_pairs={{0,6},{1,7},{2,4},{3,5},{4,2},{5,3},{6,0},{7,1},{8,14},{9,15},{10,... | collective-permute-start | bytes 98312 | tf_op jit(solution)/shard_map/ppermute | solution.py:166
  9.7 20.7 %copy-start.1 = (bf16[16,1024]{1,0:T(8,128)(2,1)}, bf16[16,1024]{1,0:T(8,128)(2,1)S(1)}, u32[]{:S(2)}) copy-start(bf16[16,1024]{1,0:T(8,128)(2,1)S(1)} %collective-permute-done.1.refs_2_) | copy-start | bytes 98308
  9.7 6.6 %collective-permute-start.6 = (bf16[16,1024]{1,0:T(8,128)(2,1)}, bf16[16,1024]{1,0:T(8,128)(2,1)S(1)}, u32[]{:S(2)}, u32[]{:S(2)}) collective-permute-start(bf16[16,1024]{1,0:T(8,128)(2,1)} %get-tuple-element.44), channel_id=1, source_target_pairs={{0,7},{1,6},{2,5},{3,4},{4,3},{5,2},{6,1},{7,0},{8,15},{9,14},{10,... | collective-permute-start | bytes 98312 | tf_op jit(solution)/shard_map/ppermute | solution.py:166
  9.8 20.6 %copy-start.2 = (bf16[16,1024]{1,0:T(8,128)(2,1)}, bf16[16,1024]{1,0:T(8,128)(2,1)S(1)}, u32[]{:S(2)}) copy-start(bf16[16,1024]{1,0:T(8,128)(2,1)S(1)} %collective-permute-done.2.refs_3_) | copy-start | bytes 98308
  9.8 9.9 %collective-permute-start.7 = (bf16[16,1024]{1,0:T(8,128)(2,1)}, bf16[16,1024]{1,0:T(8,128)(2,1)S(1)}, u32[]{:S(2)}, u32[]{:S(2)}) collective-permute-start(bf16[16,1024]{1,0:T(8,128)(2,1)} %get-tuple-element.45), channel_id=1, source_target_pairs={{0,8},{1,9},{2,10},{3,11},{4,12},{5,13},{6,14},{7,15},{8,0},{9,1},... | collective-permute-start | bytes 98312 | tf_op jit(solution)/shard_map/ppermute | solution.py:166
  12.5 17.9 %copy-start.3 = (bf16[16,1024]{1,0:T(8,128)(2,1)}, bf16[16,1024]{1,0:T(8,128)(2,1)S(1)}, u32[]{:S(2)}) copy-start(bf16[16,1024]{1,0:T(8,128)(2,1)S(1)} %collective-permute-done.3.refs_4_) | copy-start | bytes 98308
  12.5 7.7 %collective-permute-start.8 = (bf16[16,1024]{1,0:T(8,128)(2,1)}, bf16[16,1024]{1,0:T(8,128)(2,1)S(1)}, u32[]{:S(2)}, u32[]{:S(2)}) collective-permute-start(bf16[16,1024]{1,0:T(8,128)(2,1)} %get-tuple-element.46), channel_id=1, source_target_pairs={{0,9},{1,8},{2,11},{3,10},{4,13},{5,12},{6,15},{7,14},{8,1},{9,0},... | collective-permute-start | bytes 98312 | tf_op jit(solution)/shard_map/ppermute | solution.py:166
  13.0 17.4 %copy-start.4 = (bf16[16,1024]{1,0:T(8,128)(2,1)}, bf16[16,1024]{1,0:T(8,128)(2,1)S(1)}, u32[]{:S(2)}) copy-start(bf16[16,1024]{1,0:T(8,128)(2,1)S(1)} %collective-permute-done.4.refs_5_) | copy-start | bytes 98308
  13.0 11.1 %collective-permute-start.9 = (bf16[16,1024]{1,0:T(8,128)(2,1)}, bf16[16,1024]{1,0:T(8,128)(2,1)S(1)}, u32[]{:S(2)}, u32[]{:S(2)}) collective-permute-start(bf16[16,1024]{1,0:T(8,128)(2,1)} %get-tuple-element.47), channel_id=1, source_target_pairs={{0,10},{1,11},{2,8},{3,9},{4,14},{5,15},{6,12},{7,13},{8,2},{9,3},... | collective-permute-start | bytes 98312 | tf_op jit(solution)/shard_map/ppermute | solution.py:166
  16.0 14.4 %copy-start.5 = (bf16[16,1024]{1,0:T(8,128)(2,1)}, bf16[16,1024]{1,0:T(8,128)(2,1)S(1)}, u32[]{:S(2)}) copy-start(bf16[16,1024]{1,0:T(8,128)(2,1)S(1)} %collective-permute-done.5.refs_6_) | copy-start | bytes 98308
  16.0 8.3 %collective-permute-start.10 = (bf16[16,1024]{1,0:T(8,128)(2,1)}, bf16[16,1024]{1,0:T(8,128)(2,1)S(1)}, u32[]{:S(2)}, u32[]{:S(2)}) collective-permute-start(bf16[16,1024]{1,0:T(8,128)(2,1)} %get-tuple-element.48), channel_id=1, source_target_pairs={{0,11},{1,10},{2,9},{3,8},{4,15},{5,14},{6,13},{7,12},{8,3},{9,2},... | collective-permute-start | bytes 98312 | tf_op jit(solution)/shard_map/ppermute | solution.py:166
  16.3 14.1 %copy-start.6 = (bf16[16,1024]{1,0:T(8,128)(2,1)}, bf16[16,1024]{1,0:T(8,128)(2,1)S(1)}, u32[]{:S(2)}) copy-start(bf16[16,1024]{1,0:T(8,128)(2,1)S(1)} %collective-permute-done.6.refs_7_) | copy-start | bytes 98308
  16.3 8.0 %collective-permute-start.11 = (bf16[16,1024]{1,0:T(8,128)(2,1)}, bf16[16,1024]{1,0:T(8,128)(2,1)S(1)}, u32[]{:S(2)}, u32[]{:S(2)}) collective-permute-start(bf16[16,1024]{1,0:T(8,128)(2,1)} %get-tuple-element.49), channel_id=1, source_target_pairs={{0,12},{1,13},{2,14},{3,15},{4,8},{5,9},{6,10},{7,11},{8,4},{9,5},... | collective-permute-start | bytes 98312 | tf_op jit(solution)/shard_map/ppermute | solution.py:166
  19.7 10.7 %copy-start.7 = (bf16[16,1024]{1,0:T(8,128)(2,1)}, bf16[16,1024]{1,0:T(8,128)(2,1)S(1)}, u32[]{:S(2)}) copy-start(bf16[16,1024]{1,0:T(8,128)(2,1)S(1)} %collective-permute-done.7.refs_8_) | copy-start | bytes 98308
  19.7 5.5 %collective-permute-start.12 = (bf16[16,1024]{1,0:T(8,128)(2,1)}, bf16[16,1024]{1,0:T(8,128)(2,1)S(1)}, u32[]{:S(2)}, u32[]{:S(2)}) collective-permute-start(bf16[16,1024]{1,0:T(8,128)(2,1)} %get-tuple-element.50), channel_id=1, source_target_pairs={{0,13},{1,12},{2,15},{3,14},{4,9},{5,8},{6,11},{7,10},{8,5},{9,4},... | collective-permute-start | bytes 98312 | tf_op jit(solution)/shard_map/ppermute | solution.py:166
  20.2 10.3 %copy-start.8 = (bf16[16,1024]{1,0:T(8,128)(2,1)}, bf16[16,1024]{1,0:T(8,128)(2,1)S(1)}, u32[]{:S(2)}) copy-start(bf16[16,1024]{1,0:T(8,128)(2,1)S(1)} %collective-permute-done.8.refs_9_) | copy-start | bytes 98308
  20.2 7.0 %collective-permute-start.13 = (bf16[16,1024]{1,0:T(8,128)(2,1)}, bf16[16,1024]{1,0:T(8,128)(2,1)S(1)}, u32[]{:S(2)}, u32[]{:S(2)}) collective-permute-start(bf16[16,1024]{1,0:T(8,128)(2,1)} %get-tuple-element.51), channel_id=1, source_target_pairs={{0,14},{1,15},{2,12},{3,13},{4,10},{5,11},{6,8},{7,9},{8,6},{9,7},... | collective-permute-start | bytes 98312 | tf_op jit(solution)/shard_map/ppermute | solution.py:166
  24.1 6.3 %copy-start.9 = (bf16[16,1024]{1,0:T(8,128)(2,1)}, bf16[16,1024]{1,0:T(8,128)(2,1)S(1)}, u32[]{:S(2)}) copy-start(bf16[16,1024]{1,0:T(8,128)(2,1)S(1)} %collective-permute-done.9.refs_10_) | copy-start | bytes 98308
  24.1 6.2 %collective-permute-start.14 = (bf16[16,1024]{1,0:T(8,128)(2,1)}, bf16[16,1024]{1,0:T(8,128)(2,1)S(1)}, u32[]{:S(2)}, u32[]{:S(2)}) collective-permute-start(bf16[16,1024]{1,0:T(8,128)(2,1)} %get-tuple-element.52), channel_id=1, source_target_pairs={{0,15},{1,14},{2,13},{3,12},{4,11},{5,10},{6,9},{7,8},{8,7},{9,6},... | collective-permute-start | bytes 98312 | tf_op jit(solution)/shard_map/ppermute | solution.py:166
  24.3 6.2 %copy-start.10 = (bf16[16,1024]{1,0:T(8,128)(2,1)}, bf16[16,1024]{1,0:T(8,128)(2,1)S(1)}, u32[]{:S(2)}) copy-start(bf16[16,1024]{1,0:T(8,128)(2,1)S(1)} %collective-permute-done.10.refs_11_) | copy-start | bytes 98308
  24.3 6.2 %copy-start.11 = (bf16[16,1024]{1,0:T(8,128)(2,1)}, bf16[16,1024]{1,0:T(8,128)(2,1)S(1)}, u32[]{:S(2)}) copy-start(bf16[16,1024]{1,0:T(8,128)(2,1)S(1)} %collective-permute-done.11.refs_12_) | copy-start | bytes 98308
  25.2 5.3 %copy-start.12 = (bf16[16,1024]{1,0:T(8,128)(2,1)}, bf16[16,1024]{1,0:T(8,128)(2,1)S(1)}, u32[]{:S(2)}) copy-start(bf16[16,1024]{1,0:T(8,128)(2,1)S(1)} %collective-permute-done.12.refs_13_) | copy-start | bytes 98308
  27.1 3.4 %copy-start.13 = (bf16[16,1024]{1,0:T(8,128)(2,1)}, bf16[16,1024]{1,0:T(8,128)(2,1)S(1)}, u32[]{:S(2)}) copy-start(bf16[16,1024]{1,0:T(8,128)(2,1)S(1)} %collective-permute-done.13.refs_14_) | copy-start | bytes 98308
  33.1 6.4 %copy-start.36 = (f32[8,128]{1,0:T(8,128)S(1)}, f32[8,128]{1,0:T(8,128)}, u32[]{:S(2)}) copy-start(f32[8,128]{1,0:T(8,128)} %get-tuple-element.62) | copy-start | bytes 12292
  33.1 3.8 %collective-permute-start.15 = (f32[8,128]{1,0:T(8,128)}, f32[8,128]{1,0:T(8,128)S(1)}, u32[]{:S(2)}, u32[]{:S(2)}) collective-permute-start(f32[8,128]{1,0:T(8,128)} %get-tuple-element.54), channel_id=1, source_target_pairs={{0,1},{1,0},{2,3},{3,2},{4,5},{5,4},{6,7},{7,6},{8,9},{9,8},{10,11... | collective-permute-start | bytes 12296 | tf_op jit(solution)/shard_map/ppermute | solution.py:166
  33.3 3.8 %collective-permute-start.16 = (f32[8,128]{1,0:T(8,128)}, f32[8,128]{1,0:T(8,128)S(1)}, u32[]{:S(2)}, u32[]{:S(2)}) collective-permute-start(f32[8,128]{1,0:T(8,128)} %get-tuple-element.55), channel_id=1, source_target_pairs={{0,2},{1,3},{2,0},{3,1},{4,6},{5,7},{6,4},{7,5},{8,10},{9,11},{10,... | collective-permute-start | bytes 12296 | tf_op jit(solution)/shard_map/ppermute | solution.py:166
  33.9 8.4 %copy-start.35 = (f32[8,128]{1,0:T(8,128)S(1)}, f32[8,128]{1,0:T(8,128)}, u32[]{:S(2)}) copy-start(f32[8,128]{1,0:T(8,128)} %get-tuple-element.63) | copy-start | bytes 12292
  33.9 5.6 %collective-permute-start.17 = (f32[8,128]{1,0:T(8,128)}, f32[8,128]{1,0:T(8,128)S(1)}, u32[]{:S(2)}, u32[]{:S(2)}) collective-permute-start(f32[8,128]{1,0:T(8,128)} %get-tuple-element.56), channel_id=1, source_target_pairs={{0,3},{1,2},{2,1},{3,0},{4,7},{5,6},{6,5},{7,4},{8,11},{9,10},{10,... | collective-permute-start | bytes 12296 | tf_op jit(solution)/shard_map/ppermute | solution.py:166
  35.0 4.4 %collective-permute-start.18 = (f32[8,128]{1,0:T(8,128)}, f32[8,128]{1,0:T(8,128)S(1)}, u32[]{:S(2)}, u32[]{:S(2)}) collective-permute-start(f32[8,128]{1,0:T(8,128)} %get-tuple-element.57), channel_id=1, source_target_pairs={{0,4},{1,5},{2,6},{3,7},{4,0},{5,1},{6,2},{7,3},{8,12},{9,13},{10,... | collective-permute-start | bytes 12296 | tf_op jit(solution)/shard_map/ppermute | solution.py:166
  35.0 7.6 %copy-start.34 = (f32[8,128]{1,0:T(8,128)S(1)}, f32[8,128]{1,0:T(8,128)}, u32[]{:S(2)}) copy-start(f32[8,128]{1,0:T(8,128)} %get-tuple-element.64) | copy-start | bytes 12292
  35.0 7.2 %collective-permute-start.19 = (f32[8,128]{1,0:T(8,128)}, f32[8,128]{1,0:T(8,128)S(1)}, u32[]{:S(2)}, u32[]{:S(2)}) collective-permute-start(f32[8,128]{1,0:T(8,128)} %get-tuple-element.58), channel_id=1, source_target_pairs={{0,5},{1,4},{2,7},{3,6},{4,1},{5,0},{6,3},{7,2},{8,13},{9,12},{10,... | collective-permute-start | bytes 12296 | tf_op jit(solution)/shard_map/ppermute | solution.py:166
  36.8 5.4 %copy-start.15 = (f32[8,128]{1,0:T(8,128)}, f32[8,128]{1,0:T(8,128)S(1)}, u32[]{:S(2)}) copy-start(f32[8,128]{1,0:T(8,128)S(1)} %collective-permute-done.15.refs_1_) | copy-start | bytes 12292
  36.8 5.8 %collective-permute-start.20 = (f32[8,128]{1,0:T(8,128)}, f32[8,128]{1,0:T(8,128)S(1)}, u32[]{:S(2)}, u32[]{:S(2)}) collective-permute-start(f32[8,128]{1,0:T(8,128)} %get-tuple-element.59), channel_id=1, source_target_pairs={{0,6},{1,7},{2,4},{3,5},{4,2},{5,3},{6,0},{7,1},{8,14},{9,15},{10,... | collective-permute-start | bytes 12296 | tf_op jit(solution)/shard_map/ppermute | solution.py:166
  37.1 5.5 %copy-start.16 = (f32[8,128]{1,0:T(8,128)}, f32[8,128]{1,0:T(8,128)S(1)}, u32[]{:S(2)}) copy-start(f32[8,128]{1,0:T(8,128)S(1)} %collective-permute-done.16.refs_2_) | copy-start | bytes 12292
  37.1 8.7 %copy-start.33 = (f32[8,128]{1,0:T(8,128)S(1)}, f32[8,128]{1,0:T(8,128)}, u32[]{:S(2)}) copy-start(f32[8,128]{1,0:T(8,128)} %get-tuple-element.65) | copy-start | bytes 12292
  37.1 8.7 %collective-permute-start.21 = (f32[8,128]{1,0:T(8,128)}, f32[8,128]{1,0:T(8,128)S(1)}, u32[]{:S(2)}, u32[]{:S(2)}) collective-permute-start(f32[8,128]{1,0:T(8,128)} %get-tuple-element.60), channel_id=1, source_target_pairs={{0,7},{1,6},{2,5},{3,4},{4,3},{5,2},{6,1},{7,0},{8,15},{9,14},{10,... | collective-permute-start | bytes 12296 | tf_op jit(solution)/shard_map/ppermute | solution.py:166
  39.4 6.5 %copy-start.17 = (f32[8,128]{1,0:T(8,128)}, f32[8,128]{1,0:T(8,128)S(1)}, u32[]{:S(2)}) copy-start(f32[8,128]{1,0:T(8,128)S(1)} %collective-permute-done.17.refs_3_) | copy-start | bytes 12292
  39.4 7.1 %collective-permute-start.22 = (f32[8,128]{1,0:T(8,128)}, f32[8,128]{1,0:T(8,128)S(1)}, u32[]{:S(2)}, u32[]{:S(2)}) collective-permute-start(f32[8,128]{1,0:T(8,128)} %get-tuple-element.61), channel_id=1, source_target_pairs={{0,8},{1,9},{2,10},{3,11},{4,12},{5,13},{6,14},{7,15},{8,0},{9,1},... | collective-permute-start | bytes 12296 | tf_op jit(solution)/shard_map/ppermute | solution.py:166
  39.4 17.2 %copy-start.18 = (f32[8,128]{1,0:T(8,128)}, f32[8,128]{1,0:T(8,128)S(1)}, u32[]{:S(2)}) copy-start(f32[8,128]{1,0:T(8,128)S(1)} %collective-permute-done.18.refs_4_) | copy-start | bytes 12292
  39.5 7.1 %copy-start.32 = (f32[8,128]{1,0:T(8,128)S(1)}, f32[8,128]{1,0:T(8,128)}, u32[]{:S(2)}) copy-start(f32[8,128]{1,0:T(8,128)} %get-tuple-element.66) | copy-start | bytes 12292
  39.5 10.2 %collective-permute-start.23 = (f32[8,128]{1,0:T(8,128)S(1)}, f32[8,128]{1,0:T(8,128)S(1)}, u32[]{:S(2)}, u32[]{:S(2)}) collective-permute-start(f32[8,128]{1,0:T(8,128)S(1)} %copy-done.36), channel_id=1, source_target_pairs={{0,9},{1,8},{2,11},{3,10},{4,13},{5,12},{6,15},{7,14},{8,1},{9,0},... | collective-permute-start | bytes 12296 | tf_op jit(solution)/shard_map/ppermute | solution.py:166
  42.2 14.4 %copy-start.19 = (f32[8,128]{1,0:T(8,128)}, f32[8,128]{1,0:T(8,128)S(1)}, u32[]{:S(2)}) copy-start(f32[8,128]{1,0:T(8,128)S(1)} %collective-permute-done.19.refs_5_) | copy-start | bytes 12292
  42.2 7.4 %copy-start.31 = (f32[8,128]{1,0:T(8,128)S(1)}, f32[8,128]{1,0:T(8,128)}, u32[]{:S(2)}) copy-start(f32[8,128]{1,0:T(8,128)} %get-tuple-element.67) | copy-start | bytes 12292
  42.2 8.6 %collective-permute-start.24 = (f32[8,128]{1,0:T(8,128)S(1)}, f32[8,128]{1,0:T(8,128)S(1)}, u32[]{:S(2)}, u32[]{:S(2)}) collective-permute-start(f32[8,128]{1,0:T(8,128)S(1)} %copy-done.35), channel_id=1, source_target_pairs={{0,10},{1,11},{2,8},{3,9},{4,14},{5,15},{6,12},{7,13},{8,2},{9,3},... | collective-permute-start | bytes 12296 | tf_op jit(solution)/shard_map/ppermute | solution.py:166
  42.6 14.0 %copy-start.20 = (f32[8,128]{1,0:T(8,128)}, f32[8,128]{1,0:T(8,128)S(1)}, u32[]{:S(2)}) copy-start(f32[8,128]{1,0:T(8,128)S(1)} %collective-permute-done.20.refs_6_) | copy-start | bytes 12292
  42.6 8.2 %copy-start.30 = (f32[8,128]{1,0:T(8,128)S(1)}, f32[8,128]{1,0:T(8,128)}, u32[]{:S(2)}) copy-start(f32[8,128]{1,0:T(8,128)} %get-tuple-element.68) | copy-start | bytes 12292
  42.6 11.5 %collective-permute-start.25 = (f32[8,128]{1,0:T(8,128)S(1)}, f32[8,128]{1,0:T(8,128)S(1)}, u32[]{:S(2)}, u32[]{:S(2)}) collective-permute-start(f32[8,128]{1,0:T(8,128)S(1)} %copy-done.34), channel_id=1, source_target_pairs={{0,11},{1,10},{2,9},{3,8},{4,15},{5,14},{6,13},{7,12},{8,3},{9,2},... | collective-permute-start | bytes 12296 | tf_op jit(solution)/shard_map/ppermute | solution.py:166
  45.9 10.7 %copy-start.21 = (f32[8,128]{1,0:T(8,128)}, f32[8,128]{1,0:T(8,128)S(1)}, u32[]{:S(2)}) copy-start(f32[8,128]{1,0:T(8,128)S(1)} %collective-permute-done.21.refs_7_) | copy-start | bytes 12292
  45.9 8.3 %collective-permute-start.26 = (f32[8,128]{1,0:T(8,128)S(1)}, f32[8,128]{1,0:T(8,128)S(1)}, u32[]{:S(2)}, u32[]{:S(2)}) collective-permute-start(f32[8,128]{1,0:T(8,128)S(1)} %copy-done.33), channel_id=1, source_target_pairs={{0,12},{1,13},{2,14},{3,15},{4,8},{5,9},{6,10},{7,11},{8,4},{9,5},... | collective-permute-start | bytes 12296 | tf_op jit(solution)/shard_map/ppermute | solution.py:166
  46.6 10.0 %copy-start.22 = (f32[8,128]{1,0:T(8,128)}, f32[8,128]{1,0:T(8,128)S(1)}, u32[]{:S(2)}) copy-start(f32[8,128]{1,0:T(8,128)S(1)} %collective-permute-done.22.refs_8_) | copy-start | bytes 12292
  46.6 7.6 %collective-permute-start.27 = (f32[8,128]{1,0:T(8,128)S(1)}, f32[8,128]{1,0:T(8,128)S(1)}, u32[]{:S(2)}, u32[]{:S(2)}) collective-permute-start(f32[8,128]{1,0:T(8,128)S(1)} %copy-done.32), channel_id=1, source_target_pairs={{0,13},{1,12},{2,15},{3,14},{4,9},{5,8},{6,11},{7,10},{8,5},{9,4},... | collective-permute-start | bytes 12296 | tf_op jit(solution)/shard_map/ppermute | solution.py:166
  49.6 7.0 %copy-start.23 = (f32[8,128]{1,0:T(8,128)}, f32[8,128]{1,0:T(8,128)S(1)}, u32[]{:S(2)}) copy-start(f32[8,128]{1,0:T(8,128)S(1)} %collective-permute-done.23.refs_9_) | copy-start | bytes 12292
  49.6 6.4 %collective-permute-start.28 = (f32[8,128]{1,0:T(8,128)S(1)}, f32[8,128]{1,0:T(8,128)S(1)}, u32[]{:S(2)}, u32[]{:S(2)}) collective-permute-start(f32[8,128]{1,0:T(8,128)S(1)} %copy-done.31), channel_id=1, source_target_pairs={{0,14},{1,15},{2,12},{3,13},{4,10},{5,11},{6,8},{7,9},{8,6},{9,7},... | collective-permute-start | bytes 12296 | tf_op jit(solution)/shard_map/ppermute | solution.py:166
  50.8 5.8 %copy-start.24 = (f32[8,128]{1,0:T(8,128)}, f32[8,128]{1,0:T(8,128)S(1)}, u32[]{:S(2)}) copy-start(f32[8,128]{1,0:T(8,128)S(1)} %collective-permute-done.24.refs_10_) | copy-start | bytes 12292
  50.8 5.8 %collective-permute-start.29 = (f32[8,128]{1,0:T(8,128)S(1)}, f32[8,128]{1,0:T(8,128)S(1)}, u32[]{:S(2)}, u32[]{:S(2)}) collective-permute-start(f32[8,128]{1,0:T(8,128)S(1)} %copy-done.30), channel_id=1, source_target_pairs={{0,15},{1,14},{2,13},{3,12},{4,11},{5,10},{6,9},{7,8},{8,7},{9,6},... | collective-permute-start | bytes 12296 | tf_op jit(solution)/shard_map/ppermute | solution.py:166
  54.2 2.5 %copy-start.25 = (f32[8,128]{1,0:T(8,128)}, f32[8,128]{1,0:T(8,128)S(1)}, u32[]{:S(2)}) copy-start(f32[8,128]{1,0:T(8,128)S(1)} %collective-permute-done.25.refs_11_) | copy-start | bytes 12292
  54.2 2.5 %copy-start.26 = (f32[8,128]{1,0:T(8,128)}, f32[8,128]{1,0:T(8,128)S(1)}, u32[]{:S(2)}) copy-start(f32[8,128]{1,0:T(8,128)S(1)} %collective-permute-done.26.refs_12_) | copy-start | bytes 12292
  54.2 2.5 %copy-start.27 = (f32[8,128]{1,0:T(8,128)}, f32[8,128]{1,0:T(8,128)S(1)}, u32[]{:S(2)}) copy-start(f32[8,128]{1,0:T(8,128)S(1)} %collective-permute-done.27.refs_13_) | copy-start | bytes 12292
  (3 other events, 1.9 us)

commit v3 on v2

--- a/solution.py
+++ b/solution.py
@@ -14,6 +14,7 @@
 LANES = 128
 EMPTY = 4.0
 NONE = -2.0
+TAIL = 8
 AXES = ("blk", "shard", "sub")
 
 VMEM = pl.BlockSpec(memory_space=pltpu.VMEM)
@@ -63,32 +64,6 @@
     )(flip, embeddings, assignment.reshape(1, rows))
 
 
-def best_kernel(*refs):
-    half = len(refs) // 2
-    slots = jnp.concatenate([ref[...] for ref in refs[:half]], axis=0)
-    similar = lax.dot_general(
-        slots, slots, (((1,), (1,)), ((), ())), preferred_element_type=jnp.float32
-    )
-    used = slots[:, :1].astype(jnp.float32) < 2.0
-    row = lax.broadcasted_iota(jnp.int32, similar.shape, 0)
-    column = lax.broadcasted_iota(jnp.int32, similar.shape, 1)
-    best = jnp.max(jnp.where(used & (row != column), similar, NONE), axis=0, keepdims=True)
-    for block, out_ref in enumerate(refs[half:]):
-        piece = best[:, block * CAP : (block + 1) * CAP]
-        out_ref[:, :CAP] = jnp.broadcast_to(piece, (8, CAP))
-        out_ref[:, CAP:] = jnp.full((8, LANES - CAP), NONE)
-
-
-def best_of(blocks):
-    return pl.pallas_call(
-        best_kernel,
-        out_shape=[jax.ShapeDtypeStruct((8, LANES), jnp.float32)] * len(blocks),
-        in_specs=[VMEM] * len(blocks),
-        out_specs=[VMEM] * len(blocks),
-        name="best",
-    )(*blocks)
-
-
 def shared_best_kernel(count, first_ref, slots_ref, others_ref, out_ref, best_ref):
     step = pl.program_id(0)
     slots, others = slots_ref[...], others_ref[...]
@@ -160,18 +135,132 @@
     )(flip, assignment.reshape(1, rows), *returned).reshape(-1)
 
 
-def exchange(blocks):
-    size = len(blocks)
-    return [blocks[0]] + [
-        lax.ppermute(blocks[r], AXES, [(i, i ^ r) for i in range(size)]) for r in range(1, size)
-    ]
-
-
-def one_owner(embeddings, assignment):
-    flip = lax.axis_index(AXES).astype(jnp.int32).reshape(1, 1)
-    sent = pack(flip, embeddings, assignment, CLUSTERS)
-    best = best_of(exchange(sent))
-    return unpack(flip, exchange(best), assignment)
+def unit_of(values):
+    values = values.astype(jnp.float32)
+    scaled = values * lax.rsqrt(jnp.mean(values * values, axis=1, keepdims=True) + 1e-06)
+    return (scaled * (1.0 / math.sqrt(values.shape[1]))).astype(jnp.bfloat16)
+
+
+def normalize_kernel(rows_ref, cluster_ref, out_ref):
+    rows, width = rows_ref.shape
+    out_ref[:rows] = unit_of(rows_ref[...])
+    cluster = jnp.broadcast_to(cluster_ref[...].astype(jnp.float32), (TAIL, rows))
+    tail = jnp.concatenate([cluster, jnp.zeros((TAIL, width - rows), jnp.float32)], axis=1)
+    out_ref[rows:] = tail.astype(jnp.bfloat16)
+
+
+def normalize(embeddings, assignment):
+    rows, width = embeddings.shape
+    return pl.pallas_call(
+        normalize_kernel,
+        out_shape=jax.ShapeDtypeStruct((rows + TAIL, width), jnp.bfloat16),
+        in_specs=[VMEM, VMEM],
+        out_specs=VMEM,
+        name="normalize",
+    )(embeddings, assignment.reshape(1, rows))
+
+
+def split(block):
+    rows = block.shape[0] - TAIL
+    return block[:rows], block[rows : rows + 1, :rows].astype(jnp.float32)
+
+
+def best_against(own, others, same_rows):
+    rows, clusters = zip(*[split(block) for block in own])
+    rows, clusters = jnp.concatenate(rows, axis=0), jnp.concatenate(clusters, axis=1)
+    best = None
+    for place, other in enumerate(others):
+        other_rows, other_clusters = split(other)
+        count = other_rows.shape[0]
+        similar = lax.dot_general(
+            other_rows, rows, (((1,), (1,)), ((), ())), preferred_element_type=jnp.float32
+        )
+        down = jnp.broadcast_to(other_clusters, (count, count)).T[:, :1]
+        kept = down == clusters
+        if same_rows and place == 0:
+            row = lax.broadcasted_iota(jnp.int32, similar.shape, 0)
+            column = lax.broadcasted_iota(jnp.int32, similar.shape, 1)
+            kept = kept & (row != column)
+        found = jnp.max(jnp.where(kept, similar, NONE), axis=0, keepdims=True)
+        best = found if best is None else jnp.maximum(best, found)
+    return best
+
+
+def early_kernel(*refs):
+    *own_refs, other_ref, out_ref = refs
+    own = [ref[...] for ref in own_refs]
+    best = best_against(own, [own[0], other_ref[...]], True)
+    out_ref[...] = jnp.broadcast_to(best, out_ref.shape)
+
+
+def early(own, other):
+    rows = own[0].shape[0] - TAIL
+    return pl.pallas_call(
+        early_kernel,
+        out_shape=jax.ShapeDtypeStruct((8, len(own) * rows), jnp.float32),
+        in_specs=[VMEM] * (len(own) + 1),
+        out_specs=VMEM,
+        name="early",
+    )(*own, other)
+
+
+def late_kernel(edge_ref, best_ref, *refs):
+    own_refs, far_refs, out_refs = refs[:4], refs[4:8], refs[8:]
+    edge = edge_ref[0, 0] > 0
+    m1, m2, e2, e3 = [ref[...] for ref in far_refs]
+    others = [jnp.where(edge, e2, m1), jnp.where(edge, e3, m2)]
+    best = best_against([ref[...] for ref in own_refs], others, False)
+    best = jnp.maximum(best, best_ref[:1, :])
+    for place, out_ref in enumerate(out_refs):
+        rows = out_ref.shape[1]
+        out_ref[...] = jnp.broadcast_to(best[:, place * rows : (place + 1) * rows], out_ref.shape)
+
+
+def late(edge, best, own, far):
+    rows = own[0].shape[0] - TAIL
+    return pl.pallas_call(
+        late_kernel,
+        out_shape=[jax.ShapeDtypeStruct((8, rows), jnp.float32)] * len(own),
+        in_specs=[SMEM] + [VMEM] * (1 + len(own) + len(far)),
+        out_specs=[VMEM] * len(own),
+        name="late",
+    )(edge, best, *own, *far)
+
+
+def line(blk, plane):
+    size = 4 * plane
+
+    def within(flip, array):
+        return lax.ppermute(array, AXES, [(i, i ^ flip) for i in range(size)])
+
+    def outer(array):
+        return within(plane, array)
+
+    def inner(array):
+        swapped = [0, 2, 1, 3]
+        return lax.ppermute(
+            array, AXES, [(i, swapped[i // plane] * plane + i % plane) for i in range(size)]
+        )
+
+    def local(embeddings, assignment):
+        mine = normalize(embeddings, assignment)
+        e1 = outer(mine)
+        m1 = inner(mine)
+        others = [within(flip, mine) for flip in range(1, plane)]
+        m2 = inner(e1)
+        e2 = outer(m1)
+        e3 = outer(m2)
+        own = [mine] + others
+        best = early(own, e1)
+        place = lax.axis_index(blk)
+        edge = ((place == 0) | (place == 3)).astype(jnp.int32).reshape(1, 1)
+        bests = late(edge, best, own, [m1, m2, e2, e3])
+        found = bests[0]
+        for flip in range(1, plane):
+            found = jnp.maximum(found, within(flip, bests[flip]))
+        return found[0]
+
+    return local
 
 
 def shared_owner(embeddings, assignment):
@@ -192,9 +281,10 @@
         P(("groups", "blk", "shard", "sub"), None),
         P(("groups", "blk", "shard", "sub"), None),
     )
-    one = math.prod(mesh.shape[axis] for axis in AXES) == CLUSTERS
+    plane = mesh.shape["shard"] * mesh.shape["sub"]
+    program = line("blk", plane) if mesh.shape["blk"] == 4 and plane == 4 else shared_owner
     return jax.shard_map(
-        one_owner if one else shared_owner,
+        program,
         mesh=mesh,
         in_specs=placed,
         out_specs=P(("groups", "blk", "shard", "sub")),

time: 58.9 us -> 42.3 us (0.72)
  starting transfers between devices: 43 us -> 17.9 us
  waiting for transfers between devices: 8.56 us -> 14.2 us
  Pallas kernels: 5.65 us -> 7.53 us
  local copies, waits for them, and re-layouts: 1.12 us -> 1.94 us
    ppermute x30 -> x11, starting transfers between devices: 43 us -> 17.9 us  [the longest x9 15.7 us: within(): return lax.ppermute(array, AXES, [(i, i ^ flip) for i in range(size)])]
    ppermute x30 -> x11, waiting for transfers between devices: 8.56 us -> 14.2 us  [the longest x9 14.2 us: within(): return lax.ppermute(array, AXES, [(i, i ^ flip) for i in range(size)])]
    pallas_call x3, Pallas kernels: 5.65 us -> 7.53 us  [the longest x1 3 us: late(): pl.pallas_call(late_kernel, out_shape=[jax.ShapeDtypeStruct((8, rows), jn...]
    unnamed x74 -> x18, local copies, waits for them, and re-layouts: 1.12 us -> 1.42 us
  transfers between devices with their start and end apart: 30 -> 11, of which waited for: 5 -> 5; matrix products, arithmetic and copies ran while one was open for 0% -> 0% of each run, Pallas kernels for 0% -> 7%
where the time goes in v3:
time: 42.3 us; the launch traced here: 41.7 us
  starting transfers between devices  17.9 us (42%)
  waiting for transfers between devices  14.2 us (34%)
  Pallas kernels  7.53 us (18%)
  local copies, waits for them, and re-layouts  1.94 us (5%)
    ppermute x9, starting transfers between devices, within(): return lax.ppermute(array, AXES, [(i, i ^ flip) for i in range(size)])  15.7 us
    ppermute x9, waiting for transfers between devices, within(): return lax.ppermute(array, AXES, [(i, i ^ flip) for i in range(size)])  14.2 us
    pallas_call x1, Pallas kernels, late(): pl.pallas_call(late_kernel, out_shape=[jax.ShapeDtypeStruct((8, rows), jn...  3 us
    pallas_call x1, Pallas kernels, early(): pl.pallas_call(early_kernel, out_shape=jax.ShapeDtypeStruct((8, len(own)...  2.72 us
    ppermute x2, starting transfers between devices, inner(): lax.ppermute(array, AXES, [(i, swapped[i // plane] * plane + i % plane) f...  2.27 us
    pallas_call x1, Pallas kernels, normalize(): pl.pallas_call(normalize_kernel, out_shape=jax.ShapeDtypeStruct((rows + T...  1.81 us
    unnamed x18, local copies, waits for them, and re-layouts  1.42 us
  transfers between devices with their start and end apart: 11, of which 5 were waited for; matrix products, arithmetic and copies ran while one was open for 0% of the time, Pallas kernels for 7%

profile of v3, /device:TPU:0, one launch (start us, length us, event | category | flops | bytes accessed | tf_op | source)
XLA Modules:
  0.0 41.7 jit_solution(4996518473484644112)
XLA Ops:
  0.0 1.8 %normalize.1.refs_0_ = bf16[136,1024]{1,0:T(8,128)(2,1)} custom-call(bf16[128,1024]{1,0:T(8,128)(2,1)} %rows_ref.1, s32[1,128]{1,0:T(1,128)} %bitcast.4), custom_call_target="tpu_custom_call" | custom-call | tf_op jit(solution)/shard_map/normalize/pallas_call | solution.py:154
  1.8 3.0 %collective-permute-start.3 = (bf16[136,1024]{1,0:T(8,128)(2,1)}, bf16[136,1024]{1,0:T(8,128)(2,1)S(1)}, u32[]{:S(2)}, u32[]{:S(2)}) collective-permute-start(bf16[136,1024]{1,0:T(8,128)(2,1)} %normalize.1.refs_0_), channel_id=1, source_target_pairs={{0,4},{1,5},{2,6},{3,7},{4,0},{5,1},{6,2},{7,3},{8,12},{9,13},{10,... | collective-permute-start | bytes 835592 | tf_op jit(solution)/shard_map/ppermute | solution.py:234
  4.8 1.6 %collective-permute-start.4 = (bf16[136,1024]{1,0:T(8,128)(2,1)}, bf16[136,1024]{1,0:T(8,128)(2,1)S(1)}, u32[]{:S(2)}, u32[]{:S(2)}) collective-permute-start(bf16[136,1024]{1,0:T(8,128)(2,1)} %normalize.1.refs_0_), channel_id=1, source_target_pairs={{0,0},{1,1},{2,2},{3,3},{4,8},{5,9},{6,10},{7,11},{8,4},{9,5},{10,... | collective-permute-start | bytes 835592 | tf_op jit(solution)/shard_map/ppermute | solution.py:241
  6.4 5.3 %collective-permute-done.3.refs_4_ = bf16[136,1024]{1,0:T(8,128)(2,1)S(1)} collective-permute-done((bf16[136,1024]{1,0:T(8,128)(2,1)}, bf16[136,1024]{1,0:T(8,128)(2,1)S(1)}, u32[]{:S(2)}, u32[]{:S(2)}) %collective-permute-start.3) | collective-permute-done | bytes 278560 | tf_op jit(solution)/shard_map/ppermute | solution.py:234
  11.7 0.0 copy-start.7
  11.7 0.7 %collective-permute-start.5 = (bf16[136,1024]{1,0:T(8,128)(2,1)S(1)}, bf16[136,1024]{1,0:T(8,128)(2,1)S(1)}, u32[]{:S(2)}, u32[]{:S(2)}) collective-permute-start(bf16[136,1024]{1,0:T(8,128)(2,1)S(1)} %collective-permute-done.3.refs_4_), channel_id=1, source_target_pairs={{0,0},{1,1},{2,2},{3,3},{4,8},{5,9},{6,10},{7,11},{8,4},{9,5},{10,... | collective-permute-start | bytes 835592 | tf_op jit(solution)/shard_map/ppermute | solution.py:241
  12.4 0.1 collective-permute-start
  12.5 1.7 %collective-permute-start.1 = (bf16[136,1024]{1,0:T(8,128)(2,1)}, bf16[136,1024]{1,0:T(8,128)(2,1)S(1)}, u32[]{:S(2)}, u32[]{:S(2)}) collective-permute-start(bf16[136,1024]{1,0:T(8,128)(2,1)} %normalize.1.refs_0_), channel_id=1, source_target_pairs={{0,2},{1,3},{2,0},{3,1},{4,6},{5,7},{6,4},{7,5},{8,10},{9,11},{10,... | collective-permute-start | bytes 835592 | tf_op jit(solution)/shard_map/ppermute | solution.py:234
  14.2 0.1 collective-permute-start.2
  14.3 0.0 collective-permute-done.4.refs_4_
  14.3 0.0 copy-start.3
  14.3 4.5 %collective-permute-start.6 = (bf16[136,1024]{1,0:T(8,128)(2,1)S(1)}, bf16[136,1024]{1,0:T(8,128)(2,1)S(1)}, u32[]{:S(2)}, u32[]{:S(2)}) collective-permute-start(bf16[136,1024]{1,0:T(8,128)(2,1)S(1)} %collective-permute-done.4.refs_4_), channel_id=1, source_target_pairs={{0,4},{1,5},{2,6},{3,7},{4,0},{5,1},{6,2},{7,3},{8,12},{9,13},{10,... | collective-permute-start | bytes 835592 | tf_op jit(solution)/shard_map/ppermute | solution.py:234
  18.9 0.0 collective-permute-done.5.refs_5_
  18.9 0.0 copy-start.4
  18.9 4.0 %collective-permute-start.7 = (bf16[136,1024]{1,0:T(8,128)(2,1)S(1)}, bf16[136,1024]{1,0:T(8,128)(2,1)S(1)}, u32[]{:S(2)}, u32[]{:S(2)}) collective-permute-start(bf16[136,1024]{1,0:T(8,128)(2,1)S(1)} %collective-permute-done.5.refs_5_), channel_id=1, source_target_pairs={{0,4},{1,5},{2,6},{3,7},{4,0},{5,1},{6,2},{7,3},{8,12},{9,13},{10,... | collective-permute-start | bytes 835592 | tf_op jit(solution)/shard_map/ppermute | solution.py:234
  22.9 0.0 collective-permute-done.refs_1_
  22.9 0.0 copy-start
  22.9 0.0 collective-permute-done.1.refs_2_
  22.9 0.0 copy-start.1
  22.9 4.4 %collective-permute-done.2.refs_3_ = bf16[136,1024]{1,0:T(8,128)(2,1)S(1)} collective-permute-done((bf16[136,1024]{1,0:T(8,128)(2,1)}, bf16[136,1024]{1,0:T(8,128)(2,1)S(1)}, u32[]{:S(2)}, u32[]{:S(2)}) %collective-permute-start.2) | collective-permute-done | bytes 278560 | tf_op jit(solution)/shard_map/ppermute | solution.py:234
  27.2 0.0 copy-done.7
  27.3 0.0 copy-done
  27.3 0.0 copy-done.1
  27.3 0.0 copy-start.2
  27.3 0.7 %copy-done.2 = bf16[136,1024]{1,0:T(8,128)(2,1)} copy-done((bf16[136,1024]{1,0:T(8,128)(2,1)}, bf16[136,1024]{1,0:T(8,128)(2,1)S(1)}, u32[]{:S(2)}) %copy-start.2) | copy-done | bytes 278552
  28.0 2.7 %early.1.best_ref = f32[8,512]{1,0:T(8,128)} custom-call(bf16[136,1024]{1,0:T(8,128)(2,1)} %normalize.1.refs_0_, bf16[136,1024]{1,0:T(8,128)(2,1)} %copy-done, bf16[136,1024]{1,0:T(8,128)(2,1)} %copy-done.1, bf16[136,1024]{1,0:T(8,128)(2,1)} %copy-done.2, bf16[136,1024]{1,0:T(8,128)(2,1)} %copy-done.7), custom_call_target="tpu_custom_call" | custom-call | tf_op jit(solution)/shard_map/early/pallas_call | solution.py:198
  30.7 0.0 collective-permute-done.6.refs_6_
  30.7 0.0 copy-start.5
  30.7 1.3 %collective-permute-done.7.refs_7_ = bf16[136,1024]{1,0:T(8,128)(2,1)S(1)} collective-permute-done((bf16[136,1024]{1,0:T(8,128)(2,1)S(1)}, bf16[136,1024]{1,0:T(8,128)(2,1)S(1)}, u32[]{:S(2)}, u32[]{:S(2)}) %collective-permute-start.7) | collective-permute-done | bytes 278560 | tf_op jit(solution)/shard_map/ppermute | solution.py:234
  32.0 0.0 copy-start.6
  32.0 0.0 copy-done.3
  32.0 0.0 copy-done.4
  32.0 0.0 copy-done.5
  32.0 0.7 %copy-done.6 = bf16[136,1024]{1,0:T(8,128)(2,1)} copy-done((bf16[136,1024]{1,0:T(8,128)(2,1)}, bf16[136,1024]{1,0:T(8,128)(2,1)S(1)}, u32[]{:S(2)}) %copy-start.6) | copy-done | bytes 278552
  32.7 3.0 %late.1 = (f32[8,128]{1,0:T(8,128)}, f32[8,128]{1,0:T(8,128)}, f32[8,128]{1,0:T(8,128)}, f32[8,128]{1,0:T(8,128)}) custom-call(s32[1,1]{1,0:T(1,128)} %bitcast.edge_ref, f32[8,512]{1,0:T(8,128)} %early.1.best_ref, bf16[136,1024]{1,0:T(8,128)(2,1)} %normalize.1.refs_0_, bf16[136,1024]{1,0:T(8,128)(2,1)} %copy-done, bf16[136,1024]{1,0:T(8,128)(2,1)} %copy-done.1, ...), custom_call_target="tpu_custom_call" | custom-call | tf_op jit(solution)/shard_map/late/pallas_call | solution.py:221
  35.7 0.0 copy-start.8
  35.7 1.0 %collective-permute-start.10 = (f32[8,128]{1,0:T(8,128)}, f32[8,128]{1,0:T(8,128)S(1)}, u32[]{:S(2)}, u32[]{:S(2)}) collective-permute-start(f32[8,128]{1,0:T(8,128)} %get-tuple-element.12), channel_id=1, source_target_pairs={{0,3},{1,2},{2,1},{3,0},{4,7},{5,6},{6,5},{7,4},{8,11},{9,10},{10,... | collective-permute-start | bytes 12296 | tf_op jit(solution)/shard_map/ppermute | solution.py:234
  36.7 0.7 %collective-permute-start.8 = (f32[8,128]{1,0:T(8,128)}, f32[8,128]{1,0:T(8,128)S(1)}, u32[]{:S(2)}, u32[]{:S(2)}) collective-permute-start(f32[8,128]{1,0:T(8,128)} %get-tuple-element.10), channel_id=1, source_target_pairs={{0,1},{1,0},{2,3},{3,2},{4,5},{5,4},{6,7},{7,6},{8,9},{9,8},{10,11... | collective-permute-start | bytes 12296 | tf_op jit(solution)/shard_map/ppermute | solution.py:234
  37.4 0.5 %collective-permute-start.9 = (f32[8,128]{1,0:T(8,128)}, f32[8,128]{1,0:T(8,128)S(1)}, u32[]{:S(2)}, u32[]{:S(2)}) collective-permute-start(f32[8,128]{1,0:T(8,128)} %get-tuple-element.11), channel_id=1, source_target_pairs={{0,2},{1,3},{2,0},{3,1},{4,6},{5,7},{6,4},{7,5},{8,10},{9,11},{10,... | collective-permute-start | bytes 12296 | tf_op jit(solution)/shard_map/ppermute | solution.py:234
  37.9 1.1 %collective-permute-done.10 = f32[8,128]{1,0:T(8,128)S(1)} collective-permute-done((f32[8,128]{1,0:T(8,128)}, f32[8,128]{1,0:T(8,128)S(1)}, u32[]{:S(2)}, u32[]{:S(2)}) %collective-permute-start.10) | collective-permute-done | bytes 4128 | tf_op jit(solution)/shard_map/ppermute | solution.py:234
  39.0 0.0 collective-permute-done.8
  39.0 2.2 %collective-permute-done.9 = f32[8,128]{1,0:T(8,128)S(1)} collective-permute-done((f32[8,128]{1,0:T(8,128)}, f32[8,128]{1,0:T(8,128)S(1)}, u32[]{:S(2)}, u32[]{:S(2)}) %collective-permute-start.9) | collective-permute-done | bytes 4128 | tf_op jit(solution)/shard_map/ppermute | solution.py:234
  41.2 0.0 copy-done.8
  41.2 0.5 %slice_bitcast_fusion = f32[128]{0:T(128)} fusion(f32[8,128]{1,0:T(8,128)S(1)} %maximum_maximum_fusion), kind=kLoop, calls=%fused_computation.1 | loop fusion | bytes 1024 | tf_op jit(solution)/shard_map/squeeze | solution.py:261
  (1 shorter events, 0.0 us)
Async XLA Ops:
  1.8 9.9 %collective-permute-start.3 = (bf16[136,1024]{1,0:T(8,128)(2,1)}, bf16[136,1024]{1,0:T(8,128)(2,1)S(1)}, u32[]{:S(2)}, u32[]{:S(2)}) collective-permute-start(bf16[136,1024]{1,0:T(8,128)(2,1)} %normalize.1.refs_0_), channel_id=1, source_target_pairs={{0,4},{1,5},{2,6},{3,7},{4,0},{5,1},{6,2},{7,3},{8,12},{9,13},{10,... | collective-permute-start | bytes 835592 | tf_op jit(solution)/shard_map/ppermute | solution.py:234
  4.8 9.5 %collective-permute-start.4 = (bf16[136,1024]{1,0:T(8,128)(2,1)}, bf16[136,1024]{1,0:T(8,128)(2,1)S(1)}, u32[]{:S(2)}, u32[]{:S(2)}) collective-permute-start(bf16[136,1024]{1,0:T(8,128)(2,1)} %normalize.1.refs_0_), channel_id=1, source_target_pairs={{0,0},{1,1},{2,2},{3,3},{4,8},{5,9},{6,10},{7,11},{8,4},{9,5},{10,... | collective-permute-start | bytes 835592 | tf_op jit(solution)/shard_map/ppermute | solution.py:241
  11.7 15.6 %copy-start.7 = (bf16[136,1024]{1,0:T(8,128)(2,1)}, bf16[136,1024]{1,0:T(8,128)(2,1)S(1)}, u32[]{:S(2)}) copy-start(bf16[136,1024]{1,0:T(8,128)(2,1)S(1)} %collective-permute-done.3.refs_4_) | copy-start | bytes 835588
  11.7 7.2 %collective-permute-start.5 = (bf16[136,1024]{1,0:T(8,128)(2,1)S(1)}, bf16[136,1024]{1,0:T(8,128)(2,1)S(1)}, u32[]{:S(2)}, u32[]{:S(2)}) collective-permute-start(bf16[136,1024]{1,0:T(8,128)(2,1)S(1)} %collective-permute-done.3.refs_4_), channel_id=1, source_target_pairs={{0,0},{1,1},{2,2},{3,3},{4,8},{5,9},{6,10},{7,11},{8,4},{9,5},{10,... | collective-permute-start | bytes 835592 | tf_op jit(solution)/shard_map/ppermute | solution.py:241
  12.4 10.5 %collective-permute-start = (bf16[136,1024]{1,0:T(8,128)(2,1)}, bf16[136,1024]{1,0:T(8,128)(2,1)S(1)}, u32[]{:S(2)}, u32[]{:S(2)}) collective-permute-start(bf16[136,1024]{1,0:T(8,128)(2,1)} %normalize.1.refs_0_), channel_id=1, source_target_pairs={{0,1},{1,0},{2,3},{3,2},{4,5},{5,4},{6,7},{7,6},{8,9},{9,8},{10,11... | collective-permute-start | bytes 835592 | tf_op jit(solution)/shard_map/ppermute | solution.py:234
  12.5 10.4 %collective-permute-start.1 = (bf16[136,1024]{1,0:T(8,128)(2,1)}, bf16[136,1024]{1,0:T(8,128)(2,1)S(1)}, u32[]{:S(2)}, u32[]{:S(2)}) collective-permute-start(bf16[136,1024]{1,0:T(8,128)(2,1)} %normalize.1.refs_0_), channel_id=1, source_target_pairs={{0,2},{1,3},{2,0},{3,1},{4,6},{5,7},{6,4},{7,5},{8,10},{9,11},{10,... | collective-permute-start | bytes 835592 | tf_op jit(solution)/shard_map/ppermute | solution.py:234
  14.2 13.1 %collective-permute-start.2 = (bf16[136,1024]{1,0:T(8,128)(2,1)}, bf16[136,1024]{1,0:T(8,128)(2,1)S(1)}, u32[]{:S(2)}, u32[]{:S(2)}) collective-permute-start(bf16[136,1024]{1,0:T(8,128)(2,1)} %normalize.1.refs_0_), channel_id=1, source_target_pairs={{0,3},{1,2},{2,1},{3,0},{4,7},{5,6},{6,5},{7,4},{8,11},{9,10},{10,... | collective-permute-start | bytes 835592 | tf_op jit(solution)/shard_map/ppermute | solution.py:234
  14.3 17.7 %copy-start.3 = (bf16[136,1024]{1,0:T(8,128)(2,1)}, bf16[136,1024]{1,0:T(8,128)(2,1)S(1)}, u32[]{:S(2)}) copy-start(bf16[136,1024]{1,0:T(8,128)(2,1)S(1)} %collective-permute-done.4.refs_4_) | copy-start | bytes 835588
  14.3 16.4 %collective-permute-start.6 = (bf16[136,1024]{1,0:T(8,128)(2,1)S(1)}, bf16[136,1024]{1,0:T(8,128)(2,1)S(1)}, u32[]{:S(2)}, u32[]{:S(2)}) collective-permute-start(bf16[136,1024]{1,0:T(8,128)(2,1)S(1)} %collective-permute-done.4.refs_4_), channel_id=1, source_target_pairs={{0,4},{1,5},{2,6},{3,7},{4,0},{5,1},{6,2},{7,3},{8,12},{9,13},{10,... | collective-permute-start | bytes 835592 | tf_op jit(solution)/shard_map/ppermute | solution.py:234
  18.9 13.1 %copy-start.4 = (bf16[136,1024]{1,0:T(8,128)(2,1)}, bf16[136,1024]{1,0:T(8,128)(2,1)S(1)}, u32[]{:S(2)}) copy-start(bf16[136,1024]{1,0:T(8,128)(2,1)S(1)} %collective-permute-done.5.refs_5_) | copy-start | bytes 835588
  18.9 13.1 %collective-permute-start.7 = (bf16[136,1024]{1,0:T(8,128)(2,1)S(1)}, bf16[136,1024]{1,0:T(8,128)(2,1)S(1)}, u32[]{:S(2)}, u32[]{:S(2)}) collective-permute-start(bf16[136,1024]{1,0:T(8,128)(2,1)S(1)} %collective-permute-done.5.refs_5_), channel_id=1, source_target_pairs={{0,4},{1,5},{2,6},{3,7},{4,0},{5,1},{6,2},{7,3},{8,12},{9,13},{10,... | collective-permute-start | bytes 835592 | tf_op jit(solution)/shard_map/ppermute | solution.py:234
  22.9 4.4 %copy-start = (bf16[136,1024]{1,0:T(8,128)(2,1)}, bf16[136,1024]{1,0:T(8,128)(2,1)S(1)}, u32[]{:S(2)}) copy-start(bf16[136,1024]{1,0:T(8,128)(2,1)S(1)} %collective-permute-done.refs_1_) | copy-start | bytes 835588
  22.9 4.4 %copy-start.1 = (bf16[136,1024]{1,0:T(8,128)(2,1)}, bf16[136,1024]{1,0:T(8,128)(2,1)S(1)}, u32[]{:S(2)}) copy-start(bf16[136,1024]{1,0:T(8,128)(2,1)S(1)} %collective-permute-done.1.refs_2_) | copy-start | bytes 835588
  27.3 0.7 %copy-start.2 = (bf16[136,1024]{1,0:T(8,128)(2,1)}, bf16[136,1024]{1,0:T(8,128)(2,1)S(1)}, u32[]{:S(2)}) copy-start(bf16[136,1024]{1,0:T(8,128)(2,1)S(1)} %collective-permute-done.2.refs_3_) | copy-start | bytes 835588
  30.7 1.3 %copy-start.5 = (bf16[136,1024]{1,0:T(8,128)(2,1)}, bf16[136,1024]{1,0:T(8,128)(2,1)S(1)}, u32[]{:S(2)}) copy-start(bf16[136,1024]{1,0:T(8,128)(2,1)S(1)} %collective-permute-done.6.refs_6_) | copy-start | bytes 835588
  32.0 0.7 %copy-start.6 = (bf16[136,1024]{1,0:T(8,128)(2,1)}, bf16[136,1024]{1,0:T(8,128)(2,1)S(1)}, u32[]{:S(2)}) copy-start(bf16[136,1024]{1,0:T(8,128)(2,1)S(1)} %collective-permute-done.7.refs_7_) | copy-start | bytes 835588
  35.7 5.5 %copy-start.8 = (f32[8,128]{1,0:T(8,128)S(1)}, f32[8,128]{1,0:T(8,128)}, u32[]{:S(2)}) copy-start(f32[8,128]{1,0:T(8,128)} %get-tuple-element.9) | copy-start | bytes 12292
  35.7 3.3 %collective-permute-start.10 = (f32[8,128]{1,0:T(8,128)}, f32[8,128]{1,0:T(8,128)S(1)}, u32[]{:S(2)}, u32[]{:S(2)}) collective-permute-start(f32[8,128]{1,0:T(8,128)} %get-tuple-element.12), channel_id=1, source_target_pairs={{0,3},{1,2},{2,1},{3,0},{4,7},{5,6},{6,5},{7,4},{8,11},{9,10},{10,... | collective-permute-start | bytes 12296 | tf_op jit(solution)/shard_map/ppermute | solution.py:234
  36.7 2.3 %collective-permute-start.8 = (f32[8,128]{1,0:T(8,128)}, f32[8,128]{1,0:T(8,128)S(1)}, u32[]{:S(2)}, u32[]{:S(2)}) collective-permute-start(f32[8,128]{1,0:T(8,128)} %get-tuple-element.10), channel_id=1, source_target_pairs={{0,1},{1,0},{2,3},{3,2},{4,5},{5,4},{6,7},{7,6},{8,9},{9,8},{10,11... | collective-permute-start | bytes 12296 | tf_op jit(solution)/shard_map/ppermute | solution.py:234
  37.4 3.8 %collective-permute-start.9 = (f32[8,128]{1,0:T(8,128)}, f32[8,128]{1,0:T(8,128)S(1)}, u32[]{:S(2)}, u32[]{:S(2)}) collective-permute-start(f32[8,128]{1,0:T(8,128)} %get-tuple-element.11), channel_id=1, source_target_pairs={{0,2},{1,3},{2,0},{3,1},{4,6},{5,7},{6,4},{7,5},{8,10},{9,11},{10,... | collective-permute-start | bytes 12296 | tf_op jit(solution)/shard_map/ppermute | solution.py:234

commit v4 on v3

--- a/solution.py
+++ b/solution.py
@@ -15,6 +15,8 @@
 EMPTY = 4.0
 NONE = -2.0
 TAIL = 8
+HIGH, LOW, SHARD, SUB = 8, 4, 2, 1
+LIMIT = pltpu.CompilerParams(vmem_limit_bytes=12 << 20)
 AXES = ("blk", "shard", "sub")
 
 VMEM = pl.BlockSpec(memory_space=pltpu.VMEM)
@@ -156,6 +158,7 @@
         out_shape=jax.ShapeDtypeStruct((rows + TAIL, width), jnp.bfloat16),
         in_specs=[VMEM, VMEM],
         out_specs=VMEM,
+        compiler_params=LIMIT,
         name="normalize",
     )(embeddings, assignment.reshape(1, rows))
 
@@ -165,7 +168,7 @@
     return block[:rows], block[rows : rows + 1, :rows].astype(jnp.float32)
 
 
-def best_against(own, others, same_rows):
+def best_of(own, others, same_rows=False):
     rows, clusters = zip(*[split(block) for block in own])
     rows, clusters = jnp.concatenate(rows, axis=0), jnp.concatenate(clusters, axis=1)
     best = None
@@ -186,81 +189,64 @@
     return best
 
 
-def early_kernel(*refs):
-    *own_refs, other_ref, out_ref = refs
-    own = [ref[...] for ref in own_refs]
-    best = best_against(own, [own[0], other_ref[...]], True)
+def early_kernel(x_ref, e_ref, mine_ref, c_ref, out_ref):
+    mine = mine_ref[...]
+    best = best_of([mine, x_ref[...], e_ref[...]], [mine, c_ref[...]], True)
     out_ref[...] = jnp.broadcast_to(best, out_ref.shape)
 
 
-def early(own, other):
-    rows = own[0].shape[0] - TAIL
+def early(x, e, mine, c):
+    rows = mine.shape[0] - TAIL
     return pl.pallas_call(
         early_kernel,
-        out_shape=jax.ShapeDtypeStruct((8, len(own) * rows), jnp.float32),
-        in_specs=[VMEM] * (len(own) + 1),
+        out_shape=jax.ShapeDtypeStruct((8, 3 * rows), jnp.float32),
+        in_specs=[VMEM] * 4,
         out_specs=VMEM,
+        compiler_params=LIMIT,
         name="early",
-    )(*own, other)
-
-
-def late_kernel(edge_ref, best_ref, *refs):
-    own_refs, far_refs, out_refs = refs[:4], refs[4:8], refs[8:]
-    edge = edge_ref[0, 0] > 0
-    m1, m2, e2, e3 = [ref[...] for ref in far_refs]
-    others = [jnp.where(edge, e2, m1), jnp.where(edge, e3, m2)]
-    best = best_against([ref[...] for ref in own_refs], others, False)
+    )(x, e, mine, c)
+
+
+def late_kernel(best_ref, x_ref, e_ref, xe_ref, mine_ref, c_ref, h_ref, ch_ref, *out_refs):
+    mine, h, ch = mine_ref[...], h_ref[...], ch_ref[...]
+    best = best_of([mine, x_ref[...], e_ref[...]], [h, ch])
     best = jnp.maximum(best, best_ref[:1, :])
+    last = best_of([xe_ref[...]], [mine, c_ref[...], h, ch])
+    best = jnp.concatenate([best, last], axis=1)
     for place, out_ref in enumerate(out_refs):
         rows = out_ref.shape[1]
         out_ref[...] = jnp.broadcast_to(best[:, place * rows : (place + 1) * rows], out_ref.shape)
 
 
-def late(edge, best, own, far):
-    rows = own[0].shape[0] - TAIL
+def late(best, x, e, xe, mine, c, h, ch):
+    rows = mine.shape[0] - TAIL
     return pl.pallas_call(
         late_kernel,
-        out_shape=[jax.ShapeDtypeStruct((8, rows), jnp.float32)] * len(own),
-        in_specs=[SMEM] + [VMEM] * (1 + len(own) + len(far)),
-        out_specs=[VMEM] * len(own),
+        out_shape=[jax.ShapeDtypeStruct((8, rows), jnp.float32)] * 4,
+        in_specs=[VMEM] * 8,
+        out_specs=[VMEM] * 4,
+        compiler_params=LIMIT,
         name="late",
-    )(edge, best, *own, *far)
-
-
-def line(blk, plane):
-    size = 4 * plane
-
-    def within(flip, array):
-        return lax.ppermute(array, AXES, [(i, i ^ flip) for i in range(size)])
-
-    def outer(array):
-        return within(plane, array)
-
-    def inner(array):
-        swapped = [0, 2, 1, 3]
-        return lax.ppermute(
-            array, AXES, [(i, swapped[i // plane] * plane + i % plane) for i in range(size)]
-        )
-
-    def local(embeddings, assignment):
-        mine = normalize(embeddings, assignment)
-        e1 = outer(mine)
-        m1 = inner(mine)
-        others = [within(flip, mine) for flip in range(1, plane)]
-        m2 = inner(e1)
-        e2 = outer(m1)
-        e3 = outer(m2)
-        own = [mine] + others
-        best = early(own, e1)
-        place = lax.axis_index(blk)
-        edge = ((place == 0) | (place == 3)).astype(jnp.int32).reshape(1, 1)
-        bests = late(edge, best, own, [m1, m2, e2, e3])
-        found = bests[0]
-        for flip in range(1, plane):
-            found = jnp.maximum(found, within(flip, bests[flip]))
-        return found[0]
-
-    return local
+    )(best, x, e, xe, mine, c, h, ch)
+
+
+def square(embeddings, assignment):
+    def swap(flip, array):
+        return lax.ppermute(array, AXES, [(i, i ^ flip) for i in range(16)])
+
+    mine = normalize(embeddings, assignment)
+    e = swap(LOW, mine)
+    x = swap(SHARD, mine)
+    c = swap(SUB, mine)
+    then, c = lax.optimization_barrier((mine, c))
+    h = swap(HIGH, then)
+    xe = swap(SHARD, e)
+    ch = swap(SUB, h)
+    best = early(x, e, mine, c)
+    found, *others = late(best, x, e, xe, mine, c, h, ch)
+    for flip, other in zip((SHARD, LOW, LOW | SHARD), others):
+        found = jnp.maximum(found, swap(flip, other))
+    return found[0]
 
 
 def shared_owner(embeddings, assignment):
@@ -281,8 +267,8 @@
         P(("groups", "blk", "shard", "sub"), None),
         P(("groups", "blk", "shard", "sub"), None),
     )
-    plane = mesh.shape["shard"] * mesh.shape["sub"]
-    program = line("blk", plane) if mesh.shape["blk"] == 4 and plane == 4 else shared_owner
+    four_bits = [mesh.shape[axis] for axis in AXES] == [4, 2, 2]
+    program = square if four_bits else shared_owner
     return jax.shard_map(
         program,
         mesh=mesh,

time: 42.3 us -> 34.1 us (0.81); the launches traced: 41.7 us -> 33.9 us
  Pallas kernels: 7.53 us -> 1.68 us
  starting transfers between devices: 17.9 us -> 12.5 us
  waiting for transfers between devices: 14.2 us -> 17.6 us
    ppermute x11 -> x9, starting transfers between devices: 17.9 us -> 12.5 us  [swap(): return lax.ppermute(array, AXES, [(i, i ^ flip) for i in range(16)])]
    ppermute x11 -> x9, waiting for transfers between devices: 14.2 us -> 17.6 us  [swap(): return lax.ppermute(array, AXES, [(i, i ^ flip) for i in range(16)])]
    pallas_call x1, Pallas kernels: 3 us -> 0.9 us  [late(): pl.pallas_call(late_kernel, out_shape=[jax.ShapeDtypeStruct((8, rows), jn...]
    pallas_call x1, Pallas kernels: 2.72 us -> 0.63 us  [early(): pl.pallas_call(early_kernel, out_shape=jax.ShapeDtypeStruct((8, 3 * rows)...]
    pallas_call x1, Pallas kernels: 1.81 us -> 0.15 us  [normalize(): pl.pallas_call(normalize_kernel, out_shape=jax.ShapeDtypeStruct((rows + T...]
    unnamed x18 -> x4, local copies, waits for them, and re-layouts: 1.42 us -> 1.6 us
  transfers between devices with their start and end apart: 11 -> 9, of which waited for: 5 -> 6; matrix products, arithmetic and copies ran while one was open for 0% -> 0% of each run, Pallas kernels for 7% -> 2%
where the time goes in v4:
time: 34.1 us; the launch traced here: 33.9 us
  waiting for transfers between devices  17.6 us (52%)
  starting transfers between devices  12.5 us (37%)
  local copies, waits for them, and re-layouts  2.12 us (6%)
  Pallas kernels  1.68 us (5%)
    ppermute x9, waiting for transfers between devices, swap(): return lax.ppermute(array, AXES, [(i, i ^ flip) for i in range(16)])  17.6 us
    ppermute x9, starting transfers between devices, swap(): return lax.ppermute(array, AXES, [(i, i ^ flip) for i in range(16)])  12.5 us
    unnamed x4, local copies, waits for them, and re-layouts  1.6 us
    pallas_call x1, Pallas kernels, late(): pl.pallas_call(late_kernel, out_shape=[jax.ShapeDtypeStruct((8, rows), jn...  0.9 us
  transfers between devices with their start and end apart: 9, of which 6 were waited for; matrix products, arithmetic and copies ran while one was open for 0% of the time, Pallas kernels for 2%

profile of v4, /device:TPU:0, one launch (start us, length us, event | category | flops | bytes accessed | tf_op | source)
XLA Modules:
  0.0 33.9 jit_solution(17392717840441715207)
XLA Ops:
  0.0 0.0 copy-start.1
  0.0 0.7 %copy-done.1 = s32[128,1]{0,1:T(1,128)S(1)} copy-done((s32[128,1]{0,1:T(1,128)S(1)}, s32[128,1]{0,1:T(1,128)}, u32[]{:S(2)}) %copy-start.1) | copy-done | bytes 536
  0.7 0.0 copy-start
  0.7 0.9 %copy-done = bf16[128,1024]{1,0:T(8,128)(2,1)S(1)} copy-done((bf16[128,1024]{1,0:T(8,128)(2,1)S(1)}, bf16[128,1024]{1,0:T(8,128)(2,1)}, u32[]{:S(2)}) %copy-start) | copy-done | bytes 262168
  1.6 0.2 normalize.1.mine_ref
  1.8 0.5 %collective-permute-start.2 = (bf16[136,1024]{1,0:T(8,128)(2,1)S(1)}, bf16[136,1024]{1,0:T(8,128)(2,1)S(1)}, u32[]{:S(2)}, u32[]{:S(2)}) collective-permute-start(bf16[136,1024]{1,0:T(8,128)(2,1)S(1)} %normalize.1.mine_ref), channel_id=1, source_target_pairs={{0,1},{1,0},{2,3},{3,2},{4,5},{5,4},{6,7},{7,6},{8,9},{9,8},{10,11... | collective-permute-start | bytes 835592 | tf_op jit(solution)/shard_map/ppermute | solution.py:235
  2.3 2.6 %collective-permute-start.1 = (bf16[136,1024]{1,0:T(8,128)(2,1)S(1)}, bf16[136,1024]{1,0:T(8,128)(2,1)S(1)}, u32[]{:S(2)}, u32[]{:S(2)}) collective-permute-start(bf16[136,1024]{1,0:T(8,128)(2,1)S(1)} %normalize.1.mine_ref), channel_id=1, source_target_pairs={{0,4},{1,5},{2,6},{3,7},{4,0},{5,1},{6,2},{7,3},{8,12},{9,13},{10,... | collective-permute-start | bytes 835592 | tf_op jit(solution)/shard_map/ppermute | solution.py:235
  4.9 0.0 collective-permute-done.2.c_ref
  4.9 2.6 %collective-permute-start.4 = (bf16[136,1024]{1,0:T(8,128)(2,1)S(1)}, bf16[136,1024]{1,0:T(8,128)(2,1)S(1)}, u32[]{:S(2)}, u32[]{:S(2)}) collective-permute-start(bf16[136,1024]{1,0:T(8,128)(2,1)S(1)} %normalize.1.mine_ref), channel_id=1, source_target_pairs={{0,8},{1,9},{2,10},{3,11},{4,12},{5,13},{6,14},{7,15},{8,0},{9,1},... | collective-permute-start | bytes 835592 | tf_op jit(solution)/shard_map/ppermute | solution.py:235
  7.5 1.5 %collective-permute-start = (bf16[136,1024]{1,0:T(8,128)(2,1)S(1)}, bf16[136,1024]{1,0:T(8,128)(2,1)S(1)}, u32[]{:S(2)}, u32[]{:S(2)}) collective-permute-start(bf16[136,1024]{1,0:T(8,128)(2,1)S(1)} %normalize.1.mine_ref), channel_id=1, source_target_pairs={{0,2},{1,3},{2,0},{3,1},{4,6},{5,7},{6,4},{7,5},{8,10},{9,11},{10,... | collective-permute-start | bytes 835592 | tf_op jit(solution)/shard_map/ppermute | solution.py:235
  9.0 9.0 %collective-permute-done.1.e_ref = bf16[136,1024]{1,0:T(8,128)(2,1)S(1)} collective-permute-done((bf16[136,1024]{1,0:T(8,128)(2,1)S(1)}, bf16[136,1024]{1,0:T(8,128)(2,1)S(1)}, u32[]{:S(2)}, u32[]{:S(2)}) %collective-permute-start.1) | collective-permute-done | bytes 278560 | tf_op jit(solution)/shard_map/ppermute | solution.py:235
  18.0 1.7 %collective-permute-start.3 = (bf16[136,1024]{1,0:T(8,128)(2,1)S(1)}, bf16[136,1024]{1,0:T(8,128)(2,1)S(1)}, u32[]{:S(2)}, u32[]{:S(2)}) collective-permute-start(bf16[136,1024]{1,0:T(8,128)(2,1)S(1)} %collective-permute-done.1.e_ref), channel_id=1, source_target_pairs={{0,2},{1,3},{2,0},{3,1},{4,6},{5,7},{6,4},{7,5},{8,10},{9,11},{10,... | collective-permute-start | bytes 835592 | tf_op jit(solution)/shard_map/ppermute | solution.py:235
  19.7 0.9 %collective-permute-done.4.h_ref = bf16[136,1024]{1,0:T(8,128)(2,1)S(1)} collective-permute-done((bf16[136,1024]{1,0:T(8,128)(2,1)S(1)}, bf16[136,1024]{1,0:T(8,128)(2,1)S(1)}, u32[]{:S(2)}, u32[]{:S(2)}) %collective-permute-start.4) | collective-permute-done | bytes 278560 | tf_op jit(solution)/shard_map/ppermute | solution.py:235
  20.6 0.0 collective-permute-start.5
  20.6 0.0 collective-permute-done.x_ref
  20.6 0.6 %early.1.best_ref = f32[8,384]{1,0:T(8,128)S(1)} custom-call(bf16[136,1024]{1,0:T(8,128)(2,1)S(1)} %collective-permute-done.x_ref, bf16[136,1024]{1,0:T(8,128)(2,1)S(1)} %collective-permute-done.1.e_ref, bf16[136,1024]{1,0:T(8,128)(2,1)S(1)} %normalize.1.mine_ref, bf16[136,1024]{1,0:T(8,128)(2,1)S(1)} %collective-permute-done.2.c_ref), custom_call_target="tpu_custom_call" | custom-call | tf_op jit(solution)/shard_map/early/pallas_call | solution.py:200
  21.2 5.2 %collective-permute-done.3.xe_ref = bf16[136,1024]{1,0:T(8,128)(2,1)S(1)} collective-permute-done((bf16[136,1024]{1,0:T(8,128)(2,1)S(1)}, bf16[136,1024]{1,0:T(8,128)(2,1)S(1)}, u32[]{:S(2)}, u32[]{:S(2)}) %collective-permute-start.3) | collective-permute-done | bytes 278560 | tf_op jit(solution)/shard_map/ppermute | solution.py:235
  26.5 0.0 collective-permute-done.5.ch_ref
  26.5 0.9 %late.1 = (f32[8,128]{1,0:T(8,128)S(1)}, f32[8,128]{1,0:T(8,128)S(1)}, f32[8,128]{1,0:T(8,128)S(1)}, f32[8,128]{1,0:T(8,128)S(1)}) custom-call(f32[8,384]{1,0:T(8,128)S(1)} %early.1.best_ref, bf16[136,1024]{1,0:T(8,128)(2,1)S(1)} %collective-permute-done.x_ref, bf16[136,1024]{1,0:T(8,128)(2,1)S(1)} %collective-permute-done.1.e_ref, ...), custom_call_target="tpu_custom_call" | custom-call | tf_op jit(solution)/shard_map/late/pallas_call | solution.py:223
  27.4 1.5 %collective-permute-start.6 = (f32[8,128]{1,0:T(8,128)S(1)}, f32[8,128]{1,0:T(8,128)S(1)}, u32[]{:S(2)}, u32[]{:S(2)}) collective-permute-start(f32[8,128]{1,0:T(8,128)S(1)} %get-tuple-element.14), channel_id=1, source_target_pairs={{0,2},{1,3},{2,0},{3,1},{4,6},{5,7},{6,4},{7,5},{8,10},{9,11},{10,... | collective-permute-start | bytes 12296 | tf_op jit(solution)/shard_map/ppermute | solution.py:235
  28.9 0.0 collective-permute-start.7
  28.9 2.0 %collective-permute-start.8 = (f32[8,128]{1,0:T(8,128)S(1)}, f32[8,128]{1,0:T(8,128)S(1)}, u32[]{:S(2)}, u32[]{:S(2)}) collective-permute-start(f32[8,128]{1,0:T(8,128)S(1)} %get-tuple-element.16), channel_id=1, source_target_pairs={{0,6},{1,7},{2,4},{3,5},{4,2},{5,3},{6,0},{7,1},{8,14},{9,15},{10,... | collective-permute-start | bytes 12296 | tf_op jit(solution)/shard_map/ppermute | solution.py:235
  30.9 0.1 collective-permute-done.6
  31.0 1.5 %collective-permute-done.7 = f32[8,128]{1,0:T(8,128)S(1)} collective-permute-done((f32[8,128]{1,0:T(8,128)S(1)}, f32[8,128]{1,0:T(8,128)S(1)}, u32[]{:S(2)}, u32[]{:S(2)}) %collective-permute-start.7) | collective-permute-done | bytes 4128 | tf_op jit(solution)/shard_map/ppermute | solution.py:235
  32.5 0.9 %collective-permute-done.8 = f32[8,128]{1,0:T(8,128)S(1)} collective-permute-done((f32[8,128]{1,0:T(8,128)S(1)}, f32[8,128]{1,0:T(8,128)S(1)}, u32[]{:S(2)}, u32[]{:S(2)}) %collective-permute-start.8) | collective-permute-done | bytes 4128 | tf_op jit(solution)/shard_map/ppermute | solution.py:235
  33.4 0.5 %slice_bitcast_fusion = f32[128]{0:T(128)} fusion(f32[8,128]{1,0:T(8,128)S(1)} %maximum_maximum_fusion), kind=kLoop, calls=%fused_computation.1 | loop fusion | bytes 1024 | tf_op jit(solution)/shard_map/squeeze | solution.py:249
  (1 shorter events, 0.0 us)
Async XLA Ops:
  0.0 0.7 %copy-start.1 = (s32[128,1]{0,1:T(1,128)S(1)}, s32[128,1]{0,1:T(1,128)}, u32[]{:S(2)}) copy-start(s32[128,1]{0,1:T(1,128)} %param.3) | copy-start | bytes 1540
  0.7 0.9 %copy-start = (bf16[128,1024]{1,0:T(8,128)(2,1)S(1)}, bf16[128,1024]{1,0:T(8,128)(2,1)}, u32[]{:S(2)}) copy-start(bf16[128,1024]{1,0:T(8,128)(2,1)} %rows_ref.1) | copy-start | bytes 786436
  1.8 3.2 %collective-permute-start.2 = (bf16[136,1024]{1,0:T(8,128)(2,1)S(1)}, bf16[136,1024]{1,0:T(8,128)(2,1)S(1)}, u32[]{:S(2)}, u32[]{:S(2)}) collective-permute-start(bf16[136,1024]{1,0:T(8,128)(2,1)S(1)} %normalize.1.mine_ref), channel_id=1, source_target_pairs={{0,1},{1,0},{2,3},{3,2},{4,5},{5,4},{6,7},{7,6},{8,9},{9,8},{10,11... | collective-permute-start | bytes 835592 | tf_op jit(solution)/shard_map/ppermute | solution.py:235
  2.3 15.8 %collective-permute-start.1 = (bf16[136,1024]{1,0:T(8,128)(2,1)S(1)}, bf16[136,1024]{1,0:T(8,128)(2,1)S(1)}, u32[]{:S(2)}, u32[]{:S(2)}) collective-permute-start(bf16[136,1024]{1,0:T(8,128)(2,1)S(1)} %normalize.1.mine_ref), channel_id=1, source_target_pairs={{0,4},{1,5},{2,6},{3,7},{4,0},{5,1},{6,2},{7,3},{8,12},{9,13},{10,... | collective-permute-start | bytes 835592 | tf_op jit(solution)/shard_map/ppermute | solution.py:235
  4.9 15.6 %collective-permute-start.4 = (bf16[136,1024]{1,0:T(8,128)(2,1)S(1)}, bf16[136,1024]{1,0:T(8,128)(2,1)S(1)}, u32[]{:S(2)}, u32[]{:S(2)}) collective-permute-start(bf16[136,1024]{1,0:T(8,128)(2,1)S(1)} %normalize.1.mine_ref), channel_id=1, source_target_pairs={{0,8},{1,9},{2,10},{3,11},{4,12},{5,13},{6,14},{7,15},{8,0},{9,1},... | collective-permute-start | bytes 835592 | tf_op jit(solution)/shard_map/ppermute | solution.py:235
  7.5 13.1 %collective-permute-start = (bf16[136,1024]{1,0:T(8,128)(2,1)S(1)}, bf16[136,1024]{1,0:T(8,128)(2,1)S(1)}, u32[]{:S(2)}, u32[]{:S(2)}) collective-permute-start(bf16[136,1024]{1,0:T(8,128)(2,1)S(1)} %normalize.1.mine_ref), channel_id=1, source_target_pairs={{0,2},{1,3},{2,0},{3,1},{4,6},{5,7},{6,4},{7,5},{8,10},{9,11},{10,... | collective-permute-start | bytes 835592 | tf_op jit(solution)/shard_map/ppermute | solution.py:235
  18.0 8.4 %collective-permute-start.3 = (bf16[136,1024]{1,0:T(8,128)(2,1)S(1)}, bf16[136,1024]{1,0:T(8,128)(2,1)S(1)}, u32[]{:S(2)}, u32[]{:S(2)}) collective-permute-start(bf16[136,1024]{1,0:T(8,128)(2,1)S(1)} %collective-permute-done.1.e_ref), channel_id=1, source_target_pairs={{0,2},{1,3},{2,0},{3,1},{4,6},{5,7},{6,4},{7,5},{8,10},{9,11},{10,... | collective-permute-start | bytes 835592 | tf_op jit(solution)/shard_map/ppermute | solution.py:235
  20.6 5.9 %collective-permute-start.5 = (bf16[136,1024]{1,0:T(8,128)(2,1)S(1)}, bf16[136,1024]{1,0:T(8,128)(2,1)S(1)}, u32[]{:S(2)}, u32[]{:S(2)}) collective-permute-start(bf16[136,1024]{1,0:T(8,128)(2,1)S(1)} %collective-permute-done.4.h_ref), channel_id=1, source_target_pairs={{0,1},{1,0},{2,3},{3,2},{4,5},{5,4},{6,7},{7,6},{8,9},{9,8},{10,11... | collective-permute-start | bytes 835592 | tf_op jit(solution)/shard_map/ppermute | solution.py:235
  27.4 3.7 %collective-permute-start.6 = (f32[8,128]{1,0:T(8,128)S(1)}, f32[8,128]{1,0:T(8,128)S(1)}, u32[]{:S(2)}, u32[]{:S(2)}) collective-permute-start(f32[8,128]{1,0:T(8,128)S(1)} %get-tuple-element.14), channel_id=1, source_target_pairs={{0,2},{1,3},{2,0},{3,1},{4,6},{5,7},{6,4},{7,5},{8,10},{9,11},{10,... | collective-permute-start | bytes 12296 | tf_op jit(solution)/shard_map/ppermute | solution.py:235
  28.9 3.6 %collective-permute-start.7 = (f32[8,128]{1,0:T(8,128)S(1)}, f32[8,128]{1,0:T(8,128)S(1)}, u32[]{:S(2)}, u32[]{:S(2)}) collective-permute-start(f32[8,128]{1,0:T(8,128)S(1)} %get-tuple-element.15), channel_id=1, source_target_pairs={{0,4},{1,5},{2,6},{3,7},{4,0},{5,1},{6,2},{7,3},{8,12},{9,13},{10,... | collective-permute-start | bytes 12296 | tf_op jit(solution)/shard_map/ppermute | solution.py:235
  28.9 4.5 %collective-permute-start.8 = (f32[8,128]{1,0:T(8,128)S(1)}, f32[8,128]{1,0:T(8,128)S(1)}, u32[]{:S(2)}, u32[]{:S(2)}) collective-permute-start(f32[8,128]{1,0:T(8,128)S(1)} %get-tuple-element.16), channel_id=1, source_target_pairs={{0,6},{1,7},{2,4},{3,5},{4,2},{5,3},{6,0},{7,1},{8,14},{9,15},{10,... | collective-permute-start | bytes 12296 | tf_op jit(solution)/shard_map/ppermute | solution.py:235

commit v5 on v4

--- a/solution.py
+++ b/solution.py
@@ -143,37 +143,50 @@
     return (scaled * (1.0 / math.sqrt(values.shape[1]))).astype(jnp.bfloat16)
 
 
-def normalize_kernel(rows_ref, cluster_ref, out_ref):
+def normalize_kernel(rows_ref, cluster_ref, out_ref, front_ref, back_ref):
     rows, width = rows_ref.shape
-    out_ref[:rows] = unit_of(rows_ref[...])
+    unit = unit_of(rows_ref[...])
     cluster = jnp.broadcast_to(cluster_ref[...].astype(jnp.float32), (TAIL, rows))
     tail = jnp.concatenate([cluster, jnp.zeros((TAIL, width - rows), jnp.float32)], axis=1)
-    out_ref[rows:] = tail.astype(jnp.bfloat16)
+    tail = tail.astype(jnp.bfloat16)
+    out_ref[:rows] = unit
+    out_ref[rows:] = tail
+    front_ref[: rows // 2] = unit[: rows // 2]
+    front_ref[rows // 2 :] = tail
+    back_ref[...] = unit[rows // 2 :]
 
 
 def normalize(embeddings, assignment):
     rows, width = embeddings.shape
     return pl.pallas_call(
         normalize_kernel,
-        out_shape=jax.ShapeDtypeStruct((rows + TAIL, width), jnp.bfloat16),
+        out_shape=[
+            jax.ShapeDtypeStruct((size, width), jnp.bfloat16)
+            for size in (rows + TAIL, rows // 2 + TAIL, rows // 2)
+        ],
         in_specs=[VMEM, VMEM],
-        out_specs=VMEM,
+        out_specs=[VMEM] * 3,
         compiler_params=LIMIT,
         name="normalize",
     )(embeddings, assignment.reshape(1, rows))
 
 
-def split(block):
-    rows = block.shape[0] - TAIL
-    return block[:rows], block[rows : rows + 1, :rows].astype(jnp.float32)
+def whole(ref):
+    rows = ref.shape[0] - TAIL
+    return ref[:rows], ref[rows:, :rows][:1].astype(jnp.float32)
+
+
+def halves(front_ref, back_ref):
+    half, rows = back_ref.shape[0], 2 * back_ref.shape[0]
+    joined = jnp.concatenate([front_ref[:half], back_ref[...]], axis=0)
+    return joined, front_ref[half:, :rows][:1].astype(jnp.float32)
 
 
 def best_of(own, others, same_rows=False):
-    rows, clusters = zip(*[split(block) for block in own])
+    rows, clusters = zip(*own)
     rows, clusters = jnp.concatenate(rows, axis=0), jnp.concatenate(clusters, axis=1)
     best = None
-    for place, other in enumerate(others):
-        other_rows, other_clusters = split(other)
+    for place, (other_rows, other_clusters) in enumerate(others):
         count = other_rows.shape[0]
         similar = lax.dot_general(
             other_rows, rows, (((1,), (1,)), ((), ())), preferred_element_type=jnp.float32
@@ -189,13 +202,13 @@
     return best
 
 
-def early_kernel(x_ref, e_ref, mine_ref, c_ref, out_ref):
-    mine = mine_ref[...]
-    best = best_of([mine, x_ref[...], e_ref[...]], [mine, c_ref[...]], True)
+def early_kernel(c_ref, e_ref, mine_ref, x_ref, out_ref):
+    mine = whole(mine_ref)
+    best = best_of([mine, whole(c_ref), whole(e_ref)], [mine, whole(x_ref)], True)
     out_ref[...] = jnp.broadcast_to(best, out_ref.shape)
 
 
-def early(x, e, mine, c):
+def early(c, e, mine, x):
     rows = mine.shape[0] - TAIL
     return pl.pallas_call(
         early_kernel,
@@ -204,47 +217,49 @@
         out_specs=VMEM,
         compiler_params=LIMIT,
         name="early",
-    )(x, e, mine, c)
-
-
-def late_kernel(best_ref, x_ref, e_ref, xe_ref, mine_ref, c_ref, h_ref, ch_ref, *out_refs):
-    mine, h, ch = mine_ref[...], h_ref[...], ch_ref[...]
-    best = best_of([mine, x_ref[...], e_ref[...]], [h, ch])
+    )(c, e, mine, x)
+
+
+def late_kernel(best_ref, c_ref, e_ref, ce_ref, mine_ref, x_ref, *refs):
+    h, xh, out_refs = halves(*refs[:2]), halves(*refs[2:4]), refs[4:]
+    mine = whole(mine_ref)
+    best = best_of([mine, whole(c_ref), whole(e_ref)], [h, xh])
     best = jnp.maximum(best, best_ref[:1, :])
-    last = best_of([xe_ref[...]], [mine, c_ref[...], h, ch])
+    last = best_of([whole(ce_ref)], [mine, whole(x_ref), h, xh])
     best = jnp.concatenate([best, last], axis=1)
     for place, out_ref in enumerate(out_refs):
         rows = out_ref.shape[1]
         out_ref[...] = jnp.broadcast_to(best[:, place * rows : (place + 1) * rows], out_ref.shape)
 
 
-def late(best, x, e, xe, mine, c, h, ch):
+def late(best, c, e, ce, mine, x, h, xh):
     rows = mine.shape[0] - TAIL
     return pl.pallas_call(
         late_kernel,
         out_shape=[jax.ShapeDtypeStruct((8, rows), jnp.float32)] * 4,
-        in_specs=[VMEM] * 8,
+        in_specs=[VMEM] * 10,
         out_specs=[VMEM] * 4,
         compiler_params=LIMIT,
         name="late",
-    )(best, x, e, xe, mine, c, h, ch)
+    )(best, c, e, ce, mine, x, *h, *xh)
 
 
 def square(embeddings, assignment):
     def swap(flip, array):
         return lax.ppermute(array, AXES, [(i, i ^ flip) for i in range(16)])
 
-    mine = normalize(embeddings, assignment)
+    mine, front, back = normalize(embeddings, assignment)
+    h_front = swap(HIGH, front)
+    h_back = swap(HIGH, back)
+    x = swap(SHARD, mine)
     e = swap(LOW, mine)
-    x = swap(SHARD, mine)
     c = swap(SUB, mine)
-    then, c = lax.optimization_barrier((mine, c))
-    h = swap(HIGH, then)
-    xe = swap(SHARD, e)
-    ch = swap(SUB, h)
-    best = early(x, e, mine, c)
-    found, *others = late(best, x, e, xe, mine, c, h, ch)
-    for flip, other in zip((SHARD, LOW, LOW | SHARD), others):
+    xh_front = swap(SHARD, h_front)
+    xh_back = swap(SHARD, h_back)
+    ce = swap(SUB, e)
+    best = early(c, e, mine, x)
+    found, *others = late(best, c, e, ce, mine, x, (h_front, h_back), (xh_front, xh_back))
+    for flip, other in zip((SUB, LOW, LOW | SUB), others):
         found = jnp.maximum(found, swap(flip, other))
     return found[0]
 

time: 34.1 us -> 34.8 us (1.021)
  starting transfers between devices: 12.5 us -> 14.1 us
  waiting for transfers between devices: 17.6 us -> 16.7 us
    ppermute x9 -> x11, starting transfers between devices: 12.5 us -> 14.1 us  [swap(): return lax.ppermute(array, AXES, [(i, i ^ flip) for i in range(16)])]
    ppermute x9 -> x11, waiting for transfers between devices: 17.6 us -> 16.7 us  [swap(): return lax.ppermute(array, AXES, [(i, i ^ flip) for i in range(16)])]
  transfers between devices with their start and end apart: 9 -> 11, of which waited for: 6 -> 4; matrix products, arithmetic and copies ran while one was open for 0% -> 0% of each run, Pallas kernels for 2% -> 2%
where the time goes in v5:
time: 34.8 us; the launch traced here: 34.6 us
  waiting for transfers between devices  16.7 us (48%)
  starting transfers between devices  14.1 us (41%)
  local copies, waits for them, and re-layouts  2.12 us (6%)
  Pallas kernels  1.68 us (5%)
    ppermute x11, waiting for transfers between devices, swap(): return lax.ppermute(array, AXES, [(i, i ^ flip) for i in range(16)])  16.7 us
    ppermute x11, starting transfers between devices, swap(): return lax.ppermute(array, AXES, [(i, i ^ flip) for i in range(16)])  14.1 us
    unnamed x4, local copies, waits for them, and re-layouts  1.6 us
    pallas_call x1, Pallas kernels, late(): pl.pallas_call(late_kernel, out_shape=[jax.ShapeDtypeStruct((8, rows), jn...  0.91 us
  transfers between devices with their start and end apart: 11, of which 4 were waited for; matrix products, arithmetic and copies ran while one was open for 0% of the time, Pallas kernels for 2%

profile of v5, /device:TPU:0, one launch (start us, length us, event | category | flops | bytes accessed | tf_op | source)
XLA Modules:
  0.0 34.6 jit_solution(14589304193062157063)
XLA Ops:
  0.0 0.0 copy-start.1
  0.0 0.7 %copy-done.1 = s32[128,1]{0,1:T(1,128)S(1)} copy-done((s32[128,1]{0,1:T(1,128)S(1)}, s32[128,1]{0,1:T(1,128)}, u32[]{:S(2)}) %copy-start.1) | copy-done | bytes 536
  0.7 0.0 copy-start
  0.7 0.9 %copy-done = bf16[128,1024]{1,0:T(8,128)(2,1)S(1)} copy-done((bf16[128,1024]{1,0:T(8,128)(2,1)S(1)}, bf16[128,1024]{1,0:T(8,128)(2,1)}, u32[]{:S(2)}) %copy-start) | copy-done | bytes 262168
  1.6 0.2 normalize.1
  1.8 3.1 %collective-permute-start.1 = (bf16[136,1024]{1,0:T(8,128)(2,1)S(1)}, bf16[136,1024]{1,0:T(8,128)(2,1)S(1)}, u32[]{:S(2)}, u32[]{:S(2)}) collective-permute-start(bf16[136,1024]{1,0:T(8,128)(2,1)S(1)} %get-tuple-element.12.mine_ref), channel_id=1, source_target_pairs={{0,4},{1,5},{2,6},{3,7},{4,0},{5,1},{6,2},{7,3},{8,12},{9,13},{10,... | collective-permute-start | bytes 835592 | tf_op jit(solution)/shard_map/ppermute | solution.py:249
  4.9 2.6 %collective-permute-start.4 = (bf16[72,1024]{1,0:T(8,128)(2,1)S(1)}, bf16[72,1024]{1,0:T(8,128)(2,1)S(1)}, u32[]{:S(2)}, u32[]{:S(2)}) collective-permute-start(bf16[72,1024]{1,0:T(8,128)(2,1)S(1)} %get-tuple-element.13), channel_id=1, source_target_pairs={{0,8},{1,9},{2,10},{3,11},{4,12},{5,13},{6,14},{7,15},{8,0},{9,1},... | collective-permute-start | bytes 442376 | tf_op jit(solution)/shard_map/ppermute | solution.py:249
  7.4 1.5 %collective-permute-start.2 = (bf16[136,1024]{1,0:T(8,128)(2,1)S(1)}, bf16[136,1024]{1,0:T(8,128)(2,1)S(1)}, u32[]{:S(2)}, u32[]{:S(2)}) collective-permute-start(bf16[136,1024]{1,0:T(8,128)(2,1)S(1)} %get-tuple-element.12.mine_ref), channel_id=1, source_target_pairs={{0,2},{1,3},{2,0},{3,1},{4,6},{5,7},{6,4},{7,5},{8,10},{9,11},{10,... | collective-permute-start | bytes 835592 | tf_op jit(solution)/shard_map/ppermute | solution.py:249
  8.9 0.0 collective-permute-start
  8.9 5.7 %collective-permute-done.1.e_ref = bf16[136,1024]{1,0:T(8,128)(2,1)S(1)} collective-permute-done((bf16[136,1024]{1,0:T(8,128)(2,1)S(1)}, bf16[136,1024]{1,0:T(8,128)(2,1)S(1)}, u32[]{:S(2)}, u32[]{:S(2)}) %collective-permute-start.1) | collective-permute-done | bytes 278560 | tf_op jit(solution)/shard_map/ppermute | solution.py:249
  14.7 0.0 collective-permute-start.3
  14.7 1.8 %collective-permute-start.5 = (bf16[64,1024]{1,0:T(8,128)(2,1)S(1)}, bf16[64,1024]{1,0:T(8,128)(2,1)S(1)}, u32[]{:S(2)}, u32[]{:S(2)}) collective-permute-start(bf16[64,1024]{1,0:T(8,128)(2,1)S(1)} %get-tuple-element.14), channel_id=1, source_target_pairs={{0,8},{1,9},{2,10},{3,11},{4,12},{5,13},{6,14},{7,15},{8,0},{9,1},... | collective-permute-start | bytes 393224 | tf_op jit(solution)/shard_map/ppermute | solution.py:249
  16.5 0.0 collective-permute-done.4.refs_0_
  16.5 1.5 %collective-permute-start.6 = (bf16[72,1024]{1,0:T(8,128)(2,1)S(1)}, bf16[72,1024]{1,0:T(8,128)(2,1)S(1)}, u32[]{:S(2)}, u32[]{:S(2)}) collective-permute-start(bf16[72,1024]{1,0:T(8,128)(2,1)S(1)} %collective-permute-done.4.refs_0_), channel_id=1, source_target_pairs={{0,2},{1,3},{2,0},{3,1},{4,6},{5,7},{6,4},{7,5},{8,10},{9,11},{10,... | collective-permute-start | bytes 442376 | tf_op jit(solution)/shard_map/ppermute | solution.py:249
  18.0 6.3 %collective-permute-done.5.refs_1_ = bf16[64,1024]{1,0:T(8,128)(2,1)S(1)} collective-permute-done((bf16[64,1024]{1,0:T(8,128)(2,1)S(1)}, bf16[64,1024]{1,0:T(8,128)(2,1)S(1)}, u32[]{:S(2)}, u32[]{:S(2)}) %collective-permute-start.5) | collective-permute-done | bytes 131104 | tf_op jit(solution)/shard_map/ppermute | solution.py:249
  24.3 1.7 %collective-permute-start.7 = (bf16[64,1024]{1,0:T(8,128)(2,1)S(1)}, bf16[64,1024]{1,0:T(8,128)(2,1)S(1)}, u32[]{:S(2)}, u32[]{:S(2)}) collective-permute-start(bf16[64,1024]{1,0:T(8,128)(2,1)S(1)} %collective-permute-done.5.refs_1_), channel_id=1, source_target_pairs={{0,2},{1,3},{2,0},{3,1},{4,6},{5,7},{6,4},{7,5},{8,10},{9,11},{10,... | collective-permute-start | bytes 393224 | tf_op jit(solution)/shard_map/ppermute | solution.py:249
  25.9 0.0 collective-permute-done.2.x_ref
  26.0 0.0 collective-permute-done.c_ref
  26.0 0.6 %early.1.best_ref = f32[8,384]{1,0:T(8,128)S(1)} custom-call(bf16[136,1024]{1,0:T(8,128)(2,1)S(1)} %collective-permute-done.c_ref, bf16[136,1024]{1,0:T(8,128)(2,1)S(1)} %collective-permute-done.1.e_ref, bf16[136,1024]{1,0:T(8,128)(2,1)S(1)} %get-tuple-element.12.mine_ref, bf16[136,1024]{1,0:T(8,128)(2,1)S(1)} %collective-permute-done.2.x_ref), custom_call_target="tpu_custom_call" | custom-call | tf_op jit(solution)/shard_map/early/pallas_call | solution.py:213
  26.6 2.8 %collective-permute-done.7.refs_3_ = bf16[64,1024]{1,0:T(8,128)(2,1)S(1)} collective-permute-done((bf16[64,1024]{1,0:T(8,128)(2,1)S(1)}, bf16[64,1024]{1,0:T(8,128)(2,1)S(1)}, u32[]{:S(2)}, u32[]{:S(2)}) %collective-permute-start.7) | collective-permute-done | bytes 131104 | tf_op jit(solution)/shard_map/ppermute | solution.py:249
  29.4 0.0 collective-permute-done.6.refs_2_
  29.4 0.0 collective-permute-done.3.ce_ref
  29.4 0.9 %late.1 = (f32[8,128]{1,0:T(8,128)S(1)}, f32[8,128]{1,0:T(8,128)S(1)}, f32[8,128]{1,0:T(8,128)S(1)}, f32[8,128]{1,0:T(8,128)S(1)}) custom-call(f32[8,384]{1,0:T(8,128)S(1)} %early.1.best_ref, bf16[136,1024]{1,0:T(8,128)(2,1)S(1)} %collective-permute-done.c_ref, bf16[136,1024]{1,0:T(8,128)(2,1)S(1)} %collective-permute-done.1.e_ref, ...), custom_call_target="tpu_custom_call" | custom-call | tf_op jit(solution)/shard_map/late/pallas_call | solution.py:237
  30.3 0.1 collective-permute-start.8
  30.4 0.3 collective-permute-start.9
  30.8 1.5 %collective-permute-start.10 = (f32[8,128]{1,0:T(8,128)S(1)}, f32[8,128]{1,0:T(8,128)S(1)}, u32[]{:S(2)}, u32[]{:S(2)}) collective-permute-start(f32[8,128]{1,0:T(8,128)S(1)} %get-tuple-element.18), channel_id=1, source_target_pairs={{0,5},{1,4},{2,7},{3,6},{4,1},{5,0},{6,3},{7,2},{8,13},{9,12},{10,... | collective-permute-start | bytes 12296 | tf_op jit(solution)/shard_map/ppermute | solution.py:249
  32.3 0.0 collective-permute-done.8
  32.3 1.8 %collective-permute-done.9 = f32[8,128]{1,0:T(8,128)S(1)} collective-permute-done((f32[8,128]{1,0:T(8,128)S(1)}, f32[8,128]{1,0:T(8,128)S(1)}, u32[]{:S(2)}, u32[]{:S(2)}) %collective-permute-start.9) | collective-permute-done | bytes 4128 | tf_op jit(solution)/shard_map/ppermute | solution.py:249
  34.1 0.0 collective-permute-done.10
  34.1 0.5 %slice_bitcast_fusion = f32[128]{0:T(128)} fusion(f32[8,128]{1,0:T(8,128)S(1)} %maximum_maximum_fusion), kind=kLoop, calls=%fused_computation.1 | loop fusion | bytes 1024 | tf_op jit(solution)/shard_map/squeeze | solution.py:264
  (1 shorter events, 0.0 us)
Async XLA Ops:
  0.0 0.7 %copy-start.1 = (s32[128,1]{0,1:T(1,128)S(1)}, s32[128,1]{0,1:T(1,128)}, u32[]{:S(2)}) copy-start(s32[128,1]{0,1:T(1,128)} %param.3) | copy-start | bytes 1540
  0.7 0.9 %copy-start = (bf16[128,1024]{1,0:T(8,128)(2,1)S(1)}, bf16[128,1024]{1,0:T(8,128)(2,1)}, u32[]{:S(2)}) copy-start(bf16[128,1024]{1,0:T(8,128)(2,1)} %rows_ref.1) | copy-start | bytes 786436
  1.8 12.9 %collective-permute-start.1 = (bf16[136,1024]{1,0:T(8,128)(2,1)S(1)}, bf16[136,1024]{1,0:T(8,128)(2,1)S(1)}, u32[]{:S(2)}, u32[]{:S(2)}) collective-permute-start(bf16[136,1024]{1,0:T(8,128)(2,1)S(1)} %get-tuple-element.12.mine_ref), channel_id=1, source_target_pairs={{0,4},{1,5},{2,6},{3,7},{4,0},{5,1},{6,2},{7,3},{8,12},{9,13},{10,... | collective-permute-start | bytes 835592 | tf_op jit(solution)/shard_map/ppermute | solution.py:249
  4.9 11.7 %collective-permute-start.4 = (bf16[72,1024]{1,0:T(8,128)(2,1)S(1)}, bf16[72,1024]{1,0:T(8,128)(2,1)S(1)}, u32[]{:S(2)}, u32[]{:S(2)}) collective-permute-start(bf16[72,1024]{1,0:T(8,128)(2,1)S(1)} %get-tuple-element.13), channel_id=1, source_target_pairs={{0,8},{1,9},{2,10},{3,11},{4,12},{5,13},{6,14},{7,15},{8,0},{9,1},... | collective-permute-start | bytes 442376 | tf_op jit(solution)/shard_map/ppermute | solution.py:249
  7.4 18.5 %collective-permute-start.2 = (bf16[136,1024]{1,0:T(8,128)(2,1)S(1)}, bf16[136,1024]{1,0:T(8,128)(2,1)S(1)}, u32[]{:S(2)}, u32[]{:S(2)}) collective-permute-start(bf16[136,1024]{1,0:T(8,128)(2,1)S(1)} %get-tuple-element.12.mine_ref), channel_id=1, source_target_pairs={{0,2},{1,3},{2,0},{3,1},{4,6},{5,7},{6,4},{7,5},{8,10},{9,11},{10,... | collective-permute-start | bytes 835592 | tf_op jit(solution)/shard_map/ppermute | solution.py:249
  8.9 17.0 %collective-permute-start = (bf16[136,1024]{1,0:T(8,128)(2,1)S(1)}, bf16[136,1024]{1,0:T(8,128)(2,1)S(1)}, u32[]{:S(2)}, u32[]{:S(2)}) collective-permute-start(bf16[136,1024]{1,0:T(8,128)(2,1)S(1)} %get-tuple-element.12.mine_ref), channel_id=1, source_target_pairs={{0,1},{1,0},{2,3},{3,2},{4,5},{5,4},{6,7},{7,6},{8,9},{9,8},{10,11... | collective-permute-start | bytes 835592 | tf_op jit(solution)/shard_map/ppermute | solution.py:249
  14.7 14.8 %collective-permute-start.3 = (bf16[136,1024]{1,0:T(8,128)(2,1)S(1)}, bf16[136,1024]{1,0:T(8,128)(2,1)S(1)}, u32[]{:S(2)}, u32[]{:S(2)}) collective-permute-start(bf16[136,1024]{1,0:T(8,128)(2,1)S(1)} %collective-permute-done.1.e_ref), channel_id=1, source_target_pairs={{0,1},{1,0},{2,3},{3,2},{4,5},{5,4},{6,7},{7,6},{8,9},{9,8},{10,11... | collective-permute-start | bytes 835592 | tf_op jit(solution)/shard_map/ppermute | solution.py:249
  14.7 9.6 %collective-permute-start.5 = (bf16[64,1024]{1,0:T(8,128)(2,1)S(1)}, bf16[64,1024]{1,0:T(8,128)(2,1)S(1)}, u32[]{:S(2)}, u32[]{:S(2)}) collective-permute-start(bf16[64,1024]{1,0:T(8,128)(2,1)S(1)} %get-tuple-element.14), channel_id=1, source_target_pairs={{0,8},{1,9},{2,10},{3,11},{4,12},{5,13},{6,14},{7,15},{8,0},{9,1},... | collective-permute-start | bytes 393224 | tf_op jit(solution)/shard_map/ppermute | solution.py:249
  16.5 12.9 %collective-permute-start.6 = (bf16[72,1024]{1,0:T(8,128)(2,1)S(1)}, bf16[72,1024]{1,0:T(8,128)(2,1)S(1)}, u32[]{:S(2)}, u32[]{:S(2)}) collective-permute-start(bf16[72,1024]{1,0:T(8,128)(2,1)S(1)} %collective-permute-done.4.refs_0_), channel_id=1, source_target_pairs={{0,2},{1,3},{2,0},{3,1},{4,6},{5,7},{6,4},{7,5},{8,10},{9,11},{10,... | collective-permute-start | bytes 442376 | tf_op jit(solution)/shard_map/ppermute | solution.py:249
  24.3 5.1 %collective-permute-start.7 = (bf16[64,1024]{1,0:T(8,128)(2,1)S(1)}, bf16[64,1024]{1,0:T(8,128)(2,1)S(1)}, u32[]{:S(2)}, u32[]{:S(2)}) collective-permute-start(bf16[64,1024]{1,0:T(8,128)(2,1)S(1)} %collective-permute-done.5.refs_1_), channel_id=1, source_target_pairs={{0,2},{1,3},{2,0},{3,1},{4,6},{5,7},{6,4},{7,5},{8,10},{9,11},{10,... | collective-permute-start | bytes 393224 | tf_op jit(solution)/shard_map/ppermute | solution.py:249
  30.3 1.9 %collective-permute-start.8 = (f32[8,128]{1,0:T(8,128)S(1)}, f32[8,128]{1,0:T(8,128)S(1)}, u32[]{:S(2)}, u32[]{:S(2)}) collective-permute-start(f32[8,128]{1,0:T(8,128)S(1)} %get-tuple-element.16), channel_id=1, source_target_pairs={{0,1},{1,0},{2,3},{3,2},{4,5},{5,4},{6,7},{7,6},{8,9},{9,8},{10,11... | collective-permute-start | bytes 12296 | tf_op jit(solution)/shard_map/ppermute | solution.py:249
  30.4 3.7 %collective-permute-start.9 = (f32[8,128]{1,0:T(8,128)S(1)}, f32[8,128]{1,0:T(8,128)S(1)}, u32[]{:S(2)}, u32[]{:S(2)}) collective-permute-start(f32[8,128]{1,0:T(8,128)S(1)} %get-tuple-element.17), channel_id=1, source_target_pairs={{0,4},{1,5},{2,6},{3,7},{4,0},{5,1},{6,2},{7,3},{8,12},{9,13},{10,... | collective-permute-start | bytes 12296 | tf_op jit(solution)/shard_map/ppermute | solution.py:249
  30.8 3.3 %collective-permute-start.10 = (f32[8,128]{1,0:T(8,128)S(1)}, f32[8,128]{1,0:T(8,128)S(1)}, u32[]{:S(2)}, u32[]{:S(2)}) collective-permute-start(f32[8,128]{1,0:T(8,128)S(1)} %get-tuple-element.18), channel_id=1, source_target_pairs={{0,5},{1,4},{2,7},{3,6},{4,1},{5,0},{6,3},{7,2},{8,13},{9,12},{10,... | collective-permute-start | bytes 12296 | tf_op jit(solution)/shard_map/ppermute | solution.py:249

commit v6 on v4

--- a/solution.py
+++ b/solution.py
@@ -14,7 +14,6 @@
 LANES = 128
 EMPTY = 4.0
 NONE = -2.0
-TAIL = 8
 HIGH, LOW, SHARD, SUB = 8, 4, 2, 1
 LIMIT = pltpu.CompilerParams(vmem_limit_bytes=12 << 20)
 AXES = ("blk", "shard", "sub")
@@ -143,43 +142,15 @@
     return (scaled * (1.0 / math.sqrt(values.shape[1]))).astype(jnp.bfloat16)
 
 
-def normalize_kernel(rows_ref, cluster_ref, out_ref):
-    rows, width = rows_ref.shape
-    out_ref[:rows] = unit_of(rows_ref[...])
-    cluster = jnp.broadcast_to(cluster_ref[...].astype(jnp.float32), (TAIL, rows))
-    tail = jnp.concatenate([cluster, jnp.zeros((TAIL, width - rows), jnp.float32)], axis=1)
-    out_ref[rows:] = tail.astype(jnp.bfloat16)
-
-
-def normalize(embeddings, assignment):
-    rows, width = embeddings.shape
-    return pl.pallas_call(
-        normalize_kernel,
-        out_shape=jax.ShapeDtypeStruct((rows + TAIL, width), jnp.bfloat16),
-        in_specs=[VMEM, VMEM],
-        out_specs=VMEM,
-        compiler_params=LIMIT,
-        name="normalize",
-    )(embeddings, assignment.reshape(1, rows))
-
-
-def split(block):
-    rows = block.shape[0] - TAIL
-    return block[:rows], block[rows : rows + 1, :rows].astype(jnp.float32)
-
-
-def best_of(own, others, same_rows=False):
-    rows, clusters = zip(*[split(block) for block in own])
-    rows, clusters = jnp.concatenate(rows, axis=0), jnp.concatenate(clusters, axis=1)
+def best_of(own, own_clusters, others, other_clusters, same_rows=False):
     best = None
-    for place, other in enumerate(others):
-        other_rows, other_clusters = split(other)
-        count = other_rows.shape[0]
+    for place, (rows, clusters) in enumerate(zip(others, other_clusters)):
+        count = rows.shape[0]
         similar = lax.dot_general(
-            other_rows, rows, (((1,), (1,)), ((), ())), preferred_element_type=jnp.float32
+            rows, own, (((1,), (1,)), ((), ())), preferred_element_type=jnp.float32
         )
-        down = jnp.broadcast_to(other_clusters, (count, count)).T[:, :1]
-        kept = down == clusters
+        down = jnp.broadcast_to(clusters, (count, count)).T[:, :1]
+        kept = down == own_clusters
         if same_rows and place == 0:
             row = lax.broadcasted_iota(jnp.int32, similar.shape, 0)
             column = lax.broadcasted_iota(jnp.int32, similar.shape, 1)
@@ -189,61 +160,78 @@
     return best
 
 
-def early_kernel(x_ref, e_ref, mine_ref, c_ref, out_ref):
-    mine = mine_ref[...]
-    best = best_of([mine, x_ref[...], e_ref[...]], [mine, c_ref[...]], True)
-    out_ref[...] = jnp.broadcast_to(best, out_ref.shape)
-
-
-def early(x, e, mine, c):
-    rows = mine.shape[0] - TAIL
+def early_kernel(refs, ids_ref, x_ids_ref, c_ids_ref, e_ids_ref, best_ref, own_ref, c_ref):
+    mine, x, e, c = [unit_of(ref[...]) for ref in refs]
+    own = jnp.concatenate([mine, x, e], axis=0)
+    own_ids = jnp.concatenate([ids_ref[...], x_ids_ref[...], e_ids_ref[:1, :]], axis=1)
+    best = best_of(own, own_ids, [mine, c], [ids_ref[...], c_ids_ref[...]], True)
+    best_ref[...] = jnp.broadcast_to(best, best_ref.shape)
+    own_ref[...] = own
+    c_ref[...] = c
+
+
+def early(blocks, ids):
+    rows, width = blocks[0].shape
     return pl.pallas_call(
         early_kernel,
-        out_shape=jax.ShapeDtypeStruct((8, 3 * rows), jnp.float32),
-        in_specs=[VMEM] * 4,
-        out_specs=VMEM,
+        out_shape=[
+            jax.ShapeDtypeStruct((8, 3 * rows), jnp.float32),
+            jax.ShapeDtypeStruct((3 * rows, width), jnp.bfloat16),
+            jax.ShapeDtypeStruct((rows, width), jnp.bfloat16),
+        ],
+        in_specs=([VMEM] * len(blocks), *[VMEM] * len(ids)),
+        out_specs=[VMEM] * 3,
         compiler_params=LIMIT,
         name="early",
-    )(x, e, mine, c)
-
-
-def late_kernel(best_ref, x_ref, e_ref, xe_ref, mine_ref, c_ref, h_ref, ch_ref, *out_refs):
-    mine, h, ch = mine_ref[...], h_ref[...], ch_ref[...]
-    best = best_of([mine, x_ref[...], e_ref[...]], [h, ch])
+    )(blocks, *ids)
+
+
+def late_kernel(best_ref, own_ref, c_ref, refs, ids_ref, x_ids_ref, c_ids_ref, e_ids_ref, h_ids_ref, *out_refs):
+    xe, h, ch = [unit_of(ref[...]) for ref in refs]
+    own, c = own_ref[...], c_ref[...]
+    mine = own[: c.shape[0]]
+    own_ids = jnp.concatenate([ids_ref[...], x_ids_ref[...], e_ids_ref[:1, :]], axis=1)
+    h_ids, ch_ids = h_ids_ref[:1, :], h_ids_ref[1:, :]
+    best = best_of(own, own_ids, [h, ch], [h_ids, ch_ids])
     best = jnp.maximum(best, best_ref[:1, :])
-    last = best_of([xe_ref[...]], [mine, c_ref[...], h, ch])
+    others, other_ids = [mine, c, h, ch], [ids_ref[...], c_ids_ref[...], h_ids, ch_ids]
+    last = best_of(xe, e_ids_ref[1:, :], others, other_ids)
     best = jnp.concatenate([best, last], axis=1)
     for place, out_ref in enumerate(out_refs):
         rows = out_ref.shape[1]
         out_ref[...] = jnp.broadcast_to(best[:, place * rows : (place + 1) * rows], out_ref.shape)
 
 
-def late(best, x, e, xe, mine, c, h, ch):
-    rows = mine.shape[0] - TAIL
+def late(best, own, c, blocks, ids):
+    rows = c.shape[0]
     return pl.pallas_call(
         late_kernel,
         out_shape=[jax.ShapeDtypeStruct((8, rows), jnp.float32)] * 4,
-        in_specs=[VMEM] * 8,
+        in_specs=(VMEM, VMEM, VMEM, [VMEM] * len(blocks), *[VMEM] * len(ids)),
         out_specs=[VMEM] * 4,
         compiler_params=LIMIT,
         name="late",
-    )(best, x, e, xe, mine, c, h, ch)
+    )(best, own, c, blocks, *ids)
 
 
 def square(embeddings, assignment):
     def swap(flip, array):
         return lax.ppermute(array, AXES, [(i, i ^ flip) for i in range(16)])
 
-    mine = normalize(embeddings, assignment)
+    rows = embeddings.shape[0]
+    mine, ids = embeddings, assignment.reshape(1, rows)
     e = swap(LOW, mine)
+    h = swap(HIGH, mine)
     x = swap(SHARD, mine)
     c = swap(SUB, mine)
-    then, c = lax.optimization_barrier((mine, c))
-    h = swap(HIGH, then)
+    x_ids, c_ids = swap(SHARD, ids), swap(SUB, ids)
+    e_ids = swap(LOW, jnp.concatenate([ids, x_ids]))
+    h_ids = swap(HIGH, jnp.concatenate([ids, c_ids]))
     xe = swap(SHARD, e)
     ch = swap(SUB, h)
-    best = early(x, e, mine, c)
-    found, *others = late(best, x, e, xe, mine, c, h, ch)
+    early_ids = [ids, x_ids, c_ids, e_ids]
+    best, own, c = early([mine, x, e, c], early_ids)
+    found, *others = late(best, own, c, [xe, h, ch], [*early_ids, h_ids])
     for flip, other in zip((SHARD, LOW, LOW | SHARD), others):
         found = jnp.maximum(found, swap(flip, other))
     return found[0]

time: 34.1 us -> 39.8 us (1.17)
  waiting for transfers between devices: 17.6 us -> 21.6 us
  starting transfers between devices: 12.5 us -> 14.7 us
  local copies, waits for them, and re-layouts: 2.12 us -> 1.47 us
    ppermute x9 -> x13, waiting for transfers between devices: 17.6 us -> 21.6 us  [swap(): return lax.ppermute(array, AXES, [(i, i ^ flip) for i in range(16)])]
    ppermute x9 -> x13, starting transfers between devices: 12.5 us -> 14.7 us  [swap(): return lax.ppermute(array, AXES, [(i, i ^ flip) for i in range(16)])]
    unnamed x4, local copies, waits for them, and re-layouts: 1.6 us -> 0.95 us
    pallas_call x2 -> x1, Pallas kernels: 0.78 us -> 0.84 us  [early(): pl.pallas_call(early_kernel, out_shape=[jax.ShapeDtypeStruct((8, 3 * rows...]
  transfers between devices with their start and end apart: 9 -> 13, of which waited for: 6 -> 9; matrix products, arithmetic and copies ran while one was open for 0% -> 0% of each run, Pallas kernels for 2% -> 2%
where the time goes in v6:
time: 39.8 us; the launch traced here: 39.6 us
  waiting for transfers between devices  21.6 us (54%)
  starting transfers between devices  14.7 us (37%)
  Pallas kernels  1.83 us (5%)
  local copies, waits for them, and re-layouts  1.47 us (4%)
    ppermute x13, waiting for transfers between devices, swap(): return lax.ppermute(array, AXES, [(i, i ^ flip) for i in range(16)])  21.6 us
    ppermute x13, starting transfers between devices, swap(): return lax.ppermute(array, AXES, [(i, i ^ flip) for i in range(16)])  14.7 us
    pallas_call x1, Pallas kernels, late(): pl.pallas_call(late_kernel, out_shape=[jax.ShapeDtypeStruct((8, rows), jn...  0.99 us
    unnamed x4, local copies, waits for them, and re-layouts  0.95 us
    pallas_call x1, Pallas kernels, early(): pl.pallas_call(early_kernel, out_shape=[jax.ShapeDtypeStruct((8, 3 * rows...  0.84 us
  transfers between devices with their start and end apart: 13, of which 9 were waited for; matrix products, arithmetic and copies ran while one was open for 0% of the time, Pallas kernels for 2%

profile of v6, /device:TPU:0, one launch (start us, length us, event | category | flops | bytes accessed | tf_op | source)
XLA Modules:
  0.0 39.6 jit_solution(439196622885490339)
XLA Ops:
  0.0 0.0 copy-start.1
  0.0 3.0 %collective-permute-start.1 = (bf16[128,1024]{1,0:T(8,128)(2,1)}, bf16[128,1024]{1,0:T(8,128)(2,1)S(1)}, u32[]{:S(2)}, u32[]{:S(2)}) collective-permute-start(bf16[128,1024]{1,0:T(8,128)(2,1)} %refs_0_.1), channel_id=1, source_target_pairs={{0,4},{1,5},{2,6},{3,7},{4,0},{5,1},{6,2},{7,3},{8,12},{9,13},{10,... | collective-permute-start | bytes 786440 | tf_op jit(solution)/shard_map/ppermute | solution.py:219
  3.0 2.6 %collective-permute-start.7 = (bf16[128,1024]{1,0:T(8,128)(2,1)}, bf16[128,1024]{1,0:T(8,128)(2,1)S(1)}, u32[]{:S(2)}, u32[]{:S(2)}) collective-permute-start(bf16[128,1024]{1,0:T(8,128)(2,1)} %refs_0_.1), channel_id=1, source_target_pairs={{0,8},{1,9},{2,10},{3,11},{4,12},{5,13},{6,14},{7,15},{8,0},{9,1},... | collective-permute-start | bytes 786440 | tf_op jit(solution)/shard_map/ppermute | solution.py:219
  5.6 1.5 %collective-permute-start = (bf16[128,1024]{1,0:T(8,128)(2,1)}, bf16[128,1024]{1,0:T(8,128)(2,1)S(1)}, u32[]{:S(2)}, u32[]{:S(2)}) collective-permute-start(bf16[128,1024]{1,0:T(8,128)(2,1)} %refs_0_.1), channel_id=1, source_target_pairs={{0,2},{1,3},{2,0},{3,1},{4,6},{5,7},{6,4},{7,5},{8,10},{9,11},{10,... | collective-permute-start | bytes 786440 | tf_op jit(solution)/shard_map/ppermute | solution.py:219
  7.1 0.0 collective-permute-start.2
  7.1 7.9 %collective-permute-done.1.refs_2_ = bf16[128,1024]{1,0:T(8,128)(2,1)S(1)} collective-permute-done((bf16[128,1024]{1,0:T(8,128)(2,1)}, bf16[128,1024]{1,0:T(8,128)(2,1)S(1)}, u32[]{:S(2)}, u32[]{:S(2)}) %collective-permute-start.1) | collective-permute-done | bytes 262176 | tf_op jit(solution)/shard_map/ppermute | solution.py:219
  15.0 1.7 %collective-permute-start.6 = (bf16[128,1024]{1,0:T(8,128)(2,1)S(1)}, bf16[128,1024]{1,0:T(8,128)(2,1)S(1)}, u32[]{:S(2)}, u32[]{:S(2)}) collective-permute-start(bf16[128,1024]{1,0:T(8,128)(2,1)S(1)} %collective-permute-done.1.refs_2_), channel_id=1, source_target_pairs={{0,2},{1,3},{2,0},{3,1},{4,6},{5,7},{6,4},{7,5},{8,10},{9,11},{10,... | collective-permute-start | bytes 786440 | tf_op jit(solution)/shard_map/ppermute | solution.py:219
  16.7 0.9 %collective-permute-done.7.refs_1_ = bf16[128,1024]{1,0:T(8,128)(2,1)S(1)} collective-permute-done((bf16[128,1024]{1,0:T(8,128)(2,1)}, bf16[128,1024]{1,0:T(8,128)(2,1)S(1)}, u32[]{:S(2)}, u32[]{:S(2)}) %collective-permute-start.7) | collective-permute-done | bytes 262176 | tf_op jit(solution)/shard_map/ppermute | solution.py:219
  17.6 0.0 collective-permute-start.8
  17.6 0.0 copy-done.1
  17.6 1.5 %collective-permute-start.3 = (s32[1,128]{1,0:T(1,128)S(1)}, s32[1,128]{1,0:T(1,128)S(1)}, u32[]{:S(2)}, u32[]{:S(2)}) collective-permute-start(s32[1,128]{1,0:T(1,128)S(1)} %bitcast.3), channel_id=1, source_target_pairs={{0,2},{1,3},{2,0},{3,1},{4,6},{5,7},{6,4},{7,5},{8,10},{9,11},{10,... | collective-permute-start | bytes 1544 | tf_op jit(solution)/shard_map/ppermute | solution.py:219
  19.1 3.5 %collective-permute-done.3.x_ids_ref = s32[1,128]{1,0:T(1,128)S(1)} collective-permute-done((s32[1,128]{1,0:T(1,128)S(1)}, s32[1,128]{1,0:T(1,128)S(1)}, u32[]{:S(2)}, u32[]{:S(2)}) %collective-permute-start.3) | collective-permute-done | bytes 544 | tf_op jit(solution)/shard_map/ppermute | solution.py:219
  22.6 0.0 collective-permute-start.4
  22.6 1.1 %collective-permute-done.4.c_ids_ref = s32[1,128]{1,0:T(1,128)S(1)} collective-permute-done((s32[1,128]{1,0:T(1,128)S(1)}, s32[1,128]{1,0:T(1,128)S(1)}, u32[]{:S(2)}, u32[]{:S(2)}) %collective-permute-start.4) | collective-permute-done | bytes 544 | tf_op jit(solution)/shard_map/ppermute | solution.py:219
  23.7 0.0 collective-permute-start.5
  23.7 3.6 %collective-permute-done.5.e_ids_ref = s32[2,128]{1,0:T(2,128)S(1)} collective-permute-done((s32[2,128]{1,0:T(2,128)S(1)}, s32[2,128]{1,0:T(2,128)S(1)}, u32[]{:S(2)}, u32[]{:S(2)}) %collective-permute-start.5) | collective-permute-done | bytes 1056 | tf_op jit(solution)/shard_map/ppermute | solution.py:219
  27.3 0.9 %collective-permute-start.9 = (s32[2,128]{1,0:T(2,128)S(1)}, s32[2,128]{1,0:T(2,128)S(1)}, u32[]{:S(2)}, u32[]{:S(2)}) collective-permute-start(s32[2,128]{1,0:T(2,128)S(1)} %get-tuple-element.19), channel_id=1, source_target_pairs={{0,8},{1,9},{2,10},{3,11},{4,12},{5,13},{6,14},{7,15},{8,0},{9,1},... | collective-permute-start | bytes 3080 | tf_op jit(solution)/shard_map/ppermute | solution.py:219
  28.2 0.0 collective-permute-done.refs_1_
  28.2 0.0 collective-permute-done.2.refs_3_
  28.2 0.0 copy-start
  28.2 0.9 %copy-done = bf16[128,1024]{1,0:T(8,128)(2,1)S(1)} copy-done((bf16[128,1024]{1,0:T(8,128)(2,1)S(1)}, bf16[128,1024]{1,0:T(8,128)(2,1)}, u32[]{:S(2)}) %copy-start) | copy-done | bytes 262168
  29.1 0.8 %early.1 = (f32[8,384]{1,0:T(8,128)S(1)}, bf16[384,1024]{1,0:T(8,128)(2,1)S(1)}, bf16[128,1024]{1,0:T(8,128)(2,1)S(1)}) custom-call(bf16[128,1024]{1,0:T(8,128)(2,1)S(1)} %copy-done, bf16[128,1024]{1,0:T(8,128)(2,1)S(1)} %collective-permute-done.refs_1_, bf16[128,1024]{1,0:T(8,128)(2,1)S(1)} %collective-permute-done.1.refs_2_, ...), custom_call_target="tpu_custom_call" | custom-call | tf_op jit(solution)/shard_map/early/pallas_call | solution.py:175
  30.0 1.8 %collective-permute-done.9.h_ids_ref = s32[2,128]{1,0:T(2,128)S(1)} collective-permute-done((s32[2,128]{1,0:T(2,128)S(1)}, s32[2,128]{1,0:T(2,128)S(1)}, u32[]{:S(2)}, u32[]{:S(2)}) %collective-permute-start.9) | collective-permute-done | bytes 1056 | tf_op jit(solution)/shard_map/ppermute | solution.py:219
  31.8 0.0 collective-permute-done.6.refs_0_
  31.8 0.0 collective-permute-done.8.refs_2_
  31.8 1.0 %late.1 = (f32[8,128]{1,0:T(8,128)S(1)}, f32[8,128]{1,0:T(8,128)S(1)}, f32[8,128]{1,0:T(8,128)S(1)}, f32[8,128]{1,0:T(8,128)S(1)}) custom-call(f32[8,384]{1,0:T(8,128)S(1)} %get-tuple-element.12.best_ref, bf16[384,1024]{1,0:T(8,128)(2,1)S(1)} %get-tuple-element.13.own_ref, bf16[128,1024]{1,0:T(8,128)(2,1)S(1)} %get-tuple-element.14.c_ref, ...), custom_call_target="tpu_custom_call" | custom-call | tf_op jit(solution)/shard_map/late/pallas_call | solution.py:207
  32.8 1.4 %collective-permute-start.10 = (f32[8,128]{1,0:T(8,128)S(1)}, f32[8,128]{1,0:T(8,128)S(1)}, u32[]{:S(2)}, u32[]{:S(2)}) collective-permute-start(f32[8,128]{1,0:T(8,128)S(1)} %get-tuple-element.16), channel_id=1, source_target_pairs={{0,2},{1,3},{2,0},{3,1},{4,6},{5,7},{6,4},{7,5},{8,10},{9,11},{10,... | collective-permute-start | bytes 12296 | tf_op jit(solution)/shard_map/ppermute | solution.py:219
  34.2 0.4 %collective-permute-start.11 = (f32[8,128]{1,0:T(8,128)S(1)}, f32[8,128]{1,0:T(8,128)S(1)}, u32[]{:S(2)}, u32[]{:S(2)}) collective-permute-start(f32[8,128]{1,0:T(8,128)S(1)} %get-tuple-element.17), channel_id=1, source_target_pairs={{0,4},{1,5},{2,6},{3,7},{4,0},{5,1},{6,2},{7,3},{8,12},{9,13},{10,... | collective-permute-start | bytes 12296 | tf_op jit(solution)/shard_map/ppermute | solution.py:219
  34.6 1.7 %collective-permute-start.12 = (f32[8,128]{1,0:T(8,128)S(1)}, f32[8,128]{1,0:T(8,128)S(1)}, u32[]{:S(2)}, u32[]{:S(2)}) collective-permute-start(f32[8,128]{1,0:T(8,128)S(1)} %get-tuple-element.18), channel_id=1, source_target_pairs={{0,6},{1,7},{2,4},{3,5},{4,2},{5,3},{6,0},{7,1},{8,14},{9,15},{10,... | collective-permute-start | bytes 12296 | tf_op jit(solution)/shard_map/ppermute | solution.py:219
  36.3 0.1 collective-permute-done.10
  36.4 1.3 %collective-permute-done.11 = f32[8,128]{1,0:T(8,128)S(1)} collective-permute-done((f32[8,128]{1,0:T(8,128)S(1)}, f32[8,128]{1,0:T(8,128)S(1)}, u32[]{:S(2)}, u32[]{:S(2)}) %collective-permute-start.11) | collective-permute-done | bytes 4128 | tf_op jit(solution)/shard_map/ppermute | solution.py:219
  37.8 1.3 %collective-permute-done.12 = f32[8,128]{1,0:T(8,128)S(1)} collective-permute-done((f32[8,128]{1,0:T(8,128)S(1)}, f32[8,128]{1,0:T(8,128)S(1)}, u32[]{:S(2)}, u32[]{:S(2)}) %collective-permute-start.12) | collective-permute-done | bytes 4128 | tf_op jit(solution)/shard_map/ppermute | solution.py:219
  39.1 0.5 %slice_bitcast_fusion = f32[128]{0:T(128)} fusion(f32[8,128]{1,0:T(8,128)S(1)} %maximum_maximum_fusion), kind=kLoop, calls=%fused_computation.3 | loop fusion | bytes 1024 | tf_op jit(solution)/shard_map/squeeze | solution.py:237
  (2 shorter events, 0.0 us)
Async XLA Ops:
  0.0 17.6 %copy-start.1 = (s32[128,1]{0,1:T(1,128)S(1)}, s32[128,1]{0,1:T(1,128)}, u32[]{:S(2)}) copy-start(s32[128,1]{0,1:T(1,128)} %param.3) | copy-start | bytes 1540
  0.0 15.0 %collective-permute-start.1 = (bf16[128,1024]{1,0:T(8,128)(2,1)}, bf16[128,1024]{1,0:T(8,128)(2,1)S(1)}, u32[]{:S(2)}, u32[]{:S(2)}) collective-permute-start(bf16[128,1024]{1,0:T(8,128)(2,1)} %refs_0_.1), channel_id=1, source_target_pairs={{0,4},{1,5},{2,6},{3,7},{4,0},{5,1},{6,2},{7,3},{8,12},{9,13},{10,... | collective-permute-start | bytes 786440 | tf_op jit(solution)/shard_map/ppermute | solution.py:219
  3.0 14.6 %collective-permute-start.7 = (bf16[128,1024]{1,0:T(8,128)(2,1)}, bf16[128,1024]{1,0:T(8,128)(2,1)S(1)}, u32[]{:S(2)}, u32[]{:S(2)}) collective-permute-start(bf16[128,1024]{1,0:T(8,128)(2,1)} %refs_0_.1), channel_id=1, source_target_pairs={{0,8},{1,9},{2,10},{3,11},{4,12},{5,13},{6,14},{7,15},{8,0},{9,1},... | collective-permute-start | bytes 786440 | tf_op jit(solution)/shard_map/ppermute | solution.py:219
  5.6 22.6 %collective-permute-start = (bf16[128,1024]{1,0:T(8,128)(2,1)}, bf16[128,1024]{1,0:T(8,128)(2,1)S(1)}, u32[]{:S(2)}, u32[]{:S(2)}) collective-permute-start(bf16[128,1024]{1,0:T(8,128)(2,1)} %refs_0_.1), channel_id=1, source_target_pairs={{0,2},{1,3},{2,0},{3,1},{4,6},{5,7},{6,4},{7,5},{8,10},{9,11},{10,... | collective-permute-start | bytes 786440 | tf_op jit(solution)/shard_map/ppermute | solution.py:219
  7.1 21.1 %collective-permute-start.2 = (bf16[128,1024]{1,0:T(8,128)(2,1)}, bf16[128,1024]{1,0:T(8,128)(2,1)S(1)}, u32[]{:S(2)}, u32[]{:S(2)}) collective-permute-start(bf16[128,1024]{1,0:T(8,128)(2,1)} %refs_0_.1), channel_id=1, source_target_pairs={{0,1},{1,0},{2,3},{3,2},{4,5},{5,4},{6,7},{7,6},{8,9},{9,8},{10,11... | collective-permute-start | bytes 786440 | tf_op jit(solution)/shard_map/ppermute | solution.py:219
  15.0 16.7 %collective-permute-start.6 = (bf16[128,1024]{1,0:T(8,128)(2,1)S(1)}, bf16[128,1024]{1,0:T(8,128)(2,1)S(1)}, u32[]{:S(2)}, u32[]{:S(2)}) collective-permute-start(bf16[128,1024]{1,0:T(8,128)(2,1)S(1)} %collective-permute-done.1.refs_2_), channel_id=1, source_target_pairs={{0,2},{1,3},{2,0},{3,1},{4,6},{5,7},{6,4},{7,5},{8,10},{9,11},{10,... | collective-permute-start | bytes 786440 | tf_op jit(solution)/shard_map/ppermute | solution.py:219
  17.6 14.2 %collective-permute-start.8 = (bf16[128,1024]{1,0:T(8,128)(2,1)S(1)}, bf16[128,1024]{1,0:T(8,128)(2,1)S(1)}, u32[]{:S(2)}, u32[]{:S(2)}) collective-permute-start(bf16[128,1024]{1,0:T(8,128)(2,1)S(1)} %collective-permute-done.7.refs_1_), channel_id=1, source_target_pairs={{0,1},{1,0},{2,3},{3,2},{4,5},{5,4},{6,7},{7,6},{8,9},{9,8},{10,11... | collective-permute-start | bytes 786440 | tf_op jit(solution)/shard_map/ppermute | solution.py:219
  17.6 5.0 %collective-permute-start.3 = (s32[1,128]{1,0:T(1,128)S(1)}, s32[1,128]{1,0:T(1,128)S(1)}, u32[]{:S(2)}, u32[]{:S(2)}) collective-permute-start(s32[1,128]{1,0:T(1,128)S(1)} %bitcast.3), channel_id=1, source_target_pairs={{0,2},{1,3},{2,0},{3,1},{4,6},{5,7},{6,4},{7,5},{8,10},{9,11},{10,... | collective-permute-start | bytes 1544 | tf_op jit(solution)/shard_map/ppermute | solution.py:219
  22.6 1.1 %collective-permute-start.4 = (s32[1,128]{1,0:T(1,128)S(1)}, s32[1,128]{1,0:T(1,128)S(1)}, u32[]{:S(2)}, u32[]{:S(2)}) collective-permute-start(s32[1,128]{1,0:T(1,128)S(1)} %bitcast.4), channel_id=1, source_target_pairs={{0,1},{1,0},{2,3},{3,2},{4,5},{5,4},{6,7},{7,6},{8,9},{9,8},{10,11... | collective-permute-start | bytes 1544 | tf_op jit(solution)/shard_map/ppermute | solution.py:219
  23.7 3.6 %collective-permute-start.5 = (s32[2,128]{1,0:T(2,128)S(1)}, s32[2,128]{1,0:T(2,128)S(1)}, u32[]{:S(2)}, u32[]{:S(2)}) collective-permute-start(s32[2,128]{1,0:T(2,128)S(1)} %get-tuple-element.20), channel_id=1, source_target_pairs={{0,4},{1,5},{2,6},{3,7},{4,0},{5,1},{6,2},{7,3},{8,12},{9,13},{10,... | collective-permute-start | bytes 3080 | tf_op jit(solution)/shard_map/ppermute | solution.py:219
  27.3 4.5 %collective-permute-start.9 = (s32[2,128]{1,0:T(2,128)S(1)}, s32[2,128]{1,0:T(2,128)S(1)}, u32[]{:S(2)}, u32[]{:S(2)}) collective-permute-start(s32[2,128]{1,0:T(2,128)S(1)} %get-tuple-element.19), channel_id=1, source_target_pairs={{0,8},{1,9},{2,10},{3,11},{4,12},{5,13},{6,14},{7,15},{8,0},{9,1},... | collective-permute-start | bytes 3080 | tf_op jit(solution)/shard_map/ppermute | solution.py:219
  28.2 1.0 %copy-start = (bf16[128,1024]{1,0:T(8,128)(2,1)S(1)}, bf16[128,1024]{1,0:T(8,128)(2,1)}, u32[]{:S(2)}) copy-start(bf16[128,1024]{1,0:T(8,128)(2,1)} %refs_0_.1) | copy-start | bytes 786436
  32.8 3.7 %collective-permute-start.10 = (f32[8,128]{1,0:T(8,128)S(1)}, f32[8,128]{1,0:T(8,128)S(1)}, u32[]{:S(2)}, u32[]{:S(2)}) collective-permute-start(f32[8,128]{1,0:T(8,128)S(1)} %get-tuple-element.16), channel_id=1, source_target_pairs={{0,2},{1,3},{2,0},{3,1},{4,6},{5,7},{6,4},{7,5},{8,10},{9,11},{10,... | collective-permute-start | bytes 12296 | tf_op jit(solution)/shard_map/ppermute | solution.py:219
  34.2 3.6 %collective-permute-start.11 = (f32[8,128]{1,0:T(8,128)S(1)}, f32[8,128]{1,0:T(8,128)S(1)}, u32[]{:S(2)}, u32[]{:S(2)}) collective-permute-start(f32[8,128]{1,0:T(8,128)S(1)} %get-tuple-element.17), channel_id=1, source_target_pairs={{0,4},{1,5},{2,6},{3,7},{4,0},{5,1},{6,2},{7,3},{8,12},{9,13},{10,... | collective-permute-start | bytes 12296 | tf_op jit(solution)/shard_map/ppermute | solution.py:219
  34.6 4.5 %collective-permute-start.12 = (f32[8,128]{1,0:T(8,128)S(1)}, f32[8,128]{1,0:T(8,128)S(1)}, u32[]{:S(2)}, u32[]{:S(2)}) collective-permute-start(f32[8,128]{1,0:T(8,128)S(1)} %get-tuple-element.18), channel_id=1, source_target_pairs={{0,6},{1,7},{2,4},{3,5},{4,2},{5,3},{6,0},{7,1},{8,14},{9,15},{10,... | collective-permute-start | bytes 12296 | tf_op jit(solution)/shard_map/ppermute | solution.py:219

commit v7 on v6

--- a/solution.py
+++ b/solution.py
@@ -221,14 +221,17 @@
     rows = embeddings.shape[0]
     mine, ids = embeddings, assignment.reshape(1, rows)
     e = swap(LOW, mine)
-    h = swap(HIGH, mine)
     x = swap(SHARD, mine)
     c = swap(SUB, mine)
+    h = swap(HIGH, mine)
     x_ids, c_ids = swap(SHARD, ids), swap(SUB, ids)
     e_ids = swap(LOW, jnp.concatenate([ids, x_ids]))
     h_ids = swap(HIGH, jnp.concatenate([ids, c_ids]))
-    xe = swap(SHARD, e)
-    ch = swap(SUB, h)
+    e_then, _ = lax.optimization_barrier((e, e_ids))
+    h_then = h
+    h_then, _ = lax.optimization_barrier((h, h_ids))
+    xe = swap(SHARD, e_then)
+    ch = swap(SUB, h_then)
     early_ids = [ids, x_ids, c_ids, e_ids]
     best, own, c = early([mine, x, e, c], early_ids)
     found, *others = late(best, own, c, [xe, h, ch], [*early_ids, h_ids])

time: 39.8 us -> 33.4 us (0.84)
  waiting for transfers between devices: 21.6 us -> 15.3 us
    ppermute x13, waiting for transfers between devices: 21.6 us -> 15.3 us  [swap(): return lax.ppermute(array, AXES, [(i, i ^ flip) for i in range(16)])]
  transfers between devices with their start and end apart: 13 -> 13, of which waited for: 9 -> 7; matrix products, arithmetic and copies ran while one was open for 0% -> 0% of each run, Pallas kernels for 2% -> 3%
where the time goes in v7:
time: 33.4 us; the launch traced here: 33.3 us
  waiting for transfers between devices  15.3 us (46%)
  starting transfers between devices  14.7 us (44%)
  Pallas kernels  1.84 us (6%)
  local copies, waits for them, and re-layouts  1.46 us (4%)
    ppermute x13, waiting for transfers between devices, swap(): return lax.ppermute(array, AXES, [(i, i ^ flip) for i in range(16)])  15.3 us
    ppermute x13, starting transfers between devices, swap(): return lax.ppermute(array, AXES, [(i, i ^ flip) for i in range(16)])  14.7 us
    pallas_call x1, Pallas kernels, late(): pl.pallas_call(late_kernel, out_shape=[jax.ShapeDtypeStruct((8, rows), jn...  0.99 us
    unnamed x4, local copies, waits for them, and re-layouts  0.95 us
    pallas_call x1, Pallas kernels, early(): pl.pallas_call(early_kernel, out_shape=[jax.ShapeDtypeStruct((8, 3 * rows...  0.85 us
  transfers between devices with their start and end apart: 13, of which 7 were waited for; matrix products, arithmetic and copies ran while one was open for 0% of the time, Pallas kernels for 3%

profile of v7, /device:TPU:0, one launch (start us, length us, event | category | flops | bytes accessed | tf_op | source)
XLA Modules:
  0.0 33.3 jit_solution(3407201341719585594)
XLA Ops:
  0.0 0.0 copy-start.1
  0.0 3.0 %collective-permute-start.1 = (bf16[128,1024]{1,0:T(8,128)(2,1)}, bf16[128,1024]{1,0:T(8,128)(2,1)S(1)}, u32[]{:S(2)}, u32[]{:S(2)}) collective-permute-start(bf16[128,1024]{1,0:T(8,128)(2,1)} %refs_0_.1), channel_id=1, source_target_pairs={{0,4},{1,5},{2,6},{3,7},{4,0},{5,1},{6,2},{7,3},{8,12},{9,13},{10,... | collective-permute-start | bytes 786440 | tf_op jit(solution)/shard_map/ppermute | solution.py:219
  3.0 2.6 %collective-permute-start.7 = (bf16[128,1024]{1,0:T(8,128)(2,1)}, bf16[128,1024]{1,0:T(8,128)(2,1)S(1)}, u32[]{:S(2)}, u32[]{:S(2)}) collective-permute-start(bf16[128,1024]{1,0:T(8,128)(2,1)} %refs_0_.1), channel_id=1, source_target_pairs={{0,8},{1,9},{2,10},{3,11},{4,12},{5,13},{6,14},{7,15},{8,0},{9,1},... | collective-permute-start | bytes 786440 | tf_op jit(solution)/shard_map/ppermute | solution.py:219
  5.6 0.0 copy-done.1
  5.6 1.5 %collective-permute-start.3 = (s32[1,128]{1,0:T(1,128)S(1)}, s32[1,128]{1,0:T(1,128)S(1)}, u32[]{:S(2)}, u32[]{:S(2)}) collective-permute-start(s32[1,128]{1,0:T(1,128)S(1)} %bitcast.3), channel_id=1, source_target_pairs={{0,2},{1,3},{2,0},{3,1},{4,6},{5,7},{6,4},{7,5},{8,10},{9,11},{10,... | collective-permute-start | bytes 1544 | tf_op jit(solution)/shard_map/ppermute | solution.py:219
  7.1 0.0 collective-permute-start.4
  7.1 2.0 %collective-permute-done.3.x_ids_ref = s32[1,128]{1,0:T(1,128)S(1)} collective-permute-done((s32[1,128]{1,0:T(1,128)S(1)}, s32[1,128]{1,0:T(1,128)S(1)}, u32[]{:S(2)}, u32[]{:S(2)}) %collective-permute-start.3) | collective-permute-done | bytes 544 | tf_op jit(solution)/shard_map/ppermute | solution.py:219
  9.2 0.0 collective-permute-done.4.c_ids_ref
  9.2 0.5 %collective-permute-start.5 = (s32[2,128]{1,0:T(2,128)S(1)}, s32[2,128]{1,0:T(2,128)S(1)}, u32[]{:S(2)}, u32[]{:S(2)}) collective-permute-start(s32[2,128]{1,0:T(2,128)S(1)} %get-tuple-element.24), channel_id=1, source_target_pairs={{0,4},{1,5},{2,6},{3,7},{4,0},{5,1},{6,2},{7,3},{8,12},{9,13},{10,... | collective-permute-start | bytes 3080 | tf_op jit(solution)/shard_map/ppermute | solution.py:219
  9.7 0.2 collective-permute-start.8
  9.9 1.6 %collective-permute-start = (bf16[128,1024]{1,0:T(8,128)(2,1)}, bf16[128,1024]{1,0:T(8,128)(2,1)S(1)}, u32[]{:S(2)}, u32[]{:S(2)}) collective-permute-start(bf16[128,1024]{1,0:T(8,128)(2,1)} %refs_0_.1), channel_id=1, source_target_pairs={{0,2},{1,3},{2,0},{3,1},{4,6},{5,7},{6,4},{7,5},{8,10},{9,11},{10,... | collective-permute-start | bytes 786440 | tf_op jit(solution)/shard_map/ppermute | solution.py:219
  11.5 3.6 %collective-permute-done.5.e_ids_ref = s32[2,128]{1,0:T(2,128)S(1)} collective-permute-done((s32[2,128]{1,0:T(2,128)S(1)}, s32[2,128]{1,0:T(2,128)S(1)}, u32[]{:S(2)}, u32[]{:S(2)}) %collective-permute-start.5) | collective-permute-done | bytes 1056 | tf_op jit(solution)/shard_map/ppermute | solution.py:219
  15.1 0.0 collective-permute-start.2
  15.1 0.0 collective-permute-done.1.refs_2_
  15.1 1.7 %collective-permute-start.6 = (bf16[128,1024]{1,0:T(8,128)(2,1)S(1)}, bf16[128,1024]{1,0:T(8,128)(2,1)S(1)}, u32[]{:S(2)}, u32[]{:S(2)}) collective-permute-start(bf16[128,1024]{1,0:T(8,128)(2,1)S(1)} %collective-permute-done.1.refs_2_), channel_id=1, source_target_pairs={{0,2},{1,3},{2,0},{3,1},{4,6},{5,7},{6,4},{7,5},{8,10},{9,11},{10,... | collective-permute-start | bytes 786440 | tf_op jit(solution)/shard_map/ppermute | solution.py:219
  16.8 0.9 %collective-permute-done.8.h_ids_ref = s32[2,128]{1,0:T(2,128)S(1)} collective-permute-done((s32[2,128]{1,0:T(2,128)S(1)}, s32[2,128]{1,0:T(2,128)S(1)}, u32[]{:S(2)}, u32[]{:S(2)}) %collective-permute-start.8) | collective-permute-done | bytes 1056 | tf_op jit(solution)/shard_map/ppermute | solution.py:219
  17.7 0.0 collective-permute-done.7.refs_1_
  17.7 0.0 collective-permute-start.9
  17.7 0.0 collective-permute-done.refs_1_
  17.7 0.0 collective-permute-done.2.refs_3_
  17.7 0.0 copy-start
  17.7 0.9 %copy-done = bf16[128,1024]{1,0:T(8,128)(2,1)S(1)} copy-done((bf16[128,1024]{1,0:T(8,128)(2,1)S(1)}, bf16[128,1024]{1,0:T(8,128)(2,1)}, u32[]{:S(2)}) %copy-start) | copy-done | bytes 262168
  18.6 0.8 %early.1 = (f32[8,384]{1,0:T(8,128)S(1)}, bf16[384,1024]{1,0:T(8,128)(2,1)S(1)}, bf16[128,1024]{1,0:T(8,128)(2,1)S(1)}) custom-call(bf16[128,1024]{1,0:T(8,128)(2,1)S(1)} %copy-done, bf16[128,1024]{1,0:T(8,128)(2,1)S(1)} %collective-permute-done.refs_1_, bf16[128,1024]{1,0:T(8,128)(2,1)S(1)} %collective-permute-done.1.refs_2_, ...), custom_call_target="tpu_custom_call" | custom-call | tf_op jit(solution)/shard_map/early/pallas_call | solution.py:175
  19.5 4.3 %collective-permute-done.6.refs_0_ = bf16[128,1024]{1,0:T(8,128)(2,1)S(1)} collective-permute-done((bf16[128,1024]{1,0:T(8,128)(2,1)S(1)}, bf16[128,1024]{1,0:T(8,128)(2,1)S(1)}, u32[]{:S(2)}, u32[]{:S(2)}) %collective-permute-start.6) | collective-permute-done | bytes 262176 | tf_op jit(solution)/shard_map/ppermute | solution.py:219
  23.8 0.0 collective-permute-done.9.refs_2_
  23.8 1.0 %late.1 = (f32[8,128]{1,0:T(8,128)S(1)}, f32[8,128]{1,0:T(8,128)S(1)}, f32[8,128]{1,0:T(8,128)S(1)}, f32[8,128]{1,0:T(8,128)S(1)}) custom-call(f32[8,384]{1,0:T(8,128)S(1)} %get-tuple-element.14.best_ref, bf16[384,1024]{1,0:T(8,128)(2,1)S(1)} %get-tuple-element.15.own_ref, bf16[128,1024]{1,0:T(8,128)(2,1)S(1)} %get-tuple-element.16.c_ref, ...), custom_call_target="tpu_custom_call" | custom-call | tf_op jit(solution)/shard_map/late/pallas_call | solution.py:207
  24.8 1.7 %collective-permute-start.10 = (f32[8,128]{1,0:T(8,128)S(1)}, f32[8,128]{1,0:T(8,128)S(1)}, u32[]{:S(2)}, u32[]{:S(2)}) collective-permute-start(f32[8,128]{1,0:T(8,128)S(1)} %get-tuple-element.20), channel_id=1, source_target_pairs={{0,2},{1,3},{2,0},{3,1},{4,6},{5,7},{6,4},{7,5},{8,10},{9,11},{10,... | collective-permute-start | bytes 12296 | tf_op jit(solution)/shard_map/ppermute | solution.py:219
  26.5 1.7 %collective-permute-start.11 = (f32[8,128]{1,0:T(8,128)S(1)}, f32[8,128]{1,0:T(8,128)S(1)}, u32[]{:S(2)}, u32[]{:S(2)}) collective-permute-start(f32[8,128]{1,0:T(8,128)S(1)} %get-tuple-element.21), channel_id=1, source_target_pairs={{0,4},{1,5},{2,6},{3,7},{4,0},{5,1},{6,2},{7,3},{8,12},{9,13},{10,... | collective-permute-start | bytes 12296 | tf_op jit(solution)/shard_map/ppermute | solution.py:219
  28.2 0.1 collective-permute-start.12
  28.4 0.1 collective-permute-done.10
  28.5 1.7 %collective-permute-done.11 = f32[8,128]{1,0:T(8,128)S(1)} collective-permute-done((f32[8,128]{1,0:T(8,128)S(1)}, f32[8,128]{1,0:T(8,128)S(1)}, u32[]{:S(2)}, u32[]{:S(2)}) %collective-permute-start.11) | collective-permute-done | bytes 4128 | tf_op jit(solution)/shard_map/ppermute | solution.py:219
  30.1 2.6 %collective-permute-done.12 = f32[8,128]{1,0:T(8,128)S(1)} collective-permute-done((f32[8,128]{1,0:T(8,128)S(1)}, f32[8,128]{1,0:T(8,128)S(1)}, u32[]{:S(2)}, u32[]{:S(2)}) %collective-permute-start.12) | collective-permute-done | bytes 4128 | tf_op jit(solution)/shard_map/ppermute | solution.py:219
  32.8 0.5 %slice_bitcast_fusion = f32[128]{0:T(128)} fusion(f32[8,128]{1,0:T(8,128)S(1)} %maximum_maximum_fusion), kind=kLoop, calls=%fused_computation.3 | loop fusion | bytes 1024 | tf_op jit(solution)/shard_map/squeeze | solution.py:240
  (2 shorter events, 0.0 us)
Async XLA Ops:
  0.0 5.6 %copy-start.1 = (s32[128,1]{0,1:T(1,128)S(1)}, s32[128,1]{0,1:T(1,128)}, u32[]{:S(2)}) copy-start(s32[128,1]{0,1:T(1,128)} %param.3) | copy-start | bytes 1540
  0.0 15.1 %collective-permute-start.1 = (bf16[128,1024]{1,0:T(8,128)(2,1)}, bf16[128,1024]{1,0:T(8,128)(2,1)S(1)}, u32[]{:S(2)}, u32[]{:S(2)}) collective-permute-start(bf16[128,1024]{1,0:T(8,128)(2,1)} %refs_0_.1), channel_id=1, source_target_pairs={{0,4},{1,5},{2,6},{3,7},{4,0},{5,1},{6,2},{7,3},{8,12},{9,13},{10,... | collective-permute-start | bytes 786440 | tf_op jit(solution)/shard_map/ppermute | solution.py:219
  3.0 14.6 %collective-permute-start.7 = (bf16[128,1024]{1,0:T(8,128)(2,1)}, bf16[128,1024]{1,0:T(8,128)(2,1)S(1)}, u32[]{:S(2)}, u32[]{:S(2)}) collective-permute-start(bf16[128,1024]{1,0:T(8,128)(2,1)} %refs_0_.1), channel_id=1, source_target_pairs={{0,8},{1,9},{2,10},{3,11},{4,12},{5,13},{6,14},{7,15},{8,0},{9,1},... | collective-permute-start | bytes 786440 | tf_op jit(solution)/shard_map/ppermute | solution.py:219
  5.6 3.5 %collective-permute-start.3 = (s32[1,128]{1,0:T(1,128)S(1)}, s32[1,128]{1,0:T(1,128)S(1)}, u32[]{:S(2)}, u32[]{:S(2)}) collective-permute-start(s32[1,128]{1,0:T(1,128)S(1)} %bitcast.3), channel_id=1, source_target_pairs={{0,2},{1,3},{2,0},{3,1},{4,6},{5,7},{6,4},{7,5},{8,10},{9,11},{10,... | collective-permute-start | bytes 1544 | tf_op jit(solution)/shard_map/ppermute | solution.py:219
  7.1 2.1 %collective-permute-start.4 = (s32[1,128]{1,0:T(1,128)S(1)}, s32[1,128]{1,0:T(1,128)S(1)}, u32[]{:S(2)}, u32[]{:S(2)}) collective-permute-start(s32[1,128]{1,0:T(1,128)S(1)} %bitcast.4), channel_id=1, source_target_pairs={{0,1},{1,0},{2,3},{3,2},{4,5},{5,4},{6,7},{7,6},{8,9},{9,8},{10,11... | collective-permute-start | bytes 1544 | tf_op jit(solution)/shard_map/ppermute | solution.py:219
  9.2 5.9 %collective-permute-start.5 = (s32[2,128]{1,0:T(2,128)S(1)}, s32[2,128]{1,0:T(2,128)S(1)}, u32[]{:S(2)}, u32[]{:S(2)}) collective-permute-start(s32[2,128]{1,0:T(2,128)S(1)} %get-tuple-element.24), channel_id=1, source_target_pairs={{0,4},{1,5},{2,6},{3,7},{4,0},{5,1},{6,2},{7,3},{8,12},{9,13},{10,... | collective-permute-start | bytes 3080 | tf_op jit(solution)/shard_map/ppermute | solution.py:219
  9.7 8.0 %collective-permute-start.8 = (s32[2,128]{1,0:T(2,128)S(1)}, s32[2,128]{1,0:T(2,128)S(1)}, u32[]{:S(2)}, u32[]{:S(2)}) collective-permute-start(s32[2,128]{1,0:T(2,128)S(1)} %get-tuple-element.23), channel_id=1, source_target_pairs={{0,8},{1,9},{2,10},{3,11},{4,12},{5,13},{6,14},{7,15},{8,0},{9,1},... | collective-permute-start | bytes 3080 | tf_op jit(solution)/shard_map/ppermute | solution.py:219
  9.9 7.8 %collective-permute-start = (bf16[128,1024]{1,0:T(8,128)(2,1)}, bf16[128,1024]{1,0:T(8,128)(2,1)S(1)}, u32[]{:S(2)}, u32[]{:S(2)}) collective-permute-start(bf16[128,1024]{1,0:T(8,128)(2,1)} %refs_0_.1), channel_id=1, source_target_pairs={{0,2},{1,3},{2,0},{3,1},{4,6},{5,7},{6,4},{7,5},{8,10},{9,11},{10,... | collective-permute-start | bytes 786440 | tf_op jit(solution)/shard_map/ppermute | solution.py:219
  15.1 2.6 %collective-permute-start.2 = (bf16[128,1024]{1,0:T(8,128)(2,1)}, bf16[128,1024]{1,0:T(8,128)(2,1)S(1)}, u32[]{:S(2)}, u32[]{:S(2)}) collective-permute-start(bf16[128,1024]{1,0:T(8,128)(2,1)} %refs_0_.1), channel_id=1, source_target_pairs={{0,1},{1,0},{2,3},{3,2},{4,5},{5,4},{6,7},{7,6},{8,9},{9,8},{10,11... | collective-permute-start | bytes 786440 | tf_op jit(solution)/shard_map/ppermute | solution.py:219
  15.1 8.7 %collective-permute-start.6 = (bf16[128,1024]{1,0:T(8,128)(2,1)S(1)}, bf16[128,1024]{1,0:T(8,128)(2,1)S(1)}, u32[]{:S(2)}, u32[]{:S(2)}) collective-permute-start(bf16[128,1024]{1,0:T(8,128)(2,1)S(1)} %collective-permute-done.1.refs_2_), channel_id=1, source_target_pairs={{0,2},{1,3},{2,0},{3,1},{4,6},{5,7},{6,4},{7,5},{8,10},{9,11},{10,... | collective-permute-start | bytes 786440 | tf_op jit(solution)/shard_map/ppermute | solution.py:219
  17.7 6.1 %collective-permute-start.9 = (bf16[128,1024]{1,0:T(8,128)(2,1)S(1)}, bf16[128,1024]{1,0:T(8,128)(2,1)S(1)}, u32[]{:S(2)}, u32[]{:S(2)}) collective-permute-start(bf16[128,1024]{1,0:T(8,128)(2,1)S(1)} %collective-permute-done.7.refs_1_), channel_id=1, source_target_pairs={{0,1},{1,0},{2,3},{3,2},{4,5},{5,4},{6,7},{7,6},{8,9},{9,8},{10,11... | collective-permute-start | bytes 786440 | tf_op jit(solution)/shard_map/ppermute | solution.py:219
  17.7 1.0 %copy-start = (bf16[128,1024]{1,0:T(8,128)(2,1)S(1)}, bf16[128,1024]{1,0:T(8,128)(2,1)}, u32[]{:S(2)}) copy-start(bf16[128,1024]{1,0:T(8,128)(2,1)} %refs_0_.1) | copy-start | bytes 786436
  24.8 3.7 %collective-permute-start.10 = (f32[8,128]{1,0:T(8,128)S(1)}, f32[8,128]{1,0:T(8,128)S(1)}, u32[]{:S(2)}, u32[]{:S(2)}) collective-permute-start(f32[8,128]{1,0:T(8,128)S(1)} %get-tuple-element.20), channel_id=1, source_target_pairs={{0,2},{1,3},{2,0},{3,1},{4,6},{5,7},{6,4},{7,5},{8,10},{9,11},{10,... | collective-permute-start | bytes 12296 | tf_op jit(solution)/shard_map/ppermute | solution.py:219
  26.5 3.6 %collective-permute-start.11 = (f32[8,128]{1,0:T(8,128)S(1)}, f32[8,128]{1,0:T(8,128)S(1)}, u32[]{:S(2)}, u32[]{:S(2)}) collective-permute-start(f32[8,128]{1,0:T(8,128)S(1)} %get-tuple-element.21), channel_id=1, source_target_pairs={{0,4},{1,5},{2,6},{3,7},{4,0},{5,1},{6,2},{7,3},{8,12},{9,13},{10,... | collective-permute-start | bytes 12296 | tf_op jit(solution)/shard_map/ppermute | solution.py:219
  28.2 4.5 %collective-permute-start.12 = (f32[8,128]{1,0:T(8,128)S(1)}, f32[8,128]{1,0:T(8,128)S(1)}, u32[]{:S(2)}, u32[]{:S(2)}) collective-permute-start(f32[8,128]{1,0:T(8,128)S(1)} %get-tuple-element.22), channel_id=1, source_target_pairs={{0,6},{1,7},{2,4},{3,5},{4,2},{5,3},{6,0},{7,1},{8,14},{9,15},{10,... | collective-permute-start | bytes 12296 | tf_op jit(solution)/shard_map/ppermute | solution.py:219

commit v8 on v7

--- a/solution.py
+++ b/solution.py
@@ -186,32 +186,51 @@
     )(blocks, *ids)
 
 
-def late_kernel(best_ref, own_ref, c_ref, refs, ids_ref, x_ids_ref, c_ids_ref, e_ids_ref, h_ids_ref, *out_refs):
-    xe, h, ch = [unit_of(ref[...]) for ref in refs]
-    own, c = own_ref[...], c_ref[...]
-    mine = own[: c.shape[0]]
+def middle_kernel(
+    best_ref, own_ref, c_ref, h_ref, ch_ref, ids_ref, x_ids_ref, c_ids_ref, e_ids_ref, h_ids_ref,
+    mine_out_ref, x_out_ref, e_out_ref, far_ref,
+):
+    h, ch = unit_of(h_ref[...]), unit_of(ch_ref[...])
     own_ids = jnp.concatenate([ids_ref[...], x_ids_ref[...], e_ids_ref[:1, :]], axis=1)
-    h_ids, ch_ids = h_ids_ref[:1, :], h_ids_ref[1:, :]
-    best = best_of(own, own_ids, [h, ch], [h_ids, ch_ids])
+    best = best_of(own_ref[...], own_ids, [h, ch], [h_ids_ref[:1, :], h_ids_ref[1:, :]])
     best = jnp.maximum(best, best_ref[:1, :])
-    others, other_ids = [mine, c, h, ch], [ids_ref[...], c_ids_ref[...], h_ids, ch_ids]
-    last = best_of(xe, e_ids_ref[1:, :], others, other_ids)
-    best = jnp.concatenate([best, last], axis=1)
-    for place, out_ref in enumerate(out_refs):
-        rows = out_ref.shape[1]
+    rows = c_ref.shape[0]
+    for place, out_ref in enumerate((mine_out_ref, x_out_ref, e_out_ref)):
         out_ref[...] = jnp.broadcast_to(best[:, place * rows : (place + 1) * rows], out_ref.shape)
-
-
-def late(best, own, c, blocks, ids):
-    rows = c.shape[0]
-    return pl.pallas_call(
-        late_kernel,
-        out_shape=[jax.ShapeDtypeStruct((8, rows), jnp.float32)] * 4,
-        in_specs=(VMEM, VMEM, VMEM, [VMEM] * len(blocks), *[VMEM] * len(ids)),
+    far_ref[...] = jnp.concatenate([own_ref[:rows], c_ref[...], h, ch], axis=0)
+
+
+def middle(best, own, c, h, ch, ids):
+    rows, width = c.shape
+    return pl.pallas_call(
+        middle_kernel,
+        out_shape=[jax.ShapeDtypeStruct((8, rows), jnp.float32)] * 3
+        + [jax.ShapeDtypeStruct((4 * rows, width), jnp.bfloat16)],
+        in_specs=[VMEM] * 10,
         out_specs=[VMEM] * 4,
         compiler_params=LIMIT,
+        name="middle",
+    )(best, own, c, h, ch, *ids)
+
+
+def late_kernel(far_ref, xe_ref, ids_ref, c_ids_ref, e_ids_ref, h_ids_ref, out_ref):
+    xe = unit_of(xe_ref[...])
+    rows = xe.shape[0]
+    others = [far_ref[place * rows : (place + 1) * rows] for place in range(4)]
+    other_ids = [ids_ref[...], c_ids_ref[...], h_ids_ref[:1, :], h_ids_ref[1:, :]]
+    out_ref[...] = jnp.broadcast_to(best_of(xe, e_ids_ref[1:, :], others, other_ids), out_ref.shape)
+
+
+def late(far, xe, ids):
+    rows = xe.shape[0]
+    return pl.pallas_call(
+        late_kernel,
+        out_shape=jax.ShapeDtypeStruct((8, rows), jnp.float32),
+        in_specs=[VMEM] * 6,
+        out_specs=VMEM,
+        compiler_params=LIMIT,
         name="late",
-    )(best, own, c, blocks, *ids)
+    )(far, xe, *ids)
 
 
 def square(embeddings, assignment):
@@ -220,24 +239,24 @@
 
     rows = embeddings.shape[0]
     mine, ids = embeddings, assignment.reshape(1, rows)
+    x_ids, c_ids = swap(SHARD, ids), swap(SUB, ids)
     e = swap(LOW, mine)
     x = swap(SHARD, mine)
-    c = swap(SUB, mine)
-    h = swap(HIGH, mine)
-    x_ids, c_ids = swap(SHARD, ids), swap(SUB, ids)
+    far = mine
+    h = swap(HIGH, far)
     e_ids = swap(LOW, jnp.concatenate([ids, x_ids]))
     h_ids = swap(HIGH, jnp.concatenate([ids, c_ids]))
+    mine_c, _ = lax.optimization_barrier((mine, e))
+    c = swap(SUB, mine_c)
     e_then, _ = lax.optimization_barrier((e, e_ids))
-    h_then = h
-    h_then, _ = lax.optimization_barrier((h, h_ids))
+    h_then, _, _ = lax.optimization_barrier((h, h_ids, e_ids))
     xe = swap(SHARD, e_then)
     ch = swap(SUB, h_then)
-    early_ids = [ids, x_ids, c_ids, e_ids]
-    best, own, c = early([mine, x, e, c], early_ids)
-    found, *others = late(best, own, c, [xe, h, ch], [*early_ids, h_ids])
-    for flip, other in zip((SHARD, LOW, LOW | SHARD), others):
-        found = jnp.maximum(found, swap(flip, other))
-    return found[0]
+    best, own, c = early([mine, x, e, c], [ids, x_ids, c_ids, e_ids])
+    found, x_best, e_best, far = middle(best, own, c, h, ch, [ids, x_ids, c_ids, e_ids, h_ids])
+    x_best, e_best = swap(SHARD, x_best), swap(LOW, e_best)
+    xe_best = swap(LOW | SHARD, late(far, xe, [ids, c_ids, e_ids, h_ids]))
+    return jnp.maximum(jnp.maximum(found, x_best), jnp.maximum(e_best, xe_best))[0]
 
 
 def shared_owner(embeddings, assignment):

time: 33.4 us -> 32.2 us (0.964)
  starting transfers between devices: 14.7 us -> 13.7 us
  waiting for transfers between devices: 15.3 us -> 14.7 us
    ppermute x13, starting transfers between devices: 14.7 us -> 13.7 us  [swap(): return lax.ppermute(array, AXES, [(i, i ^ flip) for i in range(16)])]
    ppermute x13, waiting for transfers between devices: 15.3 us -> 14.7 us  [swap(): return lax.ppermute(array, AXES, [(i, i ^ flip) for i in range(16)])]
    pallas_call x1 -> x2, Pallas kernels: 0.99 us -> 1.25 us  [the longest x1 0.69 us: middle(): pl.pallas_call(middle_kernel, out_shape=[jax.ShapeDtypeStruct((8, rows),...]
  transfers between devices with their start and end apart: 13 -> 13, of which waited for: 7 -> 5; matrix products, arithmetic and copies ran while one was open for 0% -> 0% of each run, Pallas kernels for 3% -> 7%
where the time goes in v8:
time: 32.2 us; the launch traced here: 32.1 us
  waiting for transfers between devices  14.7 us (46%)
  starting transfers between devices  13.7 us (43%)
  Pallas kernels  2.09 us (6%)
  local copies, waits for them, and re-layouts  1.47 us (5%)
    ppermute x13, waiting for transfers between devices, swap(): return lax.ppermute(array, AXES, [(i, i ^ flip) for i in range(16)])  14.7 us
    ppermute x13, starting transfers between devices, swap(): return lax.ppermute(array, AXES, [(i, i ^ flip) for i in range(16)])  13.7 us
    unnamed x4, local copies, waits for them, and re-layouts  0.95 us
    pallas_call x1, Pallas kernels, early(): pl.pallas_call(early_kernel, out_shape=[jax.ShapeDtypeStruct((8, 3 * rows...  0.84 us
    pallas_call x1, Pallas kernels, middle(): pl.pallas_call(middle_kernel, out_shape=[jax.ShapeDtypeStruct((8, rows),...  0.69 us
  transfers between devices with their start and end apart: 13, of which 5 were waited for; matrix products, arithmetic and copies ran while one was open for 0% of the time, Pallas kernels for 7%

profile of v8, /device:TPU:0, one launch (start us, length us, event | category | flops | bytes accessed | tf_op | source)
XLA Modules:
  0.0 32.1 jit_solution(14231834867944533202)
XLA Ops:
  0.0 0.0 copy-start.1
  0.0 3.0 %collective-permute-start.1 = (bf16[128,1024]{1,0:T(8,128)(2,1)}, bf16[128,1024]{1,0:T(8,128)(2,1)S(1)}, u32[]{:S(2)}, u32[]{:S(2)}) collective-permute-start(bf16[128,1024]{1,0:T(8,128)(2,1)} %refs_0_.1), channel_id=1, source_target_pairs={{0,4},{1,5},{2,6},{3,7},{4,0},{5,1},{6,2},{7,3},{8,12},{9,13},{10,... | collective-permute-start | bytes 786440 | tf_op jit(solution)/shard_map/ppermute | solution.py:238
  3.0 2.6 %collective-permute-start.6 = (bf16[128,1024]{1,0:T(8,128)(2,1)}, bf16[128,1024]{1,0:T(8,128)(2,1)S(1)}, u32[]{:S(2)}, u32[]{:S(2)}) collective-permute-start(bf16[128,1024]{1,0:T(8,128)(2,1)} %refs_0_.1), channel_id=1, source_target_pairs={{0,8},{1,9},{2,10},{3,11},{4,12},{5,13},{6,14},{7,15},{8,0},{9,1},... | collective-permute-start | bytes 786440 | tf_op jit(solution)/shard_map/ppermute | solution.py:238
  5.6 0.0 copy-done.1
  5.6 0.0 collective-permute-start.4
  5.6 1.5 %collective-permute-start.3 = (s32[1,128]{1,0:T(1,128)S(1)}, s32[1,128]{1,0:T(1,128)S(1)}, u32[]{:S(2)}, u32[]{:S(2)}) collective-permute-start(s32[1,128]{1,0:T(1,128)S(1)} %bitcast.4), channel_id=1, source_target_pairs={{0,2},{1,3},{2,0},{3,1},{4,6},{5,7},{6,4},{7,5},{8,10},{9,11},{10,... | collective-permute-start | bytes 1544 | tf_op jit(solution)/shard_map/ppermute | solution.py:238
  7.1 0.0 collective-permute-done.4.c_ids_ref
  7.1 2.0 %collective-permute-done.3.x_ids_ref = s32[1,128]{1,0:T(1,128)S(1)} collective-permute-done((s32[1,128]{1,0:T(1,128)S(1)}, s32[1,128]{1,0:T(1,128)S(1)}, u32[]{:S(2)}, u32[]{:S(2)}) %collective-permute-start.3) | collective-permute-done | bytes 544 | tf_op jit(solution)/shard_map/ppermute | solution.py:238
  9.2 0.3 %collective-permute-start.7 = (s32[2,128]{1,0:T(2,128)S(1)}, s32[2,128]{1,0:T(2,128)S(1)}, u32[]{:S(2)}, u32[]{:S(2)}) collective-permute-start(s32[2,128]{1,0:T(2,128)S(1)} %get-tuple-element.25), channel_id=1, source_target_pairs={{0,8},{1,9},{2,10},{3,11},{4,12},{5,13},{6,14},{7,15},{8,0},{9,1},... | collective-permute-start | bytes 3080 | tf_op jit(solution)/shard_map/ppermute | solution.py:238
  9.5 0.3 collective-permute-start.5
  9.8 1.6 %collective-permute-start = (bf16[128,1024]{1,0:T(8,128)(2,1)}, bf16[128,1024]{1,0:T(8,128)(2,1)S(1)}, u32[]{:S(2)}, u32[]{:S(2)}) collective-permute-start(bf16[128,1024]{1,0:T(8,128)(2,1)} %refs_0_.1), channel_id=1, source_target_pairs={{0,2},{1,3},{2,0},{3,1},{4,6},{5,7},{6,4},{7,5},{8,10},{9,11},{10,... | collective-permute-start | bytes 786440 | tf_op jit(solution)/shard_map/ppermute | solution.py:238
  11.4 3.6 %collective-permute-done.1.refs_2_ = bf16[128,1024]{1,0:T(8,128)(2,1)S(1)} collective-permute-done((bf16[128,1024]{1,0:T(8,128)(2,1)}, bf16[128,1024]{1,0:T(8,128)(2,1)S(1)}, u32[]{:S(2)}, u32[]{:S(2)}) %collective-permute-start.1) | collective-permute-done | bytes 262176 | tf_op jit(solution)/shard_map/ppermute | solution.py:238
  15.0 0.0 collective-permute-start.2
  15.0 2.6 %collective-permute-done.7.h_ids_ref = s32[2,128]{1,0:T(2,128)S(1)} collective-permute-done((s32[2,128]{1,0:T(2,128)S(1)}, s32[2,128]{1,0:T(2,128)S(1)}, u32[]{:S(2)}, u32[]{:S(2)}) %collective-permute-start.7) | collective-permute-done | bytes 1056 | tf_op jit(solution)/shard_map/ppermute | solution.py:238
  17.7 0.0 collective-permute-done.5.e_ids_ref
  17.7 0.0 collective-permute-done.6.h_ref
  17.7 0.0 collective-permute-start.8
  17.7 1.6 %collective-permute-start.11 = (bf16[128,1024]{1,0:T(8,128)(2,1)S(1)}, bf16[128,1024]{1,0:T(8,128)(2,1)S(1)}, u32[]{:S(2)}, u32[]{:S(2)}) collective-permute-start(bf16[128,1024]{1,0:T(8,128)(2,1)S(1)} %collective-permute-done.1.refs_2_), channel_id=1, source_target_pairs={{0,2},{1,3},{2,0},{3,1},{4,6},{5,7},{6,4},{7,5},{8,10},{9,11},{10,... | collective-permute-start | bytes 786440 | tf_op jit(solution)/shard_map/ppermute | solution.py:238
  19.2 0.0 collective-permute-done.refs_1_
  19.2 0.0 collective-permute-done.2.refs_3_
  19.2 0.0 copy-start
  19.2 0.9 %copy-done = bf16[128,1024]{1,0:T(8,128)(2,1)S(1)} copy-done((bf16[128,1024]{1,0:T(8,128)(2,1)S(1)}, bf16[128,1024]{1,0:T(8,128)(2,1)}, u32[]{:S(2)}) %copy-start) | copy-done | bytes 262168
  20.2 0.8 %early.1 = (f32[8,384]{1,0:T(8,128)S(1)}, bf16[384,1024]{1,0:T(8,128)(2,1)S(1)}, bf16[128,1024]{1,0:T(8,128)(2,1)S(1)}) custom-call(bf16[128,1024]{1,0:T(8,128)(2,1)S(1)} %copy-done, bf16[128,1024]{1,0:T(8,128)(2,1)S(1)} %collective-permute-done.refs_1_, bf16[128,1024]{1,0:T(8,128)(2,1)S(1)} %collective-permute-done.1.refs_2_, ...), custom_call_target="tpu_custom_call" | custom-call | tf_op jit(solution)/shard_map/early/pallas_call | solution.py:175
  21.0 0.0 collective-permute-done.8.ch_ref
  21.1 0.7 %middle.1 = (f32[8,128]{1,0:T(8,128)S(1)}, f32[8,128]{1,0:T(8,128)S(1)}, f32[8,128]{1,0:T(8,128)S(1)}, bf16[512,1024]{1,0:T(8,128)(2,1)S(1)}) custom-call(f32[8,384]{1,0:T(8,128)S(1)} %get-tuple-element.16.best_ref, bf16[384,1024]{1,0:T(8,128)(2,1)S(1)} %get-tuple-element.17.own_ref, bf16[128,1024]{1,0:T(8,128)(2,1)S(1)} %get-tuple-element.18.c_ref, ...), custom_call_target="tpu_custom_call" | custom-call | tf_op jit(solution)/shard_map/middle/pallas_call | solution.py:205
  21.8 0.6 %collective-permute-start.9 = (f32[8,128]{1,0:T(8,128)S(1)}, f32[8,128]{1,0:T(8,128)S(1)}, u32[]{:S(2)}, u32[]{:S(2)}) collective-permute-start(f32[8,128]{1,0:T(8,128)S(1)} %get-tuple-element.21), channel_id=1, source_target_pairs={{0,2},{1,3},{2,0},{3,1},{4,6},{5,7},{6,4},{7,5},{8,10},{9,11},{10,... | collective-permute-start | bytes 12296 | tf_op jit(solution)/shard_map/ppermute | solution.py:238
  22.4 0.8 %collective-permute-start.10 = (f32[8,128]{1,0:T(8,128)S(1)}, f32[8,128]{1,0:T(8,128)S(1)}, u32[]{:S(2)}, u32[]{:S(2)}) collective-permute-start(f32[8,128]{1,0:T(8,128)S(1)} %get-tuple-element.22), channel_id=1, source_target_pairs={{0,4},{1,5},{2,6},{3,7},{4,0},{5,1},{6,2},{7,3},{8,12},{9,13},{10,... | collective-permute-start | bytes 12296 | tf_op jit(solution)/shard_map/ppermute | solution.py:238
  23.1 3.3 %collective-permute-done.11.xe_ref = bf16[128,1024]{1,0:T(8,128)(2,1)S(1)} collective-permute-done((bf16[128,1024]{1,0:T(8,128)(2,1)S(1)}, bf16[128,1024]{1,0:T(8,128)(2,1)S(1)}, u32[]{:S(2)}, u32[]{:S(2)}) %collective-permute-start.11) | collective-permute-done | bytes 262176 | tf_op jit(solution)/shard_map/ppermute | solution.py:238
  26.4 0.6 %late.1 = f32[8,128]{1,0:T(8,128)S(1)} custom-call(bf16[512,1024]{1,0:T(8,128)(2,1)S(1)} %get-tuple-element.23.far_ref, bf16[128,1024]{1,0:T(8,128)(2,1)S(1)} %collective-permute-done.11.xe_ref, s32[1,128]{1,0:T(1,128)S(1)} %bitcast.8, s32[1,128]{1,0:T(1,128)S(1)} %collective-permute-done.4.c_ids_ref, s32[2,128]{1,0:T(2,128)S(1)} %collective-permute-done.5.e_ids_ref, ...), custom_call_target="tpu_custom_call" | custom-call | tf_op jit(solution)/shard_map/late/pallas_call | solution.py:226
  27.0 1.4 %collective-permute-start.12 = (f32[8,128]{1,0:T(8,128)S(1)}, f32[8,128]{1,0:T(8,128)S(1)}, u32[]{:S(2)}, u32[]{:S(2)}) collective-permute-start(f32[8,128]{1,0:T(8,128)S(1)} %late.1), channel_id=1, source_target_pairs={{0,6},{1,7},{2,4},{3,5},{4,2},{5,3},{6,0},{7,1},{8,14},{9,15},{10,... | collective-permute-start | bytes 12296 | tf_op jit(solution)/shard_map/ppermute | solution.py:238
  28.4 0.0 collective-permute-done.9
  28.4 0.0 collective-permute-done.10
  28.4 3.2 %collective-permute-done.12 = f32[8,128]{1,0:T(8,128)S(1)} collective-permute-done((f32[8,128]{1,0:T(8,128)S(1)}, f32[8,128]{1,0:T(8,128)S(1)}, u32[]{:S(2)}, u32[]{:S(2)}) %collective-permute-start.12) | collective-permute-done | bytes 4128 | tf_op jit(solution)/shard_map/ppermute | solution.py:238
  31.6 0.5 %slice_bitcast_fusion = f32[128]{0:T(128)} fusion(f32[8,128]{1,0:T(8,128)S(1)} %maximum_maximum_fusion), kind=kLoop, calls=%fused_computation.3 | loop fusion | bytes 1024 | tf_op jit(solution)/shard_map/squeeze | solution.py:259
  (2 shorter events, 0.0 us)
Async XLA Ops:
  0.0 5.6 %copy-start.1 = (s32[128,1]{0,1:T(1,128)S(1)}, s32[128,1]{0,1:T(1,128)}, u32[]{:S(2)}) copy-start(s32[128,1]{0,1:T(1,128)} %param.3) | copy-start | bytes 1540
  0.0 15.0 %collective-permute-start.1 = (bf16[128,1024]{1,0:T(8,128)(2,1)}, bf16[128,1024]{1,0:T(8,128)(2,1)S(1)}, u32[]{:S(2)}, u32[]{:S(2)}) collective-permute-start(bf16[128,1024]{1,0:T(8,128)(2,1)} %refs_0_.1), channel_id=1, source_target_pairs={{0,4},{1,5},{2,6},{3,7},{4,0},{5,1},{6,2},{7,3},{8,12},{9,13},{10,... | collective-permute-start | bytes 786440 | tf_op jit(solution)/shard_map/ppermute | solution.py:238
  3.0 14.6 %collective-permute-start.6 = (bf16[128,1024]{1,0:T(8,128)(2,1)}, bf16[128,1024]{1,0:T(8,128)(2,1)S(1)}, u32[]{:S(2)}, u32[]{:S(2)}) collective-permute-start(bf16[128,1024]{1,0:T(8,128)(2,1)} %refs_0_.1), channel_id=1, source_target_pairs={{0,8},{1,9},{2,10},{3,11},{4,12},{5,13},{6,14},{7,15},{8,0},{9,1},... | collective-permute-start | bytes 786440 | tf_op jit(solution)/shard_map/ppermute | solution.py:238
  5.6 1.5 %collective-permute-start.4 = (s32[1,128]{1,0:T(1,128)S(1)}, s32[1,128]{1,0:T(1,128)S(1)}, u32[]{:S(2)}, u32[]{:S(2)}) collective-permute-start(s32[1,128]{1,0:T(1,128)S(1)} %bitcast.3), channel_id=1, source_target_pairs={{0,1},{1,0},{2,3},{3,2},{4,5},{5,4},{6,7},{7,6},{8,9},{9,8},{10,11... | collective-permute-start | bytes 1544 | tf_op jit(solution)/shard_map/ppermute | solution.py:238
  5.6 3.5 %collective-permute-start.3 = (s32[1,128]{1,0:T(1,128)S(1)}, s32[1,128]{1,0:T(1,128)S(1)}, u32[]{:S(2)}, u32[]{:S(2)}) collective-permute-start(s32[1,128]{1,0:T(1,128)S(1)} %bitcast.4), channel_id=1, source_target_pairs={{0,2},{1,3},{2,0},{3,1},{4,6},{5,7},{6,4},{7,5},{8,10},{9,11},{10,... | collective-permute-start | bytes 1544 | tf_op jit(solution)/shard_map/ppermute | solution.py:238
  9.2 8.5 %collective-permute-start.7 = (s32[2,128]{1,0:T(2,128)S(1)}, s32[2,128]{1,0:T(2,128)S(1)}, u32[]{:S(2)}, u32[]{:S(2)}) collective-permute-start(s32[2,128]{1,0:T(2,128)S(1)} %get-tuple-element.25), channel_id=1, source_target_pairs={{0,8},{1,9},{2,10},{3,11},{4,12},{5,13},{6,14},{7,15},{8,0},{9,1},... | collective-permute-start | bytes 3080 | tf_op jit(solution)/shard_map/ppermute | solution.py:238
  9.5 8.2 %collective-permute-start.5 = (s32[2,128]{1,0:T(2,128)S(1)}, s32[2,128]{1,0:T(2,128)S(1)}, u32[]{:S(2)}, u32[]{:S(2)}) collective-permute-start(s32[2,128]{1,0:T(2,128)S(1)} %get-tuple-element.26), channel_id=1, source_target_pairs={{0,4},{1,5},{2,6},{3,7},{4,0},{5,1},{6,2},{7,3},{8,12},{9,13},{10,... | collective-permute-start | bytes 3080 | tf_op jit(solution)/shard_map/ppermute | solution.py:238
  9.8 9.4 %collective-permute-start = (bf16[128,1024]{1,0:T(8,128)(2,1)}, bf16[128,1024]{1,0:T(8,128)(2,1)S(1)}, u32[]{:S(2)}, u32[]{:S(2)}) collective-permute-start(bf16[128,1024]{1,0:T(8,128)(2,1)} %refs_0_.1), channel_id=1, source_target_pairs={{0,2},{1,3},{2,0},{3,1},{4,6},{5,7},{6,4},{7,5},{8,10},{9,11},{10,... | collective-permute-start | bytes 786440 | tf_op jit(solution)/shard_map/ppermute | solution.py:238
  15.0 4.2 %collective-permute-start.2 = (bf16[128,1024]{1,0:T(8,128)(2,1)}, bf16[128,1024]{1,0:T(8,128)(2,1)S(1)}, u32[]{:S(2)}, u32[]{:S(2)}) collective-permute-start(bf16[128,1024]{1,0:T(8,128)(2,1)} %refs_0_.1), channel_id=1, source_target_pairs={{0,1},{1,0},{2,3},{3,2},{4,5},{5,4},{6,7},{7,6},{8,9},{9,8},{10,11... | collective-permute-start | bytes 786440 | tf_op jit(solution)/shard_map/ppermute | solution.py:238
  17.7 3.4 %collective-permute-start.8 = (bf16[128,1024]{1,0:T(8,128)(2,1)S(1)}, bf16[128,1024]{1,0:T(8,128)(2,1)S(1)}, u32[]{:S(2)}, u32[]{:S(2)}) collective-permute-start(bf16[128,1024]{1,0:T(8,128)(2,1)S(1)} %collective-permute-done.6.h_ref), channel_id=1, source_target_pairs={{0,1},{1,0},{2,3},{3,2},{4,5},{5,4},{6,7},{7,6},{8,9},{9,8},{10,11... | collective-permute-start | bytes 786440 | tf_op jit(solution)/shard_map/ppermute | solution.py:238
  17.7 8.8 %collective-permute-start.11 = (bf16[128,1024]{1,0:T(8,128)(2,1)S(1)}, bf16[128,1024]{1,0:T(8,128)(2,1)S(1)}, u32[]{:S(2)}, u32[]{:S(2)}) collective-permute-start(bf16[128,1024]{1,0:T(8,128)(2,1)S(1)} %collective-permute-done.1.refs_2_), channel_id=1, source_target_pairs={{0,2},{1,3},{2,0},{3,1},{4,6},{5,7},{6,4},{7,5},{8,10},{9,11},{10,... | collective-permute-start | bytes 786440 | tf_op jit(solution)/shard_map/ppermute | solution.py:238
  19.2 1.0 %copy-start = (bf16[128,1024]{1,0:T(8,128)(2,1)S(1)}, bf16[128,1024]{1,0:T(8,128)(2,1)}, u32[]{:S(2)}) copy-start(bf16[128,1024]{1,0:T(8,128)(2,1)} %refs_0_.1) | copy-start | bytes 786436
  21.8 6.7 %collective-permute-start.9 = (f32[8,128]{1,0:T(8,128)S(1)}, f32[8,128]{1,0:T(8,128)S(1)}, u32[]{:S(2)}, u32[]{:S(2)}) collective-permute-start(f32[8,128]{1,0:T(8,128)S(1)} %get-tuple-element.21), channel_id=1, source_target_pairs={{0,2},{1,3},{2,0},{3,1},{4,6},{5,7},{6,4},{7,5},{8,10},{9,11},{10,... | collective-permute-start | bytes 12296 | tf_op jit(solution)/shard_map/ppermute | solution.py:238
  22.4 6.1 %collective-permute-start.10 = (f32[8,128]{1,0:T(8,128)S(1)}, f32[8,128]{1,0:T(8,128)S(1)}, u32[]{:S(2)}, u32[]{:S(2)}) collective-permute-start(f32[8,128]{1,0:T(8,128)S(1)} %get-tuple-element.22), channel_id=1, source_target_pairs={{0,4},{1,5},{2,6},{3,7},{4,0},{5,1},{6,2},{7,3},{8,12},{9,13},{10,... | collective-permute-start | bytes 12296 | tf_op jit(solution)/shard_map/ppermute | solution.py:238
  27.0 4.6 %collective-permute-start.12 = (f32[8,128]{1,0:T(8,128)S(1)}, f32[8,128]{1,0:T(8,128)S(1)}, u32[]{:S(2)}, u32[]{:S(2)}) collective-permute-start(f32[8,128]{1,0:T(8,128)S(1)} %late.1), channel_id=1, source_target_pairs={{0,6},{1,7},{2,4},{3,5},{4,2},{5,3},{6,0},{7,1},{8,14},{9,15},{10,... | collective-permute-start | bytes 12296 | tf_op jit(solution)/shard_map/ppermute | solution.py:238

commit v9 on v8

--- a/solution.py
+++ b/solution.py
@@ -187,10 +187,11 @@
 
 
 def middle_kernel(
-    best_ref, own_ref, c_ref, h_ref, ch_ref, ids_ref, x_ids_ref, c_ids_ref, e_ids_ref, h_ids_ref,
+    best_ref, own_ref, c_ref, h_ref, ch_front_ref, ch_back_ref, ids_ref, x_ids_ref, c_ids_ref, e_ids_ref, h_ids_ref,
     mine_out_ref, x_out_ref, e_out_ref, far_ref,
 ):
-    h, ch = unit_of(h_ref[...]), unit_of(ch_ref[...])
+    h = unit_of(h_ref[...])
+    ch = jnp.concatenate([unit_of(ch_front_ref[...]), unit_of(ch_back_ref[...])], axis=0)
     own_ids = jnp.concatenate([ids_ref[...], x_ids_ref[...], e_ids_ref[:1, :]], axis=1)
     best = best_of(own_ref[...], own_ids, [h, ch], [h_ids_ref[:1, :], h_ids_ref[1:, :]])
     best = jnp.maximum(best, best_ref[:1, :])
@@ -206,11 +207,11 @@
         middle_kernel,
         out_shape=[jax.ShapeDtypeStruct((8, rows), jnp.float32)] * 3
         + [jax.ShapeDtypeStruct((4 * rows, width), jnp.bfloat16)],
-        in_specs=[VMEM] * 10,
+        in_specs=[VMEM] * 11,
         out_specs=[VMEM] * 4,
         compiler_params=LIMIT,
         name="middle",
-    )(best, own, c, h, ch, *ids)
+    )(best, own, c, h, *ch, *ids)
 
 
 def late_kernel(far_ref, xe_ref, ids_ref, c_ids_ref, e_ids_ref, h_ids_ref, out_ref):
@@ -240,18 +241,19 @@
     rows = embeddings.shape[0]
     mine, ids = embeddings, assignment.reshape(1, rows)
     x_ids, c_ids = swap(SHARD, ids), swap(SUB, ids)
+    x_ids, c_ids = swap(SHARD, ids), swap(SUB, ids)
     e = swap(LOW, mine)
     x = swap(SHARD, mine)
-    far = mine
+    far, _ = lax.optimization_barrier((mine, c_ids))
     h = swap(HIGH, far)
     e_ids = swap(LOW, jnp.concatenate([ids, x_ids]))
     h_ids = swap(HIGH, jnp.concatenate([ids, c_ids]))
-    mine_c, _ = lax.optimization_barrier((mine, e))
+    mine_c, _ = lax.optimization_barrier((mine, e_ids))
     c = swap(SUB, mine_c)
     e_then, _ = lax.optimization_barrier((e, e_ids))
-    h_then, _, _ = lax.optimization_barrier((h, h_ids, e_ids))
+    h_then, _ = lax.optimization_barrier((h, h_ids))
     xe = swap(SHARD, e_then)
-    ch = swap(SUB, h_then)
+    ch = [swap(SUB, h_then[: rows // 2]), swap(SUB, h_then[rows // 2 :])]
     best, own, c = early([mine, x, e, c], [ids, x_ids, c_ids, e_ids])
     found, x_best, e_best, far = middle(best, own, c, h, ch, [ids, x_ids, c_ids, e_ids, h_ids])
     x_best, e_best = swap(SHARD, x_best), swap(LOW, e_best)

time: 32.2 us -> 31 us (0.963)
  waiting for transfers between devices: 14.7 us -> 10.4 us
  starting transfers between devices: 13.7 us -> 17.1 us
    ppermute x13 -> x14, waiting for transfers between devices: 14.7 us -> 10.4 us  [swap(): return lax.ppermute(array, AXES, [(i, i ^ flip) for i in range(16)])]
    ppermute x13 -> x14, starting transfers between devices: 13.7 us -> 17.1 us  [swap(): return lax.ppermute(array, AXES, [(i, i ^ flip) for i in range(16)])]
  transfers between devices with their start and end apart: 13 -> 14, of which waited for: 5 -> 6; matrix products, arithmetic and copies ran while one was open for 0% -> 0% of each run, Pallas kernels for 7% -> 7%
where the time goes in v9:
time: 31 us; the launch traced here: 30.8 us
  starting transfers between devices  17.1 us (55%)
  waiting for transfers between devices  10.4 us (34%)
  Pallas kernels  2.09 us (7%)
  local copies, waits for them, and re-layouts  1.19 us (4%)
    ppermute x14, starting transfers between devices, swap(): return lax.ppermute(array, AXES, [(i, i ^ flip) for i in range(16)])  17.1 us
    ppermute x14, waiting for transfers between devices, swap(): return lax.ppermute(array, AXES, [(i, i ^ flip) for i in range(16)])  10.4 us
    pallas_call x1, Pallas kernels, early(): pl.pallas_call(early_kernel, out_shape=[jax.ShapeDtypeStruct((8, 3 * rows...  0.85 us
    pallas_call x1, Pallas kernels, middle(): pl.pallas_call(middle_kernel, out_shape=[jax.ShapeDtypeStruct((8, rows),...  0.69 us
    unnamed x4, local copies, waits for them, and re-layouts  0.66 us
  transfers between devices with their start and end apart: 14, of which 6 were waited for; matrix products, arithmetic and copies ran while one was open for 0% of the time, Pallas kernels for 7%

profile of v9, /device:TPU:0, one launch (start us, length us, event | category | flops | bytes accessed | tf_op | source)
XLA Modules:
  0.0 30.8 jit_solution(9888434813611827069)
XLA Ops:
  0.0 0.0 copy-start.1
  0.0 0.7 %copy-done.1 = s32[128,1]{0,1:T(1,128)S(1)} copy-done((s32[128,1]{0,1:T(1,128)S(1)}, s32[128,1]{0,1:T(1,128)}, u32[]{:S(2)}) %copy-start.1) | copy-done | bytes 536
  0.7 0.5 %collective-permute-start.5 = (s32[1,128]{1,0:T(1,128)S(1)}, s32[1,128]{1,0:T(1,128)S(1)}, u32[]{:S(2)}, u32[]{:S(2)}) collective-permute-start(s32[1,128]{1,0:T(1,128)S(1)} %bitcast.3), channel_id=1, source_target_pairs={{0,1},{1,0},{2,3},{3,2},{4,5},{5,4},{6,7},{7,6},{8,9},{9,8},{10,11... | collective-permute-start | bytes 1544 | tf_op jit(solution)/shard_map/ppermute | solution.py:239
  1.1 2.6 %collective-permute-start.1 = (bf16[128,1024]{1,0:T(8,128)(2,1)}, bf16[128,1024]{1,0:T(8,128)(2,1)S(1)}, u32[]{:S(2)}, u32[]{:S(2)}) collective-permute-start(bf16[128,1024]{1,0:T(8,128)(2,1)} %refs_0_.1), channel_id=1, source_target_pairs={{0,4},{1,5},{2,6},{3,7},{4,0},{5,1},{6,2},{7,3},{8,12},{9,13},{10,... | collective-permute-start | bytes 786440 | tf_op jit(solution)/shard_map/ppermute | solution.py:239
  3.7 0.0 collective-permute-done.5.c_ids_ref
  3.7 2.6 %collective-permute-start.6 = (bf16[128,1024]{1,0:T(8,128)(2,1)}, bf16[128,1024]{1,0:T(8,128)(2,1)S(1)}, u32[]{:S(2)}, u32[]{:S(2)}) collective-permute-start(bf16[128,1024]{1,0:T(8,128)(2,1)} %refs_0_.1), channel_id=1, source_target_pairs={{0,8},{1,9},{2,10},{3,11},{4,12},{5,13},{6,14},{7,15},{8,0},{9,1},... | collective-permute-start | bytes 786440 | tf_op jit(solution)/shard_map/ppermute | solution.py:239
  6.3 1.5 %collective-permute-start.2 = (s32[1,128]{1,0:T(1,128)S(1)}, s32[1,128]{1,0:T(1,128)S(1)}, u32[]{:S(2)}, u32[]{:S(2)}) collective-permute-start(s32[1,128]{1,0:T(1,128)S(1)} %bitcast.4), channel_id=1, source_target_pairs={{0,2},{1,3},{2,0},{3,1},{4,6},{5,7},{6,4},{7,5},{8,10},{9,11},{10,... | collective-permute-start | bytes 1544 | tf_op jit(solution)/shard_map/ppermute | solution.py:239
  7.8 2.0 %collective-permute-done.2.x_ids_ref = s32[1,128]{1,0:T(1,128)S(1)} collective-permute-done((s32[1,128]{1,0:T(1,128)S(1)}, s32[1,128]{1,0:T(1,128)S(1)}, u32[]{:S(2)}, u32[]{:S(2)}) %collective-permute-start.2) | collective-permute-done | bytes 544 | tf_op jit(solution)/shard_map/ppermute | solution.py:239
  9.8 1.1 %collective-permute-start.3 = (s32[2,128]{1,0:T(2,128)S(1)}, s32[2,128]{1,0:T(2,128)S(1)}, u32[]{:S(2)}, u32[]{:S(2)}) collective-permute-start(s32[2,128]{1,0:T(2,128)S(1)} %get-tuple-element.30), channel_id=1, source_target_pairs={{0,4},{1,5},{2,6},{3,7},{4,0},{5,1},{6,2},{7,3},{8,12},{9,13},{10,... | collective-permute-start | bytes 3080 | tf_op jit(solution)/shard_map/ppermute | solution.py:239
  10.9 0.0 copy-start
  10.9 0.3 %collective-permute-start.7 = (s32[2,128]{1,0:T(2,128)S(1)}, s32[2,128]{1,0:T(2,128)S(1)}, u32[]{:S(2)}, u32[]{:S(2)}) collective-permute-start(s32[2,128]{1,0:T(2,128)S(1)} %get-tuple-element.29), channel_id=1, source_target_pairs={{0,8},{1,9},{2,10},{3,11},{4,12},{5,13},{6,14},{7,15},{8,0},{9,1},... | collective-permute-start | bytes 3080 | tf_op jit(solution)/shard_map/ppermute | solution.py:239
  11.3 1.5 %collective-permute-start = (bf16[128,1024]{1,0:T(8,128)(2,1)}, bf16[128,1024]{1,0:T(8,128)(2,1)S(1)}, u32[]{:S(2)}, u32[]{:S(2)}) collective-permute-start(bf16[128,1024]{1,0:T(8,128)(2,1)} %refs_0_.1), channel_id=1, source_target_pairs={{0,2},{1,3},{2,0},{3,1},{4,6},{5,7},{6,4},{7,5},{8,10},{9,11},{10,... | collective-permute-start | bytes 786440 | tf_op jit(solution)/shard_map/ppermute | solution.py:239
  12.8 3.6 %collective-permute-done.3.e_ids_ref = s32[2,128]{1,0:T(2,128)S(1)} collective-permute-done((s32[2,128]{1,0:T(2,128)S(1)}, s32[2,128]{1,0:T(2,128)S(1)}, u32[]{:S(2)}, u32[]{:S(2)}) %collective-permute-start.3) | collective-permute-done | bytes 1056 | tf_op jit(solution)/shard_map/ppermute | solution.py:239
  16.4 0.0 collective-permute-start.4
  16.4 0.0 collective-permute-done.1.refs_2_
  16.4 1.7 %collective-permute-start.12 = (bf16[128,1024]{1,0:T(8,128)(2,1)S(1)}, bf16[128,1024]{1,0:T(8,128)(2,1)S(1)}, u32[]{:S(2)}, u32[]{:S(2)}) collective-permute-start(bf16[128,1024]{1,0:T(8,128)(2,1)S(1)} %collective-permute-done.1.refs_2_), channel_id=1, source_target_pairs={{0,2},{1,3},{2,0},{3,1},{4,6},{5,7},{6,4},{7,5},{8,10},{9,11},{10,... | collective-permute-start | bytes 786440 | tf_op jit(solution)/shard_map/ppermute | solution.py:239
  18.1 0.9 %collective-permute-done.7.h_ids_ref = s32[2,128]{1,0:T(2,128)S(1)} collective-permute-done((s32[2,128]{1,0:T(2,128)S(1)}, s32[2,128]{1,0:T(2,128)S(1)}, u32[]{:S(2)}, u32[]{:S(2)}) %collective-permute-start.7) | collective-permute-done | bytes 1056 | tf_op jit(solution)/shard_map/ppermute | solution.py:239
  19.0 0.0 collective-permute-done.6.h_ref
  19.0 0.1 collective-permute-start.9
  19.1 0.5 %collective-permute-start.8 = (bf16[64,1024]{1,0:T(8,128)(2,1)S(1)}, bf16[64,1024]{1,0:T(8,128)(2,1)S(1)}, u32[]{:S(2)}, u32[]{:S(2)}) collective-permute-start(bf16[64,1024]{1,0:T(8,128)(2,1)S(1)} %get-tuple-element.28), channel_id=1, source_target_pairs={{0,1},{1,0},{2,3},{3,2},{4,5},{5,4},{6,7},{7,6},{8,9},{9,8},{10,11... | collective-permute-start | bytes 393224 | tf_op jit(solution)/shard_map/ppermute | solution.py:239
  19.6 0.0 collective-permute-done.refs_1_
  19.6 0.0 collective-permute-done.4.refs_3_
  19.6 0.0 copy-done
  19.6 0.8 %early.1 = (f32[8,384]{1,0:T(8,128)S(1)}, bf16[384,1024]{1,0:T(8,128)(2,1)S(1)}, bf16[128,1024]{1,0:T(8,128)(2,1)S(1)}) custom-call(bf16[128,1024]{1,0:T(8,128)(2,1)S(1)} %copy-done, bf16[128,1024]{1,0:T(8,128)(2,1)S(1)} %collective-permute-done.refs_1_, bf16[128,1024]{1,0:T(8,128)(2,1)S(1)} %collective-permute-done.1.refs_2_, ...), custom_call_target="tpu_custom_call" | custom-call | tf_op jit(solution)/shard_map/early/pallas_call | solution.py:175
  20.5 0.0 collective-permute-done.9.ch_back_ref
  20.5 0.1 collective-permute-done.8.ch_front_ref
  20.6 0.7 %middle.1 = (f32[8,128]{1,0:T(8,128)S(1)}, f32[8,128]{1,0:T(8,128)S(1)}, f32[8,128]{1,0:T(8,128)S(1)}, bf16[512,1024]{1,0:T(8,128)(2,1)S(1)}) custom-call(f32[8,384]{1,0:T(8,128)S(1)} %get-tuple-element.17.best_ref, bf16[384,1024]{1,0:T(8,128)(2,1)S(1)} %get-tuple-element.18.own_ref, bf16[128,1024]{1,0:T(8,128)(2,1)S(1)} %get-tuple-element.19.c_ref, ...), custom_call_target="tpu_custom_call" | custom-call | tf_op jit(solution)/shard_map/middle/pallas_call | solution.py:206
  21.3 1.6 %collective-permute-start.10 = (f32[8,128]{1,0:T(8,128)S(1)}, f32[8,128]{1,0:T(8,128)S(1)}, u32[]{:S(2)}, u32[]{:S(2)}) collective-permute-start(f32[8,128]{1,0:T(8,128)S(1)} %get-tuple-element.23), channel_id=1, source_target_pairs={{0,2},{1,3},{2,0},{3,1},{4,6},{5,7},{6,4},{7,5},{8,10},{9,11},{10,... | collective-permute-start | bytes 12296 | tf_op jit(solution)/shard_map/ppermute | solution.py:239
  22.9 0.4 %collective-permute-start.11 = (f32[8,128]{1,0:T(8,128)S(1)}, f32[8,128]{1,0:T(8,128)S(1)}, u32[]{:S(2)}, u32[]{:S(2)}) collective-permute-start(f32[8,128]{1,0:T(8,128)S(1)} %get-tuple-element.24), channel_id=1, source_target_pairs={{0,4},{1,5},{2,6},{3,7},{4,0},{5,1},{6,2},{7,3},{8,12},{9,13},{10,... | collective-permute-start | bytes 12296 | tf_op jit(solution)/shard_map/ppermute | solution.py:239
  23.3 1.9 %collective-permute-done.12.xe_ref = bf16[128,1024]{1,0:T(8,128)(2,1)S(1)} collective-permute-done((bf16[128,1024]{1,0:T(8,128)(2,1)S(1)}, bf16[128,1024]{1,0:T(8,128)(2,1)S(1)}, u32[]{:S(2)}, u32[]{:S(2)}) %collective-permute-start.12) | collective-permute-done | bytes 262176 | tf_op jit(solution)/shard_map/ppermute | solution.py:239
  25.2 0.6 %late.1 = f32[8,128]{1,0:T(8,128)S(1)} custom-call(bf16[512,1024]{1,0:T(8,128)(2,1)S(1)} %get-tuple-element.25.far_ref, bf16[128,1024]{1,0:T(8,128)(2,1)S(1)} %collective-permute-done.12.xe_ref, s32[1,128]{1,0:T(1,128)S(1)} %bitcast.8, s32[1,128]{1,0:T(1,128)S(1)} %collective-permute-done.5.c_ids_ref, s32[2,128]{1,0:T(2,128)S(1)} %collective-permute-done.3.e_ids_ref, ...), custom_call_target="tpu_custom_call" | custom-call | tf_op jit(solution)/shard_map/late/pallas_call | solution.py:227
  25.7 2.9 %collective-permute-start.13 = (f32[8,128]{1,0:T(8,128)S(1)}, f32[8,128]{1,0:T(8,128)S(1)}, u32[]{:S(2)}, u32[]{:S(2)}) collective-permute-start(f32[8,128]{1,0:T(8,128)S(1)} %late.1), channel_id=1, source_target_pairs={{0,6},{1,7},{2,4},{3,5},{4,2},{5,3},{6,0},{7,1},{8,14},{9,15},{10,... | collective-permute-start | bytes 12296 | tf_op jit(solution)/shard_map/ppermute | solution.py:239
  28.6 0.0 collective-permute-done.10
  28.6 0.0 collective-permute-done.11
  28.6 1.7 %collective-permute-done.13 = f32[8,128]{1,0:T(8,128)S(1)} collective-permute-done((f32[8,128]{1,0:T(8,128)S(1)}, f32[8,128]{1,0:T(8,128)S(1)}, u32[]{:S(2)}, u32[]{:S(2)}) %collective-permute-start.13) | collective-permute-done | bytes 4128 | tf_op jit(solution)/shard_map/ppermute | solution.py:239
  30.3 0.5 %slice_bitcast_fusion = f32[128]{0:T(128)} fusion(f32[8,128]{1,0:T(8,128)S(1)} %maximum_maximum_fusion), kind=kLoop, calls=%fused_computation.3 | loop fusion | bytes 1024 | tf_op jit(solution)/shard_map/squeeze | solution.py:261
  (3 shorter events, 0.0 us)
Async XLA Ops:
  0.0 0.7 %copy-start.1 = (s32[128,1]{0,1:T(1,128)S(1)}, s32[128,1]{0,1:T(1,128)}, u32[]{:S(2)}) copy-start(s32[128,1]{0,1:T(1,128)} %param.3) | copy-start | bytes 1540
  0.7 3.0 %collective-permute-start.5 = (s32[1,128]{1,0:T(1,128)S(1)}, s32[1,128]{1,0:T(1,128)S(1)}, u32[]{:S(2)}, u32[]{:S(2)}) collective-permute-start(s32[1,128]{1,0:T(1,128)S(1)} %bitcast.3), channel_id=1, source_target_pairs={{0,1},{1,0},{2,3},{3,2},{4,5},{5,4},{6,7},{7,6},{8,9},{9,8},{10,11... | collective-permute-start | bytes 1544 | tf_op jit(solution)/shard_map/ppermute | solution.py:239
  1.1 15.3 %collective-permute-start.1 = (bf16[128,1024]{1,0:T(8,128)(2,1)}, bf16[128,1024]{1,0:T(8,128)(2,1)S(1)}, u32[]{:S(2)}, u32[]{:S(2)}) collective-permute-start(bf16[128,1024]{1,0:T(8,128)(2,1)} %refs_0_.1), channel_id=1, source_target_pairs={{0,4},{1,5},{2,6},{3,7},{4,0},{5,1},{6,2},{7,3},{8,12},{9,13},{10,... | collective-permute-start | bytes 786440 | tf_op jit(solution)/shard_map/ppermute | solution.py:239
  3.7 15.3 %collective-permute-start.6 = (bf16[128,1024]{1,0:T(8,128)(2,1)}, bf16[128,1024]{1,0:T(8,128)(2,1)S(1)}, u32[]{:S(2)}, u32[]{:S(2)}) collective-permute-start(bf16[128,1024]{1,0:T(8,128)(2,1)} %refs_0_.1), channel_id=1, source_target_pairs={{0,8},{1,9},{2,10},{3,11},{4,12},{5,13},{6,14},{7,15},{8,0},{9,1},... | collective-permute-start | bytes 786440 | tf_op jit(solution)/shard_map/ppermute | solution.py:239
  6.3 3.5 %collective-permute-start.2 = (s32[1,128]{1,0:T(1,128)S(1)}, s32[1,128]{1,0:T(1,128)S(1)}, u32[]{:S(2)}, u32[]{:S(2)}) collective-permute-start(s32[1,128]{1,0:T(1,128)S(1)} %bitcast.4), channel_id=1, source_target_pairs={{0,2},{1,3},{2,0},{3,1},{4,6},{5,7},{6,4},{7,5},{8,10},{9,11},{10,... | collective-permute-start | bytes 1544 | tf_op jit(solution)/shard_map/ppermute | solution.py:239
  9.8 6.6 %collective-permute-start.3 = (s32[2,128]{1,0:T(2,128)S(1)}, s32[2,128]{1,0:T(2,128)S(1)}, u32[]{:S(2)}, u32[]{:S(2)}) collective-permute-start(s32[2,128]{1,0:T(2,128)S(1)} %get-tuple-element.30), channel_id=1, source_target_pairs={{0,4},{1,5},{2,6},{3,7},{4,0},{5,1},{6,2},{7,3},{8,12},{9,13},{10,... | collective-permute-start | bytes 3080 | tf_op jit(solution)/shard_map/ppermute | solution.py:239
  10.9 8.7 %copy-start = (bf16[128,1024]{1,0:T(8,128)(2,1)S(1)}, bf16[128,1024]{1,0:T(8,128)(2,1)}, u32[]{:S(2)}) copy-start(bf16[128,1024]{1,0:T(8,128)(2,1)} %refs_0_.1) | copy-start | bytes 786436
  10.9 8.0 %collective-permute-start.7 = (s32[2,128]{1,0:T(2,128)S(1)}, s32[2,128]{1,0:T(2,128)S(1)}, u32[]{:S(2)}, u32[]{:S(2)}) collective-permute-start(s32[2,128]{1,0:T(2,128)S(1)} %get-tuple-element.29), channel_id=1, source_target_pairs={{0,8},{1,9},{2,10},{3,11},{4,12},{5,13},{6,14},{7,15},{8,0},{9,1},... | collective-permute-start | bytes 3080 | tf_op jit(solution)/shard_map/ppermute | solution.py:239
  11.3 8.3 %collective-permute-start = (bf16[128,1024]{1,0:T(8,128)(2,1)}, bf16[128,1024]{1,0:T(8,128)(2,1)S(1)}, u32[]{:S(2)}, u32[]{:S(2)}) collective-permute-start(bf16[128,1024]{1,0:T(8,128)(2,1)} %refs_0_.1), channel_id=1, source_target_pairs={{0,2},{1,3},{2,0},{3,1},{4,6},{5,7},{6,4},{7,5},{8,10},{9,11},{10,... | collective-permute-start | bytes 786440 | tf_op jit(solution)/shard_map/ppermute | solution.py:239
  16.4 3.2 %collective-permute-start.4 = (bf16[128,1024]{1,0:T(8,128)(2,1)}, bf16[128,1024]{1,0:T(8,128)(2,1)S(1)}, u32[]{:S(2)}, u32[]{:S(2)}) collective-permute-start(bf16[128,1024]{1,0:T(8,128)(2,1)} %refs_0_.1), channel_id=1, source_target_pairs={{0,1},{1,0},{2,3},{3,2},{4,5},{5,4},{6,7},{7,6},{8,9},{9,8},{10,11... | collective-permute-start | bytes 786440 | tf_op jit(solution)/shard_map/ppermute | solution.py:239
  16.4 8.8 %collective-permute-start.12 = (bf16[128,1024]{1,0:T(8,128)(2,1)S(1)}, bf16[128,1024]{1,0:T(8,128)(2,1)S(1)}, u32[]{:S(2)}, u32[]{:S(2)}) collective-permute-start(bf16[128,1024]{1,0:T(8,128)(2,1)S(1)} %collective-permute-done.1.refs_2_), channel_id=1, source_target_pairs={{0,2},{1,3},{2,0},{3,1},{4,6},{5,7},{6,4},{7,5},{8,10},{9,11},{10,... | collective-permute-start | bytes 786440 | tf_op jit(solution)/shard_map/ppermute | solution.py:239
  19.0 1.4 %collective-permute-start.9 = (bf16[64,1024]{1,0:T(8,128)(2,1)S(1)}, bf16[64,1024]{1,0:T(8,128)(2,1)S(1)}, u32[]{:S(2)}, u32[]{:S(2)}) collective-permute-start(bf16[64,1024]{1,0:T(8,128)(2,1)S(1)} %get-tuple-element.27), channel_id=1, source_target_pairs={{0,1},{1,0},{2,3},{3,2},{4,5},{5,4},{6,7},{7,6},{8,9},{9,8},{10,11... | collective-permute-start | bytes 393224 | tf_op jit(solution)/shard_map/ppermute | solution.py:239
  19.1 1.5 %collective-permute-start.8 = (bf16[64,1024]{1,0:T(8,128)(2,1)S(1)}, bf16[64,1024]{1,0:T(8,128)(2,1)S(1)}, u32[]{:S(2)}, u32[]{:S(2)}) collective-permute-start(bf16[64,1024]{1,0:T(8,128)(2,1)S(1)} %get-tuple-element.28), channel_id=1, source_target_pairs={{0,1},{1,0},{2,3},{3,2},{4,5},{5,4},{6,7},{7,6},{8,9},{9,8},{10,11... | collective-permute-start | bytes 393224 | tf_op jit(solution)/shard_map/ppermute | solution.py:239
  21.3 7.3 %collective-permute-start.10 = (f32[8,128]{1,0:T(8,128)S(1)}, f32[8,128]{1,0:T(8,128)S(1)}, u32[]{:S(2)}, u32[]{:S(2)}) collective-permute-start(f32[8,128]{1,0:T(8,128)S(1)} %get-tuple-element.23), channel_id=1, source_target_pairs={{0,2},{1,3},{2,0},{3,1},{4,6},{5,7},{6,4},{7,5},{8,10},{9,11},{10,... | collective-permute-start | bytes 12296 | tf_op jit(solution)/shard_map/ppermute | solution.py:239
  22.9 5.8 %collective-permute-start.11 = (f32[8,128]{1,0:T(8,128)S(1)}, f32[8,128]{1,0:T(8,128)S(1)}, u32[]{:S(2)}, u32[]{:S(2)}) collective-permute-start(f32[8,128]{1,0:T(8,128)S(1)} %get-tuple-element.24), channel_id=1, source_target_pairs={{0,4},{1,5},{2,6},{3,7},{4,0},{5,1},{6,2},{7,3},{8,12},{9,13},{10,... | collective-permute-start | bytes 12296 | tf_op jit(solution)/shard_map/ppermute | solution.py:239
  25.7 4.6 %collective-permute-start.13 = (f32[8,128]{1,0:T(8,128)S(1)}, f32[8,128]{1,0:T(8,128)S(1)}, u32[]{:S(2)}, u32[]{:S(2)}) collective-permute-start(f32[8,128]{1,0:T(8,128)S(1)} %late.1), channel_id=1, source_target_pairs={{0,6},{1,7},{2,4},{3,5},{4,2},{5,3},{6,0},{7,1},{8,14},{9,15},{10,... | collective-permute-start | bytes 12296 | tf_op jit(solution)/shard_map/ppermute | solution.py:239

commit v10 on v9

--- a/solution.py
+++ b/solution.py
@@ -244,13 +244,12 @@
     x_ids, c_ids = swap(SHARD, ids), swap(SUB, ids)
     e = swap(LOW, mine)
     x = swap(SHARD, mine)
-    far, _ = lax.optimization_barrier((mine, c_ids))
-    h = swap(HIGH, far)
+    h = swap(HIGH, mine)
     e_ids = swap(LOW, jnp.concatenate([ids, x_ids]))
     h_ids = swap(HIGH, jnp.concatenate([ids, c_ids]))
-    mine_c, _ = lax.optimization_barrier((mine, e_ids))
+    mine_c = mine
     c = swap(SUB, mine_c)
-    e_then, _ = lax.optimization_barrier((e, e_ids))
+    e_then, _, _ = lax.optimization_barrier((e, e_ids, x))
     h_then, _ = lax.optimization_barrier((h, h_ids))
     xe = swap(SHARD, e_then)
     ch = [swap(SUB, h_then[: rows // 2]), swap(SUB, h_then[rows // 2 :])]

time: 31 us -> 29.6 us (0.955)
  waiting for transfers between devices: 10.4 us -> 9.52 us
  local copies, waits for them, and re-layouts: 1.19 us -> 0.54 us
    ppermute x14, waiting for transfers between devices: 10.4 us -> 9.52 us  [swap(): return lax.ppermute(array, AXES, [(i, i ^ flip) for i in range(16)])]
    unnamed x4, local copies, waits for them, and re-layouts: 0.66 us -> 0.01 us
  transfers between devices with their start and end apart: 14 -> 14, of which waited for: 6 -> 7; matrix products, arithmetic and copies ran while one was open for 0% -> 0% of each run, Pallas kernels for 7% -> 7%
where the time goes in v10:
time: 29.6 us; the launch traced here: 29.4 us
  starting transfers between devices  17.2 us (58%)
  waiting for transfers between devices  9.52 us (32%)
  Pallas kernels  2.1 us (7%)
  local copies, waits for them, and re-layouts  0.54 us (2%)
    ppermute x14, starting transfers between devices, swap(): return lax.ppermute(array, AXES, [(i, i ^ flip) for i in range(16)])  17.2 us
    ppermute x14, waiting for transfers between devices, swap(): return lax.ppermute(array, AXES, [(i, i ^ flip) for i in range(16)])  9.52 us
    pallas_call x1, Pallas kernels, early(): pl.pallas_call(early_kernel, out_shape=[jax.ShapeDtypeStruct((8, 3 * rows...  0.85 us
    pallas_call x1, Pallas kernels, middle(): pl.pallas_call(middle_kernel, out_shape=[jax.ShapeDtypeStruct((8, rows),...  0.69 us
  transfers between devices with their start and end apart: 14, of which 7 were waited for; matrix products, arithmetic and copies ran while one was open for 0% of the time, Pallas kernels for 7%

profile of v10, /device:TPU:0, one launch (start us, length us, event | category | flops | bytes accessed | tf_op | source)
XLA Modules:
  0.0 29.4 jit_solution(2063708363834904184)
XLA Ops:
  0.0 0.0 copy-start.1
  0.0 3.0 %collective-permute-start.1 = (bf16[128,1024]{1,0:T(8,128)(2,1)}, bf16[128,1024]{1,0:T(8,128)(2,1)S(1)}, u32[]{:S(2)}, u32[]{:S(2)}) collective-permute-start(bf16[128,1024]{1,0:T(8,128)(2,1)} %refs_0_.1), channel_id=1, source_target_pairs={{0,4},{1,5},{2,6},{3,7},{4,0},{5,1},{6,2},{7,3},{8,12},{9,13},{10,... | collective-permute-start | bytes 786440 | tf_op jit(solution)/shard_map/ppermute | solution.py:239
  3.0 1.5 %collective-permute-start = (bf16[128,1024]{1,0:T(8,128)(2,1)}, bf16[128,1024]{1,0:T(8,128)(2,1)S(1)}, u32[]{:S(2)}, u32[]{:S(2)}) collective-permute-start(bf16[128,1024]{1,0:T(8,128)(2,1)} %refs_0_.1), channel_id=1, source_target_pairs={{0,2},{1,3},{2,0},{3,1},{4,6},{5,7},{6,4},{7,5},{8,10},{9,11},{10,... | collective-permute-start | bytes 786440 | tf_op jit(solution)/shard_map/ppermute | solution.py:239
  4.5 2.6 %collective-permute-start.6 = (bf16[128,1024]{1,0:T(8,128)(2,1)}, bf16[128,1024]{1,0:T(8,128)(2,1)S(1)}, u32[]{:S(2)}, u32[]{:S(2)}) collective-permute-start(bf16[128,1024]{1,0:T(8,128)(2,1)} %refs_0_.1), channel_id=1, source_target_pairs={{0,8},{1,9},{2,10},{3,11},{4,12},{5,13},{6,14},{7,15},{8,0},{9,1},... | collective-permute-start | bytes 786440 | tf_op jit(solution)/shard_map/ppermute | solution.py:239
  7.1 0.0 copy-done.1
  7.1 0.0 collective-permute-start.4
  7.1 0.5 %collective-permute-start.3 = (s32[1,128]{1,0:T(1,128)S(1)}, s32[1,128]{1,0:T(1,128)S(1)}, u32[]{:S(2)}, u32[]{:S(2)}) collective-permute-start(s32[1,128]{1,0:T(1,128)S(1)} %bitcast.4), channel_id=1, source_target_pairs={{0,2},{1,3},{2,0},{3,1},{4,6},{5,7},{6,4},{7,5},{8,10},{9,11},{10,... | collective-permute-start | bytes 1544 | tf_op jit(solution)/shard_map/ppermute | solution.py:239
  7.6 0.6 %collective-permute-done.4.c_ids_ref = s32[1,128]{1,0:T(1,128)S(1)} collective-permute-done((s32[1,128]{1,0:T(1,128)S(1)}, s32[1,128]{1,0:T(1,128)S(1)}, u32[]{:S(2)}, u32[]{:S(2)}) %collective-permute-start.4) | collective-permute-done | bytes 544 | tf_op jit(solution)/shard_map/ppermute | solution.py:239
  8.2 2.8 %collective-permute-done.3.x_ids_ref = s32[1,128]{1,0:T(1,128)S(1)} collective-permute-done((s32[1,128]{1,0:T(1,128)S(1)}, s32[1,128]{1,0:T(1,128)S(1)}, u32[]{:S(2)}, u32[]{:S(2)}) %collective-permute-start.3) | collective-permute-done | bytes 544 | tf_op jit(solution)/shard_map/ppermute | solution.py:239
  11.1 0.3 %collective-permute-start.5 = (s32[2,128]{1,0:T(2,128)S(1)}, s32[2,128]{1,0:T(2,128)S(1)}, u32[]{:S(2)}, u32[]{:S(2)}) collective-permute-start(s32[2,128]{1,0:T(2,128)S(1)} %get-tuple-element.26), channel_id=1, source_target_pairs={{0,4},{1,5},{2,6},{3,7},{4,0},{5,1},{6,2},{7,3},{8,12},{9,13},{10,... | collective-permute-start | bytes 3080 | tf_op jit(solution)/shard_map/ppermute | solution.py:239
  11.4 0.0 copy-start
  11.4 2.7 %collective-permute-start.7 = (s32[2,128]{1,0:T(2,128)S(1)}, s32[2,128]{1,0:T(2,128)S(1)}, u32[]{:S(2)}, u32[]{:S(2)}) collective-permute-start(s32[2,128]{1,0:T(2,128)S(1)} %get-tuple-element.25), channel_id=1, source_target_pairs={{0,8},{1,9},{2,10},{3,11},{4,12},{5,13},{6,14},{7,15},{8,0},{9,1},... | collective-permute-start | bytes 3080 | tf_op jit(solution)/shard_map/ppermute | solution.py:239
  14.1 0.5 %collective-permute-done.5.e_ids_ref = s32[2,128]{1,0:T(2,128)S(1)} collective-permute-done((s32[2,128]{1,0:T(2,128)S(1)}, s32[2,128]{1,0:T(2,128)S(1)}, u32[]{:S(2)}, u32[]{:S(2)}) %collective-permute-start.5) | collective-permute-done | bytes 1056 | tf_op jit(solution)/shard_map/ppermute | solution.py:239
  14.6 0.0 collective-permute-start.2
  14.7 0.0 collective-permute-done.1.refs_2_
  14.7 0.0 collective-permute-done.refs_1_
  14.7 1.9 %collective-permute-start.12 = (bf16[128,1024]{1,0:T(8,128)(2,1)S(1)}, bf16[128,1024]{1,0:T(8,128)(2,1)S(1)}, u32[]{:S(2)}, u32[]{:S(2)}) collective-permute-start(bf16[128,1024]{1,0:T(8,128)(2,1)S(1)} %collective-permute-done.1.refs_2_), channel_id=1, source_target_pairs={{0,2},{1,3},{2,0},{3,1},{4,6},{5,7},{6,4},{7,5},{8,10},{9,11},{10,... | collective-permute-start | bytes 786440 | tf_op jit(solution)/shard_map/ppermute | solution.py:239
  16.6 2.3 %collective-permute-done.7.h_ids_ref = s32[2,128]{1,0:T(2,128)S(1)} collective-permute-done((s32[2,128]{1,0:T(2,128)S(1)}, s32[2,128]{1,0:T(2,128)S(1)}, u32[]{:S(2)}, u32[]{:S(2)}) %collective-permute-start.7) | collective-permute-done | bytes 1056 | tf_op jit(solution)/shard_map/ppermute | solution.py:239
  18.9 0.0 collective-permute-done.6.h_ref
  18.9 0.1 collective-permute-start.9
  19.0 0.5 %collective-permute-start.8 = (bf16[64,1024]{1,0:T(8,128)(2,1)S(1)}, bf16[64,1024]{1,0:T(8,128)(2,1)S(1)}, u32[]{:S(2)}, u32[]{:S(2)}) collective-permute-start(bf16[64,1024]{1,0:T(8,128)(2,1)S(1)} %get-tuple-element.24), channel_id=1, source_target_pairs={{0,1},{1,0},{2,3},{3,2},{4,5},{5,4},{6,7},{7,6},{8,9},{9,8},{10,11... | collective-permute-start | bytes 393224 | tf_op jit(solution)/shard_map/ppermute | solution.py:239
  19.5 0.0 collective-permute-done.2.refs_3_
  19.5 0.0 copy-done
  19.5 0.9 %early.1 = (f32[8,384]{1,0:T(8,128)S(1)}, bf16[384,1024]{1,0:T(8,128)(2,1)S(1)}, bf16[128,1024]{1,0:T(8,128)(2,1)S(1)}) custom-call(bf16[128,1024]{1,0:T(8,128)(2,1)S(1)} %copy-done, bf16[128,1024]{1,0:T(8,128)(2,1)S(1)} %collective-permute-done.refs_1_, bf16[128,1024]{1,0:T(8,128)(2,1)S(1)} %collective-permute-done.1.refs_2_, ...), custom_call_target="tpu_custom_call" | custom-call | tf_op jit(solution)/shard_map/early/pallas_call | solution.py:175
  20.3 0.0 collective-permute-done.9.ch_back_ref
  20.4 0.1 collective-permute-done.8.ch_front_ref
  20.5 0.7 %middle.1 = (f32[8,128]{1,0:T(8,128)S(1)}, f32[8,128]{1,0:T(8,128)S(1)}, f32[8,128]{1,0:T(8,128)S(1)}, bf16[512,1024]{1,0:T(8,128)(2,1)S(1)}) custom-call(f32[8,384]{1,0:T(8,128)S(1)} %get-tuple-element.14.best_ref, bf16[384,1024]{1,0:T(8,128)(2,1)S(1)} %get-tuple-element.15.own_ref, bf16[128,1024]{1,0:T(8,128)(2,1)S(1)} %get-tuple-element.16.c_ref, ...), custom_call_target="tpu_custom_call" | custom-call | tf_op jit(solution)/shard_map/middle/pallas_call | solution.py:206
  21.2 0.6 %collective-permute-start.10 = (f32[8,128]{1,0:T(8,128)S(1)}, f32[8,128]{1,0:T(8,128)S(1)}, u32[]{:S(2)}, u32[]{:S(2)}) collective-permute-start(f32[8,128]{1,0:T(8,128)S(1)} %get-tuple-element.19), channel_id=1, source_target_pairs={{0,2},{1,3},{2,0},{3,1},{4,6},{5,7},{6,4},{7,5},{8,10},{9,11},{10,... | collective-permute-start | bytes 12296 | tf_op jit(solution)/shard_map/ppermute | solution.py:239
  21.8 0.2 collective-permute-start.11
  22.0 1.5 %collective-permute-done.12.xe_ref = bf16[128,1024]{1,0:T(8,128)(2,1)S(1)} collective-permute-done((bf16[128,1024]{1,0:T(8,128)(2,1)S(1)}, bf16[128,1024]{1,0:T(8,128)(2,1)S(1)}, u32[]{:S(2)}, u32[]{:S(2)}) %collective-permute-start.12) | collective-permute-done | bytes 262176 | tf_op jit(solution)/shard_map/ppermute | solution.py:239
  23.5 0.6 %late.1 = f32[8,128]{1,0:T(8,128)S(1)} custom-call(bf16[512,1024]{1,0:T(8,128)(2,1)S(1)} %get-tuple-element.21.far_ref, bf16[128,1024]{1,0:T(8,128)(2,1)S(1)} %collective-permute-done.12.xe_ref, s32[1,128]{1,0:T(1,128)S(1)} %bitcast.8, s32[1,128]{1,0:T(1,128)S(1)} %collective-permute-done.4.c_ids_ref, s32[2,128]{1,0:T(2,128)S(1)} %collective-permute-done.5.e_ids_ref, ...), custom_call_target="tpu_custom_call" | custom-call | tf_op jit(solution)/shard_map/late/pallas_call | solution.py:227
  24.0 3.3 %collective-permute-start.13 = (f32[8,128]{1,0:T(8,128)S(1)}, f32[8,128]{1,0:T(8,128)S(1)}, u32[]{:S(2)}, u32[]{:S(2)}) collective-permute-start(f32[8,128]{1,0:T(8,128)S(1)} %late.1), channel_id=1, source_target_pairs={{0,6},{1,7},{2,4},{3,5},{4,2},{5,3},{6,0},{7,1},{8,14},{9,15},{10,... | collective-permute-start | bytes 12296 | tf_op jit(solution)/shard_map/ppermute | solution.py:239
  27.3 0.0 collective-permute-done.10
  27.3 0.0 collective-permute-done.11
  27.3 1.6 %collective-permute-done.13 = f32[8,128]{1,0:T(8,128)S(1)} collective-permute-done((f32[8,128]{1,0:T(8,128)S(1)}, f32[8,128]{1,0:T(8,128)S(1)}, u32[]{:S(2)}, u32[]{:S(2)}) %collective-permute-start.13) | collective-permute-done | bytes 4128 | tf_op jit(solution)/shard_map/ppermute | solution.py:239
  28.9 0.5 %slice_bitcast_fusion = f32[128]{0:T(128)} fusion(f32[8,128]{1,0:T(8,128)S(1)} %maximum_maximum_fusion), kind=kLoop, calls=%fused_computation.3 | loop fusion | bytes 1024 | tf_op jit(solution)/shard_map/squeeze | solution.py:260
  (3 shorter events, 0.0 us)
Async XLA Ops:
  0.0 7.1 %copy-start.1 = (s32[128,1]{0,1:T(1,128)S(1)}, s32[128,1]{0,1:T(1,128)}, u32[]{:S(2)}) copy-start(s32[128,1]{0,1:T(1,128)} %param.3) | copy-start | bytes 1540
  0.0 14.7 %collective-permute-start.1 = (bf16[128,1024]{1,0:T(8,128)(2,1)}, bf16[128,1024]{1,0:T(8,128)(2,1)S(1)}, u32[]{:S(2)}, u32[]{:S(2)}) collective-permute-start(bf16[128,1024]{1,0:T(8,128)(2,1)} %refs_0_.1), channel_id=1, source_target_pairs={{0,4},{1,5},{2,6},{3,7},{4,0},{5,1},{6,2},{7,3},{8,12},{9,13},{10,... | collective-permute-start | bytes 786440 | tf_op jit(solution)/shard_map/ppermute | solution.py:239
  3.0 11.6 %collective-permute-start = (bf16[128,1024]{1,0:T(8,128)(2,1)}, bf16[128,1024]{1,0:T(8,128)(2,1)S(1)}, u32[]{:S(2)}, u32[]{:S(2)}) collective-permute-start(bf16[128,1024]{1,0:T(8,128)(2,1)} %refs_0_.1), channel_id=1, source_target_pairs={{0,2},{1,3},{2,0},{3,1},{4,6},{5,7},{6,4},{7,5},{8,10},{9,11},{10,... | collective-permute-start | bytes 786440 | tf_op jit(solution)/shard_map/ppermute | solution.py:239
  4.5 14.4 %collective-permute-start.6 = (bf16[128,1024]{1,0:T(8,128)(2,1)}, bf16[128,1024]{1,0:T(8,128)(2,1)S(1)}, u32[]{:S(2)}, u32[]{:S(2)}) collective-permute-start(bf16[128,1024]{1,0:T(8,128)(2,1)} %refs_0_.1), channel_id=1, source_target_pairs={{0,8},{1,9},{2,10},{3,11},{4,12},{5,13},{6,14},{7,15},{8,0},{9,1},... | collective-permute-start | bytes 786440 | tf_op jit(solution)/shard_map/ppermute | solution.py:239
  7.1 1.1 %collective-permute-start.4 = (s32[1,128]{1,0:T(1,128)S(1)}, s32[1,128]{1,0:T(1,128)S(1)}, u32[]{:S(2)}, u32[]{:S(2)}) collective-permute-start(s32[1,128]{1,0:T(1,128)S(1)} %bitcast.3), channel_id=1, source_target_pairs={{0,1},{1,0},{2,3},{3,2},{4,5},{5,4},{6,7},{7,6},{8,9},{9,8},{10,11... | collective-permute-start | bytes 1544 | tf_op jit(solution)/shard_map/ppermute | solution.py:239
  7.1 4.0 %collective-permute-start.3 = (s32[1,128]{1,0:T(1,128)S(1)}, s32[1,128]{1,0:T(1,128)S(1)}, u32[]{:S(2)}, u32[]{:S(2)}) collective-permute-start(s32[1,128]{1,0:T(1,128)S(1)} %bitcast.4), channel_id=1, source_target_pairs={{0,2},{1,3},{2,0},{3,1},{4,6},{5,7},{6,4},{7,5},{8,10},{9,11},{10,... | collective-permute-start | bytes 1544 | tf_op jit(solution)/shard_map/ppermute | solution.py:239
  11.1 3.6 %collective-permute-start.5 = (s32[2,128]{1,0:T(2,128)S(1)}, s32[2,128]{1,0:T(2,128)S(1)}, u32[]{:S(2)}, u32[]{:S(2)}) collective-permute-start(s32[2,128]{1,0:T(2,128)S(1)} %get-tuple-element.26), channel_id=1, source_target_pairs={{0,4},{1,5},{2,6},{3,7},{4,0},{5,1},{6,2},{7,3},{8,12},{9,13},{10,... | collective-permute-start | bytes 3080 | tf_op jit(solution)/shard_map/ppermute | solution.py:239
  11.4 8.1 %copy-start = (bf16[128,1024]{1,0:T(8,128)(2,1)S(1)}, bf16[128,1024]{1,0:T(8,128)(2,1)}, u32[]{:S(2)}) copy-start(bf16[128,1024]{1,0:T(8,128)(2,1)} %refs_0_.1) | copy-start | bytes 786436
  11.4 7.4 %collective-permute-start.7 = (s32[2,128]{1,0:T(2,128)S(1)}, s32[2,128]{1,0:T(2,128)S(1)}, u32[]{:S(2)}, u32[]{:S(2)}) collective-permute-start(s32[2,128]{1,0:T(2,128)S(1)} %get-tuple-element.25), channel_id=1, source_target_pairs={{0,8},{1,9},{2,10},{3,11},{4,12},{5,13},{6,14},{7,15},{8,0},{9,1},... | collective-permute-start | bytes 3080 | tf_op jit(solution)/shard_map/ppermute | solution.py:239
  14.6 4.8 %collective-permute-start.2 = (bf16[128,1024]{1,0:T(8,128)(2,1)}, bf16[128,1024]{1,0:T(8,128)(2,1)S(1)}, u32[]{:S(2)}, u32[]{:S(2)}) collective-permute-start(bf16[128,1024]{1,0:T(8,128)(2,1)} %refs_0_.1), channel_id=1, source_target_pairs={{0,1},{1,0},{2,3},{3,2},{4,5},{5,4},{6,7},{7,6},{8,9},{9,8},{10,11... | collective-permute-start | bytes 786440 | tf_op jit(solution)/shard_map/ppermute | solution.py:239
  14.7 8.8 %collective-permute-start.12 = (bf16[128,1024]{1,0:T(8,128)(2,1)S(1)}, bf16[128,1024]{1,0:T(8,128)(2,1)S(1)}, u32[]{:S(2)}, u32[]{:S(2)}) collective-permute-start(bf16[128,1024]{1,0:T(8,128)(2,1)S(1)} %collective-permute-done.1.refs_2_), channel_id=1, source_target_pairs={{0,2},{1,3},{2,0},{3,1},{4,6},{5,7},{6,4},{7,5},{8,10},{9,11},{10,... | collective-permute-start | bytes 786440 | tf_op jit(solution)/shard_map/ppermute | solution.py:239
  18.9 1.4 %collective-permute-start.9 = (bf16[64,1024]{1,0:T(8,128)(2,1)S(1)}, bf16[64,1024]{1,0:T(8,128)(2,1)S(1)}, u32[]{:S(2)}, u32[]{:S(2)}) collective-permute-start(bf16[64,1024]{1,0:T(8,128)(2,1)S(1)} %get-tuple-element.23), channel_id=1, source_target_pairs={{0,1},{1,0},{2,3},{3,2},{4,5},{5,4},{6,7},{7,6},{8,9},{9,8},{10,11... | collective-permute-start | bytes 393224 | tf_op jit(solution)/shard_map/ppermute | solution.py:239
  19.0 1.5 %collective-permute-start.8 = (bf16[64,1024]{1,0:T(8,128)(2,1)S(1)}, bf16[64,1024]{1,0:T(8,128)(2,1)S(1)}, u32[]{:S(2)}, u32[]{:S(2)}) collective-permute-start(bf16[64,1024]{1,0:T(8,128)(2,1)S(1)} %get-tuple-element.24), channel_id=1, source_target_pairs={{0,1},{1,0},{2,3},{3,2},{4,5},{5,4},{6,7},{7,6},{8,9},{9,8},{10,11... | collective-permute-start | bytes 393224 | tf_op jit(solution)/shard_map/ppermute | solution.py:239
  21.2 6.1 %collective-permute-start.10 = (f32[8,128]{1,0:T(8,128)S(1)}, f32[8,128]{1,0:T(8,128)S(1)}, u32[]{:S(2)}, u32[]{:S(2)}) collective-permute-start(f32[8,128]{1,0:T(8,128)S(1)} %get-tuple-element.19), channel_id=1, source_target_pairs={{0,2},{1,3},{2,0},{3,1},{4,6},{5,7},{6,4},{7,5},{8,10},{9,11},{10,... | collective-permute-start | bytes 12296 | tf_op jit(solution)/shard_map/ppermute | solution.py:239
  21.8 5.5 %collective-permute-start.11 = (f32[8,128]{1,0:T(8,128)S(1)}, f32[8,128]{1,0:T(8,128)S(1)}, u32[]{:S(2)}, u32[]{:S(2)}) collective-permute-start(f32[8,128]{1,0:T(8,128)S(1)} %get-tuple-element.20), channel_id=1, source_target_pairs={{0,4},{1,5},{2,6},{3,7},{4,0},{5,1},{6,2},{7,3},{8,12},{9,13},{10,... | collective-permute-start | bytes 12296 | tf_op jit(solution)/shard_map/ppermute | solution.py:239
  24.0 4.9 %collective-permute-start.13 = (f32[8,128]{1,0:T(8,128)S(1)}, f32[8,128]{1,0:T(8,128)S(1)}, u32[]{:S(2)}, u32[]{:S(2)}) collective-permute-start(f32[8,128]{1,0:T(8,128)S(1)} %late.1), channel_id=1, source_target_pairs={{0,6},{1,7},{2,4},{3,5},{4,2},{5,3},{6,0},{7,1},{8,14},{9,15},{10,... | collective-permute-start | bytes 12296 | tf_op jit(solution)/shard_map/ppermute | solution.py:239

commit v11 on v9

--- a/solution.py
+++ b/solution.py
@@ -160,9 +160,13 @@
     return best
 
 
-def early_kernel(refs, ids_ref, x_ids_ref, c_ids_ref, e_ids_ref, best_ref, own_ref, c_ref):
-    mine, x, e, c = [unit_of(ref[...]) for ref in refs]
-    own = jnp.concatenate([mine, x, e], axis=0)
+def block(refs):
+    return jnp.concatenate([unit_of(ref[...]) for ref in refs], axis=0)
+
+
+def early_kernel(mine_ref, x_refs, e_refs, c_refs, ids_ref, x_ids_ref, c_ids_ref, e_ids_ref, best_ref, own_ref, c_ref):
+    mine, c = unit_of(mine_ref[...]), block(c_refs)
+    own = jnp.concatenate([mine, block(x_refs), block(e_refs)], axis=0)
     own_ids = jnp.concatenate([ids_ref[...], x_ids_ref[...], e_ids_ref[:1, :]], axis=1)
     best = best_of(own, own_ids, [mine, c], [ids_ref[...], c_ids_ref[...]], True)
     best_ref[...] = jnp.broadcast_to(best, best_ref.shape)
@@ -170,8 +174,8 @@
     c_ref[...] = c
 
 
-def early(blocks, ids):
-    rows, width = blocks[0].shape
+def early(mine, x, e, c, ids):
+    rows, width = mine.shape
     return pl.pallas_call(
         early_kernel,
         out_shape=[
@@ -179,19 +183,18 @@
             jax.ShapeDtypeStruct((3 * rows, width), jnp.bfloat16),
             jax.ShapeDtypeStruct((rows, width), jnp.bfloat16),
         ],
-        in_specs=([VMEM] * len(blocks), *[VMEM] * len(ids)),
+        in_specs=(VMEM, [VMEM] * len(x), [VMEM] * len(e), [VMEM] * len(c), *[VMEM] * len(ids)),
         out_specs=[VMEM] * 3,
         compiler_params=LIMIT,
         name="early",
-    )(blocks, *ids)
+    )(mine, x, e, c, *ids)
 
 
 def middle_kernel(
-    best_ref, own_ref, c_ref, h_ref, ch_front_ref, ch_back_ref, ids_ref, x_ids_ref, c_ids_ref, e_ids_ref, h_ids_ref,
+    best_ref, own_ref, c_ref, h_refs, ch_refs, ids_ref, x_ids_ref, c_ids_ref, e_ids_ref, h_ids_ref,
     mine_out_ref, x_out_ref, e_out_ref, far_ref,
 ):
-    h = unit_of(h_ref[...])
-    ch = jnp.concatenate([unit_of(ch_front_ref[...]), unit_of(ch_back_ref[...])], axis=0)
+    h, ch = block(h_refs), block(ch_refs)
     own_ids = jnp.concatenate([ids_ref[...], x_ids_ref[...], e_ids_ref[:1, :]], axis=1)
     best = best_of(own_ref[...], own_ids, [h, ch], [h_ids_ref[:1, :], h_ids_ref[1:, :]])
     best = jnp.maximum(best, best_ref[:1, :])
@@ -207,15 +210,15 @@
         middle_kernel,
         out_shape=[jax.ShapeDtypeStruct((8, rows), jnp.float32)] * 3
         + [jax.ShapeDtypeStruct((4 * rows, width), jnp.bfloat16)],
-        in_specs=[VMEM] * 11,
+        in_specs=(VMEM, VMEM, VMEM, [VMEM] * len(h), [VMEM] * len(ch), *[VMEM] * len(ids)),
         out_specs=[VMEM] * 4,
         compiler_params=LIMIT,
         name="middle",
-    )(best, own, c, h, *ch, *ids)
-
-
-def late_kernel(far_ref, xe_ref, ids_ref, c_ids_ref, e_ids_ref, h_ids_ref, out_ref):
-    xe = unit_of(xe_ref[...])
+    )(best, own, c, h, ch, *ids)
+
+
+def late_kernel(far_ref, xe_refs, ids_ref, c_ids_ref, e_ids_ref, h_ids_ref, out_ref):
+    xe = block(xe_refs)
     rows = xe.shape[0]
     others = [far_ref[place * rows : (place + 1) * rows] for place in range(4)]
     other_ids = [ids_ref[...], c_ids_ref[...], h_ids_ref[:1, :], h_ids_ref[1:, :]]
@@ -223,11 +226,10 @@
 
 
 def late(far, xe, ids):
-    rows = xe.shape[0]
     return pl.pallas_call(
         late_kernel,
-        out_shape=jax.ShapeDtypeStruct((8, rows), jnp.float32),
-        in_specs=[VMEM] * 6,
+        out_shape=jax.ShapeDtypeStruct((8, far.shape[0] // 4), jnp.float32),
+        in_specs=(VMEM, [VMEM] * len(xe), *[VMEM] * len(ids)),
         out_specs=VMEM,
         compiler_params=LIMIT,
         name="late",
@@ -240,25 +242,25 @@
 
     rows = embeddings.shape[0]
     mine, ids = embeddings, assignment.reshape(1, rows)
-    x_ids, c_ids = swap(SHARD, ids), swap(SUB, ids)
-    x_ids, c_ids = swap(SHARD, ids), swap(SUB, ids)
+    c = swap(SUB, mine)
     e = swap(LOW, mine)
     x = swap(SHARD, mine)
-    far, _ = lax.optimization_barrier((mine, c_ids))
+    far, _ = lax.optimization_barrier((mine, c))
     h = swap(HIGH, far)
+    x_ids, c_ids = swap(SHARD, ids), swap(SUB, ids)
     e_ids = swap(LOW, jnp.concatenate([ids, x_ids]))
     h_ids = swap(HIGH, jnp.concatenate([ids, c_ids]))
-    mine_c, _ = lax.optimization_barrier((mine, e_ids))
-    c = swap(SUB, mine_c)
-    e_then, _ = lax.optimization_barrier((e, e_ids))
+    e_then, _, _ = lax.optimization_barrier((e, x, e_ids))
+    xe = [swap(SHARD, e_then[:rows * 3 // 4]), swap(LOW, x[rows * 3 // 4:])]
     h_then, _ = lax.optimization_barrier((h, h_ids))
-    xe = swap(SHARD, e_then)
     ch = [swap(SUB, h_then[: rows // 2]), swap(SUB, h_then[rows // 2 :])]
-    best, own, c = early([mine, x, e, c], [ids, x_ids, c_ids, e_ids])
+    x, e, h, c = [x], [e], [h], [c]
+    best, own, c = early(mine, x, e, c, [ids, x_ids, c_ids, e_ids])
     found, x_best, e_best, far = middle(best, own, c, h, ch, [ids, x_ids, c_ids, e_ids, h_ids])
-    x_best, e_best = swap(SHARD, x_best), swap(LOW, e_best)
-    xe_best = swap(LOW | SHARD, late(far, xe, [ids, c_ids, e_ids, h_ids]))
-    return jnp.maximum(jnp.maximum(found, x_best), jnp.maximum(e_best, xe_best))[0]
+    xe_best = late(far, xe, [ids, c_ids, e_ids, h_ids])
+    x_best, e_best, xe_best = lax.optimization_barrier((x_best, e_best, xe_best))
+    xe_best, e_best, x_best = swap(LOW | SHARD, xe_best), swap(LOW, e_best), swap(SHARD, x_best)
+    return jnp.maximum(jnp.maximum(jnp.maximum(xe_best, e_best), x_best), found)[0]
 
 
 def shared_owner(embeddings, assignment):

time: 31 us -> 31.3 us (level)
  waiting for transfers between devices: 10.4 us -> 11.7 us
  local copies, waits for them, and re-layouts: 1.19 us -> 0.56 us
    ppermute x14 -> x15, waiting for transfers between devices: 10.4 us -> 11.7 us  [swap(): return lax.ppermute(array, AXES, [(i, i ^ flip) for i in range(16)])]
    unnamed x4, local copies, waits for them, and re-layouts: 0.66 us -> 0.01 us
    ppermute x14 -> x15, starting transfers between devices: 17.1 us -> 16.8 us  [swap(): return lax.ppermute(array, AXES, [(i, i ^ flip) for i in range(16)])]
  transfers between devices with their start and end apart: 14 -> 15, of which waited for: 6 -> 8; matrix products, arithmetic and copies ran while one was open for 0% -> 0% of each run, Pallas kernels for 7% -> 5%
where the time goes in v11:
time: 31.3 us; the launch traced here: 31.2 us
  starting transfers between devices  16.8 us (54%)
  waiting for transfers between devices  11.7 us (37%)
  Pallas kernels  2.1 us (7%)
  local copies, waits for them, and re-layouts  0.56 us (2%)
    ppermute x15, starting transfers between devices, swap(): return lax.ppermute(array, AXES, [(i, i ^ flip) for i in range(16)])  16.8 us
    ppermute x15, waiting for transfers between devices, swap(): return lax.ppermute(array, AXES, [(i, i ^ flip) for i in range(16)])  11.7 us
    pallas_call x1, Pallas kernels, early(): pl.pallas_call(early_kernel, out_shape=[jax.ShapeDtypeStruct((8, 3 * rows...  0.85 us
    pallas_call x1, Pallas kernels, middle(): pl.pallas_call(middle_kernel, out_shape=[jax.ShapeDtypeStruct((8, rows),...  0.68 us
  transfers between devices with their start and end apart: 15, of which 8 were waited for; matrix products, arithmetic and copies ran while one was open for 0% of the time, Pallas kernels for 5%

profile of v11, /device:TPU:0, one launch (start us, length us, event | category | flops | bytes accessed | tf_op | source)
XLA Modules:
  0.0 31.2 jit_solution(2259059746111806365)
XLA Ops:
  0.0 0.0 copy-start.1
  0.0 0.5 %collective-permute-start.2 = (bf16[128,1024]{1,0:T(8,128)(2,1)}, bf16[128,1024]{1,0:T(8,128)(2,1)S(1)}, u32[]{:S(2)}, u32[]{:S(2)}) collective-permute-start(bf16[128,1024]{1,0:T(8,128)(2,1)} %mine_ref.1), channel_id=1, source_target_pairs={{0,1},{1,0},{2,3},{3,2},{4,5},{5,4},{6,7},{7,6},{8,9},{9,8},{10,11... | collective-permute-start | bytes 786440 | tf_op jit(solution)/shard_map/ppermute | solution.py:241
  0.5 2.6 %collective-permute-start.1 = (bf16[128,1024]{1,0:T(8,128)(2,1)}, bf16[128,1024]{1,0:T(8,128)(2,1)S(1)}, u32[]{:S(2)}, u32[]{:S(2)}) collective-permute-start(bf16[128,1024]{1,0:T(8,128)(2,1)} %mine_ref.1), channel_id=1, source_target_pairs={{0,4},{1,5},{2,6},{3,7},{4,0},{5,1},{6,2},{7,3},{8,12},{9,13},{10,... | collective-permute-start | bytes 786440 | tf_op jit(solution)/shard_map/ppermute | solution.py:241
  3.1 1.5 %collective-permute-start = (bf16[128,1024]{1,0:T(8,128)(2,1)}, bf16[128,1024]{1,0:T(8,128)(2,1)S(1)}, u32[]{:S(2)}, u32[]{:S(2)}) collective-permute-start(bf16[128,1024]{1,0:T(8,128)(2,1)} %mine_ref.1), channel_id=1, source_target_pairs={{0,2},{1,3},{2,0},{3,1},{4,6},{5,7},{6,4},{7,5},{8,10},{9,11},{10,... | collective-permute-start | bytes 786440 | tf_op jit(solution)/shard_map/ppermute | solution.py:241
  4.6 0.0 collective-permute-done.2.c_refs_0_
  4.6 2.6 %collective-permute-start.6 = (bf16[128,1024]{1,0:T(8,128)(2,1)}, bf16[128,1024]{1,0:T(8,128)(2,1)S(1)}, u32[]{:S(2)}, u32[]{:S(2)}) collective-permute-start(bf16[128,1024]{1,0:T(8,128)(2,1)} %mine_ref.1), channel_id=1, source_target_pairs={{0,8},{1,9},{2,10},{3,11},{4,12},{5,13},{6,14},{7,15},{8,0},{9,1},... | collective-permute-start | bytes 786440 | tf_op jit(solution)/shard_map/ppermute | solution.py:241
  7.2 0.0 copy-done.1
  7.2 0.0 collective-permute-start.4
  7.2 0.5 %collective-permute-start.3 = (s32[1,128]{1,0:T(1,128)S(1)}, s32[1,128]{1,0:T(1,128)S(1)}, u32[]{:S(2)}, u32[]{:S(2)}) collective-permute-start(s32[1,128]{1,0:T(1,128)S(1)} %bitcast.4), channel_id=1, source_target_pairs={{0,2},{1,3},{2,0},{3,1},{4,6},{5,7},{6,4},{7,5},{8,10},{9,11},{10,... | collective-permute-start | bytes 1544 | tf_op jit(solution)/shard_map/ppermute | solution.py:241
  7.7 0.6 %collective-permute-done.4.c_ids_ref = s32[1,128]{1,0:T(1,128)S(1)} collective-permute-done((s32[1,128]{1,0:T(1,128)S(1)}, s32[1,128]{1,0:T(1,128)S(1)}, u32[]{:S(2)}, u32[]{:S(2)}) %collective-permute-start.4) | collective-permute-done | bytes 544 | tf_op jit(solution)/shard_map/ppermute | solution.py:241
  8.3 3.4 %collective-permute-done.3.x_ids_ref = s32[1,128]{1,0:T(1,128)S(1)} collective-permute-done((s32[1,128]{1,0:T(1,128)S(1)}, s32[1,128]{1,0:T(1,128)S(1)}, u32[]{:S(2)}, u32[]{:S(2)}) %collective-permute-start.3) | collective-permute-done | bytes 544 | tf_op jit(solution)/shard_map/ppermute | solution.py:241
  11.8 0.3 collective-permute-start.5
  12.0 2.8 %collective-permute-start.7 = (s32[2,128]{1,0:T(2,128)S(1)}, s32[2,128]{1,0:T(2,128)S(1)}, u32[]{:S(2)}, u32[]{:S(2)}) collective-permute-start(s32[2,128]{1,0:T(2,128)S(1)} %get-tuple-element.33), channel_id=1, source_target_pairs={{0,8},{1,9},{2,10},{3,11},{4,12},{5,13},{6,14},{7,15},{8,0},{9,1},... | collective-permute-start | bytes 3080 | tf_op jit(solution)/shard_map/ppermute | solution.py:241
  14.8 0.5 %collective-permute-done.5.e_ids_ref = s32[2,128]{1,0:T(2,128)S(1)} collective-permute-done((s32[2,128]{1,0:T(2,128)S(1)}, s32[2,128]{1,0:T(2,128)S(1)}, u32[]{:S(2)}, u32[]{:S(2)}) %collective-permute-start.5) | collective-permute-done | bytes 1056 | tf_op jit(solution)/shard_map/ppermute | solution.py:241
  15.3 0.0 collective-permute-done.1.e_refs_0_
  15.3 0.0 collective-permute-done.x_refs_0_
  15.3 0.0 copy-start
  15.4 1.9 %collective-permute-start.10 = (bf16[96,1024]{1,0:T(8,128)(2,1)S(1)}, bf16[96,1024]{1,0:T(8,128)(2,1)S(1)}, u32[]{:S(2)}, u32[]{:S(2)}) collective-permute-start(bf16[96,1024]{1,0:T(8,128)(2,1)S(1)} %slice.17), channel_id=1, source_target_pairs={{0,2},{1,3},{2,0},{3,1},{4,6},{5,7},{6,4},{7,5},{8,10},{9,11},{10,... | collective-permute-start | bytes 589832 | tf_op jit(solution)/shard_map/ppermute | solution.py:241
  17.3 2.3 %collective-permute-done.7.h_ids_ref = s32[2,128]{1,0:T(2,128)S(1)} collective-permute-done((s32[2,128]{1,0:T(2,128)S(1)}, s32[2,128]{1,0:T(2,128)S(1)}, u32[]{:S(2)}, u32[]{:S(2)}) %collective-permute-start.7) | collective-permute-done | bytes 1056 | tf_op jit(solution)/shard_map/ppermute | solution.py:241
  19.6 0.0 collective-permute-done.6.h_refs_0_
  19.6 0.1 collective-permute-start.9
  19.7 0.5 %collective-permute-start.8 = (bf16[64,1024]{1,0:T(8,128)(2,1)S(1)}, bf16[64,1024]{1,0:T(8,128)(2,1)S(1)}, u32[]{:S(2)}, u32[]{:S(2)}) collective-permute-start(bf16[64,1024]{1,0:T(8,128)(2,1)S(1)} %get-tuple-element.32), channel_id=1, source_target_pairs={{0,1},{1,0},{2,3},{3,2},{4,5},{5,4},{6,7},{7,6},{8,9},{9,8},{10,11... | collective-permute-start | bytes 393224 | tf_op jit(solution)/shard_map/ppermute | solution.py:241
  20.2 0.0 collective-permute-start.11
  20.2 0.0 copy-done
  20.2 0.9 %early.1 = (f32[8,384]{1,0:T(8,128)S(1)}, bf16[384,1024]{1,0:T(8,128)(2,1)S(1)}, bf16[128,1024]{1,0:T(8,128)(2,1)S(1)}) custom-call(bf16[128,1024]{1,0:T(8,128)(2,1)S(1)} %copy-done, bf16[128,1024]{1,0:T(8,128)(2,1)S(1)} %collective-permute-done.x_refs_0_, bf16[128,1024]{1,0:T(8,128)(2,1)S(1)} %collective-permute-done.1.e_refs_0_, ...), custom_call_target="tpu_custom_call" | custom-call | tf_op jit(solution)/shard_map/early/pallas_call | solution.py:179
  21.0 0.0 collective-permute-done.9.ch_refs_1_
  21.0 0.1 collective-permute-done.8.ch_refs_0_
  21.2 0.7 %middle.1 = (f32[8,128]{1,0:T(8,128)S(1)}, f32[8,128]{1,0:T(8,128)S(1)}, f32[8,128]{1,0:T(8,128)S(1)}, bf16[512,1024]{1,0:T(8,128)(2,1)S(1)}) custom-call(f32[8,384]{1,0:T(8,128)S(1)} %get-tuple-element.18.best_ref, bf16[384,1024]{1,0:T(8,128)(2,1)S(1)} %get-tuple-element.19.own_ref, bf16[128,1024]{1,0:T(8,128)(2,1)S(1)} %get-tuple-element.20.c_ref, ...), custom_call_target="tpu_custom_call" | custom-call | tf_op jit(solution)/shard_map/middle/pallas_call | solution.py:209
  21.9 2.6 %collective-permute-done.11.xe_refs_1_ = bf16[32,1024]{1,0:T(8,128)(2,1)S(1)} collective-permute-done((bf16[32,1024]{1,0:T(8,128)(2,1)S(1)}, bf16[32,1024]{1,0:T(8,128)(2,1)S(1)}, u32[]{:S(2)}, u32[]{:S(2)}) %collective-permute-start.11) | collective-permute-done | bytes 65568 | tf_op jit(solution)/shard_map/ppermute | solution.py:241
  24.4 0.0 collective-permute-done.10.xe_refs_0_
  24.4 0.6 %late.1 = f32[8,128]{1,0:T(8,128)S(1)} custom-call(bf16[512,1024]{1,0:T(8,128)(2,1)S(1)} %get-tuple-element.25.far_ref, bf16[96,1024]{1,0:T(8,128)(2,1)S(1)} %collective-permute-done.10.xe_refs_0_, bf16[32,1024]{1,0:T(8,128)(2,1)S(1)} %collective-permute-done.11.xe_refs_1_, s32[1,128]{1,0:T(1,128)S(1)} %bitcast.8, ...), custom_call_target="tpu_custom_call" | custom-call | tf_op jit(solution)/shard_map/late/pallas_call | solution.py:229
  25.0 0.8 %collective-permute-start.12 = (f32[8,128]{1,0:T(8,128)S(1)}, f32[8,128]{1,0:T(8,128)S(1)}, u32[]{:S(2)}, u32[]{:S(2)}) collective-permute-start(f32[8,128]{1,0:T(8,128)S(1)} %late.1), channel_id=1, source_target_pairs={{0,6},{1,7},{2,4},{3,5},{4,2},{5,3},{6,0},{7,1},{8,14},{9,15},{10,... | collective-permute-start | bytes 12296 | tf_op jit(solution)/shard_map/ppermute | solution.py:241
  25.8 1.3 %collective-permute-start.13 = (f32[8,128]{1,0:T(8,128)S(1)}, f32[8,128]{1,0:T(8,128)S(1)}, u32[]{:S(2)}, u32[]{:S(2)}) collective-permute-start(f32[8,128]{1,0:T(8,128)S(1)} %get-tuple-element.28), channel_id=1, source_target_pairs={{0,4},{1,5},{2,6},{3,7},{4,0},{5,1},{6,2},{7,3},{8,12},{9,13},{10,... | collective-permute-start | bytes 12296 | tf_op jit(solution)/shard_map/ppermute | solution.py:241
  27.1 1.5 %collective-permute-start.14 = (f32[8,128]{1,0:T(8,128)S(1)}, f32[8,128]{1,0:T(8,128)S(1)}, u32[]{:S(2)}, u32[]{:S(2)}) collective-permute-start(f32[8,128]{1,0:T(8,128)S(1)} %get-tuple-element.29), channel_id=1, source_target_pairs={{0,2},{1,3},{2,0},{3,1},{4,6},{5,7},{6,4},{7,5},{8,10},{9,11},{10,... | collective-permute-start | bytes 12296 | tf_op jit(solution)/shard_map/ppermute | solution.py:241
  28.5 1.0 %collective-permute-done.12 = f32[8,128]{1,0:T(8,128)S(1)} collective-permute-done((f32[8,128]{1,0:T(8,128)S(1)}, f32[8,128]{1,0:T(8,128)S(1)}, u32[]{:S(2)}, u32[]{:S(2)}) %collective-permute-start.12) | collective-permute-done | bytes 4128 | tf_op jit(solution)/shard_map/ppermute | solution.py:241
  29.6 0.0 collective-permute-done.13
  29.6 1.1 %collective-permute-done.14 = f32[8,128]{1,0:T(8,128)S(1)} collective-permute-done((f32[8,128]{1,0:T(8,128)S(1)}, f32[8,128]{1,0:T(8,128)S(1)}, u32[]{:S(2)}, u32[]{:S(2)}) %collective-permute-start.14) | collective-permute-done | bytes 4128 | tf_op jit(solution)/shard_map/ppermute | solution.py:241
  30.7 0.5 %slice_bitcast_fusion = f32[128]{0:T(128)} fusion(f32[8,128]{1,0:T(8,128)S(1)} %maximum_maximum_fusion), kind=kLoop, calls=%fused_computation.3 | loop fusion | bytes 1024 | tf_op jit(solution)/shard_map/squeeze | solution.py:263
  (5 shorter events, 0.1 us)
Async XLA Ops:
  0.0 7.2 %copy-start.1 = (s32[128,1]{0,1:T(1,128)S(1)}, s32[128,1]{0,1:T(1,128)}, u32[]{:S(2)}) copy-start(s32[128,1]{0,1:T(1,128)} %param.3) | copy-start | bytes 1540
  0.0 4.6 %collective-permute-start.2 = (bf16[128,1024]{1,0:T(8,128)(2,1)}, bf16[128,1024]{1,0:T(8,128)(2,1)S(1)}, u32[]{:S(2)}, u32[]{:S(2)}) collective-permute-start(bf16[128,1024]{1,0:T(8,128)(2,1)} %mine_ref.1), channel_id=1, source_target_pairs={{0,1},{1,0},{2,3},{3,2},{4,5},{5,4},{6,7},{7,6},{8,9},{9,8},{10,11... | collective-permute-start | bytes 786440 | tf_op jit(solution)/shard_map/ppermute | solution.py:241
  0.5 14.9 %collective-permute-start.1 = (bf16[128,1024]{1,0:T(8,128)(2,1)}, bf16[128,1024]{1,0:T(8,128)(2,1)S(1)}, u32[]{:S(2)}, u32[]{:S(2)}) collective-permute-start(bf16[128,1024]{1,0:T(8,128)(2,1)} %mine_ref.1), channel_id=1, source_target_pairs={{0,4},{1,5},{2,6},{3,7},{4,0},{5,1},{6,2},{7,3},{8,12},{9,13},{10,... | collective-permute-start | bytes 786440 | tf_op jit(solution)/shard_map/ppermute | solution.py:241
  3.1 12.2 %collective-permute-start = (bf16[128,1024]{1,0:T(8,128)(2,1)}, bf16[128,1024]{1,0:T(8,128)(2,1)S(1)}, u32[]{:S(2)}, u32[]{:S(2)}) collective-permute-start(bf16[128,1024]{1,0:T(8,128)(2,1)} %mine_ref.1), channel_id=1, source_target_pairs={{0,2},{1,3},{2,0},{3,1},{4,6},{5,7},{6,4},{7,5},{8,10},{9,11},{10,... | collective-permute-start | bytes 786440 | tf_op jit(solution)/shard_map/ppermute | solution.py:241
  4.6 15.0 %collective-permute-start.6 = (bf16[128,1024]{1,0:T(8,128)(2,1)}, bf16[128,1024]{1,0:T(8,128)(2,1)S(1)}, u32[]{:S(2)}, u32[]{:S(2)}) collective-permute-start(bf16[128,1024]{1,0:T(8,128)(2,1)} %mine_ref.1), channel_id=1, source_target_pairs={{0,8},{1,9},{2,10},{3,11},{4,12},{5,13},{6,14},{7,15},{8,0},{9,1},... | collective-permute-start | bytes 786440 | tf_op jit(solution)/shard_map/ppermute | solution.py:241
  7.2 1.1 %collective-permute-start.4 = (s32[1,128]{1,0:T(1,128)S(1)}, s32[1,128]{1,0:T(1,128)S(1)}, u32[]{:S(2)}, u32[]{:S(2)}) collective-permute-start(s32[1,128]{1,0:T(1,128)S(1)} %bitcast.3), channel_id=1, source_target_pairs={{0,1},{1,0},{2,3},{3,2},{4,5},{5,4},{6,7},{7,6},{8,9},{9,8},{10,11... | collective-permute-start | bytes 1544 | tf_op jit(solution)/shard_map/ppermute | solution.py:241
  7.2 4.6 %collective-permute-start.3 = (s32[1,128]{1,0:T(1,128)S(1)}, s32[1,128]{1,0:T(1,128)S(1)}, u32[]{:S(2)}, u32[]{:S(2)}) collective-permute-start(s32[1,128]{1,0:T(1,128)S(1)} %bitcast.4), channel_id=1, source_target_pairs={{0,2},{1,3},{2,0},{3,1},{4,6},{5,7},{6,4},{7,5},{8,10},{9,11},{10,... | collective-permute-start | bytes 1544 | tf_op jit(solution)/shard_map/ppermute | solution.py:241
  11.8 3.6 %collective-permute-start.5 = (s32[2,128]{1,0:T(2,128)S(1)}, s32[2,128]{1,0:T(2,128)S(1)}, u32[]{:S(2)}, u32[]{:S(2)}) collective-permute-start(s32[2,128]{1,0:T(2,128)S(1)} %get-tuple-element.34), channel_id=1, source_target_pairs={{0,4},{1,5},{2,6},{3,7},{4,0},{5,1},{6,2},{7,3},{8,12},{9,13},{10,... | collective-permute-start | bytes 3080 | tf_op jit(solution)/shard_map/ppermute | solution.py:241
  12.0 7.5 %collective-permute-start.7 = (s32[2,128]{1,0:T(2,128)S(1)}, s32[2,128]{1,0:T(2,128)S(1)}, u32[]{:S(2)}, u32[]{:S(2)}) collective-permute-start(s32[2,128]{1,0:T(2,128)S(1)} %get-tuple-element.33), channel_id=1, source_target_pairs={{0,8},{1,9},{2,10},{3,11},{4,12},{5,13},{6,14},{7,15},{8,0},{9,1},... | collective-permute-start | bytes 3080 | tf_op jit(solution)/shard_map/ppermute | solution.py:241
  15.3 4.8 %copy-start = (bf16[128,1024]{1,0:T(8,128)(2,1)S(1)}, bf16[128,1024]{1,0:T(8,128)(2,1)}, u32[]{:S(2)}) copy-start(bf16[128,1024]{1,0:T(8,128)(2,1)} %mine_ref.1) | copy-start | bytes 786436
  15.4 9.1 %collective-permute-start.10 = (bf16[96,1024]{1,0:T(8,128)(2,1)S(1)}, bf16[96,1024]{1,0:T(8,128)(2,1)S(1)}, u32[]{:S(2)}, u32[]{:S(2)}) collective-permute-start(bf16[96,1024]{1,0:T(8,128)(2,1)S(1)} %slice.17), channel_id=1, source_target_pairs={{0,2},{1,3},{2,0},{3,1},{4,6},{5,7},{6,4},{7,5},{8,10},{9,11},{10,... | collective-permute-start | bytes 589832 | tf_op jit(solution)/shard_map/ppermute | solution.py:241
  19.6 1.5 %collective-permute-start.9 = (bf16[64,1024]{1,0:T(8,128)(2,1)S(1)}, bf16[64,1024]{1,0:T(8,128)(2,1)S(1)}, u32[]{:S(2)}, u32[]{:S(2)}) collective-permute-start(bf16[64,1024]{1,0:T(8,128)(2,1)S(1)} %get-tuple-element.31), channel_id=1, source_target_pairs={{0,1},{1,0},{2,3},{3,2},{4,5},{5,4},{6,7},{7,6},{8,9},{9,8},{10,11... | collective-permute-start | bytes 393224 | tf_op jit(solution)/shard_map/ppermute | solution.py:241
  19.7 1.5 %collective-permute-start.8 = (bf16[64,1024]{1,0:T(8,128)(2,1)S(1)}, bf16[64,1024]{1,0:T(8,128)(2,1)S(1)}, u32[]{:S(2)}, u32[]{:S(2)}) collective-permute-start(bf16[64,1024]{1,0:T(8,128)(2,1)S(1)} %get-tuple-element.32), channel_id=1, source_target_pairs={{0,1},{1,0},{2,3},{3,2},{4,5},{5,4},{6,7},{7,6},{8,9},{9,8},{10,11... | collective-permute-start | bytes 393224 | tf_op jit(solution)/shard_map/ppermute | solution.py:241
  20.2 4.3 %collective-permute-start.11 = (bf16[32,1024]{1,0:T(8,128)(2,1)S(1)}, bf16[32,1024]{1,0:T(8,128)(2,1)S(1)}, u32[]{:S(2)}, u32[]{:S(2)}) collective-permute-start(bf16[32,1024]{1,0:T(8,128)(2,1)S(1)} %slice.20), channel_id=1, source_target_pairs={{0,4},{1,5},{2,6},{3,7},{4,0},{5,1},{6,2},{7,3},{8,12},{9,13},{10,... | collective-permute-start | bytes 196616 | tf_op jit(solution)/shard_map/ppermute | solution.py:241
  25.0 4.6 %collective-permute-start.12 = (f32[8,128]{1,0:T(8,128)S(1)}, f32[8,128]{1,0:T(8,128)S(1)}, u32[]{:S(2)}, u32[]{:S(2)}) collective-permute-start(f32[8,128]{1,0:T(8,128)S(1)} %late.1), channel_id=1, source_target_pairs={{0,6},{1,7},{2,4},{3,5},{4,2},{5,3},{6,0},{7,1},{8,14},{9,15},{10,... | collective-permute-start | bytes 12296 | tf_op jit(solution)/shard_map/ppermute | solution.py:241
  25.8 3.8 %collective-permute-start.13 = (f32[8,128]{1,0:T(8,128)S(1)}, f32[8,128]{1,0:T(8,128)S(1)}, u32[]{:S(2)}, u32[]{:S(2)}) collective-permute-start(f32[8,128]{1,0:T(8,128)S(1)} %get-tuple-element.28), channel_id=1, source_target_pairs={{0,4},{1,5},{2,6},{3,7},{4,0},{5,1},{6,2},{7,3},{8,12},{9,13},{10,... | collective-permute-start | bytes 12296 | tf_op jit(solution)/shard_map/ppermute | solution.py:241
  27.1 3.6 %collective-permute-start.14 = (f32[8,128]{1,0:T(8,128)S(1)}, f32[8,128]{1,0:T(8,128)S(1)}, u32[]{:S(2)}, u32[]{:S(2)}) collective-permute-start(f32[8,128]{1,0:T(8,128)S(1)} %get-tuple-element.29), channel_id=1, source_target_pairs={{0,2},{1,3},{2,0},{3,1},{4,6},{5,7},{6,4},{7,5},{8,10},{9,11},{10,... | collective-permute-start | bytes 12296 | tf_op jit(solution)/shard_map/ppermute | solution.py:241

commit v12 on v5

--- a/solution.py
+++ b/solution.py
@@ -143,43 +143,38 @@
     return (scaled * (1.0 / math.sqrt(values.shape[1]))).astype(jnp.bfloat16)
 
 
-def normalize_kernel(rows_ref, cluster_ref, out_ref, front_ref, back_ref):
+def normalize_kernel(rows_ref, tail_ref, whole_ref, front_ref, back_ref):
     rows, width = rows_ref.shape
+    half = rows // 2
     unit = unit_of(rows_ref[...])
-    cluster = jnp.broadcast_to(cluster_ref[...].astype(jnp.float32), (TAIL, rows))
-    tail = jnp.concatenate([cluster, jnp.zeros((TAIL, width - rows), jnp.float32)], axis=1)
-    tail = tail.astype(jnp.bfloat16)
-    out_ref[:rows] = unit
-    out_ref[rows:] = tail
-    front_ref[: rows // 2] = unit[: rows // 2]
-    front_ref[rows // 2 :] = tail
-    back_ref[...] = unit[rows // 2 :]
+    tail = jnp.concatenate([tail_ref[...], jnp.zeros((TAIL, width - rows), jnp.bfloat16)], axis=1)
+    whole_ref[:rows] = unit
+    whole_ref[rows:] = tail
+    front_ref[...] = unit[:half]
+    back_ref[:half] = unit[half:]
+    back_ref[half:] = tail
 
 
 def normalize(embeddings, assignment):
     rows, width = embeddings.shape
+    tail = jnp.broadcast_to(assignment.reshape(1, rows).astype(jnp.bfloat16), (TAIL, rows))
     return pl.pallas_call(
         normalize_kernel,
         out_shape=[
             jax.ShapeDtypeStruct((size, width), jnp.bfloat16)
-            for size in (rows + TAIL, rows // 2 + TAIL, rows // 2)
+            for size in (rows + TAIL, rows // 2, rows // 2 + TAIL)
         ],
         in_specs=[VMEM, VMEM],
         out_specs=[VMEM] * 3,
         compiler_params=LIMIT,
         name="normalize",
-    )(embeddings, assignment.reshape(1, rows))
-
-
-def whole(ref):
-    rows = ref.shape[0] - TAIL
-    return ref[:rows], ref[rows:, :rows][:1].astype(jnp.float32)
-
-
-def halves(front_ref, back_ref):
-    half, rows = back_ref.shape[0], 2 * back_ref.shape[0]
-    joined = jnp.concatenate([front_ref[:half], back_ref[...]], axis=0)
-    return joined, front_ref[half:, :rows][:1].astype(jnp.float32)
+    )(embeddings, tail)
+
+
+def block(refs):
+    pieces = [ref[...] for ref in refs[:-1]] + [refs[-1][: refs[-1].shape[0] - TAIL]]
+    rows = pieces[0] if len(pieces) == 1 else jnp.concatenate(pieces, axis=0)
+    return rows, refs[-1][pieces[-1].shape[0] :, : rows.shape[0]][:1].astype(jnp.float32)
 
 
 def best_of(own, others, same_rows=False):
@@ -202,66 +197,59 @@
     return best
 
 
-def early_kernel(c_ref, e_ref, mine_ref, x_ref, out_ref):
-    mine = whole(mine_ref)
-    best = best_of([mine, whole(c_ref), whole(e_ref)], [mine, whole(x_ref)], True)
+def early_kernel(mine_refs, x_refs, e_refs, c_refs, out_ref):
+    mine = block(mine_refs)
+    best = best_of([mine, block(x_refs), block(e_refs)], [mine, block(c_refs)], True)
     out_ref[...] = jnp.broadcast_to(best, out_ref.shape)
 
 
-def early(c, e, mine, x):
-    rows = mine.shape[0] - TAIL
-    return pl.pallas_call(
-        early_kernel,
-        out_shape=jax.ShapeDtypeStruct((8, 3 * rows), jnp.float32),
-        in_specs=[VMEM] * 4,
-        out_specs=VMEM,
-        compiler_params=LIMIT,
-        name="early",
-    )(c, e, mine, x)
-
-
-def late_kernel(best_ref, c_ref, e_ref, ce_ref, mine_ref, x_ref, *refs):
-    h, xh, out_refs = halves(*refs[:2]), halves(*refs[2:4]), refs[4:]
-    mine = whole(mine_ref)
-    best = best_of([mine, whole(c_ref), whole(e_ref)], [h, xh])
+def middle_kernel(best_ref, mine_refs, x_refs, e_refs, h_refs, ch_refs, *out_refs):
+    best = best_of([block(mine_refs), block(x_refs), block(e_refs)], [block(h_refs), block(ch_refs)])
     best = jnp.maximum(best, best_ref[:1, :])
-    last = best_of([whole(ce_ref)], [mine, whole(x_ref), h, xh])
-    best = jnp.concatenate([best, last], axis=1)
     for place, out_ref in enumerate(out_refs):
         rows = out_ref.shape[1]
         out_ref[...] = jnp.broadcast_to(best[:, place * rows : (place + 1) * rows], out_ref.shape)
 
 
-def late(best, c, e, ce, mine, x, h, xh):
-    rows = mine.shape[0] - TAIL
-    return pl.pallas_call(
-        late_kernel,
-        out_shape=[jax.ShapeDtypeStruct((8, rows), jnp.float32)] * 4,
-        in_specs=[VMEM] * 10,
-        out_specs=[VMEM] * 4,
+def late_kernel(xe_refs, mine_refs, c_refs, h_refs, ch_refs, out_ref):
+    others = [block(refs) for refs in (mine_refs, c_refs, h_refs, ch_refs)]
+    out_ref[...] = jnp.broadcast_to(best_of([block(xe_refs)], others), out_ref.shape)
+
+
+def call(kernel, name, out_shape, arrays):
+    return pl.pallas_call(
+        kernel,
+        out_shape=out_shape,
+        in_specs=jax.tree.map(lambda _: VMEM, tuple(arrays)),
+        out_specs=jax.tree.map(lambda _: VMEM, out_shape),
         compiler_params=LIMIT,
-        name="late",
-    )(best, c, e, ce, mine, x, *h, *xh)
+        name=name,
+    )(*arrays)
 
 
 def square(embeddings, assignment):
     def swap(flip, array):
         return lax.ppermute(array, AXES, [(i, i ^ flip) for i in range(16)])
 
+    rows = embeddings.shape[0]
+    bests = jax.ShapeDtypeStruct((8, rows), jnp.float32)
     mine, front, back = normalize(embeddings, assignment)
-    h_front = swap(HIGH, front)
-    h_back = swap(HIGH, back)
     x = swap(SHARD, mine)
-    e = swap(LOW, mine)
-    c = swap(SUB, mine)
-    xh_front = swap(SHARD, h_front)
-    xh_back = swap(SHARD, h_back)
-    ce = swap(SUB, e)
-    best = early(c, e, mine, x)
-    found, *others = late(best, c, e, ce, mine, x, (h_front, h_back), (xh_front, xh_back))
-    for flip, other in zip((SUB, LOW, LOW | SUB), others):
-        found = jnp.maximum(found, swap(flip, other))
-    return found[0]
+    h = swap(HIGH, mine)
+    e_front, e_back = swap(LOW, front), swap(LOW, back)
+    mine_then, _ = lax.optimization_barrier((mine, x))
+    c = swap(SUB, mine_then)
+    xe_front, xe_back = swap(SHARD, e_front), swap(SHARD, e_back)
+    h_then, _ = lax.optimization_barrier((h, xe_front))
+    cuts = [rows * k // 4 for k in range(4)] + [rows + TAIL]
+    ch = [swap(SUB, h_then[begin:end]) for begin, end in zip(cuts, cuts[1:])]
+    x, h, c, e, xe = [x], [h], [c], [e_front, e_back], [xe_front, xe_back]
+    mine = [mine]
+    best = call(early_kernel, "early", jax.ShapeDtypeStruct((8, 3 * rows), jnp.float32), (mine, x, e, c))
+    found, x_best, e_best = call(middle_kernel, "middle", [bests] * 3, (best, mine, x, e, h, ch))
+    x_best, e_best = swap(SHARD, x_best), swap(LOW, e_best)
+    xe_best = swap(LOW | SHARD, call(late_kernel, "late", bests, (xe, mine, c, h, ch)))
+    return jnp.maximum(jnp.maximum(found, x_best), jnp.maximum(e_best, xe_best))[0]
 
 
 def shared_owner(embeddings, assignment):

time: 34.8 us -> 34.6 us (level)
  other arithmetic: 0.01 us -> 0.66 us
  local copies, waits for them, and re-layouts: 2.12 us -> 1.49 us
    convert_element_type x0 -> x1, other arithmetic: none -> 0.66 us  [normalize(): assignment.reshape(1, rows).astype(jnp.bfloat16)]
    unnamed x4 -> x2, local copies, waits for them, and re-layouts: 1.6 us -> 0.95 us
    ppermute x11 -> x14, starting transfers between devices: 14.1 us -> 13.9 us  [swap(): return lax.ppermute(array, AXES, [(i, i ^ flip) for i in range(16)])]
    ppermute x11 -> x14, waiting for transfers between devices: 16.7 us -> 16.5 us  [swap(): return lax.ppermute(array, AXES, [(i, i ^ flip) for i in range(16)])]
    pallas_call x2 -> x3, Pallas kernels: 1.53 us -> 1.69 us  [call(): pl.pallas_call(kernel, out_shape=out_shape, in_specs=jax.tree.map(lambda...]
  transfers between devices with their start and end apart: 11 -> 14, of which waited for: 4 -> 6; matrix products, arithmetic and copies ran while one was open for 0% -> 0% of each run, Pallas kernels for 2% -> 5%
where the time goes in v12:
time: 34.6 us; the launch traced here: 34.4 us
  waiting for transfers between devices  16.5 us (48%)
  starting transfers between devices  13.9 us (40%)
  Pallas kernels  1.84 us (5%)
  local copies, waits for them, and re-layouts  1.49 us (4%)
  other arithmetic  0.66 us (2%)
    ppermute x14, waiting for transfers between devices, swap(): return lax.ppermute(array, AXES, [(i, i ^ flip) for i in range(16)])  16.5 us
    ppermute x14, starting transfers between devices, swap(): return lax.ppermute(array, AXES, [(i, i ^ flip) for i in range(16)])  13.9 us
    pallas_call x3, Pallas kernels, call(): pl.pallas_call(kernel, out_shape=out_shape, in_specs=jax.tree.map(lambda...  1.69 us
    unnamed x2, local copies, waits for them, and re-layouts  0.95 us
  transfers between devices with their start and end apart: 14, of which 6 were waited for; matrix products, arithmetic and copies ran while one was open for 0% of the time, Pallas kernels for 5%

profile of v12, /device:TPU:0, one launch (start us, length us, event | category | flops | bytes accessed | tf_op | source)
XLA Modules:
  0.0 34.4 jit_solution(16798386231558116818)
XLA Ops:
  0.0 0.7 %convert_bitcast_fusion = bf16[128]{0:T(256)(128)(2,1)S(1)} fusion(s32[128,1]{0,1:T(1,128)} %param.3), kind=kLoop, calls=%fused_computation.2 | loop fusion | flops 128 | bytes 768 | tf_op jit(solution)/shard_map/convert_element_type | solution.py:160
  0.7 0.0 copy-start
  0.7 0.9 %copy-done = bf16[128,1024]{1,0:T(8,128)(2,1)S(1)} copy-done((bf16[128,1024]{1,0:T(8,128)(2,1)S(1)}, bf16[128,1024]{1,0:T(8,128)(2,1)}, u32[]{:S(2)}) %copy-start) | copy-done | bytes 262168
  1.6 0.2 normalize.1
  1.8 3.0 %collective-permute-start = (bf16[136,1024]{1,0:T(8,128)(2,1)S(1)}, bf16[136,1024]{1,0:T(8,128)(2,1)S(1)}, u32[]{:S(2)}, u32[]{:S(2)}) collective-permute-start(bf16[136,1024]{1,0:T(8,128)(2,1)S(1)} %get-tuple-element.16.mine_refs_0_), channel_id=1, source_target_pairs={{0,2},{1,3},{2,0},{3,1},{4,6},{5,7},{6,4},{7,5},{8,10},{9,11},{10,... | collective-permute-start | bytes 835592 | tf_op jit(solution)/shard_map/ppermute | solution.py:232
  4.8 2.6 %collective-permute-start.4 = (bf16[136,1024]{1,0:T(8,128)(2,1)S(1)}, bf16[136,1024]{1,0:T(8,128)(2,1)S(1)}, u32[]{:S(2)}, u32[]{:S(2)}) collective-permute-start(bf16[136,1024]{1,0:T(8,128)(2,1)S(1)} %get-tuple-element.16.mine_refs_0_), channel_id=1, source_target_pairs={{0,8},{1,9},{2,10},{3,11},{4,12},{5,13},{6,14},{7,15},{8,0},{9,1},... | collective-permute-start | bytes 835592 | tf_op jit(solution)/shard_map/ppermute | solution.py:232
  7.4 1.6 %collective-permute-start.1 = (bf16[64,1024]{1,0:T(8,128)(2,1)S(1)}, bf16[64,1024]{1,0:T(8,128)(2,1)S(1)}, u32[]{:S(2)}, u32[]{:S(2)}) collective-permute-start(bf16[64,1024]{1,0:T(8,128)(2,1)S(1)} %get-tuple-element.14), channel_id=1, source_target_pairs={{0,4},{1,5},{2,6},{3,7},{4,0},{5,1},{6,2},{7,3},{8,12},{9,13},{10,... | collective-permute-start | bytes 393224 | tf_op jit(solution)/shard_map/ppermute | solution.py:232
  8.9 0.4 %collective-permute-start.2 = (bf16[72,1024]{1,0:T(8,128)(2,1)S(1)}, bf16[72,1024]{1,0:T(8,128)(2,1)S(1)}, u32[]{:S(2)}, u32[]{:S(2)}) collective-permute-start(bf16[72,1024]{1,0:T(8,128)(2,1)S(1)} %get-tuple-element.15), channel_id=1, source_target_pairs={{0,4},{1,5},{2,6},{3,7},{4,0},{5,1},{6,2},{7,3},{8,12},{9,13},{10,... | collective-permute-start | bytes 442376 | tf_op jit(solution)/shard_map/ppermute | solution.py:232
  9.4 7.9 %collective-permute-done.1.e_refs_0_ = bf16[64,1024]{1,0:T(8,128)(2,1)S(1)} collective-permute-done((bf16[64,1024]{1,0:T(8,128)(2,1)S(1)}, bf16[64,1024]{1,0:T(8,128)(2,1)S(1)}, u32[]{:S(2)}, u32[]{:S(2)}) %collective-permute-start.1) | collective-permute-done | bytes 131104 | tf_op jit(solution)/shard_map/ppermute | solution.py:232
  17.3 0.5 %collective-permute-start.5 = (bf16[64,1024]{1,0:T(8,128)(2,1)S(1)}, bf16[64,1024]{1,0:T(8,128)(2,1)S(1)}, u32[]{:S(2)}, u32[]{:S(2)}) collective-permute-start(bf16[64,1024]{1,0:T(8,128)(2,1)S(1)} %collective-permute-done.1.e_refs_0_), channel_id=1, source_target_pairs={{0,2},{1,3},{2,0},{3,1},{4,6},{5,7},{6,4},{7,5},{8,10},{9,11},{10,... | collective-permute-start | bytes 393224 | tf_op jit(solution)/shard_map/ppermute | solution.py:232
  17.9 0.0 collective-permute-done.x_refs_0_
  17.9 0.0 collective-permute-start.3
  17.9 2.2 %collective-permute-done.2.e_refs_1_ = bf16[72,1024]{1,0:T(8,128)(2,1)S(1)} collective-permute-done((bf16[72,1024]{1,0:T(8,128)(2,1)S(1)}, bf16[72,1024]{1,0:T(8,128)(2,1)S(1)}, u32[]{:S(2)}, u32[]{:S(2)}) %collective-permute-start.2) | collective-permute-done | bytes 147488 | tf_op jit(solution)/shard_map/ppermute | solution.py:232
  20.1 0.5 %collective-permute-start.12 = (bf16[72,1024]{1,0:T(8,128)(2,1)S(1)}, bf16[72,1024]{1,0:T(8,128)(2,1)S(1)}, u32[]{:S(2)}, u32[]{:S(2)}) collective-permute-start(bf16[72,1024]{1,0:T(8,128)(2,1)S(1)} %collective-permute-done.2.e_refs_1_), channel_id=1, source_target_pairs={{0,2},{1,3},{2,0},{3,1},{4,6},{5,7},{6,4},{7,5},{8,10},{9,11},{10,... | collective-permute-start | bytes 442376 | tf_op jit(solution)/shard_map/ppermute | solution.py:232
  20.5 3.1 %collective-permute-done.5.xe_refs_0_ = bf16[64,1024]{1,0:T(8,128)(2,1)S(1)} collective-permute-done((bf16[64,1024]{1,0:T(8,128)(2,1)S(1)}, bf16[64,1024]{1,0:T(8,128)(2,1)S(1)}, u32[]{:S(2)}, u32[]{:S(2)}) %collective-permute-start.5) | collective-permute-done | bytes 131104 | tf_op jit(solution)/shard_map/ppermute | solution.py:232
  23.6 0.0 collective-permute-done.4.h_refs_0_
  23.6 0.1 collective-permute-start.9
  23.7 0.6 %collective-permute-start.6 = (bf16[32,1024]{1,0:T(8,128)(2,1)S(1)}, bf16[32,1024]{1,0:T(8,128)(2,1)S(1)}, u32[]{:S(2)}, u32[]{:S(2)}) collective-permute-start(bf16[32,1024]{1,0:T(8,128)(2,1)S(1)} %get-tuple-element.23), channel_id=1, source_target_pairs={{0,1},{1,0},{2,3},{3,2},{4,5},{5,4},{6,7},{7,6},{8,9},{9,8},{10,11... | collective-permute-start | bytes 196616 | tf_op jit(solution)/shard_map/ppermute | solution.py:232
  24.3 0.1 collective-permute-start.7
  24.4 0.0 collective-permute-done.3.c_refs_0_
  24.4 0.4 %collective-permute-start.8 = (bf16[32,1024]{1,0:T(8,128)(2,1)S(1)}, bf16[32,1024]{1,0:T(8,128)(2,1)S(1)}, u32[]{:S(2)}, u32[]{:S(2)}) collective-permute-start(bf16[32,1024]{1,0:T(8,128)(2,1)S(1)} %get-tuple-element.21), channel_id=1, source_target_pairs={{0,1},{1,0},{2,3},{3,2},{4,5},{5,4},{6,7},{7,6},{8,9},{9,8},{10,11... | collective-permute-start | bytes 196616 | tf_op jit(solution)/shard_map/ppermute | solution.py:232
  24.8 0.6 %early.1.best_ref = f32[8,384]{1,0:T(8,128)S(1)} custom-call(bf16[136,1024]{1,0:T(8,128)(2,1)S(1)} %get-tuple-element.16.mine_refs_0_, bf16[136,1024]{1,0:T(8,128)(2,1)S(1)} %collective-permute-done.x_refs_0_, bf16[64,1024]{1,0:T(8,128)(2,1)S(1)} %collective-permute-done.1.e_refs_0_, bf16[72,1024]{1,0:T(8,128)(2,1)S(1)} %collective-permute-done.2.e_refs_1_, ...), custom_call_target="tpu_custom_call" | custom-call | tf_op jit(solution)/shard_map/early/pallas_call | solution.py:220
  25.4 0.0 collective-permute-done.6.ch_refs_0_
  25.4 0.1 collective-permute-done.7.ch_refs_1_
  25.5 0.2 collective-permute-done.8.ch_refs_2_
  25.7 0.0 collective-permute-done.9.ch_refs_3_
  25.7 0.6 %middle.1 = (f32[8,128]{1,0:T(8,128)S(1)}, f32[8,128]{1,0:T(8,128)S(1)}, f32[8,128]{1,0:T(8,128)S(1)}) custom-call(f32[8,384]{1,0:T(8,128)S(1)} %early.1.best_ref, bf16[136,1024]{1,0:T(8,128)(2,1)S(1)} %get-tuple-element.16.mine_refs_0_, bf16[136,1024]{1,0:T(8,128)(2,1)S(1)} %collective-permute-done.x_refs_0_, ...), custom_call_target="tpu_custom_call" | custom-call | tf_op jit(solution)/shard_map/middle/pallas_call | solution.py:220
  26.3 2.5 %collective-permute-start.11 = (f32[8,128]{1,0:T(8,128)S(1)}, f32[8,128]{1,0:T(8,128)S(1)}, u32[]{:S(2)}, u32[]{:S(2)}) collective-permute-start(f32[8,128]{1,0:T(8,128)S(1)} %get-tuple-element.20), channel_id=1, source_target_pairs={{0,4},{1,5},{2,6},{3,7},{4,0},{5,1},{6,2},{7,3},{8,12},{9,13},{10,... | collective-permute-start | bytes 12296 | tf_op jit(solution)/shard_map/ppermute | solution.py:232
  28.9 0.0 collective-permute-done.12.xe_refs_1_
  28.9 0.4 %late.1 = f32[8,128]{1,0:T(8,128)S(1)} custom-call(bf16[64,1024]{1,0:T(8,128)(2,1)S(1)} %collective-permute-done.5.xe_refs_0_, bf16[72,1024]{1,0:T(8,128)(2,1)S(1)} %collective-permute-done.12.xe_refs_1_, bf16[136,1024]{1,0:T(8,128)(2,1)S(1)} %get-tuple-element.16.mine_refs_0_, bf16[136,1024]{1,0:T(8,128)(2,1)S(1)} %collective-permute-done.3.c_refs_0_, ...), custom_call_target="tpu_custom_call" | custom-call | tf_op jit(solution)/shard_map/late/pallas_call | solution.py:220
  29.3 0.1 collective-permute-start.13
  29.4 1.5 %collective-permute-start.10 = (f32[8,128]{1,0:T(8,128)S(1)}, f32[8,128]{1,0:T(8,128)S(1)}, u32[]{:S(2)}, u32[]{:S(2)}) collective-permute-start(f32[8,128]{1,0:T(8,128)S(1)} %get-tuple-element.19), channel_id=1, source_target_pairs={{0,2},{1,3},{2,0},{3,1},{4,6},{5,7},{6,4},{7,5},{8,10},{9,11},{10,... | collective-permute-start | bytes 12296 | tf_op jit(solution)/shard_map/ppermute | solution.py:232
  30.9 0.0 collective-permute-done.11
  30.9 3.0 %collective-permute-done.13 = f32[8,128]{1,0:T(8,128)S(1)} collective-permute-done((f32[8,128]{1,0:T(8,128)S(1)}, f32[8,128]{1,0:T(8,128)S(1)}, u32[]{:S(2)}, u32[]{:S(2)}) %collective-permute-start.13) | collective-permute-done | bytes 4128 | tf_op jit(solution)/shard_map/ppermute | solution.py:232
  33.9 0.0 collective-permute-done.10
  33.9 0.5 %slice_bitcast_fusion = f32[128]{0:T(128)} fusion(f32[8,128]{1,0:T(8,128)S(1)} %maximum_maximum_fusion), kind=kLoop, calls=%fused_computation.1 | loop fusion | bytes 1024 | tf_op jit(solution)/shard_map/squeeze | solution.py:252
  (4 shorter events, 0.0 us)
Async XLA Ops:
  0.7 0.9 %copy-start = (bf16[128,1024]{1,0:T(8,128)(2,1)S(1)}, bf16[128,1024]{1,0:T(8,128)(2,1)}, u32[]{:S(2)}) copy-start(bf16[128,1024]{1,0:T(8,128)(2,1)} %rows_ref.1) | copy-start | bytes 786436
  1.8 16.1 %collective-permute-start = (bf16[136,1024]{1,0:T(8,128)(2,1)S(1)}, bf16[136,1024]{1,0:T(8,128)(2,1)S(1)}, u32[]{:S(2)}, u32[]{:S(2)}) collective-permute-start(bf16[136,1024]{1,0:T(8,128)(2,1)S(1)} %get-tuple-element.16.mine_refs_0_), channel_id=1, source_target_pairs={{0,2},{1,3},{2,0},{3,1},{4,6},{5,7},{6,4},{7,5},{8,10},{9,11},{10,... | collective-permute-start | bytes 835592 | tf_op jit(solution)/shard_map/ppermute | solution.py:232
  4.8 18.8 %collective-permute-start.4 = (bf16[136,1024]{1,0:T(8,128)(2,1)S(1)}, bf16[136,1024]{1,0:T(8,128)(2,1)S(1)}, u32[]{:S(2)}, u32[]{:S(2)}) collective-permute-start(bf16[136,1024]{1,0:T(8,128)(2,1)S(1)} %get-tuple-element.16.mine_refs_0_), channel_id=1, source_target_pairs={{0,8},{1,9},{2,10},{3,11},{4,12},{5,13},{6,14},{7,15},{8,0},{9,1},... | collective-permute-start | bytes 835592 | tf_op jit(solution)/shard_map/ppermute | solution.py:232
  7.4 10.0 %collective-permute-start.1 = (bf16[64,1024]{1,0:T(8,128)(2,1)S(1)}, bf16[64,1024]{1,0:T(8,128)(2,1)S(1)}, u32[]{:S(2)}, u32[]{:S(2)}) collective-permute-start(bf16[64,1024]{1,0:T(8,128)(2,1)S(1)} %get-tuple-element.14), channel_id=1, source_target_pairs={{0,4},{1,5},{2,6},{3,7},{4,0},{5,1},{6,2},{7,3},{8,12},{9,13},{10,... | collective-permute-start | bytes 393224 | tf_op jit(solution)/shard_map/ppermute | solution.py:232
  8.9 11.1 %collective-permute-start.2 = (bf16[72,1024]{1,0:T(8,128)(2,1)S(1)}, bf16[72,1024]{1,0:T(8,128)(2,1)S(1)}, u32[]{:S(2)}, u32[]{:S(2)}) collective-permute-start(bf16[72,1024]{1,0:T(8,128)(2,1)S(1)} %get-tuple-element.15), channel_id=1, source_target_pairs={{0,4},{1,5},{2,6},{3,7},{4,0},{5,1},{6,2},{7,3},{8,12},{9,13},{10,... | collective-permute-start | bytes 442376 | tf_op jit(solution)/shard_map/ppermute | solution.py:232
  17.3 6.3 %collective-permute-start.5 = (bf16[64,1024]{1,0:T(8,128)(2,1)S(1)}, bf16[64,1024]{1,0:T(8,128)(2,1)S(1)}, u32[]{:S(2)}, u32[]{:S(2)}) collective-permute-start(bf16[64,1024]{1,0:T(8,128)(2,1)S(1)} %collective-permute-done.1.e_refs_0_), channel_id=1, source_target_pairs={{0,2},{1,3},{2,0},{3,1},{4,6},{5,7},{6,4},{7,5},{8,10},{9,11},{10,... | collective-permute-start | bytes 393224 | tf_op jit(solution)/shard_map/ppermute | solution.py:232
  17.9 6.5 %collective-permute-start.3 = (bf16[136,1024]{1,0:T(8,128)(2,1)S(1)}, bf16[136,1024]{1,0:T(8,128)(2,1)S(1)}, u32[]{:S(2)}, u32[]{:S(2)}) collective-permute-start(bf16[136,1024]{1,0:T(8,128)(2,1)S(1)} %get-tuple-element.16.mine_refs_0_), channel_id=1, source_target_pairs={{0,1},{1,0},{2,3},{3,2},{4,5},{5,4},{6,7},{7,6},{8,9},{9,8},{10,11... | collective-permute-start | bytes 835592 | tf_op jit(solution)/shard_map/ppermute | solution.py:232
  20.1 8.8 %collective-permute-start.12 = (bf16[72,1024]{1,0:T(8,128)(2,1)S(1)}, bf16[72,1024]{1,0:T(8,128)(2,1)S(1)}, u32[]{:S(2)}, u32[]{:S(2)}) collective-permute-start(bf16[72,1024]{1,0:T(8,128)(2,1)S(1)} %collective-permute-done.2.e_refs_1_), channel_id=1, source_target_pairs={{0,2},{1,3},{2,0},{3,1},{4,6},{5,7},{6,4},{7,5},{8,10},{9,11},{10,... | collective-permute-start | bytes 442376 | tf_op jit(solution)/shard_map/ppermute | solution.py:232
  23.6 2.1 %collective-permute-start.9 = (bf16[40,1024]{1,0:T(8,128)(2,1)S(1)}, bf16[40,1024]{1,0:T(8,128)(2,1)S(1)}, u32[]{:S(2)}, u32[]{:S(2)}) collective-permute-start(bf16[40,1024]{1,0:T(8,128)(2,1)S(1)} %slice.18), channel_id=1, source_target_pairs={{0,1},{1,0},{2,3},{3,2},{4,5},{5,4},{6,7},{7,6},{8,9},{9,8},{10,11... | collective-permute-start | bytes 245768 | tf_op jit(solution)/shard_map/ppermute | solution.py:232
  23.7 1.7 %collective-permute-start.6 = (bf16[32,1024]{1,0:T(8,128)(2,1)S(1)}, bf16[32,1024]{1,0:T(8,128)(2,1)S(1)}, u32[]{:S(2)}, u32[]{:S(2)}) collective-permute-start(bf16[32,1024]{1,0:T(8,128)(2,1)S(1)} %get-tuple-element.23), channel_id=1, source_target_pairs={{0,1},{1,0},{2,3},{3,2},{4,5},{5,4},{6,7},{7,6},{8,9},{9,8},{10,11... | collective-permute-start | bytes 196616 | tf_op jit(solution)/shard_map/ppermute | solution.py:232
  24.3 1.3 %collective-permute-start.7 = (bf16[32,1024]{1,0:T(8,128)(2,1)S(1)}, bf16[32,1024]{1,0:T(8,128)(2,1)S(1)}, u32[]{:S(2)}, u32[]{:S(2)}) collective-permute-start(bf16[32,1024]{1,0:T(8,128)(2,1)S(1)} %get-tuple-element.22), channel_id=1, source_target_pairs={{0,1},{1,0},{2,3},{3,2},{4,5},{5,4},{6,7},{7,6},{8,9},{9,8},{10,11... | collective-permute-start | bytes 196616 | tf_op jit(solution)/shard_map/ppermute | solution.py:232
  24.4 1.3 %collective-permute-start.8 = (bf16[32,1024]{1,0:T(8,128)(2,1)S(1)}, bf16[32,1024]{1,0:T(8,128)(2,1)S(1)}, u32[]{:S(2)}, u32[]{:S(2)}) collective-permute-start(bf16[32,1024]{1,0:T(8,128)(2,1)S(1)} %get-tuple-element.21), channel_id=1, source_target_pairs={{0,1},{1,0},{2,3},{3,2},{4,5},{5,4},{6,7},{7,6},{8,9},{9,8},{10,11... | collective-permute-start | bytes 196616 | tf_op jit(solution)/shard_map/ppermute | solution.py:232
  26.3 4.6 %collective-permute-start.11 = (f32[8,128]{1,0:T(8,128)S(1)}, f32[8,128]{1,0:T(8,128)S(1)}, u32[]{:S(2)}, u32[]{:S(2)}) collective-permute-start(f32[8,128]{1,0:T(8,128)S(1)} %get-tuple-element.20), channel_id=1, source_target_pairs={{0,4},{1,5},{2,6},{3,7},{4,0},{5,1},{6,2},{7,3},{8,12},{9,13},{10,... | collective-permute-start | bytes 12296 | tf_op jit(solution)/shard_map/ppermute | solution.py:232
  29.3 4.6 %collective-permute-start.13 = (f32[8,128]{1,0:T(8,128)S(1)}, f32[8,128]{1,0:T(8,128)S(1)}, u32[]{:S(2)}, u32[]{:S(2)}) collective-permute-start(f32[8,128]{1,0:T(8,128)S(1)} %late.1), channel_id=1, source_target_pairs={{0,6},{1,7},{2,4},{3,5},{4,2},{5,3},{6,0},{7,1},{8,14},{9,15},{10,... | collective-permute-start | bytes 12296 | tf_op jit(solution)/shard_map/ppermute | solution.py:232
  29.4 4.5 %collective-permute-start.10 = (f32[8,128]{1,0:T(8,128)S(1)}, f32[8,128]{1,0:T(8,128)S(1)}, u32[]{:S(2)}, u32[]{:S(2)}) collective-permute-start(f32[8,128]{1,0:T(8,128)S(1)} %get-tuple-element.19), channel_id=1, source_target_pairs={{0,2},{1,3},{2,0},{3,1},{4,6},{5,7},{6,4},{7,5},{8,10},{9,11},{10,... | collective-permute-start | bytes 12296 | tf_op jit(solution)/shard_map/ppermute | solution.py:232

commit v13 on v11

--- a/solution.py
+++ b/solution.py
@@ -250,17 +250,15 @@
     x_ids, c_ids = swap(SHARD, ids), swap(SUB, ids)
     e_ids = swap(LOW, jnp.concatenate([ids, x_ids]))
     h_ids = swap(HIGH, jnp.concatenate([ids, c_ids]))
-    e_then, _, _ = lax.optimization_barrier((e, x, e_ids))
-    xe = [swap(SHARD, e_then[:rows * 3 // 4]), swap(LOW, x[rows * 3 // 4:])]
-    h_then, _ = lax.optimization_barrier((h, h_ids))
+    xe = swap(SHARD, e)
+    h_then, _, _, _ = lax.optimization_barrier((h, h_ids, e_ids, x))
     ch = [swap(SUB, h_then[: rows // 2]), swap(SUB, h_then[rows // 2 :])]
-    x, e, h, c = [x], [e], [h], [c]
+    x, e, h, c, xe = [x], [e], [h], [c], [xe]
     best, own, c = early(mine, x, e, c, [ids, x_ids, c_ids, e_ids])
     found, x_best, e_best, far = middle(best, own, c, h, ch, [ids, x_ids, c_ids, e_ids, h_ids])
-    xe_best = late(far, xe, [ids, c_ids, e_ids, h_ids])
-    x_best, e_best, xe_best = lax.optimization_barrier((x_best, e_best, xe_best))
-    xe_best, e_best, x_best = swap(LOW | SHARD, xe_best), swap(LOW, e_best), swap(SHARD, x_best)
-    return jnp.maximum(jnp.maximum(jnp.maximum(xe_best, e_best), x_best), found)[0]
+    x_best, e_best = swap(SHARD, x_best), swap(LOW, e_best)
+    xe_best = swap(LOW | SHARD, late(far, xe, [ids, c_ids, e_ids, h_ids]))
+    return jnp.maximum(jnp.maximum(found, x_best), jnp.maximum(e_best, xe_best))[0]
 
 
 def shared_owner(embeddings, assignment):

time: 31.3 us -> 29 us (0.927)
  waiting for transfers between devices: 11.7 us -> 9.05 us
    ppermute x15 -> x14, waiting for transfers between devices: 11.7 us -> 9.05 us  [swap(): return lax.ppermute(array, AXES, [(i, i ^ flip) for i in range(16)])]
    ppermute x15 -> x14, starting transfers between devices: 16.8 us -> 17.1 us  [swap(): return lax.ppermute(array, AXES, [(i, i ^ flip) for i in range(16)])]
  transfers between devices with their start and end apart: 15 -> 14, of which waited for: 8 -> 6; matrix products, arithmetic and copies ran while one was open for 0% -> 0% of each run, Pallas kernels for 5% -> 7%
where the time goes in v13:
time: 29 us; the launch traced here: 28.9 us
  starting transfers between devices  17.1 us (59%)
  waiting for transfers between devices  9.05 us (31%)
  Pallas kernels  2.09 us (7%)
  local copies, waits for them, and re-layouts  0.54 us (2%)
    ppermute x14, starting transfers between devices, swap(): return lax.ppermute(array, AXES, [(i, i ^ flip) for i in range(16)])  17.1 us
    ppermute x14, waiting for transfers between devices, swap(): return lax.ppermute(array, AXES, [(i, i ^ flip) for i in range(16)])  9.05 us
    pallas_call x1, Pallas kernels, early(): pl.pallas_call(early_kernel, out_shape=[jax.ShapeDtypeStruct((8, 3 * rows...  0.84 us
    pallas_call x1, Pallas kernels, middle(): pl.pallas_call(middle_kernel, out_shape=[jax.ShapeDtypeStruct((8, rows),...  0.68 us
  transfers between devices with their start and end apart: 14, of which 6 were waited for; matrix products, arithmetic and copies ran while one was open for 0% of the time, Pallas kernels for 7%

profile of v13, /device:TPU:0, one launch (start us, length us, event | category | flops | bytes accessed | tf_op | source)
XLA Modules:
  0.0 28.9 jit_solution(6153842770321151267)
XLA Ops:
  0.0 0.0 copy-start.1
  0.0 0.5 %collective-permute-start.2 = (bf16[128,1024]{1,0:T(8,128)(2,1)}, bf16[128,1024]{1,0:T(8,128)(2,1)S(1)}, u32[]{:S(2)}, u32[]{:S(2)}) collective-permute-start(bf16[128,1024]{1,0:T(8,128)(2,1)} %mine_ref.1), channel_id=1, source_target_pairs={{0,1},{1,0},{2,3},{3,2},{4,5},{5,4},{6,7},{7,6},{8,9},{9,8},{10,11... | collective-permute-start | bytes 786440 | tf_op jit(solution)/shard_map/ppermute | solution.py:241
  0.5 2.6 %collective-permute-start.1 = (bf16[128,1024]{1,0:T(8,128)(2,1)}, bf16[128,1024]{1,0:T(8,128)(2,1)S(1)}, u32[]{:S(2)}, u32[]{:S(2)}) collective-permute-start(bf16[128,1024]{1,0:T(8,128)(2,1)} %mine_ref.1), channel_id=1, source_target_pairs={{0,4},{1,5},{2,6},{3,7},{4,0},{5,1},{6,2},{7,3},{8,12},{9,13},{10,... | collective-permute-start | bytes 786440 | tf_op jit(solution)/shard_map/ppermute | solution.py:241
  3.1 1.5 %collective-permute-start = (bf16[128,1024]{1,0:T(8,128)(2,1)}, bf16[128,1024]{1,0:T(8,128)(2,1)S(1)}, u32[]{:S(2)}, u32[]{:S(2)}) collective-permute-start(bf16[128,1024]{1,0:T(8,128)(2,1)} %mine_ref.1), channel_id=1, source_target_pairs={{0,2},{1,3},{2,0},{3,1},{4,6},{5,7},{6,4},{7,5},{8,10},{9,11},{10,... | collective-permute-start | bytes 786440 | tf_op jit(solution)/shard_map/ppermute | solution.py:241
  4.6 0.0 collective-permute-done.2.c_refs_0_
  4.6 2.6 %collective-permute-start.6 = (bf16[128,1024]{1,0:T(8,128)(2,1)}, bf16[128,1024]{1,0:T(8,128)(2,1)S(1)}, u32[]{:S(2)}, u32[]{:S(2)}) collective-permute-start(bf16[128,1024]{1,0:T(8,128)(2,1)} %mine_ref.1), channel_id=1, source_target_pairs={{0,8},{1,9},{2,10},{3,11},{4,12},{5,13},{6,14},{7,15},{8,0},{9,1},... | collective-permute-start | bytes 786440 | tf_op jit(solution)/shard_map/ppermute | solution.py:241
  7.2 0.0 copy-done.1
  7.2 0.0 collective-permute-start.4
  7.2 0.5 %collective-permute-start.3 = (s32[1,128]{1,0:T(1,128)S(1)}, s32[1,128]{1,0:T(1,128)S(1)}, u32[]{:S(2)}, u32[]{:S(2)}) collective-permute-start(s32[1,128]{1,0:T(1,128)S(1)} %bitcast.4), channel_id=1, source_target_pairs={{0,2},{1,3},{2,0},{3,1},{4,6},{5,7},{6,4},{7,5},{8,10},{9,11},{10,... | collective-permute-start | bytes 1544 | tf_op jit(solution)/shard_map/ppermute | solution.py:241
  7.7 0.6 %collective-permute-done.4.c_ids_ref = s32[1,128]{1,0:T(1,128)S(1)} collective-permute-done((s32[1,128]{1,0:T(1,128)S(1)}, s32[1,128]{1,0:T(1,128)S(1)}, u32[]{:S(2)}, u32[]{:S(2)}) %collective-permute-start.4) | collective-permute-done | bytes 544 | tf_op jit(solution)/shard_map/ppermute | solution.py:241
  8.3 3.4 %collective-permute-done.3.x_ids_ref = s32[1,128]{1,0:T(1,128)S(1)} collective-permute-done((s32[1,128]{1,0:T(1,128)S(1)}, s32[1,128]{1,0:T(1,128)S(1)}, u32[]{:S(2)}, u32[]{:S(2)}) %collective-permute-start.3) | collective-permute-done | bytes 544 | tf_op jit(solution)/shard_map/ppermute | solution.py:241
  11.8 2.6 %collective-permute-start.7 = (s32[2,128]{1,0:T(2,128)S(1)}, s32[2,128]{1,0:T(2,128)S(1)}, u32[]{:S(2)}, u32[]{:S(2)}) collective-permute-start(s32[2,128]{1,0:T(2,128)S(1)} %get-tuple-element.25), channel_id=1, source_target_pairs={{0,8},{1,9},{2,10},{3,11},{4,12},{5,13},{6,14},{7,15},{8,0},{9,1},... | collective-permute-start | bytes 3080 | tf_op jit(solution)/shard_map/ppermute | solution.py:241
  14.3 0.0 copy-start
  14.3 0.4 %collective-permute-start.5 = (s32[2,128]{1,0:T(2,128)S(1)}, s32[2,128]{1,0:T(2,128)S(1)}, u32[]{:S(2)}, u32[]{:S(2)}) collective-permute-start(s32[2,128]{1,0:T(2,128)S(1)} %get-tuple-element.26), channel_id=1, source_target_pairs={{0,4},{1,5},{2,6},{3,7},{4,0},{5,1},{6,2},{7,3},{8,12},{9,13},{10,... | collective-permute-start | bytes 3080 | tf_op jit(solution)/shard_map/ppermute | solution.py:241
  14.8 0.0 collective-permute-done.1.e_refs_0_
  14.8 2.3 %collective-permute-start.12 = (bf16[128,1024]{1,0:T(8,128)(2,1)S(1)}, bf16[128,1024]{1,0:T(8,128)(2,1)S(1)}, u32[]{:S(2)}, u32[]{:S(2)}) collective-permute-start(bf16[128,1024]{1,0:T(8,128)(2,1)S(1)} %collective-permute-done.1.e_refs_0_), channel_id=1, source_target_pairs={{0,2},{1,3},{2,0},{3,1},{4,6},{5,7},{6,4},{7,5},{8,10},{9,11},{10,... | collective-permute-start | bytes 786440 | tf_op jit(solution)/shard_map/ppermute | solution.py:241
  17.1 2.4 %collective-permute-done.7.h_ids_ref = s32[2,128]{1,0:T(2,128)S(1)} collective-permute-done((s32[2,128]{1,0:T(2,128)S(1)}, s32[2,128]{1,0:T(2,128)S(1)}, u32[]{:S(2)}, u32[]{:S(2)}) %collective-permute-start.7) | collective-permute-done | bytes 1056 | tf_op jit(solution)/shard_map/ppermute | solution.py:241
  19.6 0.0 collective-permute-done.5.e_ids_ref
  19.6 0.0 collective-permute-done.x_refs_0_
  19.6 0.0 collective-permute-done.6.h_refs_0_
  19.6 0.1 collective-permute-start.9
  19.7 0.5 %collective-permute-start.8 = (bf16[64,1024]{1,0:T(8,128)(2,1)S(1)}, bf16[64,1024]{1,0:T(8,128)(2,1)S(1)}, u32[]{:S(2)}, u32[]{:S(2)}) collective-permute-start(bf16[64,1024]{1,0:T(8,128)(2,1)S(1)} %get-tuple-element.24), channel_id=1, source_target_pairs={{0,1},{1,0},{2,3},{3,2},{4,5},{5,4},{6,7},{7,6},{8,9},{9,8},{10,11... | collective-permute-start | bytes 393224 | tf_op jit(solution)/shard_map/ppermute | solution.py:241
  20.2 0.0 copy-done
  20.2 0.8 %early.1 = (f32[8,384]{1,0:T(8,128)S(1)}, bf16[384,1024]{1,0:T(8,128)(2,1)S(1)}, bf16[128,1024]{1,0:T(8,128)(2,1)S(1)}) custom-call(bf16[128,1024]{1,0:T(8,128)(2,1)S(1)} %copy-done, bf16[128,1024]{1,0:T(8,128)(2,1)S(1)} %collective-permute-done.x_refs_0_, bf16[128,1024]{1,0:T(8,128)(2,1)S(1)} %collective-permute-done.1.e_refs_0_, ...), custom_call_target="tpu_custom_call" | custom-call | tf_op jit(solution)/shard_map/early/pallas_call | solution.py:179
  21.0 0.0 collective-permute-done.9.ch_refs_1_
  21.0 0.2 collective-permute-done.8.ch_refs_0_
  21.2 0.7 %middle.1 = (f32[8,128]{1,0:T(8,128)S(1)}, f32[8,128]{1,0:T(8,128)S(1)}, f32[8,128]{1,0:T(8,128)S(1)}, bf16[512,1024]{1,0:T(8,128)(2,1)S(1)}) custom-call(f32[8,384]{1,0:T(8,128)S(1)} %get-tuple-element.14.best_ref, bf16[384,1024]{1,0:T(8,128)(2,1)S(1)} %get-tuple-element.15.own_ref, bf16[128,1024]{1,0:T(8,128)(2,1)S(1)} %get-tuple-element.16.c_ref, ...), custom_call_target="tpu_custom_call" | custom-call | tf_op jit(solution)/shard_map/middle/pallas_call | solution.py:209
  21.9 0.6 %collective-permute-start.10 = (f32[8,128]{1,0:T(8,128)S(1)}, f32[8,128]{1,0:T(8,128)S(1)}, u32[]{:S(2)}, u32[]{:S(2)}) collective-permute-start(f32[8,128]{1,0:T(8,128)S(1)} %get-tuple-element.20), channel_id=1, source_target_pairs={{0,2},{1,3},{2,0},{3,1},{4,6},{5,7},{6,4},{7,5},{8,10},{9,11},{10,... | collective-permute-start | bytes 12296 | tf_op jit(solution)/shard_map/ppermute | solution.py:241
  22.5 0.6 %collective-permute-start.11 = (f32[8,128]{1,0:T(8,128)S(1)}, f32[8,128]{1,0:T(8,128)S(1)}, u32[]{:S(2)}, u32[]{:S(2)}) collective-permute-start(f32[8,128]{1,0:T(8,128)S(1)} %get-tuple-element.21), channel_id=1, source_target_pairs={{0,4},{1,5},{2,6},{3,7},{4,0},{5,1},{6,2},{7,3},{8,12},{9,13},{10,... | collective-permute-start | bytes 12296 | tf_op jit(solution)/shard_map/ppermute | solution.py:241
  23.1 0.1 collective-permute-done.12.xe_refs_0_
  23.2 0.6 %late.1 = f32[8,128]{1,0:T(8,128)S(1)} custom-call(bf16[512,1024]{1,0:T(8,128)(2,1)S(1)} %get-tuple-element.22.far_ref, bf16[128,1024]{1,0:T(8,128)(2,1)S(1)} %collective-permute-done.12.xe_refs_0_, s32[1,128]{1,0:T(1,128)S(1)} %bitcast.8, s32[1,128]{1,0:T(1,128)S(1)} %collective-permute-done.4.c_ids_ref, s32[2,128]{1,0:T(2,128)S(1)} %collective-permute-done.5.e_ids_ref, ...), custom_call_target="tpu_custom_call" | custom-call | tf_op jit(solution)/shard_map/late/pallas_call | solution.py:229
  23.8 2.3 %collective-permute-start.13 = (f32[8,128]{1,0:T(8,128)S(1)}, f32[8,128]{1,0:T(8,128)S(1)}, u32[]{:S(2)}, u32[]{:S(2)}) collective-permute-start(f32[8,128]{1,0:T(8,128)S(1)} %late.1), channel_id=1, source_target_pairs={{0,6},{1,7},{2,4},{3,5},{4,2},{5,3},{6,0},{7,1},{8,14},{9,15},{10,... | collective-permute-start | bytes 12296 | tf_op jit(solution)/shard_map/ppermute | solution.py:241
  26.1 0.0 collective-permute-done.10
  26.1 0.0 collective-permute-done.11
  26.1 2.3 %collective-permute-done.13 = f32[8,128]{1,0:T(8,128)S(1)} collective-permute-done((f32[8,128]{1,0:T(8,128)S(1)}, f32[8,128]{1,0:T(8,128)S(1)}, u32[]{:S(2)}, u32[]{:S(2)}) %collective-permute-start.13) | collective-permute-done | bytes 4128 | tf_op jit(solution)/shard_map/ppermute | solution.py:241
  28.4 0.5 %slice_bitcast_fusion = f32[128]{0:T(128)} fusion(f32[8,128]{1,0:T(8,128)S(1)} %maximum_maximum_fusion), kind=kLoop, calls=%fused_computation.3 | loop fusion | bytes 1024 | tf_op jit(solution)/shard_map/squeeze | solution.py:261
  (3 shorter events, 0.0 us)
Async XLA Ops:
  0.0 7.2 %copy-start.1 = (s32[128,1]{0,1:T(1,128)S(1)}, s32[128,1]{0,1:T(1,128)}, u32[]{:S(2)}) copy-start(s32[128,1]{0,1:T(1,128)} %param.3) | copy-start | bytes 1540
  0.0 4.6 %collective-permute-start.2 = (bf16[128,1024]{1,0:T(8,128)(2,1)}, bf16[128,1024]{1,0:T(8,128)(2,1)S(1)}, u32[]{:S(2)}, u32[]{:S(2)}) collective-permute-start(bf16[128,1024]{1,0:T(8,128)(2,1)} %mine_ref.1), channel_id=1, source_target_pairs={{0,1},{1,0},{2,3},{3,2},{4,5},{5,4},{6,7},{7,6},{8,9},{9,8},{10,11... | collective-permute-start | bytes 786440 | tf_op jit(solution)/shard_map/ppermute | solution.py:241
  0.5 14.3 %collective-permute-start.1 = (bf16[128,1024]{1,0:T(8,128)(2,1)}, bf16[128,1024]{1,0:T(8,128)(2,1)S(1)}, u32[]{:S(2)}, u32[]{:S(2)}) collective-permute-start(bf16[128,1024]{1,0:T(8,128)(2,1)} %mine_ref.1), channel_id=1, source_target_pairs={{0,4},{1,5},{2,6},{3,7},{4,0},{5,1},{6,2},{7,3},{8,12},{9,13},{10,... | collective-permute-start | bytes 786440 | tf_op jit(solution)/shard_map/ppermute | solution.py:241
  3.1 16.5 %collective-permute-start = (bf16[128,1024]{1,0:T(8,128)(2,1)}, bf16[128,1024]{1,0:T(8,128)(2,1)S(1)}, u32[]{:S(2)}, u32[]{:S(2)}) collective-permute-start(bf16[128,1024]{1,0:T(8,128)(2,1)} %mine_ref.1), channel_id=1, source_target_pairs={{0,2},{1,3},{2,0},{3,1},{4,6},{5,7},{6,4},{7,5},{8,10},{9,11},{10,... | collective-permute-start | bytes 786440 | tf_op jit(solution)/shard_map/ppermute | solution.py:241
  4.6 15.0 %collective-permute-start.6 = (bf16[128,1024]{1,0:T(8,128)(2,1)}, bf16[128,1024]{1,0:T(8,128)(2,1)S(1)}, u32[]{:S(2)}, u32[]{:S(2)}) collective-permute-start(bf16[128,1024]{1,0:T(8,128)(2,1)} %mine_ref.1), channel_id=1, source_target_pairs={{0,8},{1,9},{2,10},{3,11},{4,12},{5,13},{6,14},{7,15},{8,0},{9,1},... | collective-permute-start | bytes 786440 | tf_op jit(solution)/shard_map/ppermute | solution.py:241
  7.2 1.1 %collective-permute-start.4 = (s32[1,128]{1,0:T(1,128)S(1)}, s32[1,128]{1,0:T(1,128)S(1)}, u32[]{:S(2)}, u32[]{:S(2)}) collective-permute-start(s32[1,128]{1,0:T(1,128)S(1)} %bitcast.3), channel_id=1, source_target_pairs={{0,1},{1,0},{2,3},{3,2},{4,5},{5,4},{6,7},{7,6},{8,9},{9,8},{10,11... | collective-permute-start | bytes 1544 | tf_op jit(solution)/shard_map/ppermute | solution.py:241
  7.2 4.6 %collective-permute-start.3 = (s32[1,128]{1,0:T(1,128)S(1)}, s32[1,128]{1,0:T(1,128)S(1)}, u32[]{:S(2)}, u32[]{:S(2)}) collective-permute-start(s32[1,128]{1,0:T(1,128)S(1)} %bitcast.4), channel_id=1, source_target_pairs={{0,2},{1,3},{2,0},{3,1},{4,6},{5,7},{6,4},{7,5},{8,10},{9,11},{10,... | collective-permute-start | bytes 1544 | tf_op jit(solution)/shard_map/ppermute | solution.py:241
  11.8 7.8 %collective-permute-start.7 = (s32[2,128]{1,0:T(2,128)S(1)}, s32[2,128]{1,0:T(2,128)S(1)}, u32[]{:S(2)}, u32[]{:S(2)}) collective-permute-start(s32[2,128]{1,0:T(2,128)S(1)} %get-tuple-element.25), channel_id=1, source_target_pairs={{0,8},{1,9},{2,10},{3,11},{4,12},{5,13},{6,14},{7,15},{8,0},{9,1},... | collective-permute-start | bytes 3080 | tf_op jit(solution)/shard_map/ppermute | solution.py:241
  14.3 5.8 %copy-start = (bf16[128,1024]{1,0:T(8,128)(2,1)S(1)}, bf16[128,1024]{1,0:T(8,128)(2,1)}, u32[]{:S(2)}) copy-start(bf16[128,1024]{1,0:T(8,128)(2,1)} %mine_ref.1) | copy-start | bytes 786436
  14.3 5.2 %collective-permute-start.5 = (s32[2,128]{1,0:T(2,128)S(1)}, s32[2,128]{1,0:T(2,128)S(1)}, u32[]{:S(2)}, u32[]{:S(2)}) collective-permute-start(s32[2,128]{1,0:T(2,128)S(1)} %get-tuple-element.26), channel_id=1, source_target_pairs={{0,4},{1,5},{2,6},{3,7},{4,0},{5,1},{6,2},{7,3},{8,12},{9,13},{10,... | collective-permute-start | bytes 3080 | tf_op jit(solution)/shard_map/ppermute | solution.py:241
  14.8 8.4 %collective-permute-start.12 = (bf16[128,1024]{1,0:T(8,128)(2,1)S(1)}, bf16[128,1024]{1,0:T(8,128)(2,1)S(1)}, u32[]{:S(2)}, u32[]{:S(2)}) collective-permute-start(bf16[128,1024]{1,0:T(8,128)(2,1)S(1)} %collective-permute-done.1.e_refs_0_), channel_id=1, source_target_pairs={{0,2},{1,3},{2,0},{3,1},{4,6},{5,7},{6,4},{7,5},{8,10},{9,11},{10,... | collective-permute-start | bytes 786440 | tf_op jit(solution)/shard_map/ppermute | solution.py:241
  19.6 1.4 %collective-permute-start.9 = (bf16[64,1024]{1,0:T(8,128)(2,1)S(1)}, bf16[64,1024]{1,0:T(8,128)(2,1)S(1)}, u32[]{:S(2)}, u32[]{:S(2)}) collective-permute-start(bf16[64,1024]{1,0:T(8,128)(2,1)S(1)} %get-tuple-element.23), channel_id=1, source_target_pairs={{0,1},{1,0},{2,3},{3,2},{4,5},{5,4},{6,7},{7,6},{8,9},{9,8},{10,11... | collective-permute-start | bytes 393224 | tf_op jit(solution)/shard_map/ppermute | solution.py:241
  19.7 1.5 %collective-permute-start.8 = (bf16[64,1024]{1,0:T(8,128)(2,1)S(1)}, bf16[64,1024]{1,0:T(8,128)(2,1)S(1)}, u32[]{:S(2)}, u32[]{:S(2)}) collective-permute-start(bf16[64,1024]{1,0:T(8,128)(2,1)S(1)} %get-tuple-element.24), channel_id=1, source_target_pairs={{0,1},{1,0},{2,3},{3,2},{4,5},{5,4},{6,7},{7,6},{8,9},{9,8},{10,11... | collective-permute-start | bytes 393224 | tf_op jit(solution)/shard_map/ppermute | solution.py:241
  21.9 4.2 %collective-permute-start.10 = (f32[8,128]{1,0:T(8,128)S(1)}, f32[8,128]{1,0:T(8,128)S(1)}, u32[]{:S(2)}, u32[]{:S(2)}) collective-permute-start(f32[8,128]{1,0:T(8,128)S(1)} %get-tuple-element.20), channel_id=1, source_target_pairs={{0,2},{1,3},{2,0},{3,1},{4,6},{5,7},{6,4},{7,5},{8,10},{9,11},{10,... | collective-permute-start | bytes 12296 | tf_op jit(solution)/shard_map/ppermute | solution.py:241
  22.5 3.6 %collective-permute-start.11 = (f32[8,128]{1,0:T(8,128)S(1)}, f32[8,128]{1,0:T(8,128)S(1)}, u32[]{:S(2)}, u32[]{:S(2)}) collective-permute-start(f32[8,128]{1,0:T(8,128)S(1)} %get-tuple-element.21), channel_id=1, source_target_pairs={{0,4},{1,5},{2,6},{3,7},{4,0},{5,1},{6,2},{7,3},{8,12},{9,13},{10,... | collective-permute-start | bytes 12296 | tf_op jit(solution)/shard_map/ppermute | solution.py:241
  23.8 4.6 %collective-permute-start.13 = (f32[8,128]{1,0:T(8,128)S(1)}, f32[8,128]{1,0:T(8,128)S(1)}, u32[]{:S(2)}, u32[]{:S(2)}) collective-permute-start(f32[8,128]{1,0:T(8,128)S(1)} %late.1), channel_id=1, source_target_pairs={{0,6},{1,7},{2,4},{3,5},{4,2},{5,3},{6,0},{7,1},{8,14},{9,15},{10,... | collective-permute-start | bytes 12296 | tf_op jit(solution)/shard_map/ppermute | solution.py:241

commit v14 on v13

--- a/solution.py
+++ b/solution.py
@@ -14,6 +14,7 @@
 LANES = 128
 EMPTY = 4.0
 NONE = -2.0
+TAIL = 8
 HIGH, LOW, SHARD, SUB = 8, 4, 2, 1
 LIMIT = pltpu.CompilerParams(vmem_limit_bytes=12 << 20)
 AXES = ("blk", "shard", "sub")
@@ -164,6 +165,13 @@
     return jnp.concatenate([unit_of(ref[...]) for ref in refs], axis=0)
 
 
+def labelled(refs):
+    last = refs[-1][...]
+    pieces = [ref[...] for ref in refs[:-1]] + [last[: last.shape[0] - TAIL]]
+    rows = jnp.concatenate([unit_of(piece) for piece in pieces], axis=0)
+    return rows, last[last.shape[0] - TAIL :, : rows.shape[0]].astype(jnp.float32)[:1].astype(jnp.int32)
+
+
 def early_kernel(mine_ref, x_refs, e_refs, c_refs, ids_ref, x_ids_ref, c_ids_ref, e_ids_ref, best_ref, own_ref, c_ref):
     mine, c = unit_of(mine_ref[...]), block(c_refs)
     own = jnp.concatenate([mine, block(x_refs), block(e_refs)], axis=0)
@@ -190,18 +198,38 @@
     )(mine, x, e, c, *ids)
 
 
+def label_kernel(rows_ref, ids_ref, out_ref):
+    rows, width = rows_ref.shape
+    out_ref[:rows] = rows_ref[...]
+    ids = jnp.broadcast_to(ids_ref[...].astype(jnp.float32), (TAIL, rows))
+    tail = jnp.concatenate([ids, jnp.zeros((TAIL, width - rows), jnp.float32)], axis=1)
+    out_ref[rows:] = tail.astype(jnp.bfloat16)
+
+
+def label(rows, ids):
+    return pl.pallas_call(
+        label_kernel,
+        out_shape=jax.ShapeDtypeStruct((rows.shape[0] + TAIL, rows.shape[1]), rows.dtype),
+        in_specs=[VMEM, VMEM],
+        out_specs=VMEM,
+        compiler_params=LIMIT,
+        name="label",
+    )(rows, ids)
+
+
 def middle_kernel(
-    best_ref, own_ref, c_ref, h_refs, ch_refs, ids_ref, x_ids_ref, c_ids_ref, e_ids_ref, h_ids_ref,
-    mine_out_ref, x_out_ref, e_out_ref, far_ref,
+    best_ref, own_ref, c_ref, h_refs, ch_refs, ids_ref, x_ids_ref, e_ids_ref,
+    mine_out_ref, x_out_ref, e_out_ref, far_ref, far_ids_ref,
 ):
-    h, ch = block(h_refs), block(ch_refs)
+    (h, h_ids), (ch, ch_ids) = labelled(h_refs), labelled(ch_refs)
     own_ids = jnp.concatenate([ids_ref[...], x_ids_ref[...], e_ids_ref[:1, :]], axis=1)
-    best = best_of(own_ref[...], own_ids, [h, ch], [h_ids_ref[:1, :], h_ids_ref[1:, :]])
+    best = best_of(own_ref[...], own_ids, [h, ch], [h_ids, ch_ids])
     best = jnp.maximum(best, best_ref[:1, :])
     rows = c_ref.shape[0]
     for place, out_ref in enumerate((mine_out_ref, x_out_ref, e_out_ref)):
         out_ref[...] = jnp.broadcast_to(best[:, place * rows : (place + 1) * rows], out_ref.shape)
     far_ref[...] = jnp.concatenate([own_ref[:rows], c_ref[...], h, ch], axis=0)
+    far_ids_ref[...] = jnp.concatenate([h_ids, ch_ids], axis=0)
 
 
 def middle(best, own, c, h, ch, ids):
@@ -209,9 +237,9 @@
     return pl.pallas_call(
         middle_kernel,
         out_shape=[jax.ShapeDtypeStruct((8, rows), jnp.float32)] * 3
-        + [jax.ShapeDtypeStruct((4 * rows, width), jnp.bfloat16)],
+        + [jax.ShapeDtypeStruct((4 * rows, width), jnp.bfloat16), jax.ShapeDtypeStruct((2, rows), jnp.int32)],
         in_specs=(VMEM, VMEM, VMEM, [VMEM] * len(h), [VMEM] * len(ch), *[VMEM] * len(ids)),
-        out_specs=[VMEM] * 4,
+        out_specs=[VMEM] * 5,
         compiler_params=LIMIT,
         name="middle",
     )(best, own, c, h, ch, *ids)
@@ -242,20 +270,19 @@
 
     rows = embeddings.shape[0]
     mine, ids = embeddings, assignment.reshape(1, rows)
-    c = swap(SUB, mine)
     e = swap(LOW, mine)
     x = swap(SHARD, mine)
-    far, _ = lax.optimization_barrier((mine, c))
-    h = swap(HIGH, far)
+    c = swap(SUB, mine)
+    h = swap(HIGH, label(mine, ids))
     x_ids, c_ids = swap(SHARD, ids), swap(SUB, ids)
     e_ids = swap(LOW, jnp.concatenate([ids, x_ids]))
-    h_ids = swap(HIGH, jnp.concatenate([ids, c_ids]))
-    xe = swap(SHARD, e)
-    h_then, _, _, _ = lax.optimization_barrier((h, h_ids, e_ids, x))
+    e_then, _, _ = lax.optimization_barrier((e, x, x_ids))
+    xe = swap(SHARD, e_then)
+    h_then, *_ = lax.optimization_barrier((h, e_ids, x, c_ids, c))
     ch = [swap(SUB, h_then[: rows // 2]), swap(SUB, h_then[rows // 2 :])]
     x, e, h, c, xe = [x], [e], [h], [c], [xe]
     best, own, c = early(mine, x, e, c, [ids, x_ids, c_ids, e_ids])
-    found, x_best, e_best, far = middle(best, own, c, h, ch, [ids, x_ids, c_ids, e_ids, h_ids])
+    found, x_best, e_best, far, h_ids = middle(best, own, c, h, ch, [ids, x_ids, e_ids])
     x_best, e_best = swap(SHARD, x_best), swap(LOW, e_best)
     xe_best = swap(LOW | SHARD, late(far, xe, [ids, c_ids, e_ids, h_ids]))
     return jnp.maximum(jnp.maximum(found, x_best), jnp.maximum(e_best, xe_best))[0]

time: 29 us -> 29.2 us (level)
  starting transfers between devices: 17.1 us -> 14.8 us
  waiting for transfers between devices: 9.05 us -> 10.5 us
  local copies, waits for them, and re-layouts: 0.54 us -> 1.52 us
    ppermute x14 -> x13, starting transfers between devices: 17.1 us -> 14.8 us  [swap(): return lax.ppermute(array, AXES, [(i, i ^ flip) for i in range(16)])]
    ppermute x14 -> x13, waiting for transfers between devices: 9.05 us -> 10.5 us  [swap(): return lax.ppermute(array, AXES, [(i, i ^ flip) for i in range(16)])]
    unnamed x4, local copies, waits for them, and re-layouts: 0.01 us -> 0.98 us
  transfers between devices with their start and end apart: 14 -> 13, of which waited for: 6 -> 7; matrix products, arithmetic and copies ran while one was open for 0% -> 0% of each run, Pallas kernels for 7% -> 7%
where the time goes in v14:
time: 29.2 us; the launch traced here: 29 us
  starting transfers between devices  14.8 us (51%)
  waiting for transfers between devices  10.5 us (36%)
  Pallas kernels  2.11 us (7%)
  local copies, waits for them, and re-layouts  1.52 us (5%)
    ppermute x13, starting transfers between devices, swap(): return lax.ppermute(array, AXES, [(i, i ^ flip) for i in range(16)])  14.8 us
    ppermute x13, waiting for transfers between devices, swap(): return lax.ppermute(array, AXES, [(i, i ^ flip) for i in range(16)])  10.5 us
    unnamed x4, local copies, waits for them, and re-layouts  0.98 us
    pallas_call x1, Pallas kernels, early(): pl.pallas_call(early_kernel, out_shape=[jax.ShapeDtypeStruct((8, 3 * rows...  0.84 us
    pallas_call x1, Pallas kernels, middle(): pl.pallas_call(middle_kernel, out_shape=[jax.ShapeDtypeStruct((8, rows),...  0.69 us
  transfers between devices with their start and end apart: 13, of which 7 were waited for; matrix products, arithmetic and copies ran while one was open for 0% of the time, Pallas kernels for 7%

profile of v14, /device:TPU:0, one launch (start us, length us, event | category | flops | bytes accessed | tf_op | source)
XLA Modules:
  0.0 29.0 jit_solution(10583437645340460245)
XLA Ops:
  0.0 0.0 copy-start.1
  0.0 3.0 %collective-permute-start.1 = (bf16[128,1024]{1,0:T(8,128)(2,1)}, bf16[128,1024]{1,0:T(8,128)(2,1)S(1)}, u32[]{:S(2)}, u32[]{:S(2)}) collective-permute-start(bf16[128,1024]{1,0:T(8,128)(2,1)} %rows_ref.1), channel_id=1, source_target_pairs={{0,4},{1,5},{2,6},{3,7},{4,0},{5,1},{6,2},{7,3},{8,12},{9,13},{10,... | collective-permute-start | bytes 786440 | tf_op jit(solution)/shard_map/ppermute | solution.py:269
  3.0 1.5 %collective-permute-start = (bf16[128,1024]{1,0:T(8,128)(2,1)}, bf16[128,1024]{1,0:T(8,128)(2,1)S(1)}, u32[]{:S(2)}, u32[]{:S(2)}) collective-permute-start(bf16[128,1024]{1,0:T(8,128)(2,1)} %rows_ref.1), channel_id=1, source_target_pairs={{0,2},{1,3},{2,0},{3,1},{4,6},{5,7},{6,4},{7,5},{8,10},{9,11},{10,... | collective-permute-start | bytes 786440 | tf_op jit(solution)/shard_map/ppermute | solution.py:269
  4.5 0.0 copy-done.1
  4.5 0.0 copy-start
  4.5 1.0 %copy-done = bf16[128,1024]{1,0:T(8,128)(2,1)S(1)} copy-done((bf16[128,1024]{1,0:T(8,128)(2,1)S(1)}, bf16[128,1024]{1,0:T(8,128)(2,1)}, u32[]{:S(2)}) %copy-start) | copy-done | bytes 262168
  5.5 2.7 %collective-permute-start.6 = (bf16[136,1024]{1,0:T(8,128)(2,1)S(1)}, bf16[136,1024]{1,0:T(8,128)(2,1)S(1)}, u32[]{:S(2)}, u32[]{:S(2)}) collective-permute-start(bf16[136,1024]{1,0:T(8,128)(2,1)S(1)} %label.1), channel_id=1, source_target_pairs={{0,8},{1,9},{2,10},{3,11},{4,12},{5,13},{6,14},{7,15},{8,0},{9,1},... | collective-permute-start | bytes 835592 | tf_op jit(solution)/shard_map/ppermute | solution.py:269
  8.2 0.0 collective-permute-start.2
  8.2 0.5 %collective-permute-start.3 = (s32[1,128]{1,0:T(1,128)S(1)}, s32[1,128]{1,0:T(1,128)S(1)}, u32[]{:S(2)}, u32[]{:S(2)}) collective-permute-start(s32[1,128]{1,0:T(1,128)S(1)} %bitcast.4), channel_id=1, source_target_pairs={{0,2},{1,3},{2,0},{3,1},{4,6},{5,7},{6,4},{7,5},{8,10},{9,11},{10,... | collective-permute-start | bytes 1544 | tf_op jit(solution)/shard_map/ppermute | solution.py:269
  8.7 3.0 %collective-permute-done.3.x_ids_ref = s32[1,128]{1,0:T(1,128)S(1)} collective-permute-done((s32[1,128]{1,0:T(1,128)S(1)}, s32[1,128]{1,0:T(1,128)S(1)}, u32[]{:S(2)}, u32[]{:S(2)}) %collective-permute-start.3) | collective-permute-done | bytes 544 | tf_op jit(solution)/shard_map/ppermute | solution.py:269
  11.7 1.1 %collective-permute-done.1.e_refs_0_ = bf16[128,1024]{1,0:T(8,128)(2,1)S(1)} collective-permute-done((bf16[128,1024]{1,0:T(8,128)(2,1)}, bf16[128,1024]{1,0:T(8,128)(2,1)S(1)}, u32[]{:S(2)}, u32[]{:S(2)}) %collective-permute-start.1) | collective-permute-done | bytes 262176 | tf_op jit(solution)/shard_map/ppermute | solution.py:269
  12.9 0.0 collective-permute-done.x_refs_0_
  12.9 2.7 %collective-permute-start.11 = (bf16[128,1024]{1,0:T(8,128)(2,1)S(1)}, bf16[128,1024]{1,0:T(8,128)(2,1)S(1)}, u32[]{:S(2)}, u32[]{:S(2)}) collective-permute-start(bf16[128,1024]{1,0:T(8,128)(2,1)S(1)} %collective-permute-done.1.e_refs_0_), channel_id=1, source_target_pairs={{0,2},{1,3},{2,0},{3,1},{4,6},{5,7},{6,4},{7,5},{8,10},{9,11},{10,... | collective-permute-start | bytes 786440 | tf_op jit(solution)/shard_map/ppermute | solution.py:269
  15.6 0.0 collective-permute-start.5
  15.6 0.1 collective-permute-start.4
  15.7 1.1 %collective-permute-done.4.c_ids_ref = s32[1,128]{1,0:T(1,128)S(1)} collective-permute-done((s32[1,128]{1,0:T(1,128)S(1)}, s32[1,128]{1,0:T(1,128)S(1)}, u32[]{:S(2)}, u32[]{:S(2)}) %collective-permute-start.4) | collective-permute-done | bytes 544 | tf_op jit(solution)/shard_map/ppermute | solution.py:269
  16.8 2.5 %collective-permute-done.5.e_ids_ref = s32[2,128]{1,0:T(2,128)S(1)} collective-permute-done((s32[2,128]{1,0:T(2,128)S(1)}, s32[2,128]{1,0:T(2,128)S(1)}, u32[]{:S(2)}, u32[]{:S(2)}) %collective-permute-start.5) | collective-permute-done | bytes 1056 | tf_op jit(solution)/shard_map/ppermute | solution.py:269
  19.3 0.0 collective-permute-done.2.c_refs_0_
  19.3 1.1 %collective-permute-done.6.h_refs_0_ = bf16[136,1024]{1,0:T(8,128)(2,1)S(1)} collective-permute-done((bf16[136,1024]{1,0:T(8,128)(2,1)S(1)}, bf16[136,1024]{1,0:T(8,128)(2,1)S(1)}, u32[]{:S(2)}, u32[]{:S(2)}) %collective-permute-start.6) | collective-permute-done | bytes 278560 | tf_op jit(solution)/shard_map/ppermute | solution.py:269
  20.4 0.1 collective-permute-start.8
  20.5 0.6 %collective-permute-start.7 = (bf16[64,1024]{1,0:T(8,128)(2,1)S(1)}, bf16[64,1024]{1,0:T(8,128)(2,1)S(1)}, u32[]{:S(2)}, u32[]{:S(2)}) collective-permute-start(bf16[64,1024]{1,0:T(8,128)(2,1)S(1)} %slice.9), channel_id=1, source_target_pairs={{0,1},{1,0},{2,3},{3,2},{4,5},{5,4},{6,7},{7,6},{8,9},{9,8},{10,11... | collective-permute-start | bytes 393224 | tf_op jit(solution)/shard_map/ppermute | solution.py:269
  21.0 0.8 %early.1 = (f32[8,384]{1,0:T(8,128)S(1)}, bf16[384,1024]{1,0:T(8,128)(2,1)S(1)}, bf16[128,1024]{1,0:T(8,128)(2,1)S(1)}) custom-call(bf16[128,1024]{1,0:T(8,128)(2,1)S(1)} %copy-done, bf16[128,1024]{1,0:T(8,128)(2,1)S(1)} %collective-permute-done.x_refs_0_, bf16[128,1024]{1,0:T(8,128)(2,1)S(1)} %collective-permute-done.1.e_refs_0_, ...), custom_call_target="tpu_custom_call" | custom-call | tf_op jit(solution)/shard_map/early/pallas_call | solution.py:187
  21.9 0.1 collective-permute-done.7.ch_refs_0_
  22.0 0.0 collective-permute-done.8.ch_refs_1_
  22.0 0.7 %middle.1 = (f32[8,128]{1,0:T(8,128)S(1)}, f32[8,128]{1,0:T(8,128)S(1)}, f32[8,128]{1,0:T(8,128)S(1)}, bf16[512,1024]{1,0:T(8,128)(2,1)S(1)}, s32[2,128]{1,0:T(2,128)S(1)}) custom-call(f32[8,384]{1,0:T(8,128)S(1)} %get-tuple-element.15.best_ref, bf16[384,1024]{1,0:T(8,128)(2,1)S(1)} %get-tuple-element.16.own_ref, ...), custom_call_target="tpu_custom_call" | custom-call | tf_op jit(solution)/shard_map/middle/pallas_call | solution.py:237
  22.7 0.6 %collective-permute-start.9 = (f32[8,128]{1,0:T(8,128)S(1)}, f32[8,128]{1,0:T(8,128)S(1)}, u32[]{:S(2)}, u32[]{:S(2)}) collective-permute-start(f32[8,128]{1,0:T(8,128)S(1)} %get-tuple-element.20), channel_id=1, source_target_pairs={{0,2},{1,3},{2,0},{3,1},{4,6},{5,7},{6,4},{7,5},{8,10},{9,11},{10,... | collective-permute-start | bytes 12296 | tf_op jit(solution)/shard_map/ppermute | solution.py:269
  23.3 0.0 collective-permute-start.10
  23.3 0.0 collective-permute-done.11.xe_refs_0_
  23.3 0.6 %late.1 = f32[8,128]{1,0:T(8,128)S(1)} custom-call(bf16[512,1024]{1,0:T(8,128)(2,1)S(1)} %get-tuple-element.22.far_ref, bf16[128,1024]{1,0:T(8,128)(2,1)S(1)} %collective-permute-done.11.xe_refs_0_, s32[1,128]{1,0:T(1,128)S(1)} %bitcast.9, s32[1,128]{1,0:T(1,128)S(1)} %collective-permute-done.4.c_ids_ref, s32[2,128]{1,0:T(2,128)S(1)} %collective-permute-done.5.e_ids_ref, ...), custom_call_target="tpu_custom_call" | custom-call | tf_op jit(solution)/shard_map/late/pallas_call | solution.py:257
  23.9 3.0 %collective-permute-start.12 = (f32[8,128]{1,0:T(8,128)S(1)}, f32[8,128]{1,0:T(8,128)S(1)}, u32[]{:S(2)}, u32[]{:S(2)}) collective-permute-start(f32[8,128]{1,0:T(8,128)S(1)} %late.1), channel_id=1, source_target_pairs={{0,6},{1,7},{2,4},{3,5},{4,2},{5,3},{6,0},{7,1},{8,14},{9,15},{10,... | collective-permute-start | bytes 12296 | tf_op jit(solution)/shard_map/ppermute | solution.py:269
  26.9 0.0 collective-permute-done.9
  26.9 0.0 collective-permute-done.10
  26.9 1.6 %collective-permute-done.12 = f32[8,128]{1,0:T(8,128)S(1)} collective-permute-done((f32[8,128]{1,0:T(8,128)S(1)}, f32[8,128]{1,0:T(8,128)S(1)}, u32[]{:S(2)}, u32[]{:S(2)}) %collective-permute-start.12) | collective-permute-done | bytes 4128 | tf_op jit(solution)/shard_map/ppermute | solution.py:269
  28.5 0.5 %slice_bitcast_fusion = f32[128]{0:T(128)} fusion(f32[8,128]{1,0:T(8,128)S(1)} %maximum_maximum_fusion), kind=kLoop, calls=%fused_computation.2 | loop fusion | bytes 1024 | tf_op jit(solution)/shard_map/squeeze | solution.py:288
  (5 shorter events, 0.1 us)
Async XLA Ops:
  0.0 4.5 %copy-start.1 = (s32[128,1]{0,1:T(1,128)S(1)}, s32[128,1]{0,1:T(1,128)}, u32[]{:S(2)}) copy-start(s32[128,1]{0,1:T(1,128)} %param.3) | copy-start | bytes 1540
  0.0 12.9 %collective-permute-start.1 = (bf16[128,1024]{1,0:T(8,128)(2,1)}, bf16[128,1024]{1,0:T(8,128)(2,1)S(1)}, u32[]{:S(2)}, u32[]{:S(2)}) collective-permute-start(bf16[128,1024]{1,0:T(8,128)(2,1)} %rows_ref.1), channel_id=1, source_target_pairs={{0,4},{1,5},{2,6},{3,7},{4,0},{5,1},{6,2},{7,3},{8,12},{9,13},{10,... | collective-permute-start | bytes 786440 | tf_op jit(solution)/shard_map/ppermute | solution.py:269
  3.0 9.8 %collective-permute-start = (bf16[128,1024]{1,0:T(8,128)(2,1)}, bf16[128,1024]{1,0:T(8,128)(2,1)S(1)}, u32[]{:S(2)}, u32[]{:S(2)}) collective-permute-start(bf16[128,1024]{1,0:T(8,128)(2,1)} %rows_ref.1), channel_id=1, source_target_pairs={{0,2},{1,3},{2,0},{3,1},{4,6},{5,7},{6,4},{7,5},{8,10},{9,11},{10,... | collective-permute-start | bytes 786440 | tf_op jit(solution)/shard_map/ppermute | solution.py:269
  4.5 1.0 %copy-start = (bf16[128,1024]{1,0:T(8,128)(2,1)S(1)}, bf16[128,1024]{1,0:T(8,128)(2,1)}, u32[]{:S(2)}) copy-start(bf16[128,1024]{1,0:T(8,128)(2,1)} %rows_ref.1) | copy-start | bytes 786436
  5.5 14.8 %collective-permute-start.6 = (bf16[136,1024]{1,0:T(8,128)(2,1)S(1)}, bf16[136,1024]{1,0:T(8,128)(2,1)S(1)}, u32[]{:S(2)}, u32[]{:S(2)}) collective-permute-start(bf16[136,1024]{1,0:T(8,128)(2,1)S(1)} %label.1), channel_id=1, source_target_pairs={{0,8},{1,9},{2,10},{3,11},{4,12},{5,13},{6,14},{7,15},{8,0},{9,1},... | collective-permute-start | bytes 835592 | tf_op jit(solution)/shard_map/ppermute | solution.py:269
  8.2 11.1 %collective-permute-start.2 = (bf16[128,1024]{1,0:T(8,128)(2,1)S(1)}, bf16[128,1024]{1,0:T(8,128)(2,1)S(1)}, u32[]{:S(2)}, u32[]{:S(2)}) collective-permute-start(bf16[128,1024]{1,0:T(8,128)(2,1)S(1)} %copy-done), channel_id=1, source_target_pairs={{0,1},{1,0},{2,3},{3,2},{4,5},{5,4},{6,7},{7,6},{8,9},{9,8},{10,11... | collective-permute-start | bytes 786440 | tf_op jit(solution)/shard_map/ppermute | solution.py:269
  8.2 3.5 %collective-permute-start.3 = (s32[1,128]{1,0:T(1,128)S(1)}, s32[1,128]{1,0:T(1,128)S(1)}, u32[]{:S(2)}, u32[]{:S(2)}) collective-permute-start(s32[1,128]{1,0:T(1,128)S(1)} %bitcast.4), channel_id=1, source_target_pairs={{0,2},{1,3},{2,0},{3,1},{4,6},{5,7},{6,4},{7,5},{8,10},{9,11},{10,... | collective-permute-start | bytes 1544 | tf_op jit(solution)/shard_map/ppermute | solution.py:269
  12.9 10.5 %collective-permute-start.11 = (bf16[128,1024]{1,0:T(8,128)(2,1)S(1)}, bf16[128,1024]{1,0:T(8,128)(2,1)S(1)}, u32[]{:S(2)}, u32[]{:S(2)}) collective-permute-start(bf16[128,1024]{1,0:T(8,128)(2,1)S(1)} %collective-permute-done.1.e_refs_0_), channel_id=1, source_target_pairs={{0,2},{1,3},{2,0},{3,1},{4,6},{5,7},{6,4},{7,5},{8,10},{9,11},{10,... | collective-permute-start | bytes 786440 | tf_op jit(solution)/shard_map/ppermute | solution.py:269
  15.6 3.7 %collective-permute-start.5 = (s32[2,128]{1,0:T(2,128)S(1)}, s32[2,128]{1,0:T(2,128)S(1)}, u32[]{:S(2)}, u32[]{:S(2)}) collective-permute-start(s32[2,128]{1,0:T(2,128)S(1)} %pad_add_fusion), channel_id=1, source_target_pairs={{0,4},{1,5},{2,6},{3,7},{4,0},{5,1},{6,2},{7,3},{8,12},{9,13},{10,... | collective-permute-start | bytes 3080 | tf_op jit(solution)/shard_map/ppermute | solution.py:269
  15.6 1.2 %collective-permute-start.4 = (s32[1,128]{1,0:T(1,128)S(1)}, s32[1,128]{1,0:T(1,128)S(1)}, u32[]{:S(2)}, u32[]{:S(2)}) collective-permute-start(s32[1,128]{1,0:T(1,128)S(1)} %bitcast.6), channel_id=1, source_target_pairs={{0,1},{1,0},{2,3},{3,2},{4,5},{5,4},{6,7},{7,6},{8,9},{9,8},{10,11... | collective-permute-start | bytes 1544 | tf_op jit(solution)/shard_map/ppermute | solution.py:269
  20.4 1.6 %collective-permute-start.8 = (bf16[72,1024]{1,0:T(8,128)(2,1)S(1)}, bf16[72,1024]{1,0:T(8,128)(2,1)S(1)}, u32[]{:S(2)}, u32[]{:S(2)}) collective-permute-start(bf16[72,1024]{1,0:T(8,128)(2,1)S(1)} %slice.10), channel_id=1, source_target_pairs={{0,1},{1,0},{2,3},{3,2},{4,5},{5,4},{6,7},{7,6},{8,9},{9,8},{10,11... | collective-permute-start | bytes 442376 | tf_op jit(solution)/shard_map/ppermute | solution.py:269
  20.5 1.5 %collective-permute-start.7 = (bf16[64,1024]{1,0:T(8,128)(2,1)S(1)}, bf16[64,1024]{1,0:T(8,128)(2,1)S(1)}, u32[]{:S(2)}, u32[]{:S(2)}) collective-permute-start(bf16[64,1024]{1,0:T(8,128)(2,1)S(1)} %slice.9), channel_id=1, source_target_pairs={{0,1},{1,0},{2,3},{3,2},{4,5},{5,4},{6,7},{7,6},{8,9},{9,8},{10,11... | collective-permute-start | bytes 393224 | tf_op jit(solution)/shard_map/ppermute | solution.py:269
  22.7 4.2 %collective-permute-start.9 = (f32[8,128]{1,0:T(8,128)S(1)}, f32[8,128]{1,0:T(8,128)S(1)}, u32[]{:S(2)}, u32[]{:S(2)}) collective-permute-start(f32[8,128]{1,0:T(8,128)S(1)} %get-tuple-element.20), channel_id=1, source_target_pairs={{0,2},{1,3},{2,0},{3,1},{4,6},{5,7},{6,4},{7,5},{8,10},{9,11},{10,... | collective-permute-start | bytes 12296 | tf_op jit(solution)/shard_map/ppermute | solution.py:269
  23.3 3.6 %collective-permute-start.10 = (f32[8,128]{1,0:T(8,128)S(1)}, f32[8,128]{1,0:T(8,128)S(1)}, u32[]{:S(2)}, u32[]{:S(2)}) collective-permute-start(f32[8,128]{1,0:T(8,128)S(1)} %get-tuple-element.21), channel_id=1, source_target_pairs={{0,4},{1,5},{2,6},{3,7},{4,0},{5,1},{6,2},{7,3},{8,12},{9,13},{10,... | collective-permute-start | bytes 12296 | tf_op jit(solution)/shard_map/ppermute | solution.py:269
  23.9 4.6 %collective-permute-start.12 = (f32[8,128]{1,0:T(8,128)S(1)}, f32[8,128]{1,0:T(8,128)S(1)}, u32[]{:S(2)}, u32[]{:S(2)}) collective-permute-start(f32[8,128]{1,0:T(8,128)S(1)} %late.1), channel_id=1, source_target_pairs={{0,6},{1,7},{2,4},{3,5},{4,2},{5,3},{6,0},{7,1},{8,14},{9,15},{10,... | collective-permute-start | bytes 12296 | tf_op jit(solution)/shard_map/ppermute | solution.py:269

commit v15 on v14

--- a/solution.py
+++ b/solution.py
@@ -283,9 +283,10 @@
     x, e, h, c, xe = [x], [e], [h], [c], [xe]
     best, own, c = early(mine, x, e, c, [ids, x_ids, c_ids, e_ids])
     found, x_best, e_best, far, h_ids = middle(best, own, c, h, ch, [ids, x_ids, e_ids])
-    x_best, e_best = swap(SHARD, x_best), swap(LOW, e_best)
-    xe_best = swap(LOW | SHARD, late(far, xe, [ids, c_ids, e_ids, h_ids]))
-    return jnp.maximum(jnp.maximum(found, x_best), jnp.maximum(e_best, xe_best))[0]
+    xe_best = late(far, xe, [ids, c_ids, e_ids, h_ids])
+    x_best, e_best, xe_best = lax.optimization_barrier((x_best, e_best, xe_best))
+    xe_best, e_best, x_best = swap(LOW | SHARD, xe_best), swap(LOW, e_best), swap(SHARD, x_best)
+    return jnp.maximum(jnp.maximum(jnp.maximum(xe_best, e_best), x_best), found)[0]
 
 
 def shared_owner(embeddings, assignment):

time: 29.2 us -> 29.6 us (1.014)
  waiting for transfers between devices: 10.5 us -> 11.1 us
    ppermute x13, waiting for transfers between devices: 10.5 us -> 11.1 us  [swap(): return lax.ppermute(array, AXES, [(i, i ^ flip) for i in range(16)])]
  transfers between devices with their start and end apart: 13 -> 13, of which waited for: 7 -> 8; matrix products, arithmetic and copies ran while one was open for 0% -> 0% of each run, Pallas kernels for 7% -> 5%
where the time goes in v15:
time: 29.6 us; the launch traced here: 29.5 us
  starting transfers between devices  14.7 us (50%)
  waiting for transfers between devices  11.1 us (38%)
  Pallas kernels  2.12 us (7%)
  local copies, waits for them, and re-layouts  1.52 us (5%)
    ppermute x13, starting transfers between devices, swap(): return lax.ppermute(array, AXES, [(i, i ^ flip) for i in range(16)])  14.7 us
    ppermute x13, waiting for transfers between devices, swap(): return lax.ppermute(array, AXES, [(i, i ^ flip) for i in range(16)])  11.1 us
    unnamed x4, local copies, waits for them, and re-layouts  0.98 us
    pallas_call x1, Pallas kernels, early(): pl.pallas_call(early_kernel, out_shape=[jax.ShapeDtypeStruct((8, 3 * rows...  0.84 us
    pallas_call x1, Pallas kernels, middle(): pl.pallas_call(middle_kernel, out_shape=[jax.ShapeDtypeStruct((8, rows),...  0.69 us
  transfers between devices with their start and end apart: 13, of which 8 were waited for; matrix products, arithmetic and copies ran while one was open for 0% of the time, Pallas kernels for 5%

profile of v15, /device:TPU:0, one launch (start us, length us, event | category | flops | bytes accessed | tf_op | source)
XLA Modules:
  0.0 29.5 jit_solution(9610507791295936787)
XLA Ops:
  0.0 0.0 copy-start.1
  0.0 3.0 %collective-permute-start.1 = (bf16[128,1024]{1,0:T(8,128)(2,1)}, bf16[128,1024]{1,0:T(8,128)(2,1)S(1)}, u32[]{:S(2)}, u32[]{:S(2)}) collective-permute-start(bf16[128,1024]{1,0:T(8,128)(2,1)} %rows_ref.1), channel_id=1, source_target_pairs={{0,4},{1,5},{2,6},{3,7},{4,0},{5,1},{6,2},{7,3},{8,12},{9,13},{10,... | collective-permute-start | bytes 786440 | tf_op jit(solution)/shard_map/ppermute | solution.py:269
  3.0 1.5 %collective-permute-start = (bf16[128,1024]{1,0:T(8,128)(2,1)}, bf16[128,1024]{1,0:T(8,128)(2,1)S(1)}, u32[]{:S(2)}, u32[]{:S(2)}) collective-permute-start(bf16[128,1024]{1,0:T(8,128)(2,1)} %rows_ref.1), channel_id=1, source_target_pairs={{0,2},{1,3},{2,0},{3,1},{4,6},{5,7},{6,4},{7,5},{8,10},{9,11},{10,... | collective-permute-start | bytes 786440 | tf_op jit(solution)/shard_map/ppermute | solution.py:269
  4.5 0.0 copy-done.1
  4.5 0.0 copy-start
  4.5 1.0 %copy-done = bf16[128,1024]{1,0:T(8,128)(2,1)S(1)} copy-done((bf16[128,1024]{1,0:T(8,128)(2,1)S(1)}, bf16[128,1024]{1,0:T(8,128)(2,1)}, u32[]{:S(2)}) %copy-start) | copy-done | bytes 262168
  5.5 2.7 %collective-permute-start.6 = (bf16[136,1024]{1,0:T(8,128)(2,1)S(1)}, bf16[136,1024]{1,0:T(8,128)(2,1)S(1)}, u32[]{:S(2)}, u32[]{:S(2)}) collective-permute-start(bf16[136,1024]{1,0:T(8,128)(2,1)S(1)} %label.1), channel_id=1, source_target_pairs={{0,8},{1,9},{2,10},{3,11},{4,12},{5,13},{6,14},{7,15},{8,0},{9,1},... | collective-permute-start | bytes 835592 | tf_op jit(solution)/shard_map/ppermute | solution.py:269
  8.2 0.0 collective-permute-start.2
  8.2 0.5 %collective-permute-start.3 = (s32[1,128]{1,0:T(1,128)S(1)}, s32[1,128]{1,0:T(1,128)S(1)}, u32[]{:S(2)}, u32[]{:S(2)}) collective-permute-start(s32[1,128]{1,0:T(1,128)S(1)} %bitcast.4), channel_id=1, source_target_pairs={{0,2},{1,3},{2,0},{3,1},{4,6},{5,7},{6,4},{7,5},{8,10},{9,11},{10,... | collective-permute-start | bytes 1544 | tf_op jit(solution)/shard_map/ppermute | solution.py:269
  8.7 3.0 %collective-permute-done.3.x_ids_ref = s32[1,128]{1,0:T(1,128)S(1)} collective-permute-done((s32[1,128]{1,0:T(1,128)S(1)}, s32[1,128]{1,0:T(1,128)S(1)}, u32[]{:S(2)}, u32[]{:S(2)}) %collective-permute-start.3) | collective-permute-done | bytes 544 | tf_op jit(solution)/shard_map/ppermute | solution.py:269
  11.7 1.1 %collective-permute-done.1.e_refs_0_ = bf16[128,1024]{1,0:T(8,128)(2,1)S(1)} collective-permute-done((bf16[128,1024]{1,0:T(8,128)(2,1)}, bf16[128,1024]{1,0:T(8,128)(2,1)S(1)}, u32[]{:S(2)}, u32[]{:S(2)}) %collective-permute-start.1) | collective-permute-done | bytes 262176 | tf_op jit(solution)/shard_map/ppermute | solution.py:269
  12.9 0.0 collective-permute-done.x_refs_0_
  12.9 2.7 %collective-permute-start.9 = (bf16[128,1024]{1,0:T(8,128)(2,1)S(1)}, bf16[128,1024]{1,0:T(8,128)(2,1)S(1)}, u32[]{:S(2)}, u32[]{:S(2)}) collective-permute-start(bf16[128,1024]{1,0:T(8,128)(2,1)S(1)} %collective-permute-done.1.e_refs_0_), channel_id=1, source_target_pairs={{0,2},{1,3},{2,0},{3,1},{4,6},{5,7},{6,4},{7,5},{8,10},{9,11},{10,... | collective-permute-start | bytes 786440 | tf_op jit(solution)/shard_map/ppermute | solution.py:269
  15.6 0.0 collective-permute-start.5
  15.6 0.1 collective-permute-start.4
  15.7 1.1 %collective-permute-done.4.c_ids_ref = s32[1,128]{1,0:T(1,128)S(1)} collective-permute-done((s32[1,128]{1,0:T(1,128)S(1)}, s32[1,128]{1,0:T(1,128)S(1)}, u32[]{:S(2)}, u32[]{:S(2)}) %collective-permute-start.4) | collective-permute-done | bytes 544 | tf_op jit(solution)/shard_map/ppermute | solution.py:269
  16.8 2.5 %collective-permute-done.5.e_ids_ref = s32[2,128]{1,0:T(2,128)S(1)} collective-permute-done((s32[2,128]{1,0:T(2,128)S(1)}, s32[2,128]{1,0:T(2,128)S(1)}, u32[]{:S(2)}, u32[]{:S(2)}) %collective-permute-start.5) | collective-permute-done | bytes 1056 | tf_op jit(solution)/shard_map/ppermute | solution.py:269
  19.3 0.0 collective-permute-done.2.c_refs_0_
  19.3 1.1 %collective-permute-done.6.h_refs_0_ = bf16[136,1024]{1,0:T(8,128)(2,1)S(1)} collective-permute-done((bf16[136,1024]{1,0:T(8,128)(2,1)S(1)}, bf16[136,1024]{1,0:T(8,128)(2,1)S(1)}, u32[]{:S(2)}, u32[]{:S(2)}) %collective-permute-start.6) | collective-permute-done | bytes 278560 | tf_op jit(solution)/shard_map/ppermute | solution.py:269
  20.4 0.1 collective-permute-start.8
  20.5 0.6 %collective-permute-start.7 = (bf16[64,1024]{1,0:T(8,128)(2,1)S(1)}, bf16[64,1024]{1,0:T(8,128)(2,1)S(1)}, u32[]{:S(2)}, u32[]{:S(2)}) collective-permute-start(bf16[64,1024]{1,0:T(8,128)(2,1)S(1)} %slice.9), channel_id=1, source_target_pairs={{0,1},{1,0},{2,3},{3,2},{4,5},{5,4},{6,7},{7,6},{8,9},{9,8},{10,11... | collective-permute-start | bytes 393224 | tf_op jit(solution)/shard_map/ppermute | solution.py:269
  21.0 0.8 %early.1 = (f32[8,384]{1,0:T(8,128)S(1)}, bf16[384,1024]{1,0:T(8,128)(2,1)S(1)}, bf16[128,1024]{1,0:T(8,128)(2,1)S(1)}) custom-call(bf16[128,1024]{1,0:T(8,128)(2,1)S(1)} %copy-done, bf16[128,1024]{1,0:T(8,128)(2,1)S(1)} %collective-permute-done.x_refs_0_, bf16[128,1024]{1,0:T(8,128)(2,1)S(1)} %collective-permute-done.1.e_refs_0_, ...), custom_call_target="tpu_custom_call" | custom-call | tf_op jit(solution)/shard_map/early/pallas_call | solution.py:187
  21.9 0.1 collective-permute-done.7.ch_refs_0_
  22.0 0.0 collective-permute-done.8.ch_refs_1_
  22.0 0.7 %middle.1 = (f32[8,128]{1,0:T(8,128)S(1)}, f32[8,128]{1,0:T(8,128)S(1)}, f32[8,128]{1,0:T(8,128)S(1)}, bf16[512,1024]{1,0:T(8,128)(2,1)S(1)}, s32[2,128]{1,0:T(2,128)S(1)}) custom-call(f32[8,384]{1,0:T(8,128)S(1)} %get-tuple-element.18.best_ref, bf16[384,1024]{1,0:T(8,128)(2,1)S(1)} %get-tuple-element.19.own_ref, ...), custom_call_target="tpu_custom_call" | custom-call | tf_op jit(solution)/shard_map/middle/pallas_call | solution.py:237
  22.7 0.0 collective-permute-done.9.xe_refs_0_
  22.7 0.6 %late.1 = f32[8,128]{1,0:T(8,128)S(1)} custom-call(bf16[512,1024]{1,0:T(8,128)(2,1)S(1)} %get-tuple-element.24.far_ref, bf16[128,1024]{1,0:T(8,128)(2,1)S(1)} %collective-permute-done.9.xe_refs_0_, s32[1,128]{1,0:T(1,128)S(1)} %bitcast.9, s32[1,128]{1,0:T(1,128)S(1)} %collective-permute-done.4.c_ids_ref, s32[2,128]{1,0:T(2,128)S(1)} %collective-permute-done.5.e_ids_ref, ...), custom_call_target="tpu_custom_call" | custom-call | tf_op jit(solution)/shard_map/late/pallas_call | solution.py:257
  23.3 0.1 collective-permute-start.10
  23.4 2.0 %collective-permute-start.11 = (f32[8,128]{1,0:T(8,128)S(1)}, f32[8,128]{1,0:T(8,128)S(1)}, u32[]{:S(2)}, u32[]{:S(2)}) collective-permute-start(f32[8,128]{1,0:T(8,128)S(1)} %get-tuple-element.28), channel_id=1, source_target_pairs={{0,4},{1,5},{2,6},{3,7},{4,0},{5,1},{6,2},{7,3},{8,12},{9,13},{10,... | collective-permute-start | bytes 12296 | tf_op jit(solution)/shard_map/ppermute | solution.py:269
  25.4 1.5 %collective-permute-start.12 = (f32[8,128]{1,0:T(8,128)S(1)}, f32[8,128]{1,0:T(8,128)S(1)}, u32[]{:S(2)}, u32[]{:S(2)}) collective-permute-start(f32[8,128]{1,0:T(8,128)S(1)} %get-tuple-element.29), channel_id=1, source_target_pairs={{0,2},{1,3},{2,0},{3,1},{4,6},{5,7},{6,4},{7,5},{8,10},{9,11},{10,... | collective-permute-start | bytes 12296 | tf_op jit(solution)/shard_map/ppermute | solution.py:269
  26.9 1.0 %collective-permute-done.10 = f32[8,128]{1,0:T(8,128)S(1)} collective-permute-done((f32[8,128]{1,0:T(8,128)S(1)}, f32[8,128]{1,0:T(8,128)S(1)}, u32[]{:S(2)}, u32[]{:S(2)}) %collective-permute-start.10) | collective-permute-done | bytes 4128 | tf_op jit(solution)/shard_map/ppermute | solution.py:269
  27.9 0.0 collective-permute-done.11
  27.9 1.1 %collective-permute-done.12 = f32[8,128]{1,0:T(8,128)S(1)} collective-permute-done((f32[8,128]{1,0:T(8,128)S(1)}, f32[8,128]{1,0:T(8,128)S(1)}, u32[]{:S(2)}, u32[]{:S(2)}) %collective-permute-start.12) | collective-permute-done | bytes 4128 | tf_op jit(solution)/shard_map/ppermute | solution.py:269
  29.0 0.5 %slice_bitcast_fusion = f32[128]{0:T(128)} fusion(f32[8,128]{1,0:T(8,128)S(1)} %maximum_maximum_fusion), kind=kLoop, calls=%fused_computation.2 | loop fusion | bytes 1024 | tf_op jit(solution)/shard_map/squeeze | solution.py:289
  (5 shorter events, 0.1 us)
Async XLA Ops:
  0.0 4.5 %copy-start.1 = (s32[128,1]{0,1:T(1,128)S(1)}, s32[128,1]{0,1:T(1,128)}, u32[]{:S(2)}) copy-start(s32[128,1]{0,1:T(1,128)} %param.3) | copy-start | bytes 1540
  0.0 12.9 %collective-permute-start.1 = (bf16[128,1024]{1,0:T(8,128)(2,1)}, bf16[128,1024]{1,0:T(8,128)(2,1)S(1)}, u32[]{:S(2)}, u32[]{:S(2)}) collective-permute-start(bf16[128,1024]{1,0:T(8,128)(2,1)} %rows_ref.1), channel_id=1, source_target_pairs={{0,4},{1,5},{2,6},{3,7},{4,0},{5,1},{6,2},{7,3},{8,12},{9,13},{10,... | collective-permute-start | bytes 786440 | tf_op jit(solution)/shard_map/ppermute | solution.py:269
  3.0 9.8 %collective-permute-start = (bf16[128,1024]{1,0:T(8,128)(2,1)}, bf16[128,1024]{1,0:T(8,128)(2,1)S(1)}, u32[]{:S(2)}, u32[]{:S(2)}) collective-permute-start(bf16[128,1024]{1,0:T(8,128)(2,1)} %rows_ref.1), channel_id=1, source_target_pairs={{0,2},{1,3},{2,0},{3,1},{4,6},{5,7},{6,4},{7,5},{8,10},{9,11},{10,... | collective-permute-start | bytes 786440 | tf_op jit(solution)/shard_map/ppermute | solution.py:269
  4.5 1.0 %copy-start = (bf16[128,1024]{1,0:T(8,128)(2,1)S(1)}, bf16[128,1024]{1,0:T(8,128)(2,1)}, u32[]{:S(2)}) copy-start(bf16[128,1024]{1,0:T(8,128)(2,1)} %rows_ref.1) | copy-start | bytes 786436
  5.5 14.8 %collective-permute-start.6 = (bf16[136,1024]{1,0:T(8,128)(2,1)S(1)}, bf16[136,1024]{1,0:T(8,128)(2,1)S(1)}, u32[]{:S(2)}, u32[]{:S(2)}) collective-permute-start(bf16[136,1024]{1,0:T(8,128)(2,1)S(1)} %label.1), channel_id=1, source_target_pairs={{0,8},{1,9},{2,10},{3,11},{4,12},{5,13},{6,14},{7,15},{8,0},{9,1},... | collective-permute-start | bytes 835592 | tf_op jit(solution)/shard_map/ppermute | solution.py:269
  8.2 11.1 %collective-permute-start.2 = (bf16[128,1024]{1,0:T(8,128)(2,1)S(1)}, bf16[128,1024]{1,0:T(8,128)(2,1)S(1)}, u32[]{:S(2)}, u32[]{:S(2)}) collective-permute-start(bf16[128,1024]{1,0:T(8,128)(2,1)S(1)} %copy-done), channel_id=1, source_target_pairs={{0,1},{1,0},{2,3},{3,2},{4,5},{5,4},{6,7},{7,6},{8,9},{9,8},{10,11... | collective-permute-start | bytes 786440 | tf_op jit(solution)/shard_map/ppermute | solution.py:269
  8.2 3.5 %collective-permute-start.3 = (s32[1,128]{1,0:T(1,128)S(1)}, s32[1,128]{1,0:T(1,128)S(1)}, u32[]{:S(2)}, u32[]{:S(2)}) collective-permute-start(s32[1,128]{1,0:T(1,128)S(1)} %bitcast.4), channel_id=1, source_target_pairs={{0,2},{1,3},{2,0},{3,1},{4,6},{5,7},{6,4},{7,5},{8,10},{9,11},{10,... | collective-permute-start | bytes 1544 | tf_op jit(solution)/shard_map/ppermute | solution.py:269
  12.9 9.9 %collective-permute-start.9 = (bf16[128,1024]{1,0:T(8,128)(2,1)S(1)}, bf16[128,1024]{1,0:T(8,128)(2,1)S(1)}, u32[]{:S(2)}, u32[]{:S(2)}) collective-permute-start(bf16[128,1024]{1,0:T(8,128)(2,1)S(1)} %collective-permute-done.1.e_refs_0_), channel_id=1, source_target_pairs={{0,2},{1,3},{2,0},{3,1},{4,6},{5,7},{6,4},{7,5},{8,10},{9,11},{10,... | collective-permute-start | bytes 786440 | tf_op jit(solution)/shard_map/ppermute | solution.py:269
  15.6 3.7 %collective-permute-start.5 = (s32[2,128]{1,0:T(2,128)S(1)}, s32[2,128]{1,0:T(2,128)S(1)}, u32[]{:S(2)}, u32[]{:S(2)}) collective-permute-start(s32[2,128]{1,0:T(2,128)S(1)} %pad_add_fusion), channel_id=1, source_target_pairs={{0,4},{1,5},{2,6},{3,7},{4,0},{5,1},{6,2},{7,3},{8,12},{9,13},{10,... | collective-permute-start | bytes 3080 | tf_op jit(solution)/shard_map/ppermute | solution.py:269
  15.6 1.2 %collective-permute-start.4 = (s32[1,128]{1,0:T(1,128)S(1)}, s32[1,128]{1,0:T(1,128)S(1)}, u32[]{:S(2)}, u32[]{:S(2)}) collective-permute-start(s32[1,128]{1,0:T(1,128)S(1)} %bitcast.6), channel_id=1, source_target_pairs={{0,1},{1,0},{2,3},{3,2},{4,5},{5,4},{6,7},{7,6},{8,9},{9,8},{10,11... | collective-permute-start | bytes 1544 | tf_op jit(solution)/shard_map/ppermute | solution.py:269
  20.4 1.6 %collective-permute-start.8 = (bf16[72,1024]{1,0:T(8,128)(2,1)S(1)}, bf16[72,1024]{1,0:T(8,128)(2,1)S(1)}, u32[]{:S(2)}, u32[]{:S(2)}) collective-permute-start(bf16[72,1024]{1,0:T(8,128)(2,1)S(1)} %slice.10), channel_id=1, source_target_pairs={{0,1},{1,0},{2,3},{3,2},{4,5},{5,4},{6,7},{7,6},{8,9},{9,8},{10,11... | collective-permute-start | bytes 442376 | tf_op jit(solution)/shard_map/ppermute | solution.py:269
  20.5 1.5 %collective-permute-start.7 = (bf16[64,1024]{1,0:T(8,128)(2,1)S(1)}, bf16[64,1024]{1,0:T(8,128)(2,1)S(1)}, u32[]{:S(2)}, u32[]{:S(2)}) collective-permute-start(bf16[64,1024]{1,0:T(8,128)(2,1)S(1)} %slice.9), channel_id=1, source_target_pairs={{0,1},{1,0},{2,3},{3,2},{4,5},{5,4},{6,7},{7,6},{8,9},{9,8},{10,11... | collective-permute-start | bytes 393224 | tf_op jit(solution)/shard_map/ppermute | solution.py:269
  23.3 4.6 %collective-permute-start.10 = (f32[8,128]{1,0:T(8,128)S(1)}, f32[8,128]{1,0:T(8,128)S(1)}, u32[]{:S(2)}, u32[]{:S(2)}) collective-permute-start(f32[8,128]{1,0:T(8,128)S(1)} %late.1), channel_id=1, source_target_pairs={{0,6},{1,7},{2,4},{3,5},{4,2},{5,3},{6,0},{7,1},{8,14},{9,15},{10,... | collective-permute-start | bytes 12296 | tf_op jit(solution)/shard_map/ppermute | solution.py:269
  23.4 4.5 %collective-permute-start.11 = (f32[8,128]{1,0:T(8,128)S(1)}, f32[8,128]{1,0:T(8,128)S(1)}, u32[]{:S(2)}, u32[]{:S(2)}) collective-permute-start(f32[8,128]{1,0:T(8,128)S(1)} %get-tuple-element.28), channel_id=1, source_target_pairs={{0,4},{1,5},{2,6},{3,7},{4,0},{5,1},{6,2},{7,3},{8,12},{9,13},{10,... | collective-permute-start | bytes 12296 | tf_op jit(solution)/shard_map/ppermute | solution.py:269
  25.4 3.6 %collective-permute-start.12 = (f32[8,128]{1,0:T(8,128)S(1)}, f32[8,128]{1,0:T(8,128)S(1)}, u32[]{:S(2)}, u32[]{:S(2)}) collective-permute-start(f32[8,128]{1,0:T(8,128)S(1)} %get-tuple-element.29), channel_id=1, source_target_pairs={{0,2},{1,3},{2,0},{3,1},{4,6},{5,7},{6,4},{7,5},{8,10},{9,11},{10,... | collective-permute-start | bytes 12296 | tf_op jit(solution)/shard_map/ppermute | solution.py:269

commit v16 on v15

--- a/solution.py
+++ b/solution.py
@@ -283,9 +283,10 @@
     x, e, h, c, xe = [x], [e], [h], [c], [xe]
     best, own, c = early(mine, x, e, c, [ids, x_ids, c_ids, e_ids])
     found, x_best, e_best, far, h_ids = middle(best, own, c, h, ch, [ids, x_ids, e_ids])
+    x_best = swap(SHARD, x_best)
     xe_best = late(far, xe, [ids, c_ids, e_ids, h_ids])
-    x_best, e_best, xe_best = lax.optimization_barrier((x_best, e_best, xe_best))
-    xe_best, e_best, x_best = swap(LOW | SHARD, xe_best), swap(LOW, e_best), swap(SHARD, x_best)
+    e_best, xe_best = lax.optimization_barrier((e_best, xe_best))
+    xe_best, e_best = swap(LOW | SHARD, xe_best), swap(LOW, e_best)
     return jnp.maximum(jnp.maximum(jnp.maximum(xe_best, e_best), x_best), found)[0]
 
 

time: 29.6 us -> 29.2 us (0.986)
  waiting for transfers between devices: 11.1 us -> 10.6 us
    ppermute x13, waiting for transfers between devices: 11.1 us -> 10.6 us  [swap(): return lax.ppermute(array, AXES, [(i, i ^ flip) for i in range(16)])]
  transfers between devices with their start and end apart: 13 -> 13, of which waited for: 8 -> 8; matrix products, arithmetic and copies ran while one was open for 0% -> 0% of each run, Pallas kernels for 5% -> 7%
where the time goes in v16:
time: 29.2 us; the launch traced here: 29.1 us
  starting transfers between devices  14.8 us (51%)
  waiting for transfers between devices  10.6 us (36%)
  Pallas kernels  2.12 us (7%)
  local copies, waits for them, and re-layouts  1.52 us (5%)
    ppermute x13, starting transfers between devices, swap(): return lax.ppermute(array, AXES, [(i, i ^ flip) for i in range(16)])  14.8 us
    ppermute x13, waiting for transfers between devices, swap(): return lax.ppermute(array, AXES, [(i, i ^ flip) for i in range(16)])  10.6 us
    unnamed x4, local copies, waits for them, and re-layouts  0.98 us
    pallas_call x1, Pallas kernels, early(): pl.pallas_call(early_kernel, out_shape=[jax.ShapeDtypeStruct((8, 3 * rows...  0.84 us
    pallas_call x1, Pallas kernels, middle(): pl.pallas_call(middle_kernel, out_shape=[jax.ShapeDtypeStruct((8, rows),...  0.69 us
  transfers between devices with their start and end apart: 13, of which 8 were waited for; matrix products, arithmetic and copies ran while one was open for 0% of the time, Pallas kernels for 7%

profile of v16, /device:TPU:0, one launch (start us, length us, event | category | flops | bytes accessed | tf_op | source)
XLA Modules:
  0.0 29.1 jit_solution(13832602228772351197)
XLA Ops:
  0.0 0.0 copy-start.1
  0.0 3.0 %collective-permute-start.1 = (bf16[128,1024]{1,0:T(8,128)(2,1)}, bf16[128,1024]{1,0:T(8,128)(2,1)S(1)}, u32[]{:S(2)}, u32[]{:S(2)}) collective-permute-start(bf16[128,1024]{1,0:T(8,128)(2,1)} %rows_ref.1), channel_id=1, source_target_pairs={{0,4},{1,5},{2,6},{3,7},{4,0},{5,1},{6,2},{7,3},{8,12},{9,13},{10,... | collective-permute-start | bytes 786440 | tf_op jit(solution)/shard_map/ppermute | solution.py:269
  3.0 1.5 %collective-permute-start = (bf16[128,1024]{1,0:T(8,128)(2,1)}, bf16[128,1024]{1,0:T(8,128)(2,1)S(1)}, u32[]{:S(2)}, u32[]{:S(2)}) collective-permute-start(bf16[128,1024]{1,0:T(8,128)(2,1)} %rows_ref.1), channel_id=1, source_target_pairs={{0,2},{1,3},{2,0},{3,1},{4,6},{5,7},{6,4},{7,5},{8,10},{9,11},{10,... | collective-permute-start | bytes 786440 | tf_op jit(solution)/shard_map/ppermute | solution.py:269
  4.5 0.0 copy-done.1
  4.5 0.0 copy-start
  4.5 1.0 %copy-done = bf16[128,1024]{1,0:T(8,128)(2,1)S(1)} copy-done((bf16[128,1024]{1,0:T(8,128)(2,1)S(1)}, bf16[128,1024]{1,0:T(8,128)(2,1)}, u32[]{:S(2)}) %copy-start) | copy-done | bytes 262168
  5.5 2.7 %collective-permute-start.6 = (bf16[136,1024]{1,0:T(8,128)(2,1)S(1)}, bf16[136,1024]{1,0:T(8,128)(2,1)S(1)}, u32[]{:S(2)}, u32[]{:S(2)}) collective-permute-start(bf16[136,1024]{1,0:T(8,128)(2,1)S(1)} %label.1), channel_id=1, source_target_pairs={{0,8},{1,9},{2,10},{3,11},{4,12},{5,13},{6,14},{7,15},{8,0},{9,1},... | collective-permute-start | bytes 835592 | tf_op jit(solution)/shard_map/ppermute | solution.py:269
  8.2 0.0 collective-permute-start.2
  8.2 0.5 %collective-permute-start.3 = (s32[1,128]{1,0:T(1,128)S(1)}, s32[1,128]{1,0:T(1,128)S(1)}, u32[]{:S(2)}, u32[]{:S(2)}) collective-permute-start(s32[1,128]{1,0:T(1,128)S(1)} %bitcast.4), channel_id=1, source_target_pairs={{0,2},{1,3},{2,0},{3,1},{4,6},{5,7},{6,4},{7,5},{8,10},{9,11},{10,... | collective-permute-start | bytes 1544 | tf_op jit(solution)/shard_map/ppermute | solution.py:269
  8.7 3.0 %collective-permute-done.3.x_ids_ref = s32[1,128]{1,0:T(1,128)S(1)} collective-permute-done((s32[1,128]{1,0:T(1,128)S(1)}, s32[1,128]{1,0:T(1,128)S(1)}, u32[]{:S(2)}, u32[]{:S(2)}) %collective-permute-start.3) | collective-permute-done | bytes 544 | tf_op jit(solution)/shard_map/ppermute | solution.py:269
  11.7 1.1 %collective-permute-done.1.e_refs_0_ = bf16[128,1024]{1,0:T(8,128)(2,1)S(1)} collective-permute-done((bf16[128,1024]{1,0:T(8,128)(2,1)}, bf16[128,1024]{1,0:T(8,128)(2,1)S(1)}, u32[]{:S(2)}, u32[]{:S(2)}) %collective-permute-start.1) | collective-permute-done | bytes 262176 | tf_op jit(solution)/shard_map/ppermute | solution.py:269
  12.9 0.0 collective-permute-done.x_refs_0_
  12.9 2.7 %collective-permute-start.9 = (bf16[128,1024]{1,0:T(8,128)(2,1)S(1)}, bf16[128,1024]{1,0:T(8,128)(2,1)S(1)}, u32[]{:S(2)}, u32[]{:S(2)}) collective-permute-start(bf16[128,1024]{1,0:T(8,128)(2,1)S(1)} %collective-permute-done.1.e_refs_0_), channel_id=1, source_target_pairs={{0,2},{1,3},{2,0},{3,1},{4,6},{5,7},{6,4},{7,5},{8,10},{9,11},{10,... | collective-permute-start | bytes 786440 | tf_op jit(solution)/shard_map/ppermute | solution.py:269
  15.6 0.0 collective-permute-start.5
  15.6 0.1 collective-permute-start.4
  15.7 1.1 %collective-permute-done.4.c_ids_ref = s32[1,128]{1,0:T(1,128)S(1)} collective-permute-done((s32[1,128]{1,0:T(1,128)S(1)}, s32[1,128]{1,0:T(1,128)S(1)}, u32[]{:S(2)}, u32[]{:S(2)}) %collective-permute-start.4) | collective-permute-done | bytes 544 | tf_op jit(solution)/shard_map/ppermute | solution.py:269
  16.8 2.5 %collective-permute-done.5.e_ids_ref = s32[2,128]{1,0:T(2,128)S(1)} collective-permute-done((s32[2,128]{1,0:T(2,128)S(1)}, s32[2,128]{1,0:T(2,128)S(1)}, u32[]{:S(2)}, u32[]{:S(2)}) %collective-permute-start.5) | collective-permute-done | bytes 1056 | tf_op jit(solution)/shard_map/ppermute | solution.py:269
  19.3 0.0 collective-permute-done.2.c_refs_0_
  19.3 1.1 %collective-permute-done.6.h_refs_0_ = bf16[136,1024]{1,0:T(8,128)(2,1)S(1)} collective-permute-done((bf16[136,1024]{1,0:T(8,128)(2,1)S(1)}, bf16[136,1024]{1,0:T(8,128)(2,1)S(1)}, u32[]{:S(2)}, u32[]{:S(2)}) %collective-permute-start.6) | collective-permute-done | bytes 278560 | tf_op jit(solution)/shard_map/ppermute | solution.py:269
  20.4 0.1 collective-permute-start.8
  20.5 0.6 %collective-permute-start.7 = (bf16[64,1024]{1,0:T(8,128)(2,1)S(1)}, bf16[64,1024]{1,0:T(8,128)(2,1)S(1)}, u32[]{:S(2)}, u32[]{:S(2)}) collective-permute-start(bf16[64,1024]{1,0:T(8,128)(2,1)S(1)} %slice.9), channel_id=1, source_target_pairs={{0,1},{1,0},{2,3},{3,2},{4,5},{5,4},{6,7},{7,6},{8,9},{9,8},{10,11... | collective-permute-start | bytes 393224 | tf_op jit(solution)/shard_map/ppermute | solution.py:269
  21.0 0.8 %early.1 = (f32[8,384]{1,0:T(8,128)S(1)}, bf16[384,1024]{1,0:T(8,128)(2,1)S(1)}, bf16[128,1024]{1,0:T(8,128)(2,1)S(1)}) custom-call(bf16[128,1024]{1,0:T(8,128)(2,1)S(1)} %copy-done, bf16[128,1024]{1,0:T(8,128)(2,1)S(1)} %collective-permute-done.x_refs_0_, bf16[128,1024]{1,0:T(8,128)(2,1)S(1)} %collective-permute-done.1.e_refs_0_, ...), custom_call_target="tpu_custom_call" | custom-call | tf_op jit(solution)/shard_map/early/pallas_call | solution.py:187
  21.9 0.1 collective-permute-done.7.ch_refs_0_
  22.0 0.0 collective-permute-done.8.ch_refs_1_
  22.0 0.7 %middle.1 = (f32[8,128]{1,0:T(8,128)S(1)}, f32[8,128]{1,0:T(8,128)S(1)}, f32[8,128]{1,0:T(8,128)S(1)}, bf16[512,1024]{1,0:T(8,128)(2,1)S(1)}, s32[2,128]{1,0:T(2,128)S(1)}) custom-call(f32[8,384]{1,0:T(8,128)S(1)} %get-tuple-element.17.best_ref, bf16[384,1024]{1,0:T(8,128)(2,1)S(1)} %get-tuple-element.18.own_ref, ...), custom_call_target="tpu_custom_call" | custom-call | tf_op jit(solution)/shard_map/middle/pallas_call | solution.py:237
  22.7 0.6 %collective-permute-start.12 = (f32[8,128]{1,0:T(8,128)S(1)}, f32[8,128]{1,0:T(8,128)S(1)}, u32[]{:S(2)}, u32[]{:S(2)}) collective-permute-start(f32[8,128]{1,0:T(8,128)S(1)} %get-tuple-element.27), channel_id=1, source_target_pairs={{0,2},{1,3},{2,0},{3,1},{4,6},{5,7},{6,4},{7,5},{8,10},{9,11},{10,... | collective-permute-start | bytes 12296 | tf_op jit(solution)/shard_map/ppermute | solution.py:269
  23.3 0.0 collective-permute-done.9.xe_refs_0_
  23.3 0.6 %late.1 = f32[8,128]{1,0:T(8,128)S(1)} custom-call(bf16[512,1024]{1,0:T(8,128)(2,1)S(1)} %get-tuple-element.22.far_ref, bf16[128,1024]{1,0:T(8,128)(2,1)S(1)} %collective-permute-done.9.xe_refs_0_, s32[1,128]{1,0:T(1,128)S(1)} %bitcast.9, s32[1,128]{1,0:T(1,128)S(1)} %collective-permute-done.4.c_ids_ref, s32[2,128]{1,0:T(2,128)S(1)} %collective-permute-done.5.e_ids_ref, ...), custom_call_target="tpu_custom_call" | custom-call | tf_op jit(solution)/shard_map/late/pallas_call | solution.py:257
  23.9 0.6 %collective-permute-start.10 = (f32[8,128]{1,0:T(8,128)S(1)}, f32[8,128]{1,0:T(8,128)S(1)}, u32[]{:S(2)}, u32[]{:S(2)}) collective-permute-start(f32[8,128]{1,0:T(8,128)S(1)} %late.1), channel_id=1, source_target_pairs={{0,6},{1,7},{2,4},{3,5},{4,2},{5,3},{6,0},{7,1},{8,14},{9,15},{10,... | collective-permute-start | bytes 12296 | tf_op jit(solution)/shard_map/ppermute | solution.py:269
  24.5 2.4 %collective-permute-start.11 = (f32[8,128]{1,0:T(8,128)S(1)}, f32[8,128]{1,0:T(8,128)S(1)}, u32[]{:S(2)}, u32[]{:S(2)}) collective-permute-start(f32[8,128]{1,0:T(8,128)S(1)} %get-tuple-element.26), channel_id=1, source_target_pairs={{0,4},{1,5},{2,6},{3,7},{4,0},{5,1},{6,2},{7,3},{8,12},{9,13},{10,... | collective-permute-start | bytes 12296 | tf_op jit(solution)/shard_map/ppermute | solution.py:269
  26.9 0.0 collective-permute-done.12
  26.9 1.5 %collective-permute-done.10 = f32[8,128]{1,0:T(8,128)S(1)} collective-permute-done((f32[8,128]{1,0:T(8,128)S(1)}, f32[8,128]{1,0:T(8,128)S(1)}, u32[]{:S(2)}, u32[]{:S(2)}) %collective-permute-start.10) | collective-permute-done | bytes 4128 | tf_op jit(solution)/shard_map/ppermute | solution.py:269
  28.5 0.1 collective-permute-done.11
  28.5 0.5 %slice_bitcast_fusion = f32[128]{0:T(128)} fusion(f32[8,128]{1,0:T(8,128)S(1)} %maximum_maximum_fusion), kind=kLoop, calls=%fused_computation.2 | loop fusion | bytes 1024 | tf_op jit(solution)/shard_map/squeeze | solution.py:290
  (5 shorter events, 0.1 us)
Async XLA Ops:
  0.0 4.5 %copy-start.1 = (s32[128,1]{0,1:T(1,128)S(1)}, s32[128,1]{0,1:T(1,128)}, u32[]{:S(2)}) copy-start(s32[128,1]{0,1:T(1,128)} %param.3) | copy-start | bytes 1540
  0.0 12.9 %collective-permute-start.1 = (bf16[128,1024]{1,0:T(8,128)(2,1)}, bf16[128,1024]{1,0:T(8,128)(2,1)S(1)}, u32[]{:S(2)}, u32[]{:S(2)}) collective-permute-start(bf16[128,1024]{1,0:T(8,128)(2,1)} %rows_ref.1), channel_id=1, source_target_pairs={{0,4},{1,5},{2,6},{3,7},{4,0},{5,1},{6,2},{7,3},{8,12},{9,13},{10,... | collective-permute-start | bytes 786440 | tf_op jit(solution)/shard_map/ppermute | solution.py:269
  3.0 9.8 %collective-permute-start = (bf16[128,1024]{1,0:T(8,128)(2,1)}, bf16[128,1024]{1,0:T(8,128)(2,1)S(1)}, u32[]{:S(2)}, u32[]{:S(2)}) collective-permute-start(bf16[128,1024]{1,0:T(8,128)(2,1)} %rows_ref.1), channel_id=1, source_target_pairs={{0,2},{1,3},{2,0},{3,1},{4,6},{5,7},{6,4},{7,5},{8,10},{9,11},{10,... | collective-permute-start | bytes 786440 | tf_op jit(solution)/shard_map/ppermute | solution.py:269
  4.5 1.0 %copy-start = (bf16[128,1024]{1,0:T(8,128)(2,1)S(1)}, bf16[128,1024]{1,0:T(8,128)(2,1)}, u32[]{:S(2)}) copy-start(bf16[128,1024]{1,0:T(8,128)(2,1)} %rows_ref.1) | copy-start | bytes 786436
  5.5 14.8 %collective-permute-start.6 = (bf16[136,1024]{1,0:T(8,128)(2,1)S(1)}, bf16[136,1024]{1,0:T(8,128)(2,1)S(1)}, u32[]{:S(2)}, u32[]{:S(2)}) collective-permute-start(bf16[136,1024]{1,0:T(8,128)(2,1)S(1)} %label.1), channel_id=1, source_target_pairs={{0,8},{1,9},{2,10},{3,11},{4,12},{5,13},{6,14},{7,15},{8,0},{9,1},... | collective-permute-start | bytes 835592 | tf_op jit(solution)/shard_map/ppermute | solution.py:269
  8.2 11.1 %collective-permute-start.2 = (bf16[128,1024]{1,0:T(8,128)(2,1)S(1)}, bf16[128,1024]{1,0:T(8,128)(2,1)S(1)}, u32[]{:S(2)}, u32[]{:S(2)}) collective-permute-start(bf16[128,1024]{1,0:T(8,128)(2,1)S(1)} %copy-done), channel_id=1, source_target_pairs={{0,1},{1,0},{2,3},{3,2},{4,5},{5,4},{6,7},{7,6},{8,9},{9,8},{10,11... | collective-permute-start | bytes 786440 | tf_op jit(solution)/shard_map/ppermute | solution.py:269
  8.2 3.5 %collective-permute-start.3 = (s32[1,128]{1,0:T(1,128)S(1)}, s32[1,128]{1,0:T(1,128)S(1)}, u32[]{:S(2)}, u32[]{:S(2)}) collective-permute-start(s32[1,128]{1,0:T(1,128)S(1)} %bitcast.4), channel_id=1, source_target_pairs={{0,2},{1,3},{2,0},{3,1},{4,6},{5,7},{6,4},{7,5},{8,10},{9,11},{10,... | collective-permute-start | bytes 1544 | tf_op jit(solution)/shard_map/ppermute | solution.py:269
  12.9 10.5 %collective-permute-start.9 = (bf16[128,1024]{1,0:T(8,128)(2,1)S(1)}, bf16[128,1024]{1,0:T(8,128)(2,1)S(1)}, u32[]{:S(2)}, u32[]{:S(2)}) collective-permute-start(bf16[128,1024]{1,0:T(8,128)(2,1)S(1)} %collective-permute-done.1.e_refs_0_), channel_id=1, source_target_pairs={{0,2},{1,3},{2,0},{3,1},{4,6},{5,7},{6,4},{7,5},{8,10},{9,11},{10,... | collective-permute-start | bytes 786440 | tf_op jit(solution)/shard_map/ppermute | solution.py:269
  15.6 3.7 %collective-permute-start.5 = (s32[2,128]{1,0:T(2,128)S(1)}, s32[2,128]{1,0:T(2,128)S(1)}, u32[]{:S(2)}, u32[]{:S(2)}) collective-permute-start(s32[2,128]{1,0:T(2,128)S(1)} %pad_add_fusion), channel_id=1, source_target_pairs={{0,4},{1,5},{2,6},{3,7},{4,0},{5,1},{6,2},{7,3},{8,12},{9,13},{10,... | collective-permute-start | bytes 3080 | tf_op jit(solution)/shard_map/ppermute | solution.py:269
  15.6 1.2 %collective-permute-start.4 = (s32[1,128]{1,0:T(1,128)S(1)}, s32[1,128]{1,0:T(1,128)S(1)}, u32[]{:S(2)}, u32[]{:S(2)}) collective-permute-start(s32[1,128]{1,0:T(1,128)S(1)} %bitcast.6), channel_id=1, source_target_pairs={{0,1},{1,0},{2,3},{3,2},{4,5},{5,4},{6,7},{7,6},{8,9},{9,8},{10,11... | collective-permute-start | bytes 1544 | tf_op jit(solution)/shard_map/ppermute | solution.py:269
  20.4 1.6 %collective-permute-start.8 = (bf16[72,1024]{1,0:T(8,128)(2,1)S(1)}, bf16[72,1024]{1,0:T(8,128)(2,1)S(1)}, u32[]{:S(2)}, u32[]{:S(2)}) collective-permute-start(bf16[72,1024]{1,0:T(8,128)(2,1)S(1)} %slice.10), channel_id=1, source_target_pairs={{0,1},{1,0},{2,3},{3,2},{4,5},{5,4},{6,7},{7,6},{8,9},{9,8},{10,11... | collective-permute-start | bytes 442376 | tf_op jit(solution)/shard_map/ppermute | solution.py:269
  20.5 1.5 %collective-permute-start.7 = (bf16[64,1024]{1,0:T(8,128)(2,1)S(1)}, bf16[64,1024]{1,0:T(8,128)(2,1)S(1)}, u32[]{:S(2)}, u32[]{:S(2)}) collective-permute-start(bf16[64,1024]{1,0:T(8,128)(2,1)S(1)} %slice.9), channel_id=1, source_target_pairs={{0,1},{1,0},{2,3},{3,2},{4,5},{5,4},{6,7},{7,6},{8,9},{9,8},{10,11... | collective-permute-start | bytes 393224 | tf_op jit(solution)/shard_map/ppermute | solution.py:269
  22.7 4.2 %collective-permute-start.12 = (f32[8,128]{1,0:T(8,128)S(1)}, f32[8,128]{1,0:T(8,128)S(1)}, u32[]{:S(2)}, u32[]{:S(2)}) collective-permute-start(f32[8,128]{1,0:T(8,128)S(1)} %get-tuple-element.27), channel_id=1, source_target_pairs={{0,2},{1,3},{2,0},{3,1},{4,6},{5,7},{6,4},{7,5},{8,10},{9,11},{10,... | collective-permute-start | bytes 12296 | tf_op jit(solution)/shard_map/ppermute | solution.py:269
  23.9 4.6 %collective-permute-start.10 = (f32[8,128]{1,0:T(8,128)S(1)}, f32[8,128]{1,0:T(8,128)S(1)}, u32[]{:S(2)}, u32[]{:S(2)}) collective-permute-start(f32[8,128]{1,0:T(8,128)S(1)} %late.1), channel_id=1, source_target_pairs={{0,6},{1,7},{2,4},{3,5},{4,2},{5,3},{6,0},{7,1},{8,14},{9,15},{10,... | collective-permute-start | bytes 12296 | tf_op jit(solution)/shard_map/ppermute | solution.py:269
  24.5 4.0 %collective-permute-start.11 = (f32[8,128]{1,0:T(8,128)S(1)}, f32[8,128]{1,0:T(8,128)S(1)}, u32[]{:S(2)}, u32[]{:S(2)}) collective-permute-start(f32[8,128]{1,0:T(8,128)S(1)} %get-tuple-element.26), channel_id=1, source_target_pairs={{0,4},{1,5},{2,6},{3,7},{4,0},{5,1},{6,2},{7,3},{8,12},{9,13},{10,... | collective-permute-start | bytes 12296 | tf_op jit(solution)/shard_map/ppermute | solution.py:269

commit v17 on v16

--- a/solution.py
+++ b/solution.py
@@ -276,9 +276,9 @@
     h = swap(HIGH, label(mine, ids))
     x_ids, c_ids = swap(SHARD, ids), swap(SUB, ids)
     e_ids = swap(LOW, jnp.concatenate([ids, x_ids]))
-    e_then, _, _ = lax.optimization_barrier((e, x, x_ids))
+    e_then, _ = lax.optimization_barrier((e, x_ids))
     xe = swap(SHARD, e_then)
-    h_then, *_ = lax.optimization_barrier((h, e_ids, x, c_ids, c))
+    h_then, *_ = lax.optimization_barrier((h, e_ids, c_ids, c))
     ch = [swap(SUB, h_then[: rows // 2]), swap(SUB, h_then[rows // 2 :])]
     x, e, h, c, xe = [x], [e], [h], [c], [xe]
     best, own, c = early(mine, x, e, c, [ids, x_ids, c_ids, e_ids])

time: 29.2 us -> 29.4 us (level)
  waiting for transfers between devices: 10.6 us -> 11.9 us
  starting transfers between devices: 14.8 us -> 13.6 us
    ppermute x13, waiting for transfers between devices: 10.6 us -> 11.9 us  [swap(): return lax.ppermute(array, AXES, [(i, i ^ flip) for i in range(16)])]
    ppermute x13, starting transfers between devices: 14.8 us -> 13.6 us  [swap(): return lax.ppermute(array, AXES, [(i, i ^ flip) for i in range(16)])]
  transfers between devices with their start and end apart: 13 -> 13, of which waited for: 8 -> 7; matrix products, arithmetic and copies ran while one was open for 0% -> 0% of each run, Pallas kernels for 7% -> 7%
where the time goes in v17:
time: 29.4 us; the launch traced here: 29.2 us
  starting transfers between devices  13.6 us (46%)
  waiting for transfers between devices  11.9 us (40%)
  Pallas kernels  2.11 us (7%)
  local copies, waits for them, and re-layouts  1.52 us (5%)
    ppermute x13, starting transfers between devices, swap(): return lax.ppermute(array, AXES, [(i, i ^ flip) for i in range(16)])  13.6 us
    ppermute x13, waiting for transfers between devices, swap(): return lax.ppermute(array, AXES, [(i, i ^ flip) for i in range(16)])  11.9 us
    unnamed x4, local copies, waits for them, and re-layouts  0.98 us
    pallas_call x1, Pallas kernels, early(): pl.pallas_call(early_kernel, out_shape=[jax.ShapeDtypeStruct((8, 3 * rows...  0.84 us
    pallas_call x1, Pallas kernels, middle(): pl.pallas_call(middle_kernel, out_shape=[jax.ShapeDtypeStruct((8, rows),...  0.68 us
  transfers between devices with their start and end apart: 13, of which 7 were waited for; matrix products, arithmetic and copies ran while one was open for 0% of the time, Pallas kernels for 7%

profile of v17, /device:TPU:0, one launch (start us, length us, event | category | flops | bytes accessed | tf_op | source)
XLA Modules:
  0.0 29.2 jit_solution(12903657020231702119)
XLA Ops:
  0.0 0.0 copy-start.1
  0.0 3.0 %collective-permute-start.1 = (bf16[128,1024]{1,0:T(8,128)(2,1)}, bf16[128,1024]{1,0:T(8,128)(2,1)S(1)}, u32[]{:S(2)}, u32[]{:S(2)}) collective-permute-start(bf16[128,1024]{1,0:T(8,128)(2,1)} %rows_ref.1), channel_id=1, source_target_pairs={{0,4},{1,5},{2,6},{3,7},{4,0},{5,1},{6,2},{7,3},{8,12},{9,13},{10,... | collective-permute-start | bytes 786440 | tf_op jit(solution)/shard_map/ppermute | solution.py:269
  3.0 0.0 copy-done.1
  3.0 0.0 copy-start
  3.0 1.0 %copy-done = bf16[128,1024]{1,0:T(8,128)(2,1)S(1)} copy-done((bf16[128,1024]{1,0:T(8,128)(2,1)S(1)}, bf16[128,1024]{1,0:T(8,128)(2,1)}, u32[]{:S(2)}) %copy-start) | copy-done | bytes 262168
  4.0 2.7 %collective-permute-start.6 = (bf16[136,1024]{1,0:T(8,128)(2,1)S(1)}, bf16[136,1024]{1,0:T(8,128)(2,1)S(1)}, u32[]{:S(2)}, u32[]{:S(2)}) collective-permute-start(bf16[136,1024]{1,0:T(8,128)(2,1)S(1)} %label.1), channel_id=1, source_target_pairs={{0,8},{1,9},{2,10},{3,11},{4,12},{5,13},{6,14},{7,15},{8,0},{9,1},... | collective-permute-start | bytes 835592 | tf_op jit(solution)/shard_map/ppermute | solution.py:269
  6.7 0.0 collective-permute-start.2
  6.7 1.5 %collective-permute-start.3 = (s32[1,128]{1,0:T(1,128)S(1)}, s32[1,128]{1,0:T(1,128)S(1)}, u32[]{:S(2)}, u32[]{:S(2)}) collective-permute-start(s32[1,128]{1,0:T(1,128)S(1)} %bitcast.4), channel_id=1, source_target_pairs={{0,2},{1,3},{2,0},{3,1},{4,6},{5,7},{6,4},{7,5},{8,10},{9,11},{10,... | collective-permute-start | bytes 1544 | tf_op jit(solution)/shard_map/ppermute | solution.py:269
  8.2 0.5 %collective-permute-start = (bf16[128,1024]{1,0:T(8,128)(2,1)S(1)}, bf16[128,1024]{1,0:T(8,128)(2,1)S(1)}, u32[]{:S(2)}, u32[]{:S(2)}) collective-permute-start(bf16[128,1024]{1,0:T(8,128)(2,1)S(1)} %copy-done), channel_id=1, source_target_pairs={{0,2},{1,3},{2,0},{3,1},{4,6},{5,7},{6,4},{7,5},{8,10},{9,11},{10,... | collective-permute-start | bytes 786440 | tf_op jit(solution)/shard_map/ppermute | solution.py:269
  8.7 1.5 %collective-permute-done.3.x_ids_ref = s32[1,128]{1,0:T(1,128)S(1)} collective-permute-done((s32[1,128]{1,0:T(1,128)S(1)}, s32[1,128]{1,0:T(1,128)S(1)}, u32[]{:S(2)}, u32[]{:S(2)}) %collective-permute-start.3) | collective-permute-done | bytes 544 | tf_op jit(solution)/shard_map/ppermute | solution.py:269
  10.2 3.9 %collective-permute-done.1.e_refs_0_ = bf16[128,1024]{1,0:T(8,128)(2,1)S(1)} collective-permute-done((bf16[128,1024]{1,0:T(8,128)(2,1)}, bf16[128,1024]{1,0:T(8,128)(2,1)S(1)}, u32[]{:S(2)}, u32[]{:S(2)}) %collective-permute-start.1) | collective-permute-done | bytes 262176 | tf_op jit(solution)/shard_map/ppermute | solution.py:269
  14.2 1.7 %collective-permute-start.9 = (bf16[128,1024]{1,0:T(8,128)(2,1)S(1)}, bf16[128,1024]{1,0:T(8,128)(2,1)S(1)}, u32[]{:S(2)}, u32[]{:S(2)}) collective-permute-start(bf16[128,1024]{1,0:T(8,128)(2,1)S(1)} %collective-permute-done.1.e_refs_0_), channel_id=1, source_target_pairs={{0,2},{1,3},{2,0},{3,1},{4,6},{5,7},{6,4},{7,5},{8,10},{9,11},{10,... | collective-permute-start | bytes 786440 | tf_op jit(solution)/shard_map/ppermute | solution.py:269
  15.8 0.0 collective-permute-start.4
  15.9 1.1 %collective-permute-done.4.c_ids_ref = s32[1,128]{1,0:T(1,128)S(1)} collective-permute-done((s32[1,128]{1,0:T(1,128)S(1)}, s32[1,128]{1,0:T(1,128)S(1)}, u32[]{:S(2)}, u32[]{:S(2)}) %collective-permute-start.4) | collective-permute-done | bytes 544 | tf_op jit(solution)/shard_map/ppermute | solution.py:269
  17.0 0.0 collective-permute-start.5
  17.0 3.6 %collective-permute-done.5.e_ids_ref = s32[2,128]{1,0:T(2,128)S(1)} collective-permute-done((s32[2,128]{1,0:T(2,128)S(1)}, s32[2,128]{1,0:T(2,128)S(1)}, u32[]{:S(2)}, u32[]{:S(2)}) %collective-permute-start.5) | collective-permute-done | bytes 1056 | tf_op jit(solution)/shard_map/ppermute | solution.py:269
  20.5 0.0 collective-permute-done.2.c_refs_0_
  20.5 0.0 collective-permute-done.6.h_refs_0_
  20.6 0.1 collective-permute-start.8
  20.7 0.6 %collective-permute-start.7 = (bf16[64,1024]{1,0:T(8,128)(2,1)S(1)}, bf16[64,1024]{1,0:T(8,128)(2,1)S(1)}, u32[]{:S(2)}, u32[]{:S(2)}) collective-permute-start(bf16[64,1024]{1,0:T(8,128)(2,1)S(1)} %slice.9), channel_id=1, source_target_pairs={{0,1},{1,0},{2,3},{3,2},{4,5},{5,4},{6,7},{7,6},{8,9},{9,8},{10,11... | collective-permute-start | bytes 393224 | tf_op jit(solution)/shard_map/ppermute | solution.py:269
  21.2 0.0 collective-permute-done.x_refs_0_
  21.2 0.8 %early.1 = (f32[8,384]{1,0:T(8,128)S(1)}, bf16[384,1024]{1,0:T(8,128)(2,1)S(1)}, bf16[128,1024]{1,0:T(8,128)(2,1)S(1)}) custom-call(bf16[128,1024]{1,0:T(8,128)(2,1)S(1)} %copy-done, bf16[128,1024]{1,0:T(8,128)(2,1)S(1)} %collective-permute-done.x_refs_0_, bf16[128,1024]{1,0:T(8,128)(2,1)S(1)} %collective-permute-done.1.e_refs_0_, ...), custom_call_target="tpu_custom_call" | custom-call | tf_op jit(solution)/shard_map/early/pallas_call | solution.py:187
  22.1 0.1 collective-permute-done.7.ch_refs_0_
  22.2 0.0 collective-permute-done.8.ch_refs_1_
  22.2 0.7 %middle.1 = (f32[8,128]{1,0:T(8,128)S(1)}, f32[8,128]{1,0:T(8,128)S(1)}, f32[8,128]{1,0:T(8,128)S(1)}, bf16[512,1024]{1,0:T(8,128)(2,1)S(1)}, s32[2,128]{1,0:T(2,128)S(1)}) custom-call(f32[8,384]{1,0:T(8,128)S(1)} %get-tuple-element.17.best_ref, bf16[384,1024]{1,0:T(8,128)(2,1)S(1)} %get-tuple-element.18.own_ref, ...), custom_call_target="tpu_custom_call" | custom-call | tf_op jit(solution)/shard_map/middle/pallas_call | solution.py:237
  22.9 0.4 %collective-permute-start.12 = (f32[8,128]{1,0:T(8,128)S(1)}, f32[8,128]{1,0:T(8,128)S(1)}, u32[]{:S(2)}, u32[]{:S(2)}) collective-permute-start(f32[8,128]{1,0:T(8,128)S(1)} %get-tuple-element.27), channel_id=1, source_target_pairs={{0,2},{1,3},{2,0},{3,1},{4,6},{5,7},{6,4},{7,5},{8,10},{9,11},{10,... | collective-permute-start | bytes 12296 | tf_op jit(solution)/shard_map/ppermute | solution.py:269
  23.3 0.0 collective-permute-done.9.xe_refs_0_
  23.3 0.6 %late.1 = f32[8,128]{1,0:T(8,128)S(1)} custom-call(bf16[512,1024]{1,0:T(8,128)(2,1)S(1)} %get-tuple-element.22.far_ref, bf16[128,1024]{1,0:T(8,128)(2,1)S(1)} %collective-permute-done.9.xe_refs_0_, s32[1,128]{1,0:T(1,128)S(1)} %bitcast.9, s32[1,128]{1,0:T(1,128)S(1)} %collective-permute-done.4.c_ids_ref, s32[2,128]{1,0:T(2,128)S(1)} %collective-permute-done.5.e_ids_ref, ...), custom_call_target="tpu_custom_call" | custom-call | tf_op jit(solution)/shard_map/late/pallas_call | solution.py:257
  23.9 1.2 %collective-permute-start.10 = (f32[8,128]{1,0:T(8,128)S(1)}, f32[8,128]{1,0:T(8,128)S(1)}, u32[]{:S(2)}, u32[]{:S(2)}) collective-permute-start(f32[8,128]{1,0:T(8,128)S(1)} %late.1), channel_id=1, source_target_pairs={{0,6},{1,7},{2,4},{3,5},{4,2},{5,3},{6,0},{7,1},{8,14},{9,15},{10,... | collective-permute-start | bytes 12296 | tf_op jit(solution)/shard_map/ppermute | solution.py:269
  25.1 2.0 %collective-permute-start.11 = (f32[8,128]{1,0:T(8,128)S(1)}, f32[8,128]{1,0:T(8,128)S(1)}, u32[]{:S(2)}, u32[]{:S(2)}) collective-permute-start(f32[8,128]{1,0:T(8,128)S(1)} %get-tuple-element.26), channel_id=1, source_target_pairs={{0,4},{1,5},{2,6},{3,7},{4,0},{5,1},{6,2},{7,3},{8,12},{9,13},{10,... | collective-permute-start | bytes 12296 | tf_op jit(solution)/shard_map/ppermute | solution.py:269
  27.1 0.0 collective-permute-done.12
  27.1 1.4 %collective-permute-done.10 = f32[8,128]{1,0:T(8,128)S(1)} collective-permute-done((f32[8,128]{1,0:T(8,128)S(1)}, f32[8,128]{1,0:T(8,128)S(1)}, u32[]{:S(2)}, u32[]{:S(2)}) %collective-permute-start.10) | collective-permute-done | bytes 4128 | tf_op jit(solution)/shard_map/ppermute | solution.py:269
  28.5 0.2 collective-permute-done.11
  28.7 0.5 %slice_bitcast_fusion = f32[128]{0:T(128)} fusion(f32[8,128]{1,0:T(8,128)S(1)} %maximum_maximum_fusion), kind=kLoop, calls=%fused_computation.2 | loop fusion | bytes 1024 | tf_op jit(solution)/shard_map/squeeze | solution.py:290
  (5 shorter events, 0.1 us)
Async XLA Ops:
  0.0 3.0 %copy-start.1 = (s32[128,1]{0,1:T(1,128)S(1)}, s32[128,1]{0,1:T(1,128)}, u32[]{:S(2)}) copy-start(s32[128,1]{0,1:T(1,128)} %param.3) | copy-start | bytes 1540
  0.0 14.2 %collective-permute-start.1 = (bf16[128,1024]{1,0:T(8,128)(2,1)}, bf16[128,1024]{1,0:T(8,128)(2,1)S(1)}, u32[]{:S(2)}, u32[]{:S(2)}) collective-permute-start(bf16[128,1024]{1,0:T(8,128)(2,1)} %rows_ref.1), channel_id=1, source_target_pairs={{0,4},{1,5},{2,6},{3,7},{4,0},{5,1},{6,2},{7,3},{8,12},{9,13},{10,... | collective-permute-start | bytes 786440 | tf_op jit(solution)/shard_map/ppermute | solution.py:269
  3.0 1.0 %copy-start = (bf16[128,1024]{1,0:T(8,128)(2,1)S(1)}, bf16[128,1024]{1,0:T(8,128)(2,1)}, u32[]{:S(2)}) copy-start(bf16[128,1024]{1,0:T(8,128)(2,1)} %rows_ref.1) | copy-start | bytes 786436
  4.0 16.5 %collective-permute-start.6 = (bf16[136,1024]{1,0:T(8,128)(2,1)S(1)}, bf16[136,1024]{1,0:T(8,128)(2,1)S(1)}, u32[]{:S(2)}, u32[]{:S(2)}) collective-permute-start(bf16[136,1024]{1,0:T(8,128)(2,1)S(1)} %label.1), channel_id=1, source_target_pairs={{0,8},{1,9},{2,10},{3,11},{4,12},{5,13},{6,14},{7,15},{8,0},{9,1},... | collective-permute-start | bytes 835592 | tf_op jit(solution)/shard_map/ppermute | solution.py:269
  6.7 13.8 %collective-permute-start.2 = (bf16[128,1024]{1,0:T(8,128)(2,1)S(1)}, bf16[128,1024]{1,0:T(8,128)(2,1)S(1)}, u32[]{:S(2)}, u32[]{:S(2)}) collective-permute-start(bf16[128,1024]{1,0:T(8,128)(2,1)S(1)} %copy-done), channel_id=1, source_target_pairs={{0,1},{1,0},{2,3},{3,2},{4,5},{5,4},{6,7},{7,6},{8,9},{9,8},{10,11... | collective-permute-start | bytes 786440 | tf_op jit(solution)/shard_map/ppermute | solution.py:269
  6.7 3.5 %collective-permute-start.3 = (s32[1,128]{1,0:T(1,128)S(1)}, s32[1,128]{1,0:T(1,128)S(1)}, u32[]{:S(2)}, u32[]{:S(2)}) collective-permute-start(s32[1,128]{1,0:T(1,128)S(1)} %bitcast.4), channel_id=1, source_target_pairs={{0,2},{1,3},{2,0},{3,1},{4,6},{5,7},{6,4},{7,5},{8,10},{9,11},{10,... | collective-permute-start | bytes 1544 | tf_op jit(solution)/shard_map/ppermute | solution.py:269
  8.2 13.0 %collective-permute-start = (bf16[128,1024]{1,0:T(8,128)(2,1)S(1)}, bf16[128,1024]{1,0:T(8,128)(2,1)S(1)}, u32[]{:S(2)}, u32[]{:S(2)}) collective-permute-start(bf16[128,1024]{1,0:T(8,128)(2,1)S(1)} %copy-done), channel_id=1, source_target_pairs={{0,2},{1,3},{2,0},{3,1},{4,6},{5,7},{6,4},{7,5},{8,10},{9,11},{10,... | collective-permute-start | bytes 786440 | tf_op jit(solution)/shard_map/ppermute | solution.py:269
  14.2 9.2 %collective-permute-start.9 = (bf16[128,1024]{1,0:T(8,128)(2,1)S(1)}, bf16[128,1024]{1,0:T(8,128)(2,1)S(1)}, u32[]{:S(2)}, u32[]{:S(2)}) collective-permute-start(bf16[128,1024]{1,0:T(8,128)(2,1)S(1)} %collective-permute-done.1.e_refs_0_), channel_id=1, source_target_pairs={{0,2},{1,3},{2,0},{3,1},{4,6},{5,7},{6,4},{7,5},{8,10},{9,11},{10,... | collective-permute-start | bytes 786440 | tf_op jit(solution)/shard_map/ppermute | solution.py:269
  15.8 1.1 %collective-permute-start.4 = (s32[1,128]{1,0:T(1,128)S(1)}, s32[1,128]{1,0:T(1,128)S(1)}, u32[]{:S(2)}, u32[]{:S(2)}) collective-permute-start(s32[1,128]{1,0:T(1,128)S(1)} %bitcast.5), channel_id=1, source_target_pairs={{0,1},{1,0},{2,3},{3,2},{4,5},{5,4},{6,7},{7,6},{8,9},{9,8},{10,11... | collective-permute-start | bytes 1544 | tf_op jit(solution)/shard_map/ppermute | solution.py:269
  17.0 3.6 %collective-permute-start.5 = (s32[2,128]{1,0:T(2,128)S(1)}, s32[2,128]{1,0:T(2,128)S(1)}, u32[]{:S(2)}, u32[]{:S(2)}) collective-permute-start(s32[2,128]{1,0:T(2,128)S(1)} %pad_add_fusion), channel_id=1, source_target_pairs={{0,4},{1,5},{2,6},{3,7},{4,0},{5,1},{6,2},{7,3},{8,12},{9,13},{10,... | collective-permute-start | bytes 3080 | tf_op jit(solution)/shard_map/ppermute | solution.py:269
  20.6 1.6 %collective-permute-start.8 = (bf16[72,1024]{1,0:T(8,128)(2,1)S(1)}, bf16[72,1024]{1,0:T(8,128)(2,1)S(1)}, u32[]{:S(2)}, u32[]{:S(2)}) collective-permute-start(bf16[72,1024]{1,0:T(8,128)(2,1)S(1)} %slice.10), channel_id=1, source_target_pairs={{0,1},{1,0},{2,3},{3,2},{4,5},{5,4},{6,7},{7,6},{8,9},{9,8},{10,11... | collective-permute-start | bytes 442376 | tf_op jit(solution)/shard_map/ppermute | solution.py:269
  20.7 1.5 %collective-permute-start.7 = (bf16[64,1024]{1,0:T(8,128)(2,1)S(1)}, bf16[64,1024]{1,0:T(8,128)(2,1)S(1)}, u32[]{:S(2)}, u32[]{:S(2)}) collective-permute-start(bf16[64,1024]{1,0:T(8,128)(2,1)S(1)} %slice.9), channel_id=1, source_target_pairs={{0,1},{1,0},{2,3},{3,2},{4,5},{5,4},{6,7},{7,6},{8,9},{9,8},{10,11... | collective-permute-start | bytes 393224 | tf_op jit(solution)/shard_map/ppermute | solution.py:269
  22.9 4.2 %collective-permute-start.12 = (f32[8,128]{1,0:T(8,128)S(1)}, f32[8,128]{1,0:T(8,128)S(1)}, u32[]{:S(2)}, u32[]{:S(2)}) collective-permute-start(f32[8,128]{1,0:T(8,128)S(1)} %get-tuple-element.27), channel_id=1, source_target_pairs={{0,2},{1,3},{2,0},{3,1},{4,6},{5,7},{6,4},{7,5},{8,10},{9,11},{10,... | collective-permute-start | bytes 12296 | tf_op jit(solution)/shard_map/ppermute | solution.py:269
  23.9 4.6 %collective-permute-start.10 = (f32[8,128]{1,0:T(8,128)S(1)}, f32[8,128]{1,0:T(8,128)S(1)}, u32[]{:S(2)}, u32[]{:S(2)}) collective-permute-start(f32[8,128]{1,0:T(8,128)S(1)} %late.1), channel_id=1, source_target_pairs={{0,6},{1,7},{2,4},{3,5},{4,2},{5,3},{6,0},{7,1},{8,14},{9,15},{10,... | collective-permute-start | bytes 12296 | tf_op jit(solution)/shard_map/ppermute | solution.py:269
  25.1 3.6 %collective-permute-start.11 = (f32[8,128]{1,0:T(8,128)S(1)}, f32[8,128]{1,0:T(8,128)S(1)}, u32[]{:S(2)}, u32[]{:S(2)}) collective-permute-start(f32[8,128]{1,0:T(8,128)S(1)} %get-tuple-element.26), channel_id=1, source_target_pairs={{0,4},{1,5},{2,6},{3,7},{4,0},{5,1},{6,2},{7,3},{8,12},{9,13},{10,... | collective-permute-start | bytes 12296 | tf_op jit(solution)/shard_map/ppermute | solution.py:269

commit v18 on v17

--- a/solution.py
+++ b/solution.py
@@ -272,13 +272,14 @@
     mine, ids = embeddings, assignment.reshape(1, rows)
     e = swap(LOW, mine)
     x = swap(SHARD, mine)
-    c = swap(SUB, mine)
     h = swap(HIGH, label(mine, ids))
     x_ids, c_ids = swap(SHARD, ids), swap(SUB, ids)
     e_ids = swap(LOW, jnp.concatenate([ids, x_ids]))
+    mine_then, _ = lax.optimization_barrier((mine, e_ids))
+    c = swap(SUB, mine_then)
     e_then, _ = lax.optimization_barrier((e, x_ids))
     xe = swap(SHARD, e_then)
-    h_then, *_ = lax.optimization_barrier((h, e_ids, c_ids, c))
+    h_then, _ = lax.optimization_barrier((h, c_ids))
     ch = [swap(SUB, h_then[: rows // 2]), swap(SUB, h_then[rows // 2 :])]
     x, e, h, c, xe = [x], [e], [h], [c], [xe]
     best, own, c = early(mine, x, e, c, [ids, x_ids, c_ids, e_ids])

time: 29.4 us -> 31.9 us (1.085)
  starting transfers between devices: 13.6 us -> 16.7 us
  waiting for transfers between devices: 11.9 us -> 11.4 us
    ppermute x13, starting transfers between devices: 13.6 us -> 16.7 us  [swap(): return lax.ppermute(array, AXES, [(i, i ^ flip) for i in range(16)])]
    ppermute x13, waiting for transfers between devices: 11.9 us -> 11.4 us  [swap(): return lax.ppermute(array, AXES, [(i, i ^ flip) for i in range(16)])]
  transfers between devices with their start and end apart: 13 -> 13, of which waited for: 7 -> 8; matrix products, arithmetic and copies ran while one was open for 0% -> 0% of each run, Pallas kernels for 7% -> 7%
where the time goes in v18:
time: 31.9 us; the launch traced here: 31.8 us
  starting transfers between devices  16.7 us (52%)
  waiting for transfers between devices  11.4 us (36%)
  Pallas kernels  2.11 us (7%)
  local copies, waits for them, and re-layouts  1.52 us (5%)
    ppermute x13, starting transfers between devices, swap(): return lax.ppermute(array, AXES, [(i, i ^ flip) for i in range(16)])  16.7 us
    ppermute x13, waiting for transfers between devices, swap(): return lax.ppermute(array, AXES, [(i, i ^ flip) for i in range(16)])  11.4 us
    unnamed x4, local copies, waits for them, and re-layouts  0.98 us
    pallas_call x1, Pallas kernels, early(): pl.pallas_call(early_kernel, out_shape=[jax.ShapeDtypeStruct((8, 3 * rows...  0.85 us
    pallas_call x1, Pallas kernels, middle(): pl.pallas_call(middle_kernel, out_shape=[jax.ShapeDtypeStruct((8, rows),...  0.68 us
  transfers between devices with their start and end apart: 13, of which 8 were waited for; matrix products, arithmetic and copies ran while one was open for 0% of the time, Pallas kernels for 7%

profile of v18, /device:TPU:0, one launch (start us, length us, event | category | flops | bytes accessed | tf_op | source)
XLA Modules:
  0.0 31.8 jit_solution(16020864677027479635)
XLA Ops:
  0.0 0.0 copy-start.1
  0.0 3.0 %collective-permute-start.1 = (bf16[128,1024]{1,0:T(8,128)(2,1)}, bf16[128,1024]{1,0:T(8,128)(2,1)S(1)}, u32[]{:S(2)}, u32[]{:S(2)}) collective-permute-start(bf16[128,1024]{1,0:T(8,128)(2,1)} %rows_ref.1), channel_id=1, source_target_pairs={{0,4},{1,5},{2,6},{3,7},{4,0},{5,1},{6,2},{7,3},{8,12},{9,13},{10,... | collective-permute-start | bytes 786440 | tf_op jit(solution)/shard_map/ppermute | solution.py:269
  3.0 0.0 copy-done.1
  3.0 0.0 copy-start
  3.0 1.0 %copy-done = bf16[128,1024]{1,0:T(8,128)(2,1)S(1)} copy-done((bf16[128,1024]{1,0:T(8,128)(2,1)S(1)}, bf16[128,1024]{1,0:T(8,128)(2,1)}, u32[]{:S(2)}) %copy-start) | copy-done | bytes 262168
  4.0 2.7 %collective-permute-start.6 = (bf16[136,1024]{1,0:T(8,128)(2,1)S(1)}, bf16[136,1024]{1,0:T(8,128)(2,1)S(1)}, u32[]{:S(2)}, u32[]{:S(2)}) collective-permute-start(bf16[136,1024]{1,0:T(8,128)(2,1)S(1)} %label.1), channel_id=1, source_target_pairs={{0,8},{1,9},{2,10},{3,11},{4,12},{5,13},{6,14},{7,15},{8,0},{9,1},... | collective-permute-start | bytes 835592 | tf_op jit(solution)/shard_map/ppermute | solution.py:269
  6.7 1.5 %collective-permute-start.2 = (s32[1,128]{1,0:T(1,128)S(1)}, s32[1,128]{1,0:T(1,128)S(1)}, u32[]{:S(2)}, u32[]{:S(2)}) collective-permute-start(s32[1,128]{1,0:T(1,128)S(1)} %bitcast.4), channel_id=1, source_target_pairs={{0,2},{1,3},{2,0},{3,1},{4,6},{5,7},{6,4},{7,5},{8,10},{9,11},{10,... | collective-permute-start | bytes 1544 | tf_op jit(solution)/shard_map/ppermute | solution.py:269
  8.2 2.0 %collective-permute-done.2.x_ids_ref = s32[1,128]{1,0:T(1,128)S(1)} collective-permute-done((s32[1,128]{1,0:T(1,128)S(1)}, s32[1,128]{1,0:T(1,128)S(1)}, u32[]{:S(2)}, u32[]{:S(2)}) %collective-permute-start.2) | collective-permute-done | bytes 544 | tf_op jit(solution)/shard_map/ppermute | solution.py:269
  10.2 0.6 %collective-permute-start.3 = (s32[2,128]{1,0:T(2,128)S(1)}, s32[2,128]{1,0:T(2,128)S(1)}, u32[]{:S(2)}, u32[]{:S(2)}) collective-permute-start(s32[2,128]{1,0:T(2,128)S(1)} %pad_add_fusion), channel_id=1, source_target_pairs={{0,4},{1,5},{2,6},{3,7},{4,0},{5,1},{6,2},{7,3},{8,12},{9,13},{10,... | collective-permute-start | bytes 3080 | tf_op jit(solution)/shard_map/ppermute | solution.py:269
  10.9 1.5 %collective-permute-start = (bf16[128,1024]{1,0:T(8,128)(2,1)S(1)}, bf16[128,1024]{1,0:T(8,128)(2,1)S(1)}, u32[]{:S(2)}, u32[]{:S(2)}) collective-permute-start(bf16[128,1024]{1,0:T(8,128)(2,1)S(1)} %copy-done), channel_id=1, source_target_pairs={{0,2},{1,3},{2,0},{3,1},{4,6},{5,7},{6,4},{7,5},{8,10},{9,11},{10,... | collective-permute-start | bytes 786440 | tf_op jit(solution)/shard_map/ppermute | solution.py:269
  12.4 2.5 %collective-permute-done.3.e_ids_ref = s32[2,128]{1,0:T(2,128)S(1)} collective-permute-done((s32[2,128]{1,0:T(2,128)S(1)}, s32[2,128]{1,0:T(2,128)S(1)}, u32[]{:S(2)}, u32[]{:S(2)}) %collective-permute-start.3) | collective-permute-done | bytes 1056 | tf_op jit(solution)/shard_map/ppermute | solution.py:269
  14.9 0.0 collective-permute-start.4
  14.9 0.0 collective-permute-done.1.e_refs_0_
  14.9 1.5 %collective-permute-start.9 = (bf16[128,1024]{1,0:T(8,128)(2,1)S(1)}, bf16[128,1024]{1,0:T(8,128)(2,1)S(1)}, u32[]{:S(2)}, u32[]{:S(2)}) collective-permute-start(bf16[128,1024]{1,0:T(8,128)(2,1)S(1)} %collective-permute-done.1.e_refs_0_), channel_id=1, source_target_pairs={{0,2},{1,3},{2,0},{3,1},{4,6},{5,7},{6,4},{7,5},{8,10},{9,11},{10,... | collective-permute-start | bytes 786440 | tf_op jit(solution)/shard_map/ppermute | solution.py:269
  16.4 0.2 collective-permute-start.5
  16.6 0.9 %collective-permute-done.5.c_ids_ref = s32[1,128]{1,0:T(1,128)S(1)} collective-permute-done((s32[1,128]{1,0:T(1,128)S(1)}, s32[1,128]{1,0:T(1,128)S(1)}, u32[]{:S(2)}, u32[]{:S(2)}) %collective-permute-start.5) | collective-permute-done | bytes 544 | tf_op jit(solution)/shard_map/ppermute | solution.py:269
  17.5 1.7 %collective-permute-done.6.h_refs_0_ = bf16[136,1024]{1,0:T(8,128)(2,1)S(1)} collective-permute-done((bf16[136,1024]{1,0:T(8,128)(2,1)S(1)}, bf16[136,1024]{1,0:T(8,128)(2,1)S(1)}, u32[]{:S(2)}, u32[]{:S(2)}) %collective-permute-start.6) | collective-permute-done | bytes 278560 | tf_op jit(solution)/shard_map/ppermute | solution.py:269
  19.1 0.1 collective-permute-start.8
  19.2 0.6 %collective-permute-start.7 = (bf16[64,1024]{1,0:T(8,128)(2,1)S(1)}, bf16[64,1024]{1,0:T(8,128)(2,1)S(1)}, u32[]{:S(2)}, u32[]{:S(2)}) collective-permute-start(bf16[64,1024]{1,0:T(8,128)(2,1)S(1)} %slice.9), channel_id=1, source_target_pairs={{0,1},{1,0},{2,3},{3,2},{4,5},{5,4},{6,7},{7,6},{8,9},{9,8},{10,11... | collective-permute-start | bytes 393224 | tf_op jit(solution)/shard_map/ppermute | solution.py:269
  19.8 0.0 collective-permute-done.x_refs_0_
  19.8 0.0 collective-permute-done.4.c_refs_0_
  19.8 0.8 %early.1 = (f32[8,384]{1,0:T(8,128)S(1)}, bf16[384,1024]{1,0:T(8,128)(2,1)S(1)}, bf16[128,1024]{1,0:T(8,128)(2,1)S(1)}) custom-call(bf16[128,1024]{1,0:T(8,128)(2,1)S(1)} %copy-done, bf16[128,1024]{1,0:T(8,128)(2,1)S(1)} %collective-permute-done.x_refs_0_, bf16[128,1024]{1,0:T(8,128)(2,1)S(1)} %collective-permute-done.1.e_refs_0_, ...), custom_call_target="tpu_custom_call" | custom-call | tf_op jit(solution)/shard_map/early/pallas_call | solution.py:187
  20.7 0.1 collective-permute-done.7.ch_refs_0_
  20.8 0.0 collective-permute-done.8.ch_refs_1_
  20.8 0.7 %middle.1 = (f32[8,128]{1,0:T(8,128)S(1)}, f32[8,128]{1,0:T(8,128)S(1)}, f32[8,128]{1,0:T(8,128)S(1)}, bf16[512,1024]{1,0:T(8,128)(2,1)S(1)}, s32[2,128]{1,0:T(2,128)S(1)}) custom-call(f32[8,384]{1,0:T(8,128)S(1)} %get-tuple-element.19.best_ref, bf16[384,1024]{1,0:T(8,128)(2,1)S(1)} %get-tuple-element.20.own_ref, ...), custom_call_target="tpu_custom_call" | custom-call | tf_op jit(solution)/shard_map/middle/pallas_call | solution.py:237
  21.5 1.6 %collective-permute-start.12 = (f32[8,128]{1,0:T(8,128)S(1)}, f32[8,128]{1,0:T(8,128)S(1)}, u32[]{:S(2)}, u32[]{:S(2)}) collective-permute-start(f32[8,128]{1,0:T(8,128)S(1)} %get-tuple-element.29), channel_id=1, source_target_pairs={{0,2},{1,3},{2,0},{3,1},{4,6},{5,7},{6,4},{7,5},{8,10},{9,11},{10,... | collective-permute-start | bytes 12296 | tf_op jit(solution)/shard_map/ppermute | solution.py:269
  23.1 0.5 %collective-permute-done.9.xe_refs_0_ = bf16[128,1024]{1,0:T(8,128)(2,1)S(1)} collective-permute-done((bf16[128,1024]{1,0:T(8,128)(2,1)S(1)}, bf16[128,1024]{1,0:T(8,128)(2,1)S(1)}, u32[]{:S(2)}, u32[]{:S(2)}) %collective-permute-start.9) | collective-permute-done | bytes 262176 | tf_op jit(solution)/shard_map/ppermute | solution.py:269
  23.6 0.6 %late.1 = f32[8,128]{1,0:T(8,128)S(1)} custom-call(bf16[512,1024]{1,0:T(8,128)(2,1)S(1)} %get-tuple-element.24.far_ref, bf16[128,1024]{1,0:T(8,128)(2,1)S(1)} %collective-permute-done.9.xe_refs_0_, s32[1,128]{1,0:T(1,128)S(1)} %bitcast.9, s32[1,128]{1,0:T(1,128)S(1)} %collective-permute-done.5.c_ids_ref, s32[2,128]{1,0:T(2,128)S(1)} %collective-permute-done.3.e_ids_ref, ...), custom_call_target="tpu_custom_call" | custom-call | tf_op jit(solution)/shard_map/late/pallas_call | solution.py:257
  24.1 3.5 %collective-permute-start.10 = (f32[8,128]{1,0:T(8,128)S(1)}, f32[8,128]{1,0:T(8,128)S(1)}, u32[]{:S(2)}, u32[]{:S(2)}) collective-permute-start(f32[8,128]{1,0:T(8,128)S(1)} %late.1), channel_id=1, source_target_pairs={{0,6},{1,7},{2,4},{3,5},{4,2},{5,3},{6,0},{7,1},{8,14},{9,15},{10,... | collective-permute-start | bytes 12296 | tf_op jit(solution)/shard_map/ppermute | solution.py:269
  27.6 0.0 collective-permute-start.11
  27.6 0.0 collective-permute-done.12
  27.6 1.6 %collective-permute-done.10 = f32[8,128]{1,0:T(8,128)S(1)} collective-permute-done((f32[8,128]{1,0:T(8,128)S(1)}, f32[8,128]{1,0:T(8,128)S(1)}, u32[]{:S(2)}, u32[]{:S(2)}) %collective-permute-start.10) | collective-permute-done | bytes 4128 | tf_op jit(solution)/shard_map/ppermute | solution.py:269
  29.2 2.0 %collective-permute-done.11 = f32[8,128]{1,0:T(8,128)S(1)} collective-permute-done((f32[8,128]{1,0:T(8,128)S(1)}, f32[8,128]{1,0:T(8,128)S(1)}, u32[]{:S(2)}, u32[]{:S(2)}) %collective-permute-start.11) | collective-permute-done | bytes 4128 | tf_op jit(solution)/shard_map/ppermute | solution.py:269
  31.3 0.5 %slice_bitcast_fusion = f32[128]{0:T(128)} fusion(f32[8,128]{1,0:T(8,128)S(1)} %maximum_maximum_fusion), kind=kLoop, calls=%fused_computation.2 | loop fusion | bytes 1024 | tf_op jit(solution)/shard_map/squeeze | solution.py:291
  (5 shorter events, 0.1 us)
Async XLA Ops:
  0.0 3.0 %copy-start.1 = (s32[128,1]{0,1:T(1,128)S(1)}, s32[128,1]{0,1:T(1,128)}, u32[]{:S(2)}) copy-start(s32[128,1]{0,1:T(1,128)} %param.3) | copy-start | bytes 1540
  0.0 14.9 %collective-permute-start.1 = (bf16[128,1024]{1,0:T(8,128)(2,1)}, bf16[128,1024]{1,0:T(8,128)(2,1)S(1)}, u32[]{:S(2)}, u32[]{:S(2)}) collective-permute-start(bf16[128,1024]{1,0:T(8,128)(2,1)} %rows_ref.1), channel_id=1, source_target_pairs={{0,4},{1,5},{2,6},{3,7},{4,0},{5,1},{6,2},{7,3},{8,12},{9,13},{10,... | collective-permute-start | bytes 786440 | tf_op jit(solution)/shard_map/ppermute | solution.py:269
  3.0 1.0 %copy-start = (bf16[128,1024]{1,0:T(8,128)(2,1)S(1)}, bf16[128,1024]{1,0:T(8,128)(2,1)}, u32[]{:S(2)}) copy-start(bf16[128,1024]{1,0:T(8,128)(2,1)} %rows_ref.1) | copy-start | bytes 786436
  4.0 15.1 %collective-permute-start.6 = (bf16[136,1024]{1,0:T(8,128)(2,1)S(1)}, bf16[136,1024]{1,0:T(8,128)(2,1)S(1)}, u32[]{:S(2)}, u32[]{:S(2)}) collective-permute-start(bf16[136,1024]{1,0:T(8,128)(2,1)S(1)} %label.1), channel_id=1, source_target_pairs={{0,8},{1,9},{2,10},{3,11},{4,12},{5,13},{6,14},{7,15},{8,0},{9,1},... | collective-permute-start | bytes 835592 | tf_op jit(solution)/shard_map/ppermute | solution.py:269
  6.7 3.5 %collective-permute-start.2 = (s32[1,128]{1,0:T(1,128)S(1)}, s32[1,128]{1,0:T(1,128)S(1)}, u32[]{:S(2)}, u32[]{:S(2)}) collective-permute-start(s32[1,128]{1,0:T(1,128)S(1)} %bitcast.4), channel_id=1, source_target_pairs={{0,2},{1,3},{2,0},{3,1},{4,6},{5,7},{6,4},{7,5},{8,10},{9,11},{10,... | collective-permute-start | bytes 1544 | tf_op jit(solution)/shard_map/ppermute | solution.py:269
  10.2 4.6 %collective-permute-start.3 = (s32[2,128]{1,0:T(2,128)S(1)}, s32[2,128]{1,0:T(2,128)S(1)}, u32[]{:S(2)}, u32[]{:S(2)}) collective-permute-start(s32[2,128]{1,0:T(2,128)S(1)} %pad_add_fusion), channel_id=1, source_target_pairs={{0,4},{1,5},{2,6},{3,7},{4,0},{5,1},{6,2},{7,3},{8,12},{9,13},{10,... | collective-permute-start | bytes 3080 | tf_op jit(solution)/shard_map/ppermute | solution.py:269
  10.9 8.9 %collective-permute-start = (bf16[128,1024]{1,0:T(8,128)(2,1)S(1)}, bf16[128,1024]{1,0:T(8,128)(2,1)S(1)}, u32[]{:S(2)}, u32[]{:S(2)}) collective-permute-start(bf16[128,1024]{1,0:T(8,128)(2,1)S(1)} %copy-done), channel_id=1, source_target_pairs={{0,2},{1,3},{2,0},{3,1},{4,6},{5,7},{6,4},{7,5},{8,10},{9,11},{10,... | collective-permute-start | bytes 786440 | tf_op jit(solution)/shard_map/ppermute | solution.py:269
  14.9 5.0 %collective-permute-start.4 = (bf16[128,1024]{1,0:T(8,128)(2,1)S(1)}, bf16[128,1024]{1,0:T(8,128)(2,1)S(1)}, u32[]{:S(2)}, u32[]{:S(2)}) collective-permute-start(bf16[128,1024]{1,0:T(8,128)(2,1)S(1)} %copy-done), channel_id=1, source_target_pairs={{0,1},{1,0},{2,3},{3,2},{4,5},{5,4},{6,7},{7,6},{8,9},{9,8},{10,11... | collective-permute-start | bytes 786440 | tf_op jit(solution)/shard_map/ppermute | solution.py:269
  14.9 8.7 %collective-permute-start.9 = (bf16[128,1024]{1,0:T(8,128)(2,1)S(1)}, bf16[128,1024]{1,0:T(8,128)(2,1)S(1)}, u32[]{:S(2)}, u32[]{:S(2)}) collective-permute-start(bf16[128,1024]{1,0:T(8,128)(2,1)S(1)} %collective-permute-done.1.e_refs_0_), channel_id=1, source_target_pairs={{0,2},{1,3},{2,0},{3,1},{4,6},{5,7},{6,4},{7,5},{8,10},{9,11},{10,... | collective-permute-start | bytes 786440 | tf_op jit(solution)/shard_map/ppermute | solution.py:269
  16.4 1.1 %collective-permute-start.5 = (s32[1,128]{1,0:T(1,128)S(1)}, s32[1,128]{1,0:T(1,128)S(1)}, u32[]{:S(2)}, u32[]{:S(2)}) collective-permute-start(s32[1,128]{1,0:T(1,128)S(1)} %bitcast.6), channel_id=1, source_target_pairs={{0,1},{1,0},{2,3},{3,2},{4,5},{5,4},{6,7},{7,6},{8,9},{9,8},{10,11... | collective-permute-start | bytes 1544 | tf_op jit(solution)/shard_map/ppermute | solution.py:269
  19.1 1.6 %collective-permute-start.8 = (bf16[72,1024]{1,0:T(8,128)(2,1)S(1)}, bf16[72,1024]{1,0:T(8,128)(2,1)S(1)}, u32[]{:S(2)}, u32[]{:S(2)}) collective-permute-start(bf16[72,1024]{1,0:T(8,128)(2,1)S(1)} %slice.10), channel_id=1, source_target_pairs={{0,1},{1,0},{2,3},{3,2},{4,5},{5,4},{6,7},{7,6},{8,9},{9,8},{10,11... | collective-permute-start | bytes 442376 | tf_op jit(solution)/shard_map/ppermute | solution.py:269
  19.2 1.5 %collective-permute-start.7 = (bf16[64,1024]{1,0:T(8,128)(2,1)S(1)}, bf16[64,1024]{1,0:T(8,128)(2,1)S(1)}, u32[]{:S(2)}, u32[]{:S(2)}) collective-permute-start(bf16[64,1024]{1,0:T(8,128)(2,1)S(1)} %slice.9), channel_id=1, source_target_pairs={{0,1},{1,0},{2,3},{3,2},{4,5},{5,4},{6,7},{7,6},{8,9},{9,8},{10,11... | collective-permute-start | bytes 393224 | tf_op jit(solution)/shard_map/ppermute | solution.py:269
  21.5 6.2 %collective-permute-start.12 = (f32[8,128]{1,0:T(8,128)S(1)}, f32[8,128]{1,0:T(8,128)S(1)}, u32[]{:S(2)}, u32[]{:S(2)}) collective-permute-start(f32[8,128]{1,0:T(8,128)S(1)} %get-tuple-element.29), channel_id=1, source_target_pairs={{0,2},{1,3},{2,0},{3,1},{4,6},{5,7},{6,4},{7,5},{8,10},{9,11},{10,... | collective-permute-start | bytes 12296 | tf_op jit(solution)/shard_map/ppermute | solution.py:269
  24.1 5.1 %collective-permute-start.10 = (f32[8,128]{1,0:T(8,128)S(1)}, f32[8,128]{1,0:T(8,128)S(1)}, u32[]{:S(2)}, u32[]{:S(2)}) collective-permute-start(f32[8,128]{1,0:T(8,128)S(1)} %late.1), channel_id=1, source_target_pairs={{0,6},{1,7},{2,4},{3,5},{4,2},{5,3},{6,0},{7,1},{8,14},{9,15},{10,... | collective-permute-start | bytes 12296 | tf_op jit(solution)/shard_map/ppermute | solution.py:269
  27.6 3.6 %collective-permute-start.11 = (f32[8,128]{1,0:T(8,128)S(1)}, f32[8,128]{1,0:T(8,128)S(1)}, u32[]{:S(2)}, u32[]{:S(2)}) collective-permute-start(f32[8,128]{1,0:T(8,128)S(1)} %get-tuple-element.28), channel_id=1, source_target_pairs={{0,4},{1,5},{2,6},{3,7},{4,0},{5,1},{6,2},{7,3},{8,12},{9,13},{10,... | collective-permute-start | bytes 12296 | tf_op jit(solution)/shard_map/ppermute | solution.py:269

commit v19 on v17

--- a/solution.py
+++ b/solution.py
@@ -276,7 +276,7 @@
     h = swap(HIGH, label(mine, ids))
     x_ids, c_ids = swap(SHARD, ids), swap(SUB, ids)
     e_ids = swap(LOW, jnp.concatenate([ids, x_ids]))
-    e_then, _ = lax.optimization_barrier((e, x_ids))
+    e_then, _, _ = lax.optimization_barrier((e, x_ids, c))
     xe = swap(SHARD, e_then)
     h_then, *_ = lax.optimization_barrier((h, e_ids, c_ids, c))
     ch = [swap(SUB, h_then[: rows // 2]), swap(SUB, h_then[rows // 2 :])]

time: 29.4 us -> 29.6 us (level)
  transfers between devices with their start and end apart: 13 -> 13, of which waited for: 7 -> 6; matrix products, arithmetic and copies ran while one was open for 0% -> 0% of each run, Pallas kernels for 7% -> 7%
where the time goes in v19:
time: 29.6 us; the launch traced here: 29.4 us
  starting transfers between devices  13.8 us (47%)
  waiting for transfers between devices  11.9 us (40%)
  Pallas kernels  2.12 us (7%)
  local copies, waits for them, and re-layouts  1.52 us (5%)
    ppermute x13, starting transfers between devices, swap(): return lax.ppermute(array, AXES, [(i, i ^ flip) for i in range(16)])  13.8 us
    ppermute x13, waiting for transfers between devices, swap(): return lax.ppermute(array, AXES, [(i, i ^ flip) for i in range(16)])  11.9 us
    unnamed x4, local copies, waits for them, and re-layouts  0.98 us
    pallas_call x1, Pallas kernels, early(): pl.pallas_call(early_kernel, out_shape=[jax.ShapeDtypeStruct((8, 3 * rows...  0.85 us
    pallas_call x1, Pallas kernels, middle(): pl.pallas_call(middle_kernel, out_shape=[jax.ShapeDtypeStruct((8, rows),...  0.69 us
  transfers between devices with their start and end apart: 13, of which 6 were waited for; matrix products, arithmetic and copies ran while one was open for 0% of the time, Pallas kernels for 7%

profile of v19, /device:TPU:0, one launch (start us, length us, event | category | flops | bytes accessed | tf_op | source)
XLA Modules:
  0.0 29.4 jit_solution(3217491717191368117)
XLA Ops:
  0.0 0.0 copy-start.1
  0.0 0.5 %collective-permute-start.2 = (bf16[128,1024]{1,0:T(8,128)(2,1)}, bf16[128,1024]{1,0:T(8,128)(2,1)S(1)}, u32[]{:S(2)}, u32[]{:S(2)}) collective-permute-start(bf16[128,1024]{1,0:T(8,128)(2,1)} %rows_ref.1), channel_id=1, source_target_pairs={{0,1},{1,0},{2,3},{3,2},{4,5},{5,4},{6,7},{7,6},{8,9},{9,8},{10,11... | collective-permute-start | bytes 786440 | tf_op jit(solution)/shard_map/ppermute | solution.py:269
  0.5 2.6 %collective-permute-start.1 = (bf16[128,1024]{1,0:T(8,128)(2,1)}, bf16[128,1024]{1,0:T(8,128)(2,1)S(1)}, u32[]{:S(2)}, u32[]{:S(2)}) collective-permute-start(bf16[128,1024]{1,0:T(8,128)(2,1)} %rows_ref.1), channel_id=1, source_target_pairs={{0,4},{1,5},{2,6},{3,7},{4,0},{5,1},{6,2},{7,3},{8,12},{9,13},{10,... | collective-permute-start | bytes 786440 | tf_op jit(solution)/shard_map/ppermute | solution.py:269
  3.1 0.0 copy-done.1
  3.1 0.0 copy-start
  3.1 1.0 %copy-done = bf16[128,1024]{1,0:T(8,128)(2,1)S(1)} copy-done((bf16[128,1024]{1,0:T(8,128)(2,1)S(1)}, bf16[128,1024]{1,0:T(8,128)(2,1)}, u32[]{:S(2)}) %copy-start) | copy-done | bytes 262168
  4.1 2.7 %collective-permute-start.6 = (bf16[136,1024]{1,0:T(8,128)(2,1)S(1)}, bf16[136,1024]{1,0:T(8,128)(2,1)S(1)}, u32[]{:S(2)}, u32[]{:S(2)}) collective-permute-start(bf16[136,1024]{1,0:T(8,128)(2,1)S(1)} %label.1), channel_id=1, source_target_pairs={{0,8},{1,9},{2,10},{3,11},{4,12},{5,13},{6,14},{7,15},{8,0},{9,1},... | collective-permute-start | bytes 835592 | tf_op jit(solution)/shard_map/ppermute | solution.py:269
  6.8 1.5 %collective-permute-start.3 = (s32[1,128]{1,0:T(1,128)S(1)}, s32[1,128]{1,0:T(1,128)S(1)}, u32[]{:S(2)}, u32[]{:S(2)}) collective-permute-start(s32[1,128]{1,0:T(1,128)S(1)} %bitcast.4), channel_id=1, source_target_pairs={{0,2},{1,3},{2,0},{3,1},{4,6},{5,7},{6,4},{7,5},{8,10},{9,11},{10,... | collective-permute-start | bytes 1544 | tf_op jit(solution)/shard_map/ppermute | solution.py:269
  8.2 0.5 %collective-permute-start = (bf16[128,1024]{1,0:T(8,128)(2,1)S(1)}, bf16[128,1024]{1,0:T(8,128)(2,1)S(1)}, u32[]{:S(2)}, u32[]{:S(2)}) collective-permute-start(bf16[128,1024]{1,0:T(8,128)(2,1)S(1)} %copy-done), channel_id=1, source_target_pairs={{0,2},{1,3},{2,0},{3,1},{4,6},{5,7},{6,4},{7,5},{8,10},{9,11},{10,... | collective-permute-start | bytes 786440 | tf_op jit(solution)/shard_map/ppermute | solution.py:269
  8.8 1.5 %collective-permute-done.3.x_ids_ref = s32[1,128]{1,0:T(1,128)S(1)} collective-permute-done((s32[1,128]{1,0:T(1,128)S(1)}, s32[1,128]{1,0:T(1,128)S(1)}, u32[]{:S(2)}, u32[]{:S(2)}) %collective-permute-start.3) | collective-permute-done | bytes 544 | tf_op jit(solution)/shard_map/ppermute | solution.py:269
  10.3 0.0 collective-permute-done.2.c_refs_0_
  10.3 4.6 %collective-permute-done.1.e_refs_0_ = bf16[128,1024]{1,0:T(8,128)(2,1)S(1)} collective-permute-done((bf16[128,1024]{1,0:T(8,128)(2,1)}, bf16[128,1024]{1,0:T(8,128)(2,1)S(1)}, u32[]{:S(2)}, u32[]{:S(2)}) %collective-permute-start.1) | collective-permute-done | bytes 262176 | tf_op jit(solution)/shard_map/ppermute | solution.py:269
  14.9 1.7 %collective-permute-start.9 = (bf16[128,1024]{1,0:T(8,128)(2,1)S(1)}, bf16[128,1024]{1,0:T(8,128)(2,1)S(1)}, u32[]{:S(2)}, u32[]{:S(2)}) collective-permute-start(bf16[128,1024]{1,0:T(8,128)(2,1)S(1)} %collective-permute-done.1.e_refs_0_), channel_id=1, source_target_pairs={{0,2},{1,3},{2,0},{3,1},{4,6},{5,7},{6,4},{7,5},{8,10},{9,11},{10,... | collective-permute-start | bytes 786440 | tf_op jit(solution)/shard_map/ppermute | solution.py:269
  16.5 0.0 collective-permute-start.5
  16.5 0.1 collective-permute-start.4
  16.6 1.1 %collective-permute-done.4.c_ids_ref = s32[1,128]{1,0:T(1,128)S(1)} collective-permute-done((s32[1,128]{1,0:T(1,128)S(1)}, s32[1,128]{1,0:T(1,128)S(1)}, u32[]{:S(2)}, u32[]{:S(2)}) %collective-permute-start.4) | collective-permute-done | bytes 544 | tf_op jit(solution)/shard_map/ppermute | solution.py:269
  17.7 2.4 %collective-permute-done.5.e_ids_ref = s32[2,128]{1,0:T(2,128)S(1)} collective-permute-done((s32[2,128]{1,0:T(2,128)S(1)}, s32[2,128]{1,0:T(2,128)S(1)}, u32[]{:S(2)}, u32[]{:S(2)}) %collective-permute-start.5) | collective-permute-done | bytes 1056 | tf_op jit(solution)/shard_map/ppermute | solution.py:269
  20.1 0.0 collective-permute-done.6.h_refs_0_
  20.1 0.1 collective-permute-start.8
  20.2 0.6 %collective-permute-start.7 = (bf16[64,1024]{1,0:T(8,128)(2,1)S(1)}, bf16[64,1024]{1,0:T(8,128)(2,1)S(1)}, u32[]{:S(2)}, u32[]{:S(2)}) collective-permute-start(bf16[64,1024]{1,0:T(8,128)(2,1)S(1)} %slice.9), channel_id=1, source_target_pairs={{0,1},{1,0},{2,3},{3,2},{4,5},{5,4},{6,7},{7,6},{8,9},{9,8},{10,11... | collective-permute-start | bytes 393224 | tf_op jit(solution)/shard_map/ppermute | solution.py:269
  20.8 0.0 collective-permute-done.x_refs_0_
  20.8 0.8 %early.1 = (f32[8,384]{1,0:T(8,128)S(1)}, bf16[384,1024]{1,0:T(8,128)(2,1)S(1)}, bf16[128,1024]{1,0:T(8,128)(2,1)S(1)}) custom-call(bf16[128,1024]{1,0:T(8,128)(2,1)S(1)} %copy-done, bf16[128,1024]{1,0:T(8,128)(2,1)S(1)} %collective-permute-done.x_refs_0_, bf16[128,1024]{1,0:T(8,128)(2,1)S(1)} %collective-permute-done.1.e_refs_0_, ...), custom_call_target="tpu_custom_call" | custom-call | tf_op jit(solution)/shard_map/early/pallas_call | solution.py:187
  21.6 0.1 collective-permute-done.7.ch_refs_0_
  21.8 0.0 collective-permute-done.8.ch_refs_1_
  21.8 0.7 %middle.1 = (f32[8,128]{1,0:T(8,128)S(1)}, f32[8,128]{1,0:T(8,128)S(1)}, f32[8,128]{1,0:T(8,128)S(1)}, bf16[512,1024]{1,0:T(8,128)(2,1)S(1)}, s32[2,128]{1,0:T(2,128)S(1)}) custom-call(f32[8,384]{1,0:T(8,128)S(1)} %get-tuple-element.17.best_ref, bf16[384,1024]{1,0:T(8,128)(2,1)S(1)} %get-tuple-element.18.own_ref, ...), custom_call_target="tpu_custom_call" | custom-call | tf_op jit(solution)/shard_map/middle/pallas_call | solution.py:237
  22.4 1.3 %collective-permute-start.12 = (f32[8,128]{1,0:T(8,128)S(1)}, f32[8,128]{1,0:T(8,128)S(1)}, u32[]{:S(2)}, u32[]{:S(2)}) collective-permute-start(f32[8,128]{1,0:T(8,128)S(1)} %get-tuple-element.27), channel_id=1, source_target_pairs={{0,2},{1,3},{2,0},{3,1},{4,6},{5,7},{6,4},{7,5},{8,10},{9,11},{10,... | collective-permute-start | bytes 12296 | tf_op jit(solution)/shard_map/ppermute | solution.py:269
  23.7 0.0 collective-permute-done.9.xe_refs_0_
  23.7 0.6 %late.1 = f32[8,128]{1,0:T(8,128)S(1)} custom-call(bf16[512,1024]{1,0:T(8,128)(2,1)S(1)} %get-tuple-element.22.far_ref, bf16[128,1024]{1,0:T(8,128)(2,1)S(1)} %collective-permute-done.9.xe_refs_0_, s32[1,128]{1,0:T(1,128)S(1)} %bitcast.9, s32[1,128]{1,0:T(1,128)S(1)} %collective-permute-done.4.c_ids_ref, s32[2,128]{1,0:T(2,128)S(1)} %collective-permute-done.5.e_ids_ref, ...), custom_call_target="tpu_custom_call" | custom-call | tf_op jit(solution)/shard_map/late/pallas_call | solution.py:257
  24.3 0.3 %collective-permute-start.10 = (f32[8,128]{1,0:T(8,128)S(1)}, f32[8,128]{1,0:T(8,128)S(1)}, u32[]{:S(2)}, u32[]{:S(2)}) collective-permute-start(f32[8,128]{1,0:T(8,128)S(1)} %late.1), channel_id=1, source_target_pairs={{0,6},{1,7},{2,4},{3,5},{4,2},{5,3},{6,0},{7,1},{8,14},{9,15},{10,... | collective-permute-start | bytes 12296 | tf_op jit(solution)/shard_map/ppermute | solution.py:269
  24.6 2.0 %collective-permute-start.11 = (f32[8,128]{1,0:T(8,128)S(1)}, f32[8,128]{1,0:T(8,128)S(1)}, u32[]{:S(2)}, u32[]{:S(2)}) collective-permute-start(f32[8,128]{1,0:T(8,128)S(1)} %get-tuple-element.26), channel_id=1, source_target_pairs={{0,4},{1,5},{2,6},{3,7},{4,0},{5,1},{6,2},{7,3},{8,12},{9,13},{10,... | collective-permute-start | bytes 12296 | tf_op jit(solution)/shard_map/ppermute | solution.py:269
  26.7 0.0 collective-permute-done.12
  26.7 2.2 %collective-permute-done.10 = f32[8,128]{1,0:T(8,128)S(1)} collective-permute-done((f32[8,128]{1,0:T(8,128)S(1)}, f32[8,128]{1,0:T(8,128)S(1)}, u32[]{:S(2)}, u32[]{:S(2)}) %collective-permute-start.10) | collective-permute-done | bytes 4128 | tf_op jit(solution)/shard_map/ppermute | solution.py:269
  28.9 0.0 collective-permute-done.11
  28.9 0.5 %slice_bitcast_fusion = f32[128]{0:T(128)} fusion(f32[8,128]{1,0:T(8,128)S(1)} %maximum_maximum_fusion), kind=kLoop, calls=%fused_computation.2 | loop fusion | bytes 1024 | tf_op jit(solution)/shard_map/squeeze | solution.py:290
  (5 shorter events, 0.1 us)
Async XLA Ops:
  0.0 3.1 %copy-start.1 = (s32[128,1]{0,1:T(1,128)S(1)}, s32[128,1]{0,1:T(1,128)}, u32[]{:S(2)}) copy-start(s32[128,1]{0,1:T(1,128)} %param.3) | copy-start | bytes 1540
  0.0 10.3 %collective-permute-start.2 = (bf16[128,1024]{1,0:T(8,128)(2,1)}, bf16[128,1024]{1,0:T(8,128)(2,1)S(1)}, u32[]{:S(2)}, u32[]{:S(2)}) collective-permute-start(bf16[128,1024]{1,0:T(8,128)(2,1)} %rows_ref.1), channel_id=1, source_target_pairs={{0,1},{1,0},{2,3},{3,2},{4,5},{5,4},{6,7},{7,6},{8,9},{9,8},{10,11... | collective-permute-start | bytes 786440 | tf_op jit(solution)/shard_map/ppermute | solution.py:269
  0.5 14.4 %collective-permute-start.1 = (bf16[128,1024]{1,0:T(8,128)(2,1)}, bf16[128,1024]{1,0:T(8,128)(2,1)S(1)}, u32[]{:S(2)}, u32[]{:S(2)}) collective-permute-start(bf16[128,1024]{1,0:T(8,128)(2,1)} %rows_ref.1), channel_id=1, source_target_pairs={{0,4},{1,5},{2,6},{3,7},{4,0},{5,1},{6,2},{7,3},{8,12},{9,13},{10,... | collective-permute-start | bytes 786440 | tf_op jit(solution)/shard_map/ppermute | solution.py:269
  3.1 1.0 %copy-start = (bf16[128,1024]{1,0:T(8,128)(2,1)S(1)}, bf16[128,1024]{1,0:T(8,128)(2,1)}, u32[]{:S(2)}) copy-start(bf16[128,1024]{1,0:T(8,128)(2,1)} %rows_ref.1) | copy-start | bytes 786436
  4.1 16.0 %collective-permute-start.6 = (bf16[136,1024]{1,0:T(8,128)(2,1)S(1)}, bf16[136,1024]{1,0:T(8,128)(2,1)S(1)}, u32[]{:S(2)}, u32[]{:S(2)}) collective-permute-start(bf16[136,1024]{1,0:T(8,128)(2,1)S(1)} %label.1), channel_id=1, source_target_pairs={{0,8},{1,9},{2,10},{3,11},{4,12},{5,13},{6,14},{7,15},{8,0},{9,1},... | collective-permute-start | bytes 835592 | tf_op jit(solution)/shard_map/ppermute | solution.py:269
  6.8 3.5 %collective-permute-start.3 = (s32[1,128]{1,0:T(1,128)S(1)}, s32[1,128]{1,0:T(1,128)S(1)}, u32[]{:S(2)}, u32[]{:S(2)}) collective-permute-start(s32[1,128]{1,0:T(1,128)S(1)} %bitcast.4), channel_id=1, source_target_pairs={{0,2},{1,3},{2,0},{3,1},{4,6},{5,7},{6,4},{7,5},{8,10},{9,11},{10,... | collective-permute-start | bytes 1544 | tf_op jit(solution)/shard_map/ppermute | solution.py:269
  8.2 12.5 %collective-permute-start = (bf16[128,1024]{1,0:T(8,128)(2,1)S(1)}, bf16[128,1024]{1,0:T(8,128)(2,1)S(1)}, u32[]{:S(2)}, u32[]{:S(2)}) collective-permute-start(bf16[128,1024]{1,0:T(8,128)(2,1)S(1)} %copy-done), channel_id=1, source_target_pairs={{0,2},{1,3},{2,0},{3,1},{4,6},{5,7},{6,4},{7,5},{8,10},{9,11},{10,... | collective-permute-start | bytes 786440 | tf_op jit(solution)/shard_map/ppermute | solution.py:269
  14.9 8.9 %collective-permute-start.9 = (bf16[128,1024]{1,0:T(8,128)(2,1)S(1)}, bf16[128,1024]{1,0:T(8,128)(2,1)S(1)}, u32[]{:S(2)}, u32[]{:S(2)}) collective-permute-start(bf16[128,1024]{1,0:T(8,128)(2,1)S(1)} %collective-permute-done.1.e_refs_0_), channel_id=1, source_target_pairs={{0,2},{1,3},{2,0},{3,1},{4,6},{5,7},{6,4},{7,5},{8,10},{9,11},{10,... | collective-permute-start | bytes 786440 | tf_op jit(solution)/shard_map/ppermute | solution.py:269
  16.5 3.6 %collective-permute-start.5 = (s32[2,128]{1,0:T(2,128)S(1)}, s32[2,128]{1,0:T(2,128)S(1)}, u32[]{:S(2)}, u32[]{:S(2)}) collective-permute-start(s32[2,128]{1,0:T(2,128)S(1)} %pad_add_fusion), channel_id=1, source_target_pairs={{0,4},{1,5},{2,6},{3,7},{4,0},{5,1},{6,2},{7,3},{8,12},{9,13},{10,... | collective-permute-start | bytes 3080 | tf_op jit(solution)/shard_map/ppermute | solution.py:269
  16.5 1.2 %collective-permute-start.4 = (s32[1,128]{1,0:T(1,128)S(1)}, s32[1,128]{1,0:T(1,128)S(1)}, u32[]{:S(2)}, u32[]{:S(2)}) collective-permute-start(s32[1,128]{1,0:T(1,128)S(1)} %bitcast.6), channel_id=1, source_target_pairs={{0,1},{1,0},{2,3},{3,2},{4,5},{5,4},{6,7},{7,6},{8,9},{9,8},{10,11... | collective-permute-start | bytes 1544 | tf_op jit(solution)/shard_map/ppermute | solution.py:269
  20.1 1.6 %collective-permute-start.8 = (bf16[72,1024]{1,0:T(8,128)(2,1)S(1)}, bf16[72,1024]{1,0:T(8,128)(2,1)S(1)}, u32[]{:S(2)}, u32[]{:S(2)}) collective-permute-start(bf16[72,1024]{1,0:T(8,128)(2,1)S(1)} %slice.10), channel_id=1, source_target_pairs={{0,1},{1,0},{2,3},{3,2},{4,5},{5,4},{6,7},{7,6},{8,9},{9,8},{10,11... | collective-permute-start | bytes 442376 | tf_op jit(solution)/shard_map/ppermute | solution.py:269
  20.2 1.5 %collective-permute-start.7 = (bf16[64,1024]{1,0:T(8,128)(2,1)S(1)}, bf16[64,1024]{1,0:T(8,128)(2,1)S(1)}, u32[]{:S(2)}, u32[]{:S(2)}) collective-permute-start(bf16[64,1024]{1,0:T(8,128)(2,1)S(1)} %slice.9), channel_id=1, source_target_pairs={{0,1},{1,0},{2,3},{3,2},{4,5},{5,4},{6,7},{7,6},{8,9},{9,8},{10,11... | collective-permute-start | bytes 393224 | tf_op jit(solution)/shard_map/ppermute | solution.py:269
  22.4 4.2 %collective-permute-start.12 = (f32[8,128]{1,0:T(8,128)S(1)}, f32[8,128]{1,0:T(8,128)S(1)}, u32[]{:S(2)}, u32[]{:S(2)}) collective-permute-start(f32[8,128]{1,0:T(8,128)S(1)} %get-tuple-element.27), channel_id=1, source_target_pairs={{0,2},{1,3},{2,0},{3,1},{4,6},{5,7},{6,4},{7,5},{8,10},{9,11},{10,... | collective-permute-start | bytes 12296 | tf_op jit(solution)/shard_map/ppermute | solution.py:269
  24.3 4.6 %collective-permute-start.10 = (f32[8,128]{1,0:T(8,128)S(1)}, f32[8,128]{1,0:T(8,128)S(1)}, u32[]{:S(2)}, u32[]{:S(2)}) collective-permute-start(f32[8,128]{1,0:T(8,128)S(1)} %late.1), channel_id=1, source_target_pairs={{0,6},{1,7},{2,4},{3,5},{4,2},{5,3},{6,0},{7,1},{8,14},{9,15},{10,... | collective-permute-start | bytes 12296 | tf_op jit(solution)/shard_map/ppermute | solution.py:269
  24.6 4.3 %collective-permute-start.11 = (f32[8,128]{1,0:T(8,128)S(1)}, f32[8,128]{1,0:T(8,128)S(1)}, u32[]{:S(2)}, u32[]{:S(2)}) collective-permute-start(f32[8,128]{1,0:T(8,128)S(1)} %get-tuple-element.26), channel_id=1, source_target_pairs={{0,4},{1,5},{2,6},{3,7},{4,0},{5,1},{6,2},{7,3},{8,12},{9,13},{10,... | collective-permute-start | bytes 12296 | tf_op jit(solution)/shard_map/ppermute | solution.py:269

commit v20 on v13

--- a/solution.py
+++ b/solution.py
@@ -256,9 +256,11 @@
     x, e, h, c, xe = [x], [e], [h], [c], [xe]
     best, own, c = early(mine, x, e, c, [ids, x_ids, c_ids, e_ids])
     found, x_best, e_best, far = middle(best, own, c, h, ch, [ids, x_ids, c_ids, e_ids, h_ids])
-    x_best, e_best = swap(SHARD, x_best), swap(LOW, e_best)
-    xe_best = swap(LOW | SHARD, late(far, xe, [ids, c_ids, e_ids, h_ids]))
-    return jnp.maximum(jnp.maximum(found, x_best), jnp.maximum(e_best, xe_best))[0]
+    x_best = swap(SHARD, x_best)
+    xe_best = late(far, xe, [ids, c_ids, e_ids, h_ids])
+    e_best, xe_best = lax.optimization_barrier((e_best, xe_best))
+    xe_best, e_best = swap(LOW | SHARD, xe_best), swap(LOW, e_best)
+    return jnp.maximum(jnp.maximum(jnp.maximum(xe_best, e_best), x_best), found)[0]
 
 
 def shared_owner(embeddings, assignment):

time: 29 us -> 31.3 us (1.079)
  waiting for transfers between devices: 9.05 us -> 11.3 us
    ppermute x14, waiting for transfers between devices: 9.05 us -> 11.3 us  [swap(): return lax.ppermute(array, AXES, [(i, i ^ flip) for i in range(16)])]
  transfers between devices with their start and end apart: 14 -> 14, of which waited for: 6 -> 8; matrix products, arithmetic and copies ran while one was open for 0% -> 0% of each run, Pallas kernels for 7% -> 5%
where the time goes in v20:
time: 31.3 us; the launch traced here: 31.2 us
  starting transfers between devices  17.2 us (55%)
  waiting for transfers between devices  11.3 us (36%)
  Pallas kernels  2.09 us (7%)
  local copies, waits for them, and re-layouts  0.54 us (2%)
    ppermute x14, starting transfers between devices, swap(): return lax.ppermute(array, AXES, [(i, i ^ flip) for i in range(16)])  17.2 us
    ppermute x14, waiting for transfers between devices, swap(): return lax.ppermute(array, AXES, [(i, i ^ flip) for i in range(16)])  11.3 us
    pallas_call x1, Pallas kernels, early(): pl.pallas_call(early_kernel, out_shape=[jax.ShapeDtypeStruct((8, 3 * rows...  0.84 us
    pallas_call x1, Pallas kernels, middle(): pl.pallas_call(middle_kernel, out_shape=[jax.ShapeDtypeStruct((8, rows),...  0.68 us
  transfers between devices with their start and end apart: 14, of which 8 were waited for; matrix products, arithmetic and copies ran while one was open for 0% of the time, Pallas kernels for 5%

profile of v20, /device:TPU:0, one launch (start us, length us, event | category | flops | bytes accessed | tf_op | source)
XLA Modules:
  0.0 31.2 jit_solution(14938191185775473227)
XLA Ops:
  0.0 0.0 copy-start.1
  0.0 0.5 %collective-permute-start.2 = (bf16[128,1024]{1,0:T(8,128)(2,1)}, bf16[128,1024]{1,0:T(8,128)(2,1)S(1)}, u32[]{:S(2)}, u32[]{:S(2)}) collective-permute-start(bf16[128,1024]{1,0:T(8,128)(2,1)} %mine_ref.1), channel_id=1, source_target_pairs={{0,1},{1,0},{2,3},{3,2},{4,5},{5,4},{6,7},{7,6},{8,9},{9,8},{10,11... | collective-permute-start | bytes 786440 | tf_op jit(solution)/shard_map/ppermute | solution.py:241
  0.5 2.6 %collective-permute-start.1 = (bf16[128,1024]{1,0:T(8,128)(2,1)}, bf16[128,1024]{1,0:T(8,128)(2,1)S(1)}, u32[]{:S(2)}, u32[]{:S(2)}) collective-permute-start(bf16[128,1024]{1,0:T(8,128)(2,1)} %mine_ref.1), channel_id=1, source_target_pairs={{0,4},{1,5},{2,6},{3,7},{4,0},{5,1},{6,2},{7,3},{8,12},{9,13},{10,... | collective-permute-start | bytes 786440 | tf_op jit(solution)/shard_map/ppermute | solution.py:241
  3.1 1.5 %collective-permute-start = (bf16[128,1024]{1,0:T(8,128)(2,1)}, bf16[128,1024]{1,0:T(8,128)(2,1)S(1)}, u32[]{:S(2)}, u32[]{:S(2)}) collective-permute-start(bf16[128,1024]{1,0:T(8,128)(2,1)} %mine_ref.1), channel_id=1, source_target_pairs={{0,2},{1,3},{2,0},{3,1},{4,6},{5,7},{6,4},{7,5},{8,10},{9,11},{10,... | collective-permute-start | bytes 786440 | tf_op jit(solution)/shard_map/ppermute | solution.py:241
  4.6 0.0 collective-permute-done.2.c_refs_0_
  4.6 2.6 %collective-permute-start.6 = (bf16[128,1024]{1,0:T(8,128)(2,1)}, bf16[128,1024]{1,0:T(8,128)(2,1)S(1)}, u32[]{:S(2)}, u32[]{:S(2)}) collective-permute-start(bf16[128,1024]{1,0:T(8,128)(2,1)} %mine_ref.1), channel_id=1, source_target_pairs={{0,8},{1,9},{2,10},{3,11},{4,12},{5,13},{6,14},{7,15},{8,0},{9,1},... | collective-permute-start | bytes 786440 | tf_op jit(solution)/shard_map/ppermute | solution.py:241
  7.2 0.0 copy-done.1
  7.2 0.0 collective-permute-start.4
  7.2 0.5 %collective-permute-start.3 = (s32[1,128]{1,0:T(1,128)S(1)}, s32[1,128]{1,0:T(1,128)S(1)}, u32[]{:S(2)}, u32[]{:S(2)}) collective-permute-start(s32[1,128]{1,0:T(1,128)S(1)} %bitcast.4), channel_id=1, source_target_pairs={{0,2},{1,3},{2,0},{3,1},{4,6},{5,7},{6,4},{7,5},{8,10},{9,11},{10,... | collective-permute-start | bytes 1544 | tf_op jit(solution)/shard_map/ppermute | solution.py:241
  7.7 0.6 %collective-permute-done.4.c_ids_ref = s32[1,128]{1,0:T(1,128)S(1)} collective-permute-done((s32[1,128]{1,0:T(1,128)S(1)}, s32[1,128]{1,0:T(1,128)S(1)}, u32[]{:S(2)}, u32[]{:S(2)}) %collective-permute-start.4) | collective-permute-done | bytes 544 | tf_op jit(solution)/shard_map/ppermute | solution.py:241
  8.3 3.4 %collective-permute-done.3.x_ids_ref = s32[1,128]{1,0:T(1,128)S(1)} collective-permute-done((s32[1,128]{1,0:T(1,128)S(1)}, s32[1,128]{1,0:T(1,128)S(1)}, u32[]{:S(2)}, u32[]{:S(2)}) %collective-permute-start.3) | collective-permute-done | bytes 544 | tf_op jit(solution)/shard_map/ppermute | solution.py:241
  11.8 2.6 %collective-permute-start.7 = (s32[2,128]{1,0:T(2,128)S(1)}, s32[2,128]{1,0:T(2,128)S(1)}, u32[]{:S(2)}, u32[]{:S(2)}) collective-permute-start(s32[2,128]{1,0:T(2,128)S(1)} %get-tuple-element.29), channel_id=1, source_target_pairs={{0,8},{1,9},{2,10},{3,11},{4,12},{5,13},{6,14},{7,15},{8,0},{9,1},... | collective-permute-start | bytes 3080 | tf_op jit(solution)/shard_map/ppermute | solution.py:241
  14.3 0.0 copy-start
  14.3 0.4 %collective-permute-start.5 = (s32[2,128]{1,0:T(2,128)S(1)}, s32[2,128]{1,0:T(2,128)S(1)}, u32[]{:S(2)}, u32[]{:S(2)}) collective-permute-start(s32[2,128]{1,0:T(2,128)S(1)} %get-tuple-element.30), channel_id=1, source_target_pairs={{0,4},{1,5},{2,6},{3,7},{4,0},{5,1},{6,2},{7,3},{8,12},{9,13},{10,... | collective-permute-start | bytes 3080 | tf_op jit(solution)/shard_map/ppermute | solution.py:241
  14.8 0.0 collective-permute-done.1.e_refs_0_
  14.8 2.3 %collective-permute-start.10 = (bf16[128,1024]{1,0:T(8,128)(2,1)S(1)}, bf16[128,1024]{1,0:T(8,128)(2,1)S(1)}, u32[]{:S(2)}, u32[]{:S(2)}) collective-permute-start(bf16[128,1024]{1,0:T(8,128)(2,1)S(1)} %collective-permute-done.1.e_refs_0_), channel_id=1, source_target_pairs={{0,2},{1,3},{2,0},{3,1},{4,6},{5,7},{6,4},{7,5},{8,10},{9,11},{10,... | collective-permute-start | bytes 786440 | tf_op jit(solution)/shard_map/ppermute | solution.py:241
  17.1 2.4 %collective-permute-done.7.h_ids_ref = s32[2,128]{1,0:T(2,128)S(1)} collective-permute-done((s32[2,128]{1,0:T(2,128)S(1)}, s32[2,128]{1,0:T(2,128)S(1)}, u32[]{:S(2)}, u32[]{:S(2)}) %collective-permute-start.7) | collective-permute-done | bytes 1056 | tf_op jit(solution)/shard_map/ppermute | solution.py:241
  19.6 0.0 collective-permute-done.5.e_ids_ref
  19.6 0.0 collective-permute-done.x_refs_0_
  19.6 0.0 collective-permute-done.6.h_refs_0_
  19.6 0.1 collective-permute-start.9
  19.7 0.5 %collective-permute-start.8 = (bf16[64,1024]{1,0:T(8,128)(2,1)S(1)}, bf16[64,1024]{1,0:T(8,128)(2,1)S(1)}, u32[]{:S(2)}, u32[]{:S(2)}) collective-permute-start(bf16[64,1024]{1,0:T(8,128)(2,1)S(1)} %get-tuple-element.28), channel_id=1, source_target_pairs={{0,1},{1,0},{2,3},{3,2},{4,5},{5,4},{6,7},{7,6},{8,9},{9,8},{10,11... | collective-permute-start | bytes 393224 | tf_op jit(solution)/shard_map/ppermute | solution.py:241
  20.2 0.0 copy-done
  20.2 0.8 %early.1 = (f32[8,384]{1,0:T(8,128)S(1)}, bf16[384,1024]{1,0:T(8,128)(2,1)S(1)}, bf16[128,1024]{1,0:T(8,128)(2,1)S(1)}) custom-call(bf16[128,1024]{1,0:T(8,128)(2,1)S(1)} %copy-done, bf16[128,1024]{1,0:T(8,128)(2,1)S(1)} %collective-permute-done.x_refs_0_, bf16[128,1024]{1,0:T(8,128)(2,1)S(1)} %collective-permute-done.1.e_refs_0_, ...), custom_call_target="tpu_custom_call" | custom-call | tf_op jit(solution)/shard_map/early/pallas_call | solution.py:179
  21.0 0.0 collective-permute-done.9.ch_refs_1_
  21.0 0.2 collective-permute-done.8.ch_refs_0_
  21.2 0.7 %middle.1 = (f32[8,128]{1,0:T(8,128)S(1)}, f32[8,128]{1,0:T(8,128)S(1)}, f32[8,128]{1,0:T(8,128)S(1)}, bf16[512,1024]{1,0:T(8,128)(2,1)S(1)}) custom-call(f32[8,384]{1,0:T(8,128)S(1)} %get-tuple-element.16.best_ref, bf16[384,1024]{1,0:T(8,128)(2,1)S(1)} %get-tuple-element.17.own_ref, bf16[128,1024]{1,0:T(8,128)(2,1)S(1)} %get-tuple-element.18.c_ref, ...), custom_call_target="tpu_custom_call" | custom-call | tf_op jit(solution)/shard_map/middle/pallas_call | solution.py:209
  21.9 1.3 %collective-permute-done.10.xe_refs_0_ = bf16[128,1024]{1,0:T(8,128)(2,1)S(1)} collective-permute-done((bf16[128,1024]{1,0:T(8,128)(2,1)S(1)}, bf16[128,1024]{1,0:T(8,128)(2,1)S(1)}, u32[]{:S(2)}, u32[]{:S(2)}) %collective-permute-start.10) | collective-permute-done | bytes 262176 | tf_op jit(solution)/shard_map/ppermute | solution.py:241
  23.2 0.6 %late.1 = f32[8,128]{1,0:T(8,128)S(1)} custom-call(bf16[512,1024]{1,0:T(8,128)(2,1)S(1)} %get-tuple-element.22.far_ref, bf16[128,1024]{1,0:T(8,128)(2,1)S(1)} %collective-permute-done.10.xe_refs_0_, s32[1,128]{1,0:T(1,128)S(1)} %bitcast.8, s32[1,128]{1,0:T(1,128)S(1)} %collective-permute-done.4.c_ids_ref, s32[2,128]{1,0:T(2,128)S(1)} %collective-permute-done.5.e_ids_ref, ...), custom_call_target="tpu_custom_call" | custom-call | tf_op jit(solution)/shard_map/late/pallas_call | solution.py:229
  23.8 1.1 %collective-permute-start.11 = (f32[8,128]{1,0:T(8,128)S(1)}, f32[8,128]{1,0:T(8,128)S(1)}, u32[]{:S(2)}, u32[]{:S(2)}) collective-permute-start(f32[8,128]{1,0:T(8,128)S(1)} %late.1), channel_id=1, source_target_pairs={{0,6},{1,7},{2,4},{3,5},{4,2},{5,3},{6,0},{7,1},{8,14},{9,15},{10,... | collective-permute-start | bytes 12296 | tf_op jit(solution)/shard_map/ppermute | solution.py:241
  24.9 2.2 %collective-permute-start.12 = (f32[8,128]{1,0:T(8,128)S(1)}, f32[8,128]{1,0:T(8,128)S(1)}, u32[]{:S(2)}, u32[]{:S(2)}) collective-permute-start(f32[8,128]{1,0:T(8,128)S(1)} %get-tuple-element.24), channel_id=1, source_target_pairs={{0,4},{1,5},{2,6},{3,7},{4,0},{5,1},{6,2},{7,3},{8,12},{9,13},{10,... | collective-permute-start | bytes 12296 | tf_op jit(solution)/shard_map/ppermute | solution.py:241
  27.1 0.3 collective-permute-start.13
  27.4 1.0 %collective-permute-done.11 = f32[8,128]{1,0:T(8,128)S(1)} collective-permute-done((f32[8,128]{1,0:T(8,128)S(1)}, f32[8,128]{1,0:T(8,128)S(1)}, u32[]{:S(2)}, u32[]{:S(2)}) %collective-permute-start.11) | collective-permute-done | bytes 4128 | tf_op jit(solution)/shard_map/ppermute | solution.py:241
  28.4 0.3 %collective-permute-done.12 = f32[8,128]{1,0:T(8,128)S(1)} collective-permute-done((f32[8,128]{1,0:T(8,128)S(1)}, f32[8,128]{1,0:T(8,128)S(1)}, u32[]{:S(2)}, u32[]{:S(2)}) %collective-permute-start.12) | collective-permute-done | bytes 4128 | tf_op jit(solution)/shard_map/ppermute | solution.py:241
  28.7 2.0 %collective-permute-done.13 = f32[8,128]{1,0:T(8,128)S(1)} collective-permute-done((f32[8,128]{1,0:T(8,128)S(1)}, f32[8,128]{1,0:T(8,128)S(1)}, u32[]{:S(2)}, u32[]{:S(2)}) %collective-permute-start.13) | collective-permute-done | bytes 4128 | tf_op jit(solution)/shard_map/ppermute | solution.py:241
  30.7 0.5 %slice_bitcast_fusion = f32[128]{0:T(128)} fusion(f32[8,128]{1,0:T(8,128)S(1)} %maximum_maximum_fusion), kind=kLoop, calls=%fused_computation.3 | loop fusion | bytes 1024 | tf_op jit(solution)/shard_map/squeeze | solution.py:263
  (3 shorter events, 0.0 us)
Async XLA Ops:
  0.0 7.2 %copy-start.1 = (s32[128,1]{0,1:T(1,128)S(1)}, s32[128,1]{0,1:T(1,128)}, u32[]{:S(2)}) copy-start(s32[128,1]{0,1:T(1,128)} %param.3) | copy-start | bytes 1540
  0.0 4.6 %collective-permute-start.2 = (bf16[128,1024]{1,0:T(8,128)(2,1)}, bf16[128,1024]{1,0:T(8,128)(2,1)S(1)}, u32[]{:S(2)}, u32[]{:S(2)}) collective-permute-start(bf16[128,1024]{1,0:T(8,128)(2,1)} %mine_ref.1), channel_id=1, source_target_pairs={{0,1},{1,0},{2,3},{3,2},{4,5},{5,4},{6,7},{7,6},{8,9},{9,8},{10,11... | collective-permute-start | bytes 786440 | tf_op jit(solution)/shard_map/ppermute | solution.py:241
  0.5 14.3 %collective-permute-start.1 = (bf16[128,1024]{1,0:T(8,128)(2,1)}, bf16[128,1024]{1,0:T(8,128)(2,1)S(1)}, u32[]{:S(2)}, u32[]{:S(2)}) collective-permute-start(bf16[128,1024]{1,0:T(8,128)(2,1)} %mine_ref.1), channel_id=1, source_target_pairs={{0,4},{1,5},{2,6},{3,7},{4,0},{5,1},{6,2},{7,3},{8,12},{9,13},{10,... | collective-permute-start | bytes 786440 | tf_op jit(solution)/shard_map/ppermute | solution.py:241
  3.1 16.5 %collective-permute-start = (bf16[128,1024]{1,0:T(8,128)(2,1)}, bf16[128,1024]{1,0:T(8,128)(2,1)S(1)}, u32[]{:S(2)}, u32[]{:S(2)}) collective-permute-start(bf16[128,1024]{1,0:T(8,128)(2,1)} %mine_ref.1), channel_id=1, source_target_pairs={{0,2},{1,3},{2,0},{3,1},{4,6},{5,7},{6,4},{7,5},{8,10},{9,11},{10,... | collective-permute-start | bytes 786440 | tf_op jit(solution)/shard_map/ppermute | solution.py:241
  4.6 15.0 %collective-permute-start.6 = (bf16[128,1024]{1,0:T(8,128)(2,1)}, bf16[128,1024]{1,0:T(8,128)(2,1)S(1)}, u32[]{:S(2)}, u32[]{:S(2)}) collective-permute-start(bf16[128,1024]{1,0:T(8,128)(2,1)} %mine_ref.1), channel_id=1, source_target_pairs={{0,8},{1,9},{2,10},{3,11},{4,12},{5,13},{6,14},{7,15},{8,0},{9,1},... | collective-permute-start | bytes 786440 | tf_op jit(solution)/shard_map/ppermute | solution.py:241
  7.2 1.1 %collective-permute-start.4 = (s32[1,128]{1,0:T(1,128)S(1)}, s32[1,128]{1,0:T(1,128)S(1)}, u32[]{:S(2)}, u32[]{:S(2)}) collective-permute-start(s32[1,128]{1,0:T(1,128)S(1)} %bitcast.3), channel_id=1, source_target_pairs={{0,1},{1,0},{2,3},{3,2},{4,5},{5,4},{6,7},{7,6},{8,9},{9,8},{10,11... | collective-permute-start | bytes 1544 | tf_op jit(solution)/shard_map/ppermute | solution.py:241
  7.2 4.6 %collective-permute-start.3 = (s32[1,128]{1,0:T(1,128)S(1)}, s32[1,128]{1,0:T(1,128)S(1)}, u32[]{:S(2)}, u32[]{:S(2)}) collective-permute-start(s32[1,128]{1,0:T(1,128)S(1)} %bitcast.4), channel_id=1, source_target_pairs={{0,2},{1,3},{2,0},{3,1},{4,6},{5,7},{6,4},{7,5},{8,10},{9,11},{10,... | collective-permute-start | bytes 1544 | tf_op jit(solution)/shard_map/ppermute | solution.py:241
  11.8 7.8 %collective-permute-start.7 = (s32[2,128]{1,0:T(2,128)S(1)}, s32[2,128]{1,0:T(2,128)S(1)}, u32[]{:S(2)}, u32[]{:S(2)}) collective-permute-start(s32[2,128]{1,0:T(2,128)S(1)} %get-tuple-element.29), channel_id=1, source_target_pairs={{0,8},{1,9},{2,10},{3,11},{4,12},{5,13},{6,14},{7,15},{8,0},{9,1},... | collective-permute-start | bytes 3080 | tf_op jit(solution)/shard_map/ppermute | solution.py:241
  14.3 5.8 %copy-start = (bf16[128,1024]{1,0:T(8,128)(2,1)S(1)}, bf16[128,1024]{1,0:T(8,128)(2,1)}, u32[]{:S(2)}) copy-start(bf16[128,1024]{1,0:T(8,128)(2,1)} %mine_ref.1) | copy-start | bytes 786436
  14.3 5.2 %collective-permute-start.5 = (s32[2,128]{1,0:T(2,128)S(1)}, s32[2,128]{1,0:T(2,128)S(1)}, u32[]{:S(2)}, u32[]{:S(2)}) collective-permute-start(s32[2,128]{1,0:T(2,128)S(1)} %get-tuple-element.30), channel_id=1, source_target_pairs={{0,4},{1,5},{2,6},{3,7},{4,0},{5,1},{6,2},{7,3},{8,12},{9,13},{10,... | collective-permute-start | bytes 3080 | tf_op jit(solution)/shard_map/ppermute | solution.py:241
  14.8 8.4 %collective-permute-start.10 = (bf16[128,1024]{1,0:T(8,128)(2,1)S(1)}, bf16[128,1024]{1,0:T(8,128)(2,1)S(1)}, u32[]{:S(2)}, u32[]{:S(2)}) collective-permute-start(bf16[128,1024]{1,0:T(8,128)(2,1)S(1)} %collective-permute-done.1.e_refs_0_), channel_id=1, source_target_pairs={{0,2},{1,3},{2,0},{3,1},{4,6},{5,7},{6,4},{7,5},{8,10},{9,11},{10,... | collective-permute-start | bytes 786440 | tf_op jit(solution)/shard_map/ppermute | solution.py:241
  19.6 1.4 %collective-permute-start.9 = (bf16[64,1024]{1,0:T(8,128)(2,1)S(1)}, bf16[64,1024]{1,0:T(8,128)(2,1)S(1)}, u32[]{:S(2)}, u32[]{:S(2)}) collective-permute-start(bf16[64,1024]{1,0:T(8,128)(2,1)S(1)} %get-tuple-element.27), channel_id=1, source_target_pairs={{0,1},{1,0},{2,3},{3,2},{4,5},{5,4},{6,7},{7,6},{8,9},{9,8},{10,11... | collective-permute-start | bytes 393224 | tf_op jit(solution)/shard_map/ppermute | solution.py:241
  19.7 1.5 %collective-permute-start.8 = (bf16[64,1024]{1,0:T(8,128)(2,1)S(1)}, bf16[64,1024]{1,0:T(8,128)(2,1)S(1)}, u32[]{:S(2)}, u32[]{:S(2)}) collective-permute-start(bf16[64,1024]{1,0:T(8,128)(2,1)S(1)} %get-tuple-element.28), channel_id=1, source_target_pairs={{0,1},{1,0},{2,3},{3,2},{4,5},{5,4},{6,7},{7,6},{8,9},{9,8},{10,11... | collective-permute-start | bytes 393224 | tf_op jit(solution)/shard_map/ppermute | solution.py:241
  23.8 4.6 %collective-permute-start.11 = (f32[8,128]{1,0:T(8,128)S(1)}, f32[8,128]{1,0:T(8,128)S(1)}, u32[]{:S(2)}, u32[]{:S(2)}) collective-permute-start(f32[8,128]{1,0:T(8,128)S(1)} %late.1), channel_id=1, source_target_pairs={{0,6},{1,7},{2,4},{3,5},{4,2},{5,3},{6,0},{7,1},{8,14},{9,15},{10,... | collective-permute-start | bytes 12296 | tf_op jit(solution)/shard_map/ppermute | solution.py:241
  24.9 3.8 %collective-permute-start.12 = (f32[8,128]{1,0:T(8,128)S(1)}, f32[8,128]{1,0:T(8,128)S(1)}, u32[]{:S(2)}, u32[]{:S(2)}) collective-permute-start(f32[8,128]{1,0:T(8,128)S(1)} %get-tuple-element.24), channel_id=1, source_target_pairs={{0,4},{1,5},{2,6},{3,7},{4,0},{5,1},{6,2},{7,3},{8,12},{9,13},{10,... | collective-permute-start | bytes 12296 | tf_op jit(solution)/shard_map/ppermute | solution.py:241
  27.1 3.6 %collective-permute-start.13 = (f32[8,128]{1,0:T(8,128)S(1)}, f32[8,128]{1,0:T(8,128)S(1)}, u32[]{:S(2)}, u32[]{:S(2)}) collective-permute-start(f32[8,128]{1,0:T(8,128)S(1)} %get-tuple-element.25), channel_id=1, source_target_pairs={{0,2},{1,3},{2,0},{3,1},{4,6},{5,7},{6,4},{7,5},{8,10},{9,11},{10,... | collective-permute-start | bytes 12296 | tf_op jit(solution)/shard_map/ppermute | solution.py:241

commit v21 on v13

--- a/solution.py
+++ b/solution.py
@@ -164,57 +164,62 @@
     return jnp.concatenate([unit_of(ref[...]) for ref in refs], axis=0)
 
 
-def early_kernel(mine_ref, x_refs, e_refs, c_refs, ids_ref, x_ids_ref, c_ids_ref, e_ids_ref, best_ref, own_ref, c_ref):
-    mine, c = unit_of(mine_ref[...]), block(c_refs)
+def early_kernel(
+    mine_ref, x_refs, e_refs, c_refs, h_refs, ids_ref, x_ids_ref, c_ids_ref, e_ids_ref, h_ids_ref,
+    best_ref, own_ref, far_ref,
+):
+    mine, c, h = unit_of(mine_ref[...]), block(c_refs), block(h_refs)
     own = jnp.concatenate([mine, block(x_refs), block(e_refs)], axis=0)
     own_ids = jnp.concatenate([ids_ref[...], x_ids_ref[...], e_ids_ref[:1, :]], axis=1)
-    best = best_of(own, own_ids, [mine, c], [ids_ref[...], c_ids_ref[...]], True)
-    best_ref[...] = jnp.broadcast_to(best, best_ref.shape)
+    other_ids = [ids_ref[...], c_ids_ref[...], h_ids_ref[:1, :]]
+    best_ref[...] = jnp.broadcast_to(best_of(own, own_ids, [mine, c, h], other_ids, True), best_ref.shape)
     own_ref[...] = own
-    c_ref[...] = c
-
-
-def early(mine, x, e, c, ids):
+    far_ref[...] = jnp.concatenate([mine, c, h], axis=0)
+
+
+def early(mine, x, e, c, h, ids):
     rows, width = mine.shape
     return pl.pallas_call(
         early_kernel,
         out_shape=[
             jax.ShapeDtypeStruct((8, 3 * rows), jnp.float32),
             jax.ShapeDtypeStruct((3 * rows, width), jnp.bfloat16),
-            jax.ShapeDtypeStruct((rows, width), jnp.bfloat16),
+            jax.ShapeDtypeStruct((3 * rows, width), jnp.bfloat16),
         ],
-        in_specs=(VMEM, [VMEM] * len(x), [VMEM] * len(e), [VMEM] * len(c), *[VMEM] * len(ids)),
+        in_specs=(
+            VMEM, [VMEM] * len(x), [VMEM] * len(e), [VMEM] * len(c), [VMEM] * len(h), *[VMEM] * len(ids)
+        ),
         out_specs=[VMEM] * 3,
         compiler_params=LIMIT,
         name="early",
-    )(mine, x, e, c, *ids)
+    )(mine, x, e, c, h, *ids)
 
 
 def middle_kernel(
-    best_ref, own_ref, c_ref, h_refs, ch_refs, ids_ref, x_ids_ref, c_ids_ref, e_ids_ref, h_ids_ref,
+    best_ref, own_ref, near_ref, ch_refs, ids_ref, x_ids_ref, e_ids_ref, h_ids_ref,
     mine_out_ref, x_out_ref, e_out_ref, far_ref,
 ):
-    h, ch = block(h_refs), block(ch_refs)
+    ch = block(ch_refs)
     own_ids = jnp.concatenate([ids_ref[...], x_ids_ref[...], e_ids_ref[:1, :]], axis=1)
-    best = best_of(own_ref[...], own_ids, [h, ch], [h_ids_ref[:1, :], h_ids_ref[1:, :]])
+    best = best_of(own_ref[...], own_ids, [ch], [h_ids_ref[1:, :]])
     best = jnp.maximum(best, best_ref[:1, :])
-    rows = c_ref.shape[0]
+    rows = ch.shape[0]
     for place, out_ref in enumerate((mine_out_ref, x_out_ref, e_out_ref)):
         out_ref[...] = jnp.broadcast_to(best[:, place * rows : (place + 1) * rows], out_ref.shape)
-    far_ref[...] = jnp.concatenate([own_ref[:rows], c_ref[...], h, ch], axis=0)
-
-
-def middle(best, own, c, h, ch, ids):
-    rows, width = c.shape
+    far_ref[...] = jnp.concatenate([near_ref[...], ch], axis=0)
+
+
+def middle(best, own, near, ch, ids):
+    rows, width = own.shape[0] // 3, own.shape[1]
     return pl.pallas_call(
         middle_kernel,
         out_shape=[jax.ShapeDtypeStruct((8, rows), jnp.float32)] * 3
         + [jax.ShapeDtypeStruct((4 * rows, width), jnp.bfloat16)],
-        in_specs=(VMEM, VMEM, VMEM, [VMEM] * len(h), [VMEM] * len(ch), *[VMEM] * len(ids)),
+        in_specs=(VMEM, VMEM, VMEM, [VMEM] * len(ch), *[VMEM] * len(ids)),
         out_specs=[VMEM] * 4,
         compiler_params=LIMIT,
         name="middle",
-    )(best, own, c, h, ch, *ids)
+    )(best, own, near, ch, *ids)
 
 
 def late_kernel(far_ref, xe_refs, ids_ref, c_ids_ref, e_ids_ref, h_ids_ref, out_ref):
@@ -254,8 +259,8 @@
     h_then, _, _, _ = lax.optimization_barrier((h, h_ids, e_ids, x))
     ch = [swap(SUB, h_then[: rows // 2]), swap(SUB, h_then[rows // 2 :])]
     x, e, h, c, xe = [x], [e], [h], [c], [xe]
-    best, own, c = early(mine, x, e, c, [ids, x_ids, c_ids, e_ids])
-    found, x_best, e_best, far = middle(best, own, c, h, ch, [ids, x_ids, c_ids, e_ids, h_ids])
+    best, own, near = early(mine, x, e, c, h, [ids, x_ids, c_ids, e_ids, h_ids])
+    found, x_best, e_best, far = middle(best, own, near, ch, [ids, x_ids, e_ids, h_ids])
     x_best, e_best = swap(SHARD, x_best), swap(LOW, e_best)
     xe_best = swap(LOW | SHARD, late(far, xe, [ids, c_ids, e_ids, h_ids]))
     return jnp.maximum(jnp.maximum(found, x_best), jnp.maximum(e_best, xe_best))[0]

time: 29 us -> 29 us (level)
  transfers between devices with their start and end apart: 14 -> 14, of which waited for: 6 -> 5; matrix products, arithmetic and copies ran while one was open for 0% -> 0% of each run, Pallas kernels for 7% -> 7%
where the time goes in v21:
time: 29 us; the launch traced here: 28.9 us
  starting transfers between devices  17 us (59%)
  waiting for transfers between devices  9.15 us (32%)
  Pallas kernels  2.11 us (7%)
  local copies, waits for them, and re-layouts  0.54 us (2%)
    ppermute x14, starting transfers between devices, swap(): return lax.ppermute(array, AXES, [(i, i ^ flip) for i in range(16)])  17 us
    ppermute x14, waiting for transfers between devices, swap(): return lax.ppermute(array, AXES, [(i, i ^ flip) for i in range(16)])  9.15 us
    pallas_call x1, Pallas kernels, early(): pl.pallas_call(early_kernel, out_shape=[jax.ShapeDtypeStruct((8, 3 * rows...  1.11 us
  transfers between devices with their start and end apart: 14, of which 5 were waited for; matrix products, arithmetic and copies ran while one was open for 0% of the time, Pallas kernels for 7%

profile of v21, /device:TPU:0, one launch (start us, length us, event | category | flops | bytes accessed | tf_op | source)
XLA Modules:
  0.0 28.9 jit_solution(2089441425382828735)
XLA Ops:
  0.0 0.0 copy-start.1
  0.0 0.5 %collective-permute-start.2 = (bf16[128,1024]{1,0:T(8,128)(2,1)}, bf16[128,1024]{1,0:T(8,128)(2,1)S(1)}, u32[]{:S(2)}, u32[]{:S(2)}) collective-permute-start(bf16[128,1024]{1,0:T(8,128)(2,1)} %mine_ref.1), channel_id=1, source_target_pairs={{0,1},{1,0},{2,3},{3,2},{4,5},{5,4},{6,7},{7,6},{8,9},{9,8},{10,11... | collective-permute-start | bytes 786440 | tf_op jit(solution)/shard_map/ppermute | solution.py:246
  0.5 2.6 %collective-permute-start.1 = (bf16[128,1024]{1,0:T(8,128)(2,1)}, bf16[128,1024]{1,0:T(8,128)(2,1)S(1)}, u32[]{:S(2)}, u32[]{:S(2)}) collective-permute-start(bf16[128,1024]{1,0:T(8,128)(2,1)} %mine_ref.1), channel_id=1, source_target_pairs={{0,4},{1,5},{2,6},{3,7},{4,0},{5,1},{6,2},{7,3},{8,12},{9,13},{10,... | collective-permute-start | bytes 786440 | tf_op jit(solution)/shard_map/ppermute | solution.py:246
  3.1 1.5 %collective-permute-start = (bf16[128,1024]{1,0:T(8,128)(2,1)}, bf16[128,1024]{1,0:T(8,128)(2,1)S(1)}, u32[]{:S(2)}, u32[]{:S(2)}) collective-permute-start(bf16[128,1024]{1,0:T(8,128)(2,1)} %mine_ref.1), channel_id=1, source_target_pairs={{0,2},{1,3},{2,0},{3,1},{4,6},{5,7},{6,4},{7,5},{8,10},{9,11},{10,... | collective-permute-start | bytes 786440 | tf_op jit(solution)/shard_map/ppermute | solution.py:246
  4.6 0.0 collective-permute-done.2.c_refs_0_
  4.6 2.6 %collective-permute-start.3 = (bf16[128,1024]{1,0:T(8,128)(2,1)}, bf16[128,1024]{1,0:T(8,128)(2,1)S(1)}, u32[]{:S(2)}, u32[]{:S(2)}) collective-permute-start(bf16[128,1024]{1,0:T(8,128)(2,1)} %mine_ref.1), channel_id=1, source_target_pairs={{0,8},{1,9},{2,10},{3,11},{4,12},{5,13},{6,14},{7,15},{8,0},{9,1},... | collective-permute-start | bytes 786440 | tf_op jit(solution)/shard_map/ppermute | solution.py:246
  7.2 0.0 copy-done.1
  7.2 0.0 collective-permute-start.5
  7.2 0.5 %collective-permute-start.4 = (s32[1,128]{1,0:T(1,128)S(1)}, s32[1,128]{1,0:T(1,128)S(1)}, u32[]{:S(2)}, u32[]{:S(2)}) collective-permute-start(s32[1,128]{1,0:T(1,128)S(1)} %bitcast.4), channel_id=1, source_target_pairs={{0,2},{1,3},{2,0},{3,1},{4,6},{5,7},{6,4},{7,5},{8,10},{9,11},{10,... | collective-permute-start | bytes 1544 | tf_op jit(solution)/shard_map/ppermute | solution.py:246
  7.7 0.6 %collective-permute-done.5.c_ids_ref = s32[1,128]{1,0:T(1,128)S(1)} collective-permute-done((s32[1,128]{1,0:T(1,128)S(1)}, s32[1,128]{1,0:T(1,128)S(1)}, u32[]{:S(2)}, u32[]{:S(2)}) %collective-permute-start.5) | collective-permute-done | bytes 544 | tf_op jit(solution)/shard_map/ppermute | solution.py:246
  8.3 3.4 %collective-permute-done.4.x_ids_ref = s32[1,128]{1,0:T(1,128)S(1)} collective-permute-done((s32[1,128]{1,0:T(1,128)S(1)}, s32[1,128]{1,0:T(1,128)S(1)}, u32[]{:S(2)}, u32[]{:S(2)}) %collective-permute-start.4) | collective-permute-done | bytes 544 | tf_op jit(solution)/shard_map/ppermute | solution.py:246
  11.8 2.6 %collective-permute-start.7 = (s32[2,128]{1,0:T(2,128)S(1)}, s32[2,128]{1,0:T(2,128)S(1)}, u32[]{:S(2)}, u32[]{:S(2)}) collective-permute-start(s32[2,128]{1,0:T(2,128)S(1)} %get-tuple-element.25), channel_id=1, source_target_pairs={{0,8},{1,9},{2,10},{3,11},{4,12},{5,13},{6,14},{7,15},{8,0},{9,1},... | collective-permute-start | bytes 3080 | tf_op jit(solution)/shard_map/ppermute | solution.py:246
  14.3 0.0 copy-start
  14.3 0.4 %collective-permute-start.6 = (s32[2,128]{1,0:T(2,128)S(1)}, s32[2,128]{1,0:T(2,128)S(1)}, u32[]{:S(2)}, u32[]{:S(2)}) collective-permute-start(s32[2,128]{1,0:T(2,128)S(1)} %get-tuple-element.26), channel_id=1, source_target_pairs={{0,4},{1,5},{2,6},{3,7},{4,0},{5,1},{6,2},{7,3},{8,12},{9,13},{10,... | collective-permute-start | bytes 3080 | tf_op jit(solution)/shard_map/ppermute | solution.py:246
  14.8 0.0 collective-permute-done.1.e_refs_0_
  14.8 2.3 %collective-permute-start.12 = (bf16[128,1024]{1,0:T(8,128)(2,1)S(1)}, bf16[128,1024]{1,0:T(8,128)(2,1)S(1)}, u32[]{:S(2)}, u32[]{:S(2)}) collective-permute-start(bf16[128,1024]{1,0:T(8,128)(2,1)S(1)} %collective-permute-done.1.e_refs_0_), channel_id=1, source_target_pairs={{0,2},{1,3},{2,0},{3,1},{4,6},{5,7},{6,4},{7,5},{8,10},{9,11},{10,... | collective-permute-start | bytes 786440 | tf_op jit(solution)/shard_map/ppermute | solution.py:246
  17.1 2.4 %collective-permute-done.7.h_ids_ref = s32[2,128]{1,0:T(2,128)S(1)} collective-permute-done((s32[2,128]{1,0:T(2,128)S(1)}, s32[2,128]{1,0:T(2,128)S(1)}, u32[]{:S(2)}, u32[]{:S(2)}) %collective-permute-start.7) | collective-permute-done | bytes 1056 | tf_op jit(solution)/shard_map/ppermute | solution.py:246
  19.6 0.0 collective-permute-done.6.e_ids_ref
  19.6 0.0 collective-permute-done.x_refs_0_
  19.6 0.0 collective-permute-done.3.h_refs_0_
  19.6 0.1 collective-permute-start.9
  19.7 0.5 %collective-permute-start.8 = (bf16[64,1024]{1,0:T(8,128)(2,1)S(1)}, bf16[64,1024]{1,0:T(8,128)(2,1)S(1)}, u32[]{:S(2)}, u32[]{:S(2)}) collective-permute-start(bf16[64,1024]{1,0:T(8,128)(2,1)S(1)} %get-tuple-element.24), channel_id=1, source_target_pairs={{0,1},{1,0},{2,3},{3,2},{4,5},{5,4},{6,7},{7,6},{8,9},{9,8},{10,11... | collective-permute-start | bytes 393224 | tf_op jit(solution)/shard_map/ppermute | solution.py:246
  20.2 0.0 copy-done
  20.2 1.1 %early.1 = (f32[8,384]{1,0:T(8,128)S(1)}, bf16[384,1024]{1,0:T(8,128)(2,1)S(1)}, bf16[384,1024]{1,0:T(8,128)(2,1)S(1)}) custom-call(bf16[128,1024]{1,0:T(8,128)(2,1)S(1)} %copy-done, bf16[128,1024]{1,0:T(8,128)(2,1)S(1)} %collective-permute-done.x_refs_0_, bf16[128,1024]{1,0:T(8,128)(2,1)S(1)} %collective-permute-done.1.e_refs_0_, ...), custom_call_target="tpu_custom_call" | custom-call | tf_op jit(solution)/shard_map/early/pallas_call | solution.py:182
  21.3 0.0 collective-permute-done.9.ch_refs_1_
  21.3 0.0 collective-permute-done.8.ch_refs_0_
  21.3 0.4 %middle.1 = (f32[8,128]{1,0:T(8,128)S(1)}, f32[8,128]{1,0:T(8,128)S(1)}, f32[8,128]{1,0:T(8,128)S(1)}, bf16[512,1024]{1,0:T(8,128)(2,1)S(1)}) custom-call(f32[8,384]{1,0:T(8,128)S(1)} %get-tuple-element.15.best_ref, bf16[384,1024]{1,0:T(8,128)(2,1)S(1)} %get-tuple-element.16.own_ref, bf16[384,1024]{1,0:T(8,128)(2,1)S(1)} %get-tuple-element.17.near_ref, ...), custom_call_target="tpu_custom_call" | custom-call | tf_op jit(solution)/shard_map/middle/pallas_call | solution.py:214
  21.8 0.6 %collective-permute-start.10 = (f32[8,128]{1,0:T(8,128)S(1)}, f32[8,128]{1,0:T(8,128)S(1)}, u32[]{:S(2)}, u32[]{:S(2)}) collective-permute-start(f32[8,128]{1,0:T(8,128)S(1)} %get-tuple-element.20), channel_id=1, source_target_pairs={{0,2},{1,3},{2,0},{3,1},{4,6},{5,7},{6,4},{7,5},{8,10},{9,11},{10,... | collective-permute-start | bytes 12296 | tf_op jit(solution)/shard_map/ppermute | solution.py:246
  22.4 0.6 %collective-permute-start.11 = (f32[8,128]{1,0:T(8,128)S(1)}, f32[8,128]{1,0:T(8,128)S(1)}, u32[]{:S(2)}, u32[]{:S(2)}) collective-permute-start(f32[8,128]{1,0:T(8,128)S(1)} %get-tuple-element.21), channel_id=1, source_target_pairs={{0,4},{1,5},{2,6},{3,7},{4,0},{5,1},{6,2},{7,3},{8,12},{9,13},{10,... | collective-permute-start | bytes 12296 | tf_op jit(solution)/shard_map/ppermute | solution.py:246
  23.0 0.2 collective-permute-done.12.xe_refs_0_
  23.2 0.6 %late.1 = f32[8,128]{1,0:T(8,128)S(1)} custom-call(bf16[512,1024]{1,0:T(8,128)(2,1)S(1)} %get-tuple-element.22.far_ref, bf16[128,1024]{1,0:T(8,128)(2,1)S(1)} %collective-permute-done.12.xe_refs_0_, s32[1,128]{1,0:T(1,128)S(1)} %bitcast.8, s32[1,128]{1,0:T(1,128)S(1)} %collective-permute-done.5.c_ids_ref, s32[2,128]{1,0:T(2,128)S(1)} %collective-permute-done.6.e_ids_ref, ...), custom_call_target="tpu_custom_call" | custom-call | tf_op jit(solution)/shard_map/late/pallas_call | solution.py:234
  23.8 2.1 %collective-permute-start.13 = (f32[8,128]{1,0:T(8,128)S(1)}, f32[8,128]{1,0:T(8,128)S(1)}, u32[]{:S(2)}, u32[]{:S(2)}) collective-permute-start(f32[8,128]{1,0:T(8,128)S(1)} %late.1), channel_id=1, source_target_pairs={{0,6},{1,7},{2,4},{3,5},{4,2},{5,3},{6,0},{7,1},{8,14},{9,15},{10,... | collective-permute-start | bytes 12296 | tf_op jit(solution)/shard_map/ppermute | solution.py:246
  25.9 0.0 collective-permute-done.10
  25.9 0.0 collective-permute-done.11
  26.0 2.4 %collective-permute-done.13 = f32[8,128]{1,0:T(8,128)S(1)} collective-permute-done((f32[8,128]{1,0:T(8,128)S(1)}, f32[8,128]{1,0:T(8,128)S(1)}, u32[]{:S(2)}, u32[]{:S(2)}) %collective-permute-start.13) | collective-permute-done | bytes 4128 | tf_op jit(solution)/shard_map/ppermute | solution.py:246
  28.4 0.5 %slice_bitcast_fusion = f32[128]{0:T(128)} fusion(f32[8,128]{1,0:T(8,128)S(1)} %maximum_maximum_fusion), kind=kLoop, calls=%fused_computation.3 | loop fusion | bytes 1024 | tf_op jit(solution)/shard_map/squeeze | solution.py:266
  (3 shorter events, 0.0 us)
Async XLA Ops:
  0.0 7.2 %copy-start.1 = (s32[128,1]{0,1:T(1,128)S(1)}, s32[128,1]{0,1:T(1,128)}, u32[]{:S(2)}) copy-start(s32[128,1]{0,1:T(1,128)} %param.3) | copy-start | bytes 1540
  0.0 4.6 %collective-permute-start.2 = (bf16[128,1024]{1,0:T(8,128)(2,1)}, bf16[128,1024]{1,0:T(8,128)(2,1)S(1)}, u32[]{:S(2)}, u32[]{:S(2)}) collective-permute-start(bf16[128,1024]{1,0:T(8,128)(2,1)} %mine_ref.1), channel_id=1, source_target_pairs={{0,1},{1,0},{2,3},{3,2},{4,5},{5,4},{6,7},{7,6},{8,9},{9,8},{10,11... | collective-permute-start | bytes 786440 | tf_op jit(solution)/shard_map/ppermute | solution.py:246
  0.5 14.3 %collective-permute-start.1 = (bf16[128,1024]{1,0:T(8,128)(2,1)}, bf16[128,1024]{1,0:T(8,128)(2,1)S(1)}, u32[]{:S(2)}, u32[]{:S(2)}) collective-permute-start(bf16[128,1024]{1,0:T(8,128)(2,1)} %mine_ref.1), channel_id=1, source_target_pairs={{0,4},{1,5},{2,6},{3,7},{4,0},{5,1},{6,2},{7,3},{8,12},{9,13},{10,... | collective-permute-start | bytes 786440 | tf_op jit(solution)/shard_map/ppermute | solution.py:246
  3.1 16.5 %collective-permute-start = (bf16[128,1024]{1,0:T(8,128)(2,1)}, bf16[128,1024]{1,0:T(8,128)(2,1)S(1)}, u32[]{:S(2)}, u32[]{:S(2)}) collective-permute-start(bf16[128,1024]{1,0:T(8,128)(2,1)} %mine_ref.1), channel_id=1, source_target_pairs={{0,2},{1,3},{2,0},{3,1},{4,6},{5,7},{6,4},{7,5},{8,10},{9,11},{10,... | collective-permute-start | bytes 786440 | tf_op jit(solution)/shard_map/ppermute | solution.py:246
  4.6 15.0 %collective-permute-start.3 = (bf16[128,1024]{1,0:T(8,128)(2,1)}, bf16[128,1024]{1,0:T(8,128)(2,1)S(1)}, u32[]{:S(2)}, u32[]{:S(2)}) collective-permute-start(bf16[128,1024]{1,0:T(8,128)(2,1)} %mine_ref.1), channel_id=1, source_target_pairs={{0,8},{1,9},{2,10},{3,11},{4,12},{5,13},{6,14},{7,15},{8,0},{9,1},... | collective-permute-start | bytes 786440 | tf_op jit(solution)/shard_map/ppermute | solution.py:246
  7.2 1.1 %collective-permute-start.5 = (s32[1,128]{1,0:T(1,128)S(1)}, s32[1,128]{1,0:T(1,128)S(1)}, u32[]{:S(2)}, u32[]{:S(2)}) collective-permute-start(s32[1,128]{1,0:T(1,128)S(1)} %bitcast.3), channel_id=1, source_target_pairs={{0,1},{1,0},{2,3},{3,2},{4,5},{5,4},{6,7},{7,6},{8,9},{9,8},{10,11... | collective-permute-start | bytes 1544 | tf_op jit(solution)/shard_map/ppermute | solution.py:246
  7.2 4.6 %collective-permute-start.4 = (s32[1,128]{1,0:T(1,128)S(1)}, s32[1,128]{1,0:T(1,128)S(1)}, u32[]{:S(2)}, u32[]{:S(2)}) collective-permute-start(s32[1,128]{1,0:T(1,128)S(1)} %bitcast.4), channel_id=1, source_target_pairs={{0,2},{1,3},{2,0},{3,1},{4,6},{5,7},{6,4},{7,5},{8,10},{9,11},{10,... | collective-permute-start | bytes 1544 | tf_op jit(solution)/shard_map/ppermute | solution.py:246
  11.8 7.8 %collective-permute-start.7 = (s32[2,128]{1,0:T(2,128)S(1)}, s32[2,128]{1,0:T(2,128)S(1)}, u32[]{:S(2)}, u32[]{:S(2)}) collective-permute-start(s32[2,128]{1,0:T(2,128)S(1)} %get-tuple-element.25), channel_id=1, source_target_pairs={{0,8},{1,9},{2,10},{3,11},{4,12},{5,13},{6,14},{7,15},{8,0},{9,1},... | collective-permute-start | bytes 3080 | tf_op jit(solution)/shard_map/ppermute | solution.py:246
  14.3 5.8 %copy-start = (bf16[128,1024]{1,0:T(8,128)(2,1)S(1)}, bf16[128,1024]{1,0:T(8,128)(2,1)}, u32[]{:S(2)}) copy-start(bf16[128,1024]{1,0:T(8,128)(2,1)} %mine_ref.1) | copy-start | bytes 786436
  14.3 5.2 %collective-permute-start.6 = (s32[2,128]{1,0:T(2,128)S(1)}, s32[2,128]{1,0:T(2,128)S(1)}, u32[]{:S(2)}, u32[]{:S(2)}) collective-permute-start(s32[2,128]{1,0:T(2,128)S(1)} %get-tuple-element.26), channel_id=1, source_target_pairs={{0,4},{1,5},{2,6},{3,7},{4,0},{5,1},{6,2},{7,3},{8,12},{9,13},{10,... | collective-permute-start | bytes 3080 | tf_op jit(solution)/shard_map/ppermute | solution.py:246
  14.8 8.4 %collective-permute-start.12 = (bf16[128,1024]{1,0:T(8,128)(2,1)S(1)}, bf16[128,1024]{1,0:T(8,128)(2,1)S(1)}, u32[]{:S(2)}, u32[]{:S(2)}) collective-permute-start(bf16[128,1024]{1,0:T(8,128)(2,1)S(1)} %collective-permute-done.1.e_refs_0_), channel_id=1, source_target_pairs={{0,2},{1,3},{2,0},{3,1},{4,6},{5,7},{6,4},{7,5},{8,10},{9,11},{10,... | collective-permute-start | bytes 786440 | tf_op jit(solution)/shard_map/ppermute | solution.py:246
  19.6 1.7 %collective-permute-start.9 = (bf16[64,1024]{1,0:T(8,128)(2,1)S(1)}, bf16[64,1024]{1,0:T(8,128)(2,1)S(1)}, u32[]{:S(2)}, u32[]{:S(2)}) collective-permute-start(bf16[64,1024]{1,0:T(8,128)(2,1)S(1)} %get-tuple-element.23), channel_id=1, source_target_pairs={{0,1},{1,0},{2,3},{3,2},{4,5},{5,4},{6,7},{7,6},{8,9},{9,8},{10,11... | collective-permute-start | bytes 393224 | tf_op jit(solution)/shard_map/ppermute | solution.py:246
  19.7 1.6 %collective-permute-start.8 = (bf16[64,1024]{1,0:T(8,128)(2,1)S(1)}, bf16[64,1024]{1,0:T(8,128)(2,1)S(1)}, u32[]{:S(2)}, u32[]{:S(2)}) collective-permute-start(bf16[64,1024]{1,0:T(8,128)(2,1)S(1)} %get-tuple-element.24), channel_id=1, source_target_pairs={{0,1},{1,0},{2,3},{3,2},{4,5},{5,4},{6,7},{7,6},{8,9},{9,8},{10,11... | collective-permute-start | bytes 393224 | tf_op jit(solution)/shard_map/ppermute | solution.py:246
  21.8 4.2 %collective-permute-start.10 = (f32[8,128]{1,0:T(8,128)S(1)}, f32[8,128]{1,0:T(8,128)S(1)}, u32[]{:S(2)}, u32[]{:S(2)}) collective-permute-start(f32[8,128]{1,0:T(8,128)S(1)} %get-tuple-element.20), channel_id=1, source_target_pairs={{0,2},{1,3},{2,0},{3,1},{4,6},{5,7},{6,4},{7,5},{8,10},{9,11},{10,... | collective-permute-start | bytes 12296 | tf_op jit(solution)/shard_map/ppermute | solution.py:246
  22.4 3.6 %collective-permute-start.11 = (f32[8,128]{1,0:T(8,128)S(1)}, f32[8,128]{1,0:T(8,128)S(1)}, u32[]{:S(2)}, u32[]{:S(2)}) collective-permute-start(f32[8,128]{1,0:T(8,128)S(1)} %get-tuple-element.21), channel_id=1, source_target_pairs={{0,4},{1,5},{2,6},{3,7},{4,0},{5,1},{6,2},{7,3},{8,12},{9,13},{10,... | collective-permute-start | bytes 12296 | tf_op jit(solution)/shard_map/ppermute | solution.py:246
  23.8 4.6 %collective-permute-start.13 = (f32[8,128]{1,0:T(8,128)S(1)}, f32[8,128]{1,0:T(8,128)S(1)}, u32[]{:S(2)}, u32[]{:S(2)}) collective-permute-start(f32[8,128]{1,0:T(8,128)S(1)} %late.1), channel_id=1, source_target_pairs={{0,6},{1,7},{2,4},{3,5},{4,2},{5,3},{6,0},{7,1},{8,14},{9,15},{10,... | collective-permute-start | bytes 12296 | tf_op jit(solution)/shard_map/ppermute | solution.py:246

commit v22 on v13

--- a/solution.py
+++ b/solution.py
@@ -220,9 +220,13 @@
 def late_kernel(far_ref, xe_refs, ids_ref, c_ids_ref, e_ids_ref, h_ids_ref, out_ref):
     xe = block(xe_refs)
     rows = xe.shape[0]
-    others = [far_ref[place * rows : (place + 1) * rows] for place in range(4)]
-    other_ids = [ids_ref[...], c_ids_ref[...], h_ids_ref[:1, :], h_ids_ref[1:, :]]
-    out_ref[...] = jnp.broadcast_to(best_of(xe, e_ids_ref[1:, :], others, other_ids), out_ref.shape)
+    similar = lax.dot_general(
+        far_ref[...], xe, (((1,), (1,)), ((), ())), preferred_element_type=jnp.float32
+    )
+    ids = [ids_ref[...], c_ids_ref[...], h_ids_ref[:1, :], h_ids_ref[1:, :]]
+    down = jnp.concatenate([jnp.broadcast_to(row, (rows, rows)).T[:, :1] for row in ids], axis=0)
+    best = jnp.max(jnp.where(down == e_ids_ref[1:, :], similar, NONE), axis=0, keepdims=True)
+    out_ref[...] = jnp.broadcast_to(best, out_ref.shape)
 
 
 def late(far, xe, ids):

time: 29 us -> 29 us (level)
  no operation moved by 1% of the time
where the time goes in v22:
time: 29 us; the launch traced here: 28.9 us
  starting transfers between devices  17.1 us (59%)
  waiting for transfers between devices  9.04 us (31%)
  Pallas kernels  2.08 us (7%)
  local copies, waits for them, and re-layouts  0.54 us (2%)
    ppermute x14, starting transfers between devices, swap(): return lax.ppermute(array, AXES, [(i, i ^ flip) for i in range(16)])  17.1 us
    ppermute x14, waiting for transfers between devices, swap(): return lax.ppermute(array, AXES, [(i, i ^ flip) for i in range(16)])  9.04 us
    pallas_call x1, Pallas kernels, early(): pl.pallas_call(early_kernel, out_shape=[jax.ShapeDtypeStruct((8, 3 * rows...  0.84 us
    pallas_call x1, Pallas kernels, middle(): pl.pallas_call(middle_kernel, out_shape=[jax.ShapeDtypeStruct((8, rows),...  0.68 us
  transfers between devices with their start and end apart: 14, of which 6 were waited for; matrix products, arithmetic and copies ran while one was open for 0% of the time, Pallas kernels for 7%

profile of v22, /device:TPU:0, one launch (start us, length us, event | category | flops | bytes accessed | tf_op | source)
XLA Modules:
  0.0 28.9 jit_solution(16612830524684903063)
XLA Ops:
  0.0 0.0 copy-start.1
  0.0 0.5 %collective-permute-start.2 = (bf16[128,1024]{1,0:T(8,128)(2,1)}, bf16[128,1024]{1,0:T(8,128)(2,1)S(1)}, u32[]{:S(2)}, u32[]{:S(2)}) collective-permute-start(bf16[128,1024]{1,0:T(8,128)(2,1)} %mine_ref.1), channel_id=1, source_target_pairs={{0,1},{1,0},{2,3},{3,2},{4,5},{5,4},{6,7},{7,6},{8,9},{9,8},{10,11... | collective-permute-start | bytes 786440 | tf_op jit(solution)/shard_map/ppermute | solution.py:245
  0.5 2.6 %collective-permute-start.1 = (bf16[128,1024]{1,0:T(8,128)(2,1)}, bf16[128,1024]{1,0:T(8,128)(2,1)S(1)}, u32[]{:S(2)}, u32[]{:S(2)}) collective-permute-start(bf16[128,1024]{1,0:T(8,128)(2,1)} %mine_ref.1), channel_id=1, source_target_pairs={{0,4},{1,5},{2,6},{3,7},{4,0},{5,1},{6,2},{7,3},{8,12},{9,13},{10,... | collective-permute-start | bytes 786440 | tf_op jit(solution)/shard_map/ppermute | solution.py:245
  3.1 1.5 %collective-permute-start = (bf16[128,1024]{1,0:T(8,128)(2,1)}, bf16[128,1024]{1,0:T(8,128)(2,1)S(1)}, u32[]{:S(2)}, u32[]{:S(2)}) collective-permute-start(bf16[128,1024]{1,0:T(8,128)(2,1)} %mine_ref.1), channel_id=1, source_target_pairs={{0,2},{1,3},{2,0},{3,1},{4,6},{5,7},{6,4},{7,5},{8,10},{9,11},{10,... | collective-permute-start | bytes 786440 | tf_op jit(solution)/shard_map/ppermute | solution.py:245
  4.6 0.0 collective-permute-done.2.c_refs_0_
  4.6 2.6 %collective-permute-start.6 = (bf16[128,1024]{1,0:T(8,128)(2,1)}, bf16[128,1024]{1,0:T(8,128)(2,1)S(1)}, u32[]{:S(2)}, u32[]{:S(2)}) collective-permute-start(bf16[128,1024]{1,0:T(8,128)(2,1)} %mine_ref.1), channel_id=1, source_target_pairs={{0,8},{1,9},{2,10},{3,11},{4,12},{5,13},{6,14},{7,15},{8,0},{9,1},... | collective-permute-start | bytes 786440 | tf_op jit(solution)/shard_map/ppermute | solution.py:245
  7.2 0.0 copy-done.1
  7.2 0.0 collective-permute-start.4
  7.2 0.5 %collective-permute-start.3 = (s32[1,128]{1,0:T(1,128)S(1)}, s32[1,128]{1,0:T(1,128)S(1)}, u32[]{:S(2)}, u32[]{:S(2)}) collective-permute-start(s32[1,128]{1,0:T(1,128)S(1)} %bitcast.4), channel_id=1, source_target_pairs={{0,2},{1,3},{2,0},{3,1},{4,6},{5,7},{6,4},{7,5},{8,10},{9,11},{10,... | collective-permute-start | bytes 1544 | tf_op jit(solution)/shard_map/ppermute | solution.py:245
  7.7 0.6 %collective-permute-done.4.c_ids_ref = s32[1,128]{1,0:T(1,128)S(1)} collective-permute-done((s32[1,128]{1,0:T(1,128)S(1)}, s32[1,128]{1,0:T(1,128)S(1)}, u32[]{:S(2)}, u32[]{:S(2)}) %collective-permute-start.4) | collective-permute-done | bytes 544 | tf_op jit(solution)/shard_map/ppermute | solution.py:245
  8.3 3.4 %collective-permute-done.3.x_ids_ref = s32[1,128]{1,0:T(1,128)S(1)} collective-permute-done((s32[1,128]{1,0:T(1,128)S(1)}, s32[1,128]{1,0:T(1,128)S(1)}, u32[]{:S(2)}, u32[]{:S(2)}) %collective-permute-start.3) | collective-permute-done | bytes 544 | tf_op jit(solution)/shard_map/ppermute | solution.py:245
  11.8 2.6 %collective-permute-start.7 = (s32[2,128]{1,0:T(2,128)S(1)}, s32[2,128]{1,0:T(2,128)S(1)}, u32[]{:S(2)}, u32[]{:S(2)}) collective-permute-start(s32[2,128]{1,0:T(2,128)S(1)} %get-tuple-element.25), channel_id=1, source_target_pairs={{0,8},{1,9},{2,10},{3,11},{4,12},{5,13},{6,14},{7,15},{8,0},{9,1},... | collective-permute-start | bytes 3080 | tf_op jit(solution)/shard_map/ppermute | solution.py:245
  14.3 0.0 copy-start
  14.3 0.4 %collective-permute-start.5 = (s32[2,128]{1,0:T(2,128)S(1)}, s32[2,128]{1,0:T(2,128)S(1)}, u32[]{:S(2)}, u32[]{:S(2)}) collective-permute-start(s32[2,128]{1,0:T(2,128)S(1)} %get-tuple-element.26), channel_id=1, source_target_pairs={{0,4},{1,5},{2,6},{3,7},{4,0},{5,1},{6,2},{7,3},{8,12},{9,13},{10,... | collective-permute-start | bytes 3080 | tf_op jit(solution)/shard_map/ppermute | solution.py:245
  14.8 0.0 collective-permute-done.1.e_refs_0_
  14.8 2.3 %collective-permute-start.12 = (bf16[128,1024]{1,0:T(8,128)(2,1)S(1)}, bf16[128,1024]{1,0:T(8,128)(2,1)S(1)}, u32[]{:S(2)}, u32[]{:S(2)}) collective-permute-start(bf16[128,1024]{1,0:T(8,128)(2,1)S(1)} %collective-permute-done.1.e_refs_0_), channel_id=1, source_target_pairs={{0,2},{1,3},{2,0},{3,1},{4,6},{5,7},{6,4},{7,5},{8,10},{9,11},{10,... | collective-permute-start | bytes 786440 | tf_op jit(solution)/shard_map/ppermute | solution.py:245
  17.1 2.4 %collective-permute-done.7.h_ids_ref = s32[2,128]{1,0:T(2,128)S(1)} collective-permute-done((s32[2,128]{1,0:T(2,128)S(1)}, s32[2,128]{1,0:T(2,128)S(1)}, u32[]{:S(2)}, u32[]{:S(2)}) %collective-permute-start.7) | collective-permute-done | bytes 1056 | tf_op jit(solution)/shard_map/ppermute | solution.py:245
  19.6 0.0 collective-permute-done.5.e_ids_ref
  19.6 0.0 collective-permute-done.x_refs_0_
  19.6 0.0 collective-permute-done.6.h_refs_0_
  19.6 0.1 collective-permute-start.9
  19.7 0.5 %collective-permute-start.8 = (bf16[64,1024]{1,0:T(8,128)(2,1)S(1)}, bf16[64,1024]{1,0:T(8,128)(2,1)S(1)}, u32[]{:S(2)}, u32[]{:S(2)}) collective-permute-start(bf16[64,1024]{1,0:T(8,128)(2,1)S(1)} %get-tuple-element.24), channel_id=1, source_target_pairs={{0,1},{1,0},{2,3},{3,2},{4,5},{5,4},{6,7},{7,6},{8,9},{9,8},{10,11... | collective-permute-start | bytes 393224 | tf_op jit(solution)/shard_map/ppermute | solution.py:245
  20.2 0.0 copy-done
  20.2 0.8 %early.1 = (f32[8,384]{1,0:T(8,128)S(1)}, bf16[384,1024]{1,0:T(8,128)(2,1)S(1)}, bf16[128,1024]{1,0:T(8,128)(2,1)S(1)}) custom-call(bf16[128,1024]{1,0:T(8,128)(2,1)S(1)} %copy-done, bf16[128,1024]{1,0:T(8,128)(2,1)S(1)} %collective-permute-done.x_refs_0_, bf16[128,1024]{1,0:T(8,128)(2,1)S(1)} %collective-permute-done.1.e_refs_0_, ...), custom_call_target="tpu_custom_call" | custom-call | tf_op jit(solution)/shard_map/early/pallas_call | solution.py:179
  21.0 0.0 collective-permute-done.9.ch_refs_1_
  21.0 0.2 collective-permute-done.8.ch_refs_0_
  21.2 0.7 %middle.1 = (f32[8,128]{1,0:T(8,128)S(1)}, f32[8,128]{1,0:T(8,128)S(1)}, f32[8,128]{1,0:T(8,128)S(1)}, bf16[512,1024]{1,0:T(8,128)(2,1)S(1)}) custom-call(f32[8,384]{1,0:T(8,128)S(1)} %get-tuple-element.14.best_ref, bf16[384,1024]{1,0:T(8,128)(2,1)S(1)} %get-tuple-element.15.own_ref, bf16[128,1024]{1,0:T(8,128)(2,1)S(1)} %get-tuple-element.16.c_ref, ...), custom_call_target="tpu_custom_call" | custom-call | tf_op jit(solution)/shard_map/middle/pallas_call | solution.py:209
  21.9 0.6 %collective-permute-start.10 = (f32[8,128]{1,0:T(8,128)S(1)}, f32[8,128]{1,0:T(8,128)S(1)}, u32[]{:S(2)}, u32[]{:S(2)}) collective-permute-start(f32[8,128]{1,0:T(8,128)S(1)} %get-tuple-element.20), channel_id=1, source_target_pairs={{0,2},{1,3},{2,0},{3,1},{4,6},{5,7},{6,4},{7,5},{8,10},{9,11},{10,... | collective-permute-start | bytes 12296 | tf_op jit(solution)/shard_map/ppermute | solution.py:245
  22.5 0.6 %collective-permute-start.11 = (f32[8,128]{1,0:T(8,128)S(1)}, f32[8,128]{1,0:T(8,128)S(1)}, u32[]{:S(2)}, u32[]{:S(2)}) collective-permute-start(f32[8,128]{1,0:T(8,128)S(1)} %get-tuple-element.21), channel_id=1, source_target_pairs={{0,4},{1,5},{2,6},{3,7},{4,0},{5,1},{6,2},{7,3},{8,12},{9,13},{10,... | collective-permute-start | bytes 12296 | tf_op jit(solution)/shard_map/ppermute | solution.py:245
  23.1 0.1 collective-permute-done.12.xe_refs_0_
  23.2 0.6 %late.1 = f32[8,128]{1,0:T(8,128)S(1)} custom-call(bf16[512,1024]{1,0:T(8,128)(2,1)S(1)} %get-tuple-element.22.far_ref, bf16[128,1024]{1,0:T(8,128)(2,1)S(1)} %collective-permute-done.12.xe_refs_0_, s32[1,128]{1,0:T(1,128)S(1)} %bitcast.8, s32[1,128]{1,0:T(1,128)S(1)} %collective-permute-done.4.c_ids_ref, s32[2,128]{1,0:T(2,128)S(1)} %collective-permute-done.5.e_ids_ref, ...), custom_call_target="tpu_custom_call" | custom-call | tf_op jit(solution)/shard_map/late/pallas_call | solution.py:233
  23.8 2.3 %collective-permute-start.13 = (f32[8,128]{1,0:T(8,128)S(1)}, f32[8,128]{1,0:T(8,128)S(1)}, u32[]{:S(2)}, u32[]{:S(2)}) collective-permute-start(f32[8,128]{1,0:T(8,128)S(1)} %late.1), channel_id=1, source_target_pairs={{0,6},{1,7},{2,4},{3,5},{4,2},{5,3},{6,0},{7,1},{8,14},{9,15},{10,... | collective-permute-start | bytes 12296 | tf_op jit(solution)/shard_map/ppermute | solution.py:245
  26.1 0.0 collective-permute-done.10
  26.1 0.0 collective-permute-done.11
  26.1 2.3 %collective-permute-done.13 = f32[8,128]{1,0:T(8,128)S(1)} collective-permute-done((f32[8,128]{1,0:T(8,128)S(1)}, f32[8,128]{1,0:T(8,128)S(1)}, u32[]{:S(2)}, u32[]{:S(2)}) %collective-permute-start.13) | collective-permute-done | bytes 4128 | tf_op jit(solution)/shard_map/ppermute | solution.py:245
  28.4 0.5 %slice_bitcast_fusion = f32[128]{0:T(128)} fusion(f32[8,128]{1,0:T(8,128)S(1)} %maximum_maximum_fusion), kind=kLoop, calls=%fused_computation.3 | loop fusion | bytes 1024 | tf_op jit(solution)/shard_map/squeeze | solution.py:265
  (3 shorter events, 0.0 us)
Async XLA Ops:
  0.0 7.2 %copy-start.1 = (s32[128,1]{0,1:T(1,128)S(1)}, s32[128,1]{0,1:T(1,128)}, u32[]{:S(2)}) copy-start(s32[128,1]{0,1:T(1,128)} %param.3) | copy-start | bytes 1540
  0.0 4.6 %collective-permute-start.2 = (bf16[128,1024]{1,0:T(8,128)(2,1)}, bf16[128,1024]{1,0:T(8,128)(2,1)S(1)}, u32[]{:S(2)}, u32[]{:S(2)}) collective-permute-start(bf16[128,1024]{1,0:T(8,128)(2,1)} %mine_ref.1), channel_id=1, source_target_pairs={{0,1},{1,0},{2,3},{3,2},{4,5},{5,4},{6,7},{7,6},{8,9},{9,8},{10,11... | collective-permute-start | bytes 786440 | tf_op jit(solution)/shard_map/ppermute | solution.py:245
  0.5 14.3 %collective-permute-start.1 = (bf16[128,1024]{1,0:T(8,128)(2,1)}, bf16[128,1024]{1,0:T(8,128)(2,1)S(1)}, u32[]{:S(2)}, u32[]{:S(2)}) collective-permute-start(bf16[128,1024]{1,0:T(8,128)(2,1)} %mine_ref.1), channel_id=1, source_target_pairs={{0,4},{1,5},{2,6},{3,7},{4,0},{5,1},{6,2},{7,3},{8,12},{9,13},{10,... | collective-permute-start | bytes 786440 | tf_op jit(solution)/shard_map/ppermute | solution.py:245
  3.1 16.5 %collective-permute-start = (bf16[128,1024]{1,0:T(8,128)(2,1)}, bf16[128,1024]{1,0:T(8,128)(2,1)S(1)}, u32[]{:S(2)}, u32[]{:S(2)}) collective-permute-start(bf16[128,1024]{1,0:T(8,128)(2,1)} %mine_ref.1), channel_id=1, source_target_pairs={{0,2},{1,3},{2,0},{3,1},{4,6},{5,7},{6,4},{7,5},{8,10},{9,11},{10,... | collective-permute-start | bytes 786440 | tf_op jit(solution)/shard_map/ppermute | solution.py:245
  4.6 15.0 %collective-permute-start.6 = (bf16[128,1024]{1,0:T(8,128)(2,1)}, bf16[128,1024]{1,0:T(8,128)(2,1)S(1)}, u32[]{:S(2)}, u32[]{:S(2)}) collective-permute-start(bf16[128,1024]{1,0:T(8,128)(2,1)} %mine_ref.1), channel_id=1, source_target_pairs={{0,8},{1,9},{2,10},{3,11},{4,12},{5,13},{6,14},{7,15},{8,0},{9,1},... | collective-permute-start | bytes 786440 | tf_op jit(solution)/shard_map/ppermute | solution.py:245
  7.2 1.1 %collective-permute-start.4 = (s32[1,128]{1,0:T(1,128)S(1)}, s32[1,128]{1,0:T(1,128)S(1)}, u32[]{:S(2)}, u32[]{:S(2)}) collective-permute-start(s32[1,128]{1,0:T(1,128)S(1)} %bitcast.3), channel_id=1, source_target_pairs={{0,1},{1,0},{2,3},{3,2},{4,5},{5,4},{6,7},{7,6},{8,9},{9,8},{10,11... | collective-permute-start | bytes 1544 | tf_op jit(solution)/shard_map/ppermute | solution.py:245
  7.2 4.6 %collective-permute-start.3 = (s32[1,128]{1,0:T(1,128)S(1)}, s32[1,128]{1,0:T(1,128)S(1)}, u32[]{:S(2)}, u32[]{:S(2)}) collective-permute-start(s32[1,128]{1,0:T(1,128)S(1)} %bitcast.4), channel_id=1, source_target_pairs={{0,2},{1,3},{2,0},{3,1},{4,6},{5,7},{6,4},{7,5},{8,10},{9,11},{10,... | collective-permute-start | bytes 1544 | tf_op jit(solution)/shard_map/ppermute | solution.py:245
  11.8 7.8 %collective-permute-start.7 = (s32[2,128]{1,0:T(2,128)S(1)}, s32[2,128]{1,0:T(2,128)S(1)}, u32[]{:S(2)}, u32[]{:S(2)}) collective-permute-start(s32[2,128]{1,0:T(2,128)S(1)} %get-tuple-element.25), channel_id=1, source_target_pairs={{0,8},{1,9},{2,10},{3,11},{4,12},{5,13},{6,14},{7,15},{8,0},{9,1},... | collective-permute-start | bytes 3080 | tf_op jit(solution)/shard_map/ppermute | solution.py:245
  14.3 5.8 %copy-start = (bf16[128,1024]{1,0:T(8,128)(2,1)S(1)}, bf16[128,1024]{1,0:T(8,128)(2,1)}, u32[]{:S(2)}) copy-start(bf16[128,1024]{1,0:T(8,128)(2,1)} %mine_ref.1) | copy-start | bytes 786436
  14.3 5.2 %collective-permute-start.5 = (s32[2,128]{1,0:T(2,128)S(1)}, s32[2,128]{1,0:T(2,128)S(1)}, u32[]{:S(2)}, u32[]{:S(2)}) collective-permute-start(s32[2,128]{1,0:T(2,128)S(1)} %get-tuple-element.26), channel_id=1, source_target_pairs={{0,4},{1,5},{2,6},{3,7},{4,0},{5,1},{6,2},{7,3},{8,12},{9,13},{10,... | collective-permute-start | bytes 3080 | tf_op jit(solution)/shard_map/ppermute | solution.py:245
  14.8 8.4 %collective-permute-start.12 = (bf16[128,1024]{1,0:T(8,128)(2,1)S(1)}, bf16[128,1024]{1,0:T(8,128)(2,1)S(1)}, u32[]{:S(2)}, u32[]{:S(2)}) collective-permute-start(bf16[128,1024]{1,0:T(8,128)(2,1)S(1)} %collective-permute-done.1.e_refs_0_), channel_id=1, source_target_pairs={{0,2},{1,3},{2,0},{3,1},{4,6},{5,7},{6,4},{7,5},{8,10},{9,11},{10,... | collective-permute-start | bytes 786440 | tf_op jit(solution)/shard_map/ppermute | solution.py:245
  19.6 1.4 %collective-permute-start.9 = (bf16[64,1024]{1,0:T(8,128)(2,1)S(1)}, bf16[64,1024]{1,0:T(8,128)(2,1)S(1)}, u32[]{:S(2)}, u32[]{:S(2)}) collective-permute-start(bf16[64,1024]{1,0:T(8,128)(2,1)S(1)} %get-tuple-element.23), channel_id=1, source_target_pairs={{0,1},{1,0},{2,3},{3,2},{4,5},{5,4},{6,7},{7,6},{8,9},{9,8},{10,11... | collective-permute-start | bytes 393224 | tf_op jit(solution)/shard_map/ppermute | solution.py:245
  19.7 1.5 %collective-permute-start.8 = (bf16[64,1024]{1,0:T(8,128)(2,1)S(1)}, bf16[64,1024]{1,0:T(8,128)(2,1)S(1)}, u32[]{:S(2)}, u32[]{:S(2)}) collective-permute-start(bf16[64,1024]{1,0:T(8,128)(2,1)S(1)} %get-tuple-element.24), channel_id=1, source_target_pairs={{0,1},{1,0},{2,3},{3,2},{4,5},{5,4},{6,7},{7,6},{8,9},{9,8},{10,11... | collective-permute-start | bytes 393224 | tf_op jit(solution)/shard_map/ppermute | solution.py:245
  21.9 4.2 %collective-permute-start.10 = (f32[8,128]{1,0:T(8,128)S(1)}, f32[8,128]{1,0:T(8,128)S(1)}, u32[]{:S(2)}, u32[]{:S(2)}) collective-permute-start(f32[8,128]{1,0:T(8,128)S(1)} %get-tuple-element.20), channel_id=1, source_target_pairs={{0,2},{1,3},{2,0},{3,1},{4,6},{5,7},{6,4},{7,5},{8,10},{9,11},{10,... | collective-permute-start | bytes 12296 | tf_op jit(solution)/shard_map/ppermute | solution.py:245
  22.5 3.6 %collective-permute-start.11 = (f32[8,128]{1,0:T(8,128)S(1)}, f32[8,128]{1,0:T(8,128)S(1)}, u32[]{:S(2)}, u32[]{:S(2)}) collective-permute-start(f32[8,128]{1,0:T(8,128)S(1)} %get-tuple-element.21), channel_id=1, source_target_pairs={{0,4},{1,5},{2,6},{3,7},{4,0},{5,1},{6,2},{7,3},{8,12},{9,13},{10,... | collective-permute-start | bytes 12296 | tf_op jit(solution)/shard_map/ppermute | solution.py:245
  23.8 4.6 %collective-permute-start.13 = (f32[8,128]{1,0:T(8,128)S(1)}, f32[8,128]{1,0:T(8,128)S(1)}, u32[]{:S(2)}, u32[]{:S(2)}) collective-permute-start(f32[8,128]{1,0:T(8,128)S(1)} %late.1), channel_id=1, source_target_pairs={{0,6},{1,7},{2,4},{3,5},{4,2},{5,3},{6,0},{7,1},{8,14},{9,15},{10,... | collective-permute-start | bytes 12296 | tf_op jit(solution)/shard_map/ppermute | solution.py:245

commit v23 on v13

--- a/solution.py
+++ b/solution.py
@@ -208,7 +208,7 @@
     rows, width = c.shape
     return pl.pallas_call(
         middle_kernel,
-        out_shape=[jax.ShapeDtypeStruct((8, rows), jnp.float32)] * 3
+        out_shape=[jax.ShapeDtypeStruct((1, rows), jnp.float32)] * 3
         + [jax.ShapeDtypeStruct((4 * rows, width), jnp.bfloat16)],
         in_specs=(VMEM, VMEM, VMEM, [VMEM] * len(h), [VMEM] * len(ch), *[VMEM] * len(ids)),
         out_specs=[VMEM] * 4,
@@ -228,7 +228,7 @@
 def late(far, xe, ids):
     return pl.pallas_call(
         late_kernel,
-        out_shape=jax.ShapeDtypeStruct((8, far.shape[0] // 4), jnp.float32),
+        out_shape=jax.ShapeDtypeStruct((1, far.shape[0] // 4), jnp.float32),
         in_specs=(VMEM, [VMEM] * len(xe), *[VMEM] * len(ids)),
         out_specs=VMEM,
         compiler_params=LIMIT,

time: 29 us -> 29 us (level)
  other arithmetic: 0.01 us -> 0.52 us
  local copies, waits for them, and re-layouts: 0.54 us -> 0.03 us
    squeeze x0 -> x1, other arithmetic: none -> 0.52 us  [square(): jnp.maximum(jnp.maximum(found, x_best), jnp.maximum(e_best, xe_best))[0]]
    squeeze x1 -> x0, local copies, waits for them, and re-layouts: 0.51 us -> none  [square(): jnp.maximum(jnp.maximum(found, x_best), jnp.maximum(e_best, xe_best))[0]]
where the time goes in v23:
time: 29 us; the launch traced here: 28.8 us
  starting transfers between devices  17.1 us (59%)
  waiting for transfers between devices  8.98 us (31%)
  Pallas kernels  2.09 us (7%)
  other arithmetic  0.52 us (2%)
    ppermute x14, starting transfers between devices, swap(): return lax.ppermute(array, AXES, [(i, i ^ flip) for i in range(16)])  17.1 us
    ppermute x14, waiting for transfers between devices, swap(): return lax.ppermute(array, AXES, [(i, i ^ flip) for i in range(16)])  8.98 us
    pallas_call x1, Pallas kernels, early(): pl.pallas_call(early_kernel, out_shape=[jax.ShapeDtypeStruct((8, 3 * rows...  0.84 us
    pallas_call x1, Pallas kernels, middle(): pl.pallas_call(middle_kernel, out_shape=[jax.ShapeDtypeStruct((1, rows),...  0.68 us
  transfers between devices with their start and end apart: 14, of which 6 were waited for; matrix products, arithmetic and copies ran while one was open for 0% of the time, Pallas kernels for 7%

profile of v23, /device:TPU:0, one launch (start us, length us, event | category | flops | bytes accessed | tf_op | source)
XLA Modules:
  0.0 28.8 jit_solution(8721102113455704562)
XLA Ops:
  0.0 0.0 copy-start.1
  0.0 0.5 %collective-permute-start.2 = (bf16[128,1024]{1,0:T(8,128)(2,1)}, bf16[128,1024]{1,0:T(8,128)(2,1)S(1)}, u32[]{:S(2)}, u32[]{:S(2)}) collective-permute-start(bf16[128,1024]{1,0:T(8,128)(2,1)} %mine_ref.1), channel_id=1, source_target_pairs={{0,1},{1,0},{2,3},{3,2},{4,5},{5,4},{6,7},{7,6},{8,9},{9,8},{10,11... | collective-permute-start | bytes 786440 | tf_op jit(solution)/shard_map/ppermute | solution.py:241
  0.5 2.6 %collective-permute-start.1 = (bf16[128,1024]{1,0:T(8,128)(2,1)}, bf16[128,1024]{1,0:T(8,128)(2,1)S(1)}, u32[]{:S(2)}, u32[]{:S(2)}) collective-permute-start(bf16[128,1024]{1,0:T(8,128)(2,1)} %mine_ref.1), channel_id=1, source_target_pairs={{0,4},{1,5},{2,6},{3,7},{4,0},{5,1},{6,2},{7,3},{8,12},{9,13},{10,... | collective-permute-start | bytes 786440 | tf_op jit(solution)/shard_map/ppermute | solution.py:241
  3.1 1.5 %collective-permute-start = (bf16[128,1024]{1,0:T(8,128)(2,1)}, bf16[128,1024]{1,0:T(8,128)(2,1)S(1)}, u32[]{:S(2)}, u32[]{:S(2)}) collective-permute-start(bf16[128,1024]{1,0:T(8,128)(2,1)} %mine_ref.1), channel_id=1, source_target_pairs={{0,2},{1,3},{2,0},{3,1},{4,6},{5,7},{6,4},{7,5},{8,10},{9,11},{10,... | collective-permute-start | bytes 786440 | tf_op jit(solution)/shard_map/ppermute | solution.py:241
  4.6 0.0 collective-permute-done.2.c_refs_0_
  4.6 2.6 %collective-permute-start.6 = (bf16[128,1024]{1,0:T(8,128)(2,1)}, bf16[128,1024]{1,0:T(8,128)(2,1)S(1)}, u32[]{:S(2)}, u32[]{:S(2)}) collective-permute-start(bf16[128,1024]{1,0:T(8,128)(2,1)} %mine_ref.1), channel_id=1, source_target_pairs={{0,8},{1,9},{2,10},{3,11},{4,12},{5,13},{6,14},{7,15},{8,0},{9,1},... | collective-permute-start | bytes 786440 | tf_op jit(solution)/shard_map/ppermute | solution.py:241
  7.2 0.0 copy-done.1
  7.2 0.0 collective-permute-start.4
  7.2 0.5 %collective-permute-start.3 = (s32[1,128]{1,0:T(1,128)S(1)}, s32[1,128]{1,0:T(1,128)S(1)}, u32[]{:S(2)}, u32[]{:S(2)}) collective-permute-start(s32[1,128]{1,0:T(1,128)S(1)} %bitcast.4), channel_id=1, source_target_pairs={{0,2},{1,3},{2,0},{3,1},{4,6},{5,7},{6,4},{7,5},{8,10},{9,11},{10,... | collective-permute-start | bytes 1544 | tf_op jit(solution)/shard_map/ppermute | solution.py:241
  7.7 0.6 %collective-permute-done.4.c_ids_ref = s32[1,128]{1,0:T(1,128)S(1)} collective-permute-done((s32[1,128]{1,0:T(1,128)S(1)}, s32[1,128]{1,0:T(1,128)S(1)}, u32[]{:S(2)}, u32[]{:S(2)}) %collective-permute-start.4) | collective-permute-done | bytes 544 | tf_op jit(solution)/shard_map/ppermute | solution.py:241
  8.3 3.4 %collective-permute-done.3.x_ids_ref = s32[1,128]{1,0:T(1,128)S(1)} collective-permute-done((s32[1,128]{1,0:T(1,128)S(1)}, s32[1,128]{1,0:T(1,128)S(1)}, u32[]{:S(2)}, u32[]{:S(2)}) %collective-permute-start.3) | collective-permute-done | bytes 544 | tf_op jit(solution)/shard_map/ppermute | solution.py:241
  11.8 2.6 %collective-permute-start.7 = (s32[2,128]{1,0:T(2,128)S(1)}, s32[2,128]{1,0:T(2,128)S(1)}, u32[]{:S(2)}, u32[]{:S(2)}) collective-permute-start(s32[2,128]{1,0:T(2,128)S(1)} %get-tuple-element.25), channel_id=1, source_target_pairs={{0,8},{1,9},{2,10},{3,11},{4,12},{5,13},{6,14},{7,15},{8,0},{9,1},... | collective-permute-start | bytes 3080 | tf_op jit(solution)/shard_map/ppermute | solution.py:241
  14.3 0.0 copy-start
  14.3 0.4 %collective-permute-start.5 = (s32[2,128]{1,0:T(2,128)S(1)}, s32[2,128]{1,0:T(2,128)S(1)}, u32[]{:S(2)}, u32[]{:S(2)}) collective-permute-start(s32[2,128]{1,0:T(2,128)S(1)} %get-tuple-element.26), channel_id=1, source_target_pairs={{0,4},{1,5},{2,6},{3,7},{4,0},{5,1},{6,2},{7,3},{8,12},{9,13},{10,... | collective-permute-start | bytes 3080 | tf_op jit(solution)/shard_map/ppermute | solution.py:241
  14.8 0.0 collective-permute-done.1.e_refs_0_
  14.8 2.3 %collective-permute-start.12 = (bf16[128,1024]{1,0:T(8,128)(2,1)S(1)}, bf16[128,1024]{1,0:T(8,128)(2,1)S(1)}, u32[]{:S(2)}, u32[]{:S(2)}) collective-permute-start(bf16[128,1024]{1,0:T(8,128)(2,1)S(1)} %collective-permute-done.1.e_refs_0_), channel_id=1, source_target_pairs={{0,2},{1,3},{2,0},{3,1},{4,6},{5,7},{6,4},{7,5},{8,10},{9,11},{10,... | collective-permute-start | bytes 786440 | tf_op jit(solution)/shard_map/ppermute | solution.py:241
  17.1 2.4 %collective-permute-done.7.h_ids_ref = s32[2,128]{1,0:T(2,128)S(1)} collective-permute-done((s32[2,128]{1,0:T(2,128)S(1)}, s32[2,128]{1,0:T(2,128)S(1)}, u32[]{:S(2)}, u32[]{:S(2)}) %collective-permute-start.7) | collective-permute-done | bytes 1056 | tf_op jit(solution)/shard_map/ppermute | solution.py:241
  19.6 0.0 collective-permute-done.5.e_ids_ref
  19.6 0.0 collective-permute-done.x_refs_0_
  19.6 0.0 collective-permute-done.6.h_refs_0_
  19.6 0.1 collective-permute-start.9
  19.7 0.5 %collective-permute-start.8 = (bf16[64,1024]{1,0:T(8,128)(2,1)S(1)}, bf16[64,1024]{1,0:T(8,128)(2,1)S(1)}, u32[]{:S(2)}, u32[]{:S(2)}) collective-permute-start(bf16[64,1024]{1,0:T(8,128)(2,1)S(1)} %get-tuple-element.24), channel_id=1, source_target_pairs={{0,1},{1,0},{2,3},{3,2},{4,5},{5,4},{6,7},{7,6},{8,9},{9,8},{10,11... | collective-permute-start | bytes 393224 | tf_op jit(solution)/shard_map/ppermute | solution.py:241
  20.2 0.0 copy-done
  20.2 0.8 %early.1 = (f32[8,384]{1,0:T(8,128)S(1)}, bf16[384,1024]{1,0:T(8,128)(2,1)S(1)}, bf16[128,1024]{1,0:T(8,128)(2,1)S(1)}) custom-call(bf16[128,1024]{1,0:T(8,128)(2,1)S(1)} %copy-done, bf16[128,1024]{1,0:T(8,128)(2,1)S(1)} %collective-permute-done.x_refs_0_, bf16[128,1024]{1,0:T(8,128)(2,1)S(1)} %collective-permute-done.1.e_refs_0_, ...), custom_call_target="tpu_custom_call" | custom-call | tf_op jit(solution)/shard_map/early/pallas_call | solution.py:179
  21.0 0.0 collective-permute-done.9.ch_refs_1_
  21.0 0.2 collective-permute-done.8.ch_refs_0_
  21.2 0.7 %middle.1 = (f32[1,128]{1,0:T(1,128)S(1)}, f32[1,128]{1,0:T(1,128)S(1)}, f32[1,128]{1,0:T(1,128)S(1)}, bf16[512,1024]{1,0:T(8,128)(2,1)S(1)}) custom-call(f32[8,384]{1,0:T(8,128)S(1)} %get-tuple-element.14.best_ref, bf16[384,1024]{1,0:T(8,128)(2,1)S(1)} %get-tuple-element.15.own_ref, bf16[128,1024]{1,0:T(8,128)(2,1)S(1)} %get-tuple-element.16.c_ref, ...), custom_call_target="tpu_custom_call" | custom-call | tf_op jit(solution)/shard_map/middle/pallas_call | solution.py:209
  21.9 0.6 %collective-permute-start.10 = (f32[1,128]{1,0:T(1,128)S(1)}, f32[1,128]{1,0:T(1,128)S(1)}, u32[]{:S(2)}, u32[]{:S(2)}) collective-permute-start(f32[1,128]{1,0:T(1,128)S(1)} %get-tuple-element.20), channel_id=1, source_target_pairs={{0,2},{1,3},{2,0},{3,1},{4,6},{5,7},{6,4},{7,5},{8,10},{9,11},{10,... | collective-permute-start | bytes 1544 | tf_op jit(solution)/shard_map/ppermute | solution.py:241
  22.5 0.6 %collective-permute-start.11 = (f32[1,128]{1,0:T(1,128)S(1)}, f32[1,128]{1,0:T(1,128)S(1)}, u32[]{:S(2)}, u32[]{:S(2)}) collective-permute-start(f32[1,128]{1,0:T(1,128)S(1)} %get-tuple-element.21), channel_id=1, source_target_pairs={{0,4},{1,5},{2,6},{3,7},{4,0},{5,1},{6,2},{7,3},{8,12},{9,13},{10,... | collective-permute-start | bytes 1544 | tf_op jit(solution)/shard_map/ppermute | solution.py:241
  23.1 0.1 collective-permute-done.12.xe_refs_0_
  23.2 0.6 %late.1 = f32[1,128]{1,0:T(1,128)S(1)} custom-call(bf16[512,1024]{1,0:T(8,128)(2,1)S(1)} %get-tuple-element.22.far_ref, bf16[128,1024]{1,0:T(8,128)(2,1)S(1)} %collective-permute-done.12.xe_refs_0_, s32[1,128]{1,0:T(1,128)S(1)} %bitcast.8, s32[1,128]{1,0:T(1,128)S(1)} %collective-permute-done.4.c_ids_ref, s32[2,128]{1,0:T(2,128)S(1)} %collective-permute-done.5.e_ids_ref, ...), custom_call_target="tpu_custom_call" | custom-call | tf_op jit(solution)/shard_map/late/pallas_call | solution.py:229
  23.8 2.3 %collective-permute-start.13 = (f32[1,128]{1,0:T(1,128)S(1)}, f32[1,128]{1,0:T(1,128)S(1)}, u32[]{:S(2)}, u32[]{:S(2)}) collective-permute-start(f32[1,128]{1,0:T(1,128)S(1)} %late.1), channel_id=1, source_target_pairs={{0,6},{1,7},{2,4},{3,5},{4,2},{5,3},{6,0},{7,1},{8,14},{9,15},{10,... | collective-permute-start | bytes 1544 | tf_op jit(solution)/shard_map/ppermute | solution.py:241
  26.1 0.0 collective-permute-done.10
  26.1 0.0 collective-permute-done.11
  26.1 2.2 %collective-permute-done.13 = f32[1,128]{1,0:T(1,128)S(1)} collective-permute-done((f32[1,128]{1,0:T(1,128)S(1)}, f32[1,128]{1,0:T(1,128)S(1)}, u32[]{:S(2)}, u32[]{:S(2)}) %collective-permute-start.13) | collective-permute-done | bytes 544 | tf_op jit(solution)/shard_map/ppermute | solution.py:241
  28.3 0.5 %maximum_bitcast_fusion = f32[128]{0:T(128)} fusion(f32[1,128]{1,0:T(1,128)S(1)} %collective-permute-done.11, f32[1,128]{1,0:T(1,128)S(1)} %collective-permute-done.13, f32[1,128]{1,0:T(1,128)S(1)} %get-tuple-element.19, f32[1,128]{1,0:T(1,128)S(1)} %collective-permute-done.10), kind=kLoop, calls=%fused_computation.2 | loop fusion | flops 384 | bytes 2560 | tf_op jit(solution)/shard_map/squeeze | solution.py:261
  (2 shorter events, 0.0 us)
Async XLA Ops:
  0.0 7.2 %copy-start.1 = (s32[128,1]{0,1:T(1,128)S(1)}, s32[128,1]{0,1:T(1,128)}, u32[]{:S(2)}) copy-start(s32[128,1]{0,1:T(1,128)} %param.3) | copy-start | bytes 1540
  0.0 4.6 %collective-permute-start.2 = (bf16[128,1024]{1,0:T(8,128)(2,1)}, bf16[128,1024]{1,0:T(8,128)(2,1)S(1)}, u32[]{:S(2)}, u32[]{:S(2)}) collective-permute-start(bf16[128,1024]{1,0:T(8,128)(2,1)} %mine_ref.1), channel_id=1, source_target_pairs={{0,1},{1,0},{2,3},{3,2},{4,5},{5,4},{6,7},{7,6},{8,9},{9,8},{10,11... | collective-permute-start | bytes 786440 | tf_op jit(solution)/shard_map/ppermute | solution.py:241
  0.5 14.3 %collective-permute-start.1 = (bf16[128,1024]{1,0:T(8,128)(2,1)}, bf16[128,1024]{1,0:T(8,128)(2,1)S(1)}, u32[]{:S(2)}, u32[]{:S(2)}) collective-permute-start(bf16[128,1024]{1,0:T(8,128)(2,1)} %mine_ref.1), channel_id=1, source_target_pairs={{0,4},{1,5},{2,6},{3,7},{4,0},{5,1},{6,2},{7,3},{8,12},{9,13},{10,... | collective-permute-start | bytes 786440 | tf_op jit(solution)/shard_map/ppermute | solution.py:241
  3.1 16.5 %collective-permute-start = (bf16[128,1024]{1,0:T(8,128)(2,1)}, bf16[128,1024]{1,0:T(8,128)(2,1)S(1)}, u32[]{:S(2)}, u32[]{:S(2)}) collective-permute-start(bf16[128,1024]{1,0:T(8,128)(2,1)} %mine_ref.1), channel_id=1, source_target_pairs={{0,2},{1,3},{2,0},{3,1},{4,6},{5,7},{6,4},{7,5},{8,10},{9,11},{10,... | collective-permute-start | bytes 786440 | tf_op jit(solution)/shard_map/ppermute | solution.py:241
  4.6 15.0 %collective-permute-start.6 = (bf16[128,1024]{1,0:T(8,128)(2,1)}, bf16[128,1024]{1,0:T(8,128)(2,1)S(1)}, u32[]{:S(2)}, u32[]{:S(2)}) collective-permute-start(bf16[128,1024]{1,0:T(8,128)(2,1)} %mine_ref.1), channel_id=1, source_target_pairs={{0,8},{1,9},{2,10},{3,11},{4,12},{5,13},{6,14},{7,15},{8,0},{9,1},... | collective-permute-start | bytes 786440 | tf_op jit(solution)/shard_map/ppermute | solution.py:241
  7.2 1.1 %collective-permute-start.4 = (s32[1,128]{1,0:T(1,128)S(1)}, s32[1,128]{1,0:T(1,128)S(1)}, u32[]{:S(2)}, u32[]{:S(2)}) collective-permute-start(s32[1,128]{1,0:T(1,128)S(1)} %bitcast.3), channel_id=1, source_target_pairs={{0,1},{1,0},{2,3},{3,2},{4,5},{5,4},{6,7},{7,6},{8,9},{9,8},{10,11... | collective-permute-start | bytes 1544 | tf_op jit(solution)/shard_map/ppermute | solution.py:241
  7.2 4.6 %collective-permute-start.3 = (s32[1,128]{1,0:T(1,128)S(1)}, s32[1,128]{1,0:T(1,128)S(1)}, u32[]{:S(2)}, u32[]{:S(2)}) collective-permute-start(s32[1,128]{1,0:T(1,128)S(1)} %bitcast.4), channel_id=1, source_target_pairs={{0,2},{1,3},{2,0},{3,1},{4,6},{5,7},{6,4},{7,5},{8,10},{9,11},{10,... | collective-permute-start | bytes 1544 | tf_op jit(solution)/shard_map/ppermute | solution.py:241
  11.8 7.8 %collective-permute-start.7 = (s32[2,128]{1,0:T(2,128)S(1)}, s32[2,128]{1,0:T(2,128)S(1)}, u32[]{:S(2)}, u32[]{:S(2)}) collective-permute-start(s32[2,128]{1,0:T(2,128)S(1)} %get-tuple-element.25), channel_id=1, source_target_pairs={{0,8},{1,9},{2,10},{3,11},{4,12},{5,13},{6,14},{7,15},{8,0},{9,1},... | collective-permute-start | bytes 3080 | tf_op jit(solution)/shard_map/ppermute | solution.py:241
  14.3 5.8 %copy-start = (bf16[128,1024]{1,0:T(8,128)(2,1)S(1)}, bf16[128,1024]{1,0:T(8,128)(2,1)}, u32[]{:S(2)}) copy-start(bf16[128,1024]{1,0:T(8,128)(2,1)} %mine_ref.1) | copy-start | bytes 786436
  14.3 5.2 %collective-permute-start.5 = (s32[2,128]{1,0:T(2,128)S(1)}, s32[2,128]{1,0:T(2,128)S(1)}, u32[]{:S(2)}, u32[]{:S(2)}) collective-permute-start(s32[2,128]{1,0:T(2,128)S(1)} %get-tuple-element.26), channel_id=1, source_target_pairs={{0,4},{1,5},{2,6},{3,7},{4,0},{5,1},{6,2},{7,3},{8,12},{9,13},{10,... | collective-permute-start | bytes 3080 | tf_op jit(solution)/shard_map/ppermute | solution.py:241
  14.8 8.4 %collective-permute-start.12 = (bf16[128,1024]{1,0:T(8,128)(2,1)S(1)}, bf16[128,1024]{1,0:T(8,128)(2,1)S(1)}, u32[]{:S(2)}, u32[]{:S(2)}) collective-permute-start(bf16[128,1024]{1,0:T(8,128)(2,1)S(1)} %collective-permute-done.1.e_refs_0_), channel_id=1, source_target_pairs={{0,2},{1,3},{2,0},{3,1},{4,6},{5,7},{6,4},{7,5},{8,10},{9,11},{10,... | collective-permute-start | bytes 786440 | tf_op jit(solution)/shard_map/ppermute | solution.py:241
  19.6 1.4 %collective-permute-start.9 = (bf16[64,1024]{1,0:T(8,128)(2,1)S(1)}, bf16[64,1024]{1,0:T(8,128)(2,1)S(1)}, u32[]{:S(2)}, u32[]{:S(2)}) collective-permute-start(bf16[64,1024]{1,0:T(8,128)(2,1)S(1)} %get-tuple-element.23), channel_id=1, source_target_pairs={{0,1},{1,0},{2,3},{3,2},{4,5},{5,4},{6,7},{7,6},{8,9},{9,8},{10,11... | collective-permute-start | bytes 393224 | tf_op jit(solution)/shard_map/ppermute | solution.py:241
  19.7 1.5 %collective-permute-start.8 = (bf16[64,1024]{1,0:T(8,128)(2,1)S(1)}, bf16[64,1024]{1,0:T(8,128)(2,1)S(1)}, u32[]{:S(2)}, u32[]{:S(2)}) collective-permute-start(bf16[64,1024]{1,0:T(8,128)(2,1)S(1)} %get-tuple-element.24), channel_id=1, source_target_pairs={{0,1},{1,0},{2,3},{3,2},{4,5},{5,4},{6,7},{7,6},{8,9},{9,8},{10,11... | collective-permute-start | bytes 393224 | tf_op jit(solution)/shard_map/ppermute | solution.py:241
  21.9 4.2 %collective-permute-start.10 = (f32[1,128]{1,0:T(1,128)S(1)}, f32[1,128]{1,0:T(1,128)S(1)}, u32[]{:S(2)}, u32[]{:S(2)}) collective-permute-start(f32[1,128]{1,0:T(1,128)S(1)} %get-tuple-element.20), channel_id=1, source_target_pairs={{0,2},{1,3},{2,0},{3,1},{4,6},{5,7},{6,4},{7,5},{8,10},{9,11},{10,... | collective-permute-start | bytes 1544 | tf_op jit(solution)/shard_map/ppermute | solution.py:241
  22.5 3.6 %collective-permute-start.11 = (f32[1,128]{1,0:T(1,128)S(1)}, f32[1,128]{1,0:T(1,128)S(1)}, u32[]{:S(2)}, u32[]{:S(2)}) collective-permute-start(f32[1,128]{1,0:T(1,128)S(1)} %get-tuple-element.21), channel_id=1, source_target_pairs={{0,4},{1,5},{2,6},{3,7},{4,0},{5,1},{6,2},{7,3},{8,12},{9,13},{10,... | collective-permute-start | bytes 1544 | tf_op jit(solution)/shard_map/ppermute | solution.py:241
  23.8 4.5 %collective-permute-start.13 = (f32[1,128]{1,0:T(1,128)S(1)}, f32[1,128]{1,0:T(1,128)S(1)}, u32[]{:S(2)}, u32[]{:S(2)}) collective-permute-start(f32[1,128]{1,0:T(1,128)S(1)} %late.1), channel_id=1, source_target_pairs={{0,6},{1,7},{2,4},{3,5},{4,2},{5,3},{6,0},{7,1},{8,14},{9,15},{10,... | collective-permute-start | bytes 1544 | tf_op jit(solution)/shard_map/ppermute | solution.py:241
